TPU v7x, 32 devices: a whole 2x2x4 slice. The times are simulated.
32 devices in a mesh: dp: 8 (over z, y), fsdp: 4 (over x, core).
Axes of the slice: x: 2, y: 2, z: 4, core: 2. Of those that a mesh axis runs over, the one named last changes fastest.
Arguments:
- tokens: bfloat16 [2, 32, 512, 768], P(None, ('dp', 'fsdp')), may hold values from -6 to 6
- lengths: int32 [2, 32], P(None, ('dp', 'fsdp')), may hold values from 1 to 512, 10240 in all within a row
- cotangent: bfloat16 [2, 32, 512, 768], P(None, ('dp', 'fsdp')), may hold values from -6 to 6
- query_weight: bfloat16 [768, 768], P('dp', 'fsdp'), may hold values from -0.21875 to 0.21875
- key_weight: bfloat16 [768, 768], P('dp', 'fsdp'), may hold values from -0.21875 to 0.21875
- value_weight: bfloat16 [768, 768], P('dp', 'fsdp'), may hold values from -0.21875 to 0.21875
- output_weight: bfloat16 [768, 768], P('dp', 'fsdp'), may hold values from -1.75 to 1.75
- inner_weight: bfloat16 [768, 3072], P('dp', 'fsdp'), may hold values from -0.21875 to 0.21875
- outer_weight: bfloat16 [3072, 768], P('dp', 'fsdp'), may hold values from -0.109375 to 0.109375
- bias_vectors: bfloat16 [4, 768], P(None, 'dp'), may hold values from -3 to 3
- bias_hidden: bfloat16 [3072], P('dp'), may hold values from -3 to 3
- norm_gains: bfloat16 [2, 768], P(None, 'dp'), may hold values from 0.099609375 to 1.8984375
- norm_shifts: bfloat16 [2, 768], P(None, 'dp'), may hold values from -3 to 3
Outputs:
- activations: bfloat16 [2, 32, 512, 768], P(None, ('dp', 'fsdp'))
- input_grad: bfloat16 [2, 32, 512, 768], P(None, ('dp', 'fsdp'))
- query_grad: float32 [768, 768], P('dp', 'fsdp')
- key_grad: float32 [768, 768], P('dp', 'fsdp')
- value_grad: float32 [768, 768], P('dp', 'fsdp')
- output_grad: float32 [768, 768], P('dp', 'fsdp')
- inner_grad: float32 [768, 3072], P('dp', 'fsdp')
- outer_grad: float32 [3072, 768], P('dp', 'fsdp')
- bias_grads: float32 [4, 768], P(None, 'dp')
- hidden_grad: float32 [3072], P('dp')
- gains_grad: float32 [2, 768], P(None, 'dp')
- shifts_grad: float32 [2, 768], P(None, 'dp')
Inputs may be any that keep to these rules, and one draw needn't show every extreme that they name: In each micro-batch the lengths sum to 10240 and the largest is exactly 512.
All inputs are finite; a program needn't handle non-finite values. No bound on the sum of `lengths` on one device may be relied on, other than what follows from the above.
Results may differ from a plain program's by a relative error of at most 0.015.
Values may be sent and summed in bfloat16 or wider, within the bound.
No kernel may reach another device: no remote copies, remote signals or barrier semaphores. Data moves between devices by JAX's collectives and lax.ppermute only.
A program may use at most 192 MiB of HBM per device.

v0:
```python
import jax
import jax.numpy as jnp
from jax import lax
from jax.sharding import PartitionSpec as P

HEADS = 12


EPSILON = 1e-12
MASKED = -1000000000.0


def split_up(value, dim, size):
    before, after = (value.shape[:dim], value.shape[dim + 1 :])
    return jnp.moveaxis(value.reshape(*before, size, -1, *after), dim, 0)


def sum_at_owner(value, axis, dim):
    size = lax.axis_size(axis)
    parts = lax.all_to_all(split_up(value, dim, size), axis, 0, 0, tiled=True)
    return jnp.sum(parts.astype(jnp.float32), axis=0)


def side_by_side(arrays, axis, dim, along):
    ends, at = ([], 0)
    for a in arrays[:-1]:
        at += a.shape[along]
        ends.append(at)
    both = jnp.concatenate(arrays, axis=along)
    return tuple(jnp.split(sum_at_owner(both, axis, dim), ends, axis=along))


def normalize(values):
    centered = values - jnp.mean(values, axis=-1, keepdims=True)
    variance = jnp.mean(centered * centered, axis=-1, keepdims=True)
    factor = lax.rsqrt(variance + EPSILON)
    return (centered * factor, factor)


def norm_back(upward, normed, factor):
    return factor * (
        upward
        - jnp.mean(upward, axis=-1, keepdims=True)
        - normed * jnp.mean(upward * normed, axis=-1, keepdims=True)
    )


def gelu_slope(hidden_pre):
    cumulative = 0.5 * (1.0 + lax.erf(hidden_pre * 0.7071067811865476))
    return cumulative + hidden_pre * jnp.exp(-0.5 * hidden_pre * hidden_pre) * 0.3989422804014327


def outer_sum(left, right):
    return lax.dot_general(
        left, right, (((0,), (0,)), ((), ())), preferred_element_type=jnp.float32
    )


def back_product(upward, weight):
    return lax.dot_general(
        upward, weight, (((1,), (1,)), ((), ())), preferred_element_type=jnp.float32
    )


def column_sums(values):
    return jnp.sum(values.astype(jnp.float32), axis=0)


def masked_scores(queries, keys_seq, length):
    factor = queries.shape[-1] ** (-0.5)
    scores = (
        jnp.einsum("qhd,khd->hqk", queries, keys_seq, preferred_element_type=jnp.float32) * factor
    )
    visible = lax.broadcasted_iota(jnp.int32, scores.shape, 2) < length
    return (jnp.where(visible, scores, MASKED), factor)


def attend_forward(inputs):
    queries, keys_seq, values_seq, length = inputs
    scores, factor = masked_scores(queries, keys_seq, length)
    highest = jnp.max(scores, axis=-1, keepdims=True)
    exponent = jnp.exp(scores - highest)
    row_total = jnp.sum(exponent, axis=-1, keepdims=True)
    soft_low = (exponent / row_total).astype(jnp.bfloat16)
    blended = jnp.einsum("hqk,khd->qhd", soft_low, values_seq, preferred_element_type=jnp.float32)
    return (blended.reshape(blended.shape[0], -1), (highest + jnp.log(row_total))[..., 0])


def attend_backward(inputs):
    queries, keys_seq, values_seq, upward, logsum, length = inputs
    scores, factor = masked_scores(queries, keys_seq, length)
    soft = jnp.exp(scores - logsum[..., None])
    soft_low = soft.astype(jnp.bfloat16)
    upward_heads = upward.reshape(queries.shape)
    grad_soft = jnp.einsum(
        "qhd,khd->hqk", upward_heads, values_seq, preferred_element_type=jnp.float32
    )
    grad_values = jnp.einsum(
        "hqk,qhd->khd", soft_low, upward_heads, preferred_element_type=jnp.float32
    )
    inner = jnp.sum(soft * grad_soft, axis=-1, keepdims=True)
    scores_low = (soft * (grad_soft - inner)).astype(jnp.bfloat16)
    grad_queries = (
        jnp.einsum("hqk,khd->qhd", scores_low, keys_seq, preferred_element_type=jnp.float32)
        * factor
    )
    grad_keys = (
        jnp.einsum("hqk,qhd->khd", scores_low, queries, preferred_element_type=jnp.float32) * factor
    )
    row_count = queries.shape[0]
    return (
        grad_queries.reshape(row_count, -1),
        grad_keys.reshape(row_count, -1),
        grad_values.reshape(row_count, -1),
    )


def gather_forward(shards):
    (
        query_part,
        key_part,
        value_part,
        output_part,
        inner_part,
        outer_part,
        bias_part,
        hidden_part,
        gain_part,
        shift_part,
    ) = shards
    column_full = (
        lax.all_gather(query_part, "fsdp", axis=1, tiled=True),
        lax.all_gather(key_part, "fsdp", axis=1, tiled=True),
        lax.all_gather(value_part, "fsdp", axis=1, tiled=True),
        lax.all_gather(output_part, "fsdp", axis=1, tiled=True),
        lax.all_gather(inner_part, "fsdp", axis=1, tiled=True),
        lax.all_gather(outer_part, "fsdp", axis=1, tiled=True),
    )
    return (
        lax.all_gather(column_full[0], "dp", axis=0, tiled=True),
        lax.all_gather(column_full[1], "dp", axis=0, tiled=True),
        lax.all_gather(column_full[2], "dp", axis=0, tiled=True),
        lax.all_gather(column_full[3], "dp", axis=0, tiled=True),
        lax.all_gather(column_full[4], "dp", axis=0, tiled=True),
        lax.all_gather(column_full[5], "dp", axis=0, tiled=True),
        lax.all_gather(bias_part, "dp", axis=1, tiled=True),
        lax.all_gather(hidden_part, "dp", axis=0, tiled=True),
        lax.all_gather(gain_part, "dp", axis=1, tiled=True),
        lax.all_gather(shift_part, "dp", axis=1, tiled=True),
    )


def gather_backward(shards):
    (
        query_part,
        key_part,
        value_part,
        output_part,
        inner_part,
        outer_part,
        bias_part,
        hidden_part,
        gain_part,
        shift_part,
    ) = shards
    column_full = (
        lax.all_gather(query_part, "fsdp", axis=1, tiled=True),
        lax.all_gather(key_part, "fsdp", axis=1, tiled=True),
        lax.all_gather(value_part, "fsdp", axis=1, tiled=True),
        lax.all_gather(output_part, "fsdp", axis=1, tiled=True),
        lax.all_gather(inner_part, "fsdp", axis=1, tiled=True),
        lax.all_gather(outer_part, "fsdp", axis=1, tiled=True),
    )
    return (
        lax.all_gather(column_full[0], "dp", axis=0, tiled=True),
        lax.all_gather(column_full[1], "dp", axis=0, tiled=True),
        lax.all_gather(column_full[2], "dp", axis=0, tiled=True),
        lax.all_gather(column_full[3], "dp", axis=0, tiled=True),
        lax.all_gather(column_full[4], "dp", axis=0, tiled=True),
        lax.all_gather(column_full[5], "dp", axis=0, tiled=True),
        lax.all_gather(bias_part, "dp", axis=1, tiled=True),
        lax.all_gather(hidden_part, "dp", axis=0, tiled=True),
        lax.all_gather(gain_part, "dp", axis=1, tiled=True),
        lax.all_gather(shift_part, "dp", axis=1, tiled=True),
    )


def reduce_grads(grads):
    (
        query_grad,
        key_grad,
        value_grad,
        output_grad,
        inner_grad,
        outer_grad,
        bias_grad,
        hidden_grad,
        gain_grad,
        shift_grad,
    ) = grads
    bias_grad, hidden_grad, gain_grad, shift_grad = (
        lax.psum(bias_grad.astype(jnp.bfloat16), "fsdp").astype(jnp.float32),
        lax.psum(hidden_grad.astype(jnp.bfloat16), "fsdp").astype(jnp.float32),
        lax.psum(gain_grad.astype(jnp.bfloat16), "fsdp").astype(jnp.float32),
        lax.psum(shift_grad.astype(jnp.bfloat16), "fsdp").astype(jnp.float32),
    )
    narrow = (
        lax.psum_scatter(
            query_grad.astype(jnp.bfloat16), "fsdp", scatter_dimension=1, tiled=True
        ).astype(jnp.float32),
        lax.psum_scatter(
            key_grad.astype(jnp.bfloat16), "fsdp", scatter_dimension=1, tiled=True
        ).astype(jnp.float32),
        lax.psum_scatter(
            value_grad.astype(jnp.bfloat16), "fsdp", scatter_dimension=1, tiled=True
        ).astype(jnp.float32),
        lax.psum_scatter(
            output_grad.astype(jnp.bfloat16), "fsdp", scatter_dimension=1, tiled=True
        ).astype(jnp.float32),
        lax.psum_scatter(
            inner_grad.astype(jnp.bfloat16), "fsdp", scatter_dimension=1, tiled=True
        ).astype(jnp.float32),
        lax.psum_scatter(
            outer_grad.astype(jnp.bfloat16), "fsdp", scatter_dimension=1, tiled=True
        ).astype(jnp.float32),
    )
    return (
        *side_by_side(
            (
                narrow[0].astype(jnp.bfloat16),
                narrow[1].astype(jnp.bfloat16),
                narrow[2].astype(jnp.bfloat16),
                narrow[3].astype(jnp.bfloat16),
                narrow[4].astype(jnp.bfloat16),
            ),
            "dp",
            0,
            1,
        ),
        sum_at_owner(narrow[5].astype(jnp.bfloat16), "dp", 0),
        sum_at_owner(bias_grad.astype(jnp.bfloat16), "dp", 1),
        sum_at_owner(hidden_grad.astype(jnp.bfloat16), "dp", 0),
        *side_by_side(
            (gain_grad.astype(jnp.bfloat16), shift_grad.astype(jnp.bfloat16)), "dp", 1, 0
        ),
    )


def layer_step(inputs, length_row, upstream, forward_weights, backward_weights):
    (
        query_full,
        key_full,
        value_full,
        output_full,
        inner_full,
        outer_full,
        bias_full,
        hidden_full,
        gain_full,
        shift_full,
    ) = forward_weights
    query_back, key_back, value_back, output_back, inner_back, outer_back = backward_weights[:6]
    seq_count, seq_len, model_width = inputs.shape
    row_count = seq_count * seq_len
    flat_rows = inputs.reshape(row_count, model_width)
    row_mask = lax.broadcasted_iota(jnp.int32, (seq_count, seq_len), 1) < length_row[:, None]
    row_mask = row_mask.astype(jnp.float32).reshape(row_count, 1)
    bias_rows = bias_full.astype(jnp.float32)
    gain_rows = gain_full.astype(jnp.float32)
    shift_rows = shift_full.astype(jnp.float32)
    hidden_bias = hidden_full.astype(jnp.float32)
    shape_heads = (seq_count, seq_len, HEADS, model_width // HEADS)
    queries = (
        jnp.dot(flat_rows, query_full, preferred_element_type=jnp.float32) + bias_rows[0]
    ).astype(jnp.bfloat16)
    keys_all = jnp.dot(flat_rows, key_full, preferred_element_type=jnp.float32).astype(jnp.bfloat16)
    values_all = (
        jnp.dot(flat_rows, value_full, preferred_element_type=jnp.float32) + bias_rows[1]
    ).astype(jnp.bfloat16)
    query_heads = queries.reshape(shape_heads)
    key_heads = keys_all.reshape(shape_heads)
    value_heads = values_all.reshape(shape_heads)
    blended, logsum = lax.map(attend_forward, (query_heads, key_heads, value_heads, length_row))
    attended = blended.reshape(row_count, model_width).astype(jnp.bfloat16)
    first_sum = (
        flat_rows.astype(jnp.float32)
        + jnp.dot(attended, output_full, preferred_element_type=jnp.float32)
        + bias_rows[2]
    )
    normed_one, factor_one = normalize(first_sum)
    middle = normed_one * gain_rows[0] + shift_rows[0]
    middle_low = middle.astype(jnp.bfloat16)
    hidden_pre = jnp.dot(middle_low, inner_full, preferred_element_type=jnp.float32) + hidden_bias
    activated = jax.nn.gelu(hidden_pre, approximate=False).astype(jnp.bfloat16)
    second = (
        middle + jnp.dot(activated, outer_full, preferred_element_type=jnp.float32) + bias_rows[3]
    )
    normed_two, factor_two = normalize(second)
    outputs = ((normed_two * gain_rows[1] + shift_rows[1]) * row_mask).astype(jnp.bfloat16)
    upward = upstream.reshape(row_count, model_width).astype(jnp.float32) * row_mask
    gain_two = jnp.sum(upward * normed_two, axis=0)
    shift_two = jnp.sum(upward, axis=0)
    grad_second = norm_back(upward * gain_rows[1], normed_two, factor_two)
    second_low = grad_second.astype(jnp.bfloat16)
    outer_grad = outer_sum(activated, second_low)
    hidden_low = (back_product(second_low, outer_back) * gelu_slope(hidden_pre)).astype(
        jnp.bfloat16
    )
    inner_grad = outer_sum(middle_low, hidden_low)
    grad_middle = grad_second + back_product(hidden_low, inner_back)
    gain_one = jnp.sum(grad_middle * normed_one, axis=0)
    shift_one = jnp.sum(grad_middle, axis=0)
    grad_first = norm_back(grad_middle * gain_rows[0], normed_one, factor_one)
    branch_low = grad_first.astype(jnp.bfloat16)
    output_grad = outer_sum(attended, branch_low)
    attended_low = back_product(branch_low, output_back).astype(jnp.bfloat16)
    grad_queries, grad_keys, grad_values = lax.map(
        attend_backward,
        (
            query_heads,
            key_heads,
            value_heads,
            attended_low.reshape(seq_count, seq_len, model_width),
            logsum,
            length_row,
        ),
    )
    queries_low = grad_queries.reshape(row_count, model_width).astype(jnp.bfloat16)
    keys_low = grad_keys.reshape(row_count, model_width).astype(jnp.bfloat16)
    values_low = grad_values.reshape(row_count, model_width).astype(jnp.bfloat16)
    query_grad = outer_sum(flat_rows, queries_low)
    key_grad = outer_sum(flat_rows, keys_low)
    value_grad = outer_sum(flat_rows, values_low)
    grad_inputs = (
        grad_first
        + back_product(queries_low, query_back)
        + back_product(keys_low, key_back)
        + back_product(values_low, value_back)
    )
    bias_grad = jnp.stack(
        [
            column_sums(queries_low),
            column_sums(values_low),
            column_sums(branch_low),
            column_sums(second_low),
        ]
    )
    grads = (
        query_grad,
        key_grad,
        value_grad,
        output_grad,
        inner_grad,
        outer_grad,
        bias_grad,
        column_sums(hidden_low),
        jnp.stack([gain_one, gain_two]),
        jnp.stack([shift_one, shift_two]),
    )
    return (
        outputs.reshape(inputs.shape),
        grad_inputs.astype(jnp.bfloat16).reshape(inputs.shape),
        grads,
    )


def on_device(
    tokens,
    lengths,
    cotangent,
    query_weight,
    key_weight,
    value_weight,
    output_weight,
    inner_weight,
    outer_weight,
    bias_vectors,
    bias_hidden,
    norm_gains,
    norm_shifts,
):
    shards = (
        query_weight,
        key_weight,
        value_weight,
        output_weight,
        inner_weight,
        outer_weight,
        bias_vectors,
        bias_hidden,
        norm_gains,
        norm_shifts,
    )
    totals = None
    out_list = []
    grad_list = []
    for micro_batch in range(tokens.shape[0]):
        forward_weights = gather_forward(shards)
        backward_weights = gather_backward(shards)
        outputs, grad_inputs, step_grads = layer_step(
            tokens[micro_batch],
            lengths[micro_batch],
            cotangent[micro_batch],
            forward_weights,
            backward_weights,
        )
        out_list.append(outputs)
        grad_list.append(grad_inputs)
        if totals is None:
            totals = step_grads
        else:
            totals = jax.tree.map(jnp.add, totals, step_grads)
    totals = reduce_grads(totals)
    activations = jnp.stack(out_list)
    input_grad = jnp.stack(grad_list)
    return (
        activations,
        input_grad,
        totals[0],
        totals[1],
        totals[2],
        totals[3],
        totals[4],
        totals[5],
        totals[6],
        totals[7],
        totals[8],
        totals[9],
    )


def solution(mesh):
    placed = (
        P(None, ("dp", "fsdp"), None, None),
        P(None, ("dp", "fsdp")),
        P(None, ("dp", "fsdp"), None, None),
        P("dp", "fsdp"),
        P("dp", "fsdp"),
        P("dp", "fsdp"),
        P("dp", "fsdp"),
        P("dp", "fsdp"),
        P("dp", "fsdp"),
        P(None, "dp"),
        P("dp"),
        P(None, "dp"),
        P(None, "dp"),
    )
    return jax.shard_map(
        on_device,
        mesh=mesh,
        in_specs=placed,
        out_specs=(
            P(None, ("dp", "fsdp"), None, None),
            P(None, ("dp", "fsdp"), None, None),
            P("dp", "fsdp"),
            P("dp", "fsdp"),
            P("dp", "fsdp"),
            P("dp", "fsdp"),
            P("dp", "fsdp"),
            P("dp", "fsdp"),
            P(None, "dp"),
            P("dp"),
            P(None, "dp"),
            P(None, "dp"),
        ),
        check_vma=False,
    )
```

profile of v0, /device:TPU:0, one launch (start us, length us, event | category | flops | bytes accessed | tf_op | source)
XLA Modules:
  0.0 664.5 jit_solution(2161359432936402886)
XLA Ops:
  8.2 7.0 %all_gather.35 = bf16[96,768]{0,1:T(8,128)(2,1)S(1)} all-gather(bf16[96,192]{0,1:T(8,128)(2,1)S(1)} %copy.175), channel_id=1, replica_groups=mesh['dp'=8,'fsdp'=4] {'fsdp'}, dimensions={1}, use_global_device_ids=true | all-gather | bytes 184320 | tf_op jit(solution)/shard_map/all_gather | solution.py:132
  16.9 5.6 all_gather.37
  23.5 5.6 all_gather.32
  30.1 5.6 all_gather.39
  36.6 8.3 %all_gather.43 = bf16[96,3072]{1,0:T(8,128)(2,1)} all-gather(bf16[96,768]{1,0:T(8,128)(2,1)S(1)} %copy-done.51), channel_id=1, replica_groups=mesh['dp'=8,'fsdp'=4] {'fsdp'}, dimensions={1}, use_global_device_ids=true | all-gather | bytes 737280 | tf_op jit(solution)/shard_map/all_gather | solution.py:136
  45.1 8.1 %all_gather.46 = bf16[384,768]{0,1:T(8,128)(2,1)} all-gather(bf16[384,192]{0,1:T(8,128)(2,1)S(1)} %copy-done.52), channel_id=1, replica_groups=mesh['dp'=8,'fsdp'=4] {'fsdp'}, dimensions={1}, use_global_device_ids=true | all-gather | bytes 737280 | tf_op jit(solution)/shard_map/all_gather | solution.py:137
  57.0 20.8 %all-gather.1 = bf16[8,96,2]{1,2,0:T(2,128)(2,1)S(1)} all-gather(bf16[1,96,2]{1,2,0:T(2,128)(2,1)S(1)} %bitcast.234), channel_id=1, replica_groups=mesh['dp'=8,'fsdp'=4] {'dp'}, dimensions={0}, use_global_device_ids=true | all-gather | bytes 3456 | tf_op jit(solution)/shard_map/all_gather | solution.py:148
  78.0 16.2 %all-gather.2 = bf16[8,96,2]{1,2,0:T(2,128)(2,1)S(1)} all-gather(bf16[1,96,2]{1,2,0:T(2,128)(2,1)S(1)} %bitcast.235), channel_id=1, replica_groups=mesh['dp'=8,'fsdp'=4] {'dp'}, dimensions={0}, use_global_device_ids=true | all-gather | bytes 3456 | tf_op jit(solution)/shard_map/all_gather | solution.py:149
  94.2 18.4 %all-gather = bf16[8,96,4]{1,2,0:T(4,128)(2,1)S(1)} all-gather(bf16[1,96,4]{1,2,0:T(4,128)(2,1)S(1)} %bitcast.233), channel_id=1, replica_groups=mesh['dp'=8,'fsdp'=4] {'dp'}, dimensions={0}, use_global_device_ids=true | all-gather | bytes 6912 | tf_op jit(solution)/shard_map/all_gather | solution.py:146
  112.7 26.2 %all-gather.3 = bf16[8,1,384]{2,1,0:T(2,128)(2,1)S(1)} all-gather(bf16[1,1,384]{2,1,0:T(2,128)(2,1)S(1)} %reshape.286), channel_id=1, replica_groups=mesh['dp'=8,'fsdp'=4] {'dp'}, dimensions={0}, use_global_device_ids=true | all-gather | bytes 6912 | tf_op jit(solution)/shard_map/all_gather | solution.py:147
  148.4 3.2 convolution_convert_fusion.3
  153.1 3.2 add_convert_fusion.9
  163.8 3.7 fusion.135
  174.8 11.5 %all-gather.17.cloned.1.call-done = bf16[768,768]{1,0:T(8,128)(2,1)} async-done(((bf16[96,768]{1,0:T(8,128)(2,1)}), bf16[768,768]{1,0:T(8,128)(2,1)}) %all-gather.17.cloned.1.call-update) | async-done | bytes 1179664 | tf_op jit(solution)/shard_map/all_gather | solution.py:143
  186.4 3.3 fusion.136
  194.6 3.1 copy-done.1
  202.5 64.6 %all-gather.19.cloned.1.call-done = bf16[768,3072]{1,0:T(8,128)(2,1)} async-done(((bf16[96,3072]{1,0:T(8,128)(2,1)}), bf16[768,3072]{1,0:T(8,128)(2,1)}) %all-gather.19.cloned.1.call-update) | async-done | bytes 4718608 | tf_op jit(solution)/shard_map/all_gather | solution.py:144
  267.1 4.8 fusion.124
  274.7 32.1 %fusion.6 = (bf16[512,3072]{1,0:T(8,128)(2,1)}, bf16[512,3072]{1,0:T(8,128)(2,1)S(1)}, f32[512,3072]{1,0:T(8,128)}) fusion(f32[3072]{0:T(1024)S(1)} %bitcast.230, f32[512,3072]{1,0:T(8,128)S(1)} %fusion.124, bf16[768,3072]{1,0:T(8,128)(2,1)S(1)} %copy-done.66, f32[512,768]{1,0:T(8,128)S(1)} %copy-done.45, f32[768]{0:T(1024)S(1)} %get-tuple-element.140, ...), kind=kOutput, calls=%fused_computation.24 | convolution fusion | flops 2625503232 | bytes 25188352 | tf_op jit(solution)/shard_map/dot_general | solution.py:293
  306.8 41.4 %all-gather.21.cloned.1.call-done = bf16[3072,768]{0,1:T(8,128)(2,1)} async-done(((bf16[384,768]{0,1:T(8,128)(2,1)}), bf16[3072,768]{0,1:T(8,128)(2,1)}) %all-gather.21.cloned.1.call-update) | async-done | bytes 4718608 | tf_op jit(solution)/shard_map/all_gather | solution.py:145
  348.2 6.7 %fusion.140 = (f32[512]{0:T(512)S(1)}, f32[512,768]{1,0:T(8,128)S(1)}) fusion(f32[768]{0:T(1024)S(1)} %get-tuple-element.123, bf16[512,3072]{1,0:T(8,128)(2,1)} %get-tuple-element.162, bf16[3072,768]{0,1:T(8,128)(2,1)} %all-gather.21.cloned.1.call-done, f32[768]{0:T(1024)S(1)} %get-tuple-element.140, f32[768]{0:T(1024)S(1)} %get-tuple-element.203, ...), kind=kOutput, calls=%fused_computation.262 | convolution fusion | flops 2418671104 | bytes 11025408 | tf_op jit(solution)/shard_map/dot_general | solution.py:296
  367.8 4.4 add_convert_fusion
  373.6 8.0 %convert_reduce_fusion.1 = (f32[3072]{0:T(1024)S(1)}, bf16[512,3072]{1,0:T(8,128)(2,1)S(1)}) fusion(f32[512,3072]{1,0:T(8,128)} %get-tuple-element.180, f32[3072]{0:T(1024)S(1)} %bitcast.231, bf16[3072,768]{0,1:T(8,128)(2,1)} %all-gather.21.cloned.1.call-done, f32[512,768]{1,0:T(8,128)S(1)} %copy-done.30), kind=kOutput, calls=%fused_computation.43 | convolution fusion | flops 2436756480 | bytes 15753216 | tf_op jit(solution)/shard_map/dot_general | solution.py:60
  381.6 6.6 multiply_reduce_fusion.3
  388.3 8.0 %convert_reduce_fusion = (f32[3072]{0:T(1024)S(1)}, bf16[512,3072]{1,0:T(8,128)(2,1)S(1)}) fusion(f32[512,3072]{1,0:T(8,128)} %copy-done.72, f32[3072]{0:T(1024)S(1)} %bitcast.232, bf16[3072,768]{0,1:T(8,128)(2,1)} %all-gather.21.cloned.1.call-done, f32[512,768]{1,0:T(8,128)S(1)} %copy-done.33), kind=kOutput, calls=%fused_computation.42 | convolution fusion | flops 2436756480 | bytes 15753216 | tf_op jit(solution)/shard_map/dot_general | solution.py:60
  396.3 5.0 convert_reduce_fusion.9
  414.2 7.7 %convert_reduce_fusion.6 = (f32[12,64]{1,0:T(8,128)S(1)}, bf16[12,64,512]{2,1,0:T(8,128)(2,1)}) fusion(bf16[512,12,64]{0,2,1:T(8,128)(2,1)S(1)} %bitcast.197, f32[12,512,512]{1,2,0:T(8,128)} %copy-done.1, f32[12,512]{1,0:T(8,128)S(1)} %log_add_fusion), kind=kOutput, calls=%fused_computation.112 | convolution fusion | flops 410123520 | bytes 14183424 | tf_op jit(solution)/shard_map/while/body/eval_jaxpr/hqk,qhd->khd/dot_general | solution.py:98
  421.9 7.7 %convert_reduce_fusion.10 = (f32[12,64]{1,0:T(8,128)S(1)}, bf16[12,64,512]{2,1,0:T(8,128)(2,1)}) fusion(bf16[512,12,64]{0,2,1:T(8,128)(2,1)S(1)} %bitcast.196, f32[12,512,512]{1,2,0:T(8,128)} %copy-done, f32[12,512]{1,0:T(8,128)S(1)} %log_add_fusion.1), kind=kOutput, calls=%fused_computation.116 | convolution fusion | flops 410123520 | bytes 14183424 | tf_op jit(solution)/shard_map/while/body/eval_jaxpr/hqk,qhd->khd/dot_general | solution.py:98
  433.5 12.6 %multiply_reduce_fusion.1 = (f32[12,512]{1,0:T(8,128)S(1)}, f32[12,512,512]{1,2,0:T(8,128)}) fusion(f32[12,512,512]{1,2,0:T(8,128)} %copy-done, f32[12,512]{1,0:T(8,128)S(1)} %log_add_fusion.1, bf16[512,12,64]{0,2,1:T(8,128)(2,1)} %bitcast.195, bf16[512,12,64]{0,2,1:T(8,128)(2,1)} %bitcast.214), kind=kOutput, calls=%fused_computation.4 | convolution fusion | flops 412084224 | bytes 26787840 | tf_op jit(solution)/shard_map/while/body/eval_jaxpr/qhd,khd->hqk/dot_general | solution.py:95
  446.1 9.0 %multiply_reduce_fusion = (f32[12,512]{1,0:T(8,128)S(1)}, f32[12,512,512]{1,2,0:T(8,128)}) fusion(f32[12,512,512]{1,2,0:T(8,128)} %copy-done.1, f32[12,512]{1,0:T(8,128)S(1)} %log_add_fusion, bf16[512,12,64]{0,2,1:T(8,128)(2,1)S(1)} %bitcast.198, bf16[512,12,64]{0,2,1:T(8,128)(2,1)S(1)} %bitcast.213), kind=kOutput, calls=%fused_computation.1 | convolution fusion | flops 412084224 | bytes 26787840 | tf_op jit(solution)/shard_map/while/body/eval_jaxpr/qhd,khd->hqk/dot_general | solution.py:95
  455.2 11.1 %multiply_convert_fusion.1 = bf16[12,512,512]{1,2,0:T(8,128)(2,1)S(1)} fusion(f32[12,512,512]{1,2,0:T(8,128)} %get-tuple-element.190, f32[12,512,512]{1,2,0:T(8,128)} %copy-done, f32[12,512]{1,0:T(8,128)S(1)} %get-tuple-element.189, f32[12,512]{1,0:T(8,128)S(1)} %log_add_fusion.1), kind=kLoop, calls=%fused_computation.3 | loop fusion | flops 12582912 | bytes 31506432 | tf_op jit(solution)/shard_map/while/body/eval_jaxpr/convert_element_type | solution.py:102
  470.0 7.0 %multiply_convert_fusion = bf16[12,512,512]{1,2,0:T(8,128)(2,1)S(1)} fusion(f32[12,512,512]{1,2,0:T(8,128)S(1)} %copy-done.4, f32[12,512,512]{1,2,0:T(8,128)} %copy-done.1, f32[12,512]{1,0:T(8,128)S(1)} %get-tuple-element.187, f32[12,512]{1,0:T(8,128)S(1)} %log_add_fusion), kind=kLoop, calls=%fused_computation | loop fusion | flops 12582912 | bytes 31506432 | tf_op jit(solution)/shard_map/while/body/eval_jaxpr/convert_element_type | solution.py:102
  482.5 4.2 convert_reduce_fusion.11
  488.7 4.2 convert_reduce_fusion.7
  495.9 5.4 fusion.126
  501.3 4.8 add_convert_fusion.1
  506.8 10.2 %all-reduce = (bf16[8,4,96]{2,0,1:T(8,128)(2,1)S(1)}, bf16[8,1,384]{2,0,1:T(8,128)(2,1)S(1)}, bf16[2,768]{1,0:T(2,128)(2,1)S(1)}, bf16[2,768]{1,0:T(2,128)(2,1)S(1)}) all-reduce(bf16[8,4,96]{2,0,1:T(8,128)(2,1)S(1)} %bitcast.226, bf16[8,1,384]{2,0,1:T(8,128)(2,1)S(1)} %all_to_all.21, ...), channel_id=1, replica_groups=mesh['dp'=8,'fsdp'=4] {'fsdp'}, use_global_device_ids=true, to_apply=%region_38.39 | all-reduce | flops 9216 | bytes 36864 | tf_op jit(solution)/shard_map/psum | solution.py:202
  517.8 3.4 all-to-all-start.4
  523.0 4.7 all-to-all-done.4
  527.7 3.3 all-to-all-start.3
  531.6 5.8 all-to-all-done.3
  537.5 3.3 all-to-all-start.2
  543.3 4.0 all-to-all-done.2
  547.3 3.6 all-to-all-start.1
  557.1 31.7 %reduce-scatter.15.cloned.1.call-done = bf16[768,768]{1,0:T(8,128)(2,1)} async-done(((bf16[768,3072]{1,0:T(8,128)(2,1)}), bf16[768,768]{1,0:T(8,128)(2,1)}) %reduce-scatter.15.cloned.1.call-update) | async-done | bytes 1179664 | tf_op jit(solution)/shard_map/reduce_scatter | solution.py:220
  588.8 5.2 concatenate.6
  594.0 5.9 all-to-all-start
  614.4 39.5 %all-to-all-done = bf16[8,96,1536]{2,1,0:T(8,128)(2,1)} async-done(((bf16[8,96,1536]{2,1,0:T(8,128)(2,1)}), bf16[8,96,1536]{2,1,0:T(8,128)(2,1)}, u32[]{:S(2)}, u32[]{:S(2)}) %all-to-all-start) | async-done | bytes 2359328 | tf_op jit(solution)/shard_map/all_to_all | solution.py:20
  (323 shorter events, 122.9 us)
Async XLA Ops:
  7.2 16.2 %copy-start.53 = (bf16[96,192]{1,0:T(8,128)(2,1)S(1)}, bf16[96,192]{1,0:T(8,128)(2,1)}, u32[]{:S(2)}) copy-start(bf16[96,192]{1,0:T(8,128)(2,1)} %param.18) | copy-start | bytes 110596
  7.2 22.8 %copy-start.54 = (bf16[96,192]{1,0:T(8,128)(2,1)S(1)}, bf16[96,192]{1,0:T(8,128)(2,1)}, u32[]{:S(2)}) copy-start(bf16[96,192]{1,0:T(8,128)(2,1)} %param.19) | copy-start | bytes 110596
  7.2 132.4 %all-gather.13.cloned.1.call-start = ((), (), s32[]{:S(2)}) async-start(), calls=%async_computation.12 | async-start | bytes 1327104 | tf_op jit(solution)/shard_map/all_gather | solution.py:140
  8.2 28.5 %copy-start.51 = (bf16[96,768]{1,0:T(8,128)(2,1)S(1)}, bf16[96,768]{1,0:T(8,128)(2,1)}, u32[]{:S(2)}) copy-start(bf16[96,768]{1,0:T(8,128)(2,1)} %param.20) | copy-start | bytes 442372
  16.0 130.1 %all-gather.15.cloned.1.call-start = ((), (), s32[]{:S(2)}) async-start(), calls=%async_computation.13 | async-start | bytes 1327104 | tf_op jit(solution)/shard_map/all_gather | solution.py:141
  23.3 21.7 %copy-start.52 = (bf16[384,192]{0,1:T(8,128)(2,1)S(1)}, bf16[384,192]{0,1:T(8,128)(2,1)}, u32[]{:S(2)}) copy-start(bf16[384,192]{0,1:T(8,128)(2,1)} %param.21) | copy-start | bytes 442372
  23.4 129.8 %all-gather.11.cloned.1.call-start = ((), (), s32[]{:S(2)}) async-start(), calls=%async_computation.11 | async-start | bytes 1327104 | tf_op jit(solution)/shard_map/all_gather | solution.py:142
  30.0 156.4 %all-gather.17.cloned.1.call-start = ((), (), s32[]{:S(2)}) async-start(), calls=%async_computation.14 | async-start | bytes 1327104 | tf_op jit(solution)/shard_map/all_gather | solution.py:143
  35.7 17.5 %copy-start.61 = (s32[2,1]{0,1:T(1,128)S(1)}, s32[2,1]{0,1:T(1,128)}, u32[]{:S(2)}) copy-start(s32[2,1]{0,1:T(1,128)} %param.14) | copy-start | bytes 28
  35.7 21.3 %copy-start.63 = (bf16[384]{0:T(512)(128)(2,1)S(1)}, bf16[384]{0:T(512)(128)(2,1)}, u32[]{:S(2)}) copy-start(bf16[384]{0:T(512)(128)(2,1)} %param.23) | copy-start | bytes 2308
  35.7 21.3 %copy-start.64 = (bf16[2,96]{1,0:T(2,128)(2,1)S(1)}, bf16[2,96]{1,0:T(2,128)(2,1)}, u32[]{:S(2)}) copy-start(bf16[2,96]{1,0:T(2,128)(2,1)} %param.24) | copy-start | bytes 1156
  35.7 42.2 %copy-start.65 = (bf16[2,96]{1,0:T(2,128)(2,1)S(1)}, bf16[2,96]{1,0:T(2,128)(2,1)}, u32[]{:S(2)}) copy-start(bf16[2,96]{1,0:T(2,128)(2,1)} %param.25) | copy-start | bytes 1156
  35.7 58.5 %copy-start.62 = (bf16[4,96]{1,0:T(4,128)(2,1)S(1)}, bf16[4,96]{1,0:T(4,128)(2,1)}, u32[]{:S(2)}) copy-start(bf16[4,96]{1,0:T(4,128)(2,1)} %param.22) | copy-start | bytes 2308
  36.5 103.0 %copy-start.5 = (bf16[2,1,512,768]{3,2,1,0:T(8,128)(2,1)S(1)}, bf16[2,1,512,768]{3,2,1,0:T(8,128)(2,1)}, u32[]{:S(2)}) copy-start(bf16[2,1,512,768]{3,2,1,0:T(8,128)(2,1)} %param.13) | copy-start | bytes 4718596
  36.6 230.5 %all-gather.19.cloned.1.call-start = ((), (), s32[]{:S(2)}) async-start(), calls=%async_computation.15 | async-start | bytes 5308416 | tf_op jit(solution)/shard_map/all_gather | solution.py:144
  45.0 303.2 %all-gather.21.cloned.1.call-start = ((), (), s32[]{:S(2)}) async-start(), calls=%async_computation.16 | async-start | bytes 5308416 | tf_op jit(solution)/shard_map/all_gather | solution.py:145
  53.2 487.7 %reduce-scatter.17.cloned.1.call-start = ((), (), s32[]{:S(2)}) async-start(), calls=%async_computation.22 | async-start | bytes 5898240 | tf_op jit(solution)/shard_map/reduce_scatter | solution.py:223
  148.4 41.3 %copy-start.7 = (bf16[512,768]{0,1:T(8,128)(2,1)}, bf16[512,768]{0,1:T(8,128)(2,1)S(1)}, u32[]{:S(2)}) copy-start(bf16[512,768]{0,1:T(8,128)(2,1)S(1)} %copy.188) | copy-start | bytes 2359300
  153.1 10.8 %copy-start.9 = (bf16[512,768]{0,1:T(8,128)(2,1)}, bf16[512,768]{0,1:T(8,128)(2,1)S(1)}, u32[]{:S(2)}) copy-start(bf16[512,768]{0,1:T(8,128)(2,1)S(1)} %copy.180) | copy-start | bytes 2359300
  174.8 14.9 %copy-start.47 = (bf16[12,64,512]{2,1,0:T(8,128)(2,1)}, bf16[12,64,512]{2,1,0:T(8,128)(2,1)S(1)}, u32[]{:S(2)}) copy-start(bf16[12,64,512]{2,1,0:T(8,128)(2,1)S(1)} %fusion.74) | copy-start | bytes 2359300
  201.2 65.9 %copy-start.25 = (f32[512,768]{1,0:T(8,128)}, f32[512,768]{1,0:T(8,128)S(1)}, u32[]{:S(2)}) copy-start(f32[512,768]{1,0:T(8,128)S(1)} %get-tuple-element.179) | copy-start | bytes 4718596
  267.1 7.6 %copy-start.45 = (f32[512,768]{1,0:T(8,128)S(1)}, f32[512,768]{1,0:T(8,128)}, u32[]{:S(2)}) copy-start(f32[512,768]{1,0:T(8,128)} %get-tuple-element.175) | copy-start | bytes 4718596
  267.1 7.6 %copy-start.66 = (bf16[768,3072]{1,0:T(8,128)(2,1)S(1)}, bf16[768,3072]{1,0:T(8,128)(2,1)}, u32[]{:S(2)}) copy-start(bf16[768,3072]{1,0:T(8,128)(2,1)} %all-gather.19.cloned.1.call-done) | copy-start | bytes 14155780
  348.2 7.0 %slice-start.2 = ((s8[4718592]{0:T(1024)(128)(4,1)}), s8[4194304]{0:T(1024)(128)(4,1)S(1)}, s32[]{:S(2)}) async-start(s8[4718592]{0:T(1024)(128)(4,1)} %bitcast.238), calls=%async_computation.25 | async-start | bytes 8388608
  348.2 7.0 %slice-start.3 = ((s8[4718592]{0:T(1024)(128)(4,1)}), s8[524288]{0:T(1024)(128)(4,1)S(1)}, s32[]{:S(2)}) async-start(s8[4718592]{0:T(1024)(128)(4,1)} %bitcast.238), calls=%async_computation.26 | async-start | bytes 1048576
  372.2 178.7 %reduce-scatter.13.cloned.1.call-start = ((), (), s32[]{:S(2)}) async-start(), calls=%async_computation.20 | async-start | bytes 1474560 | tf_op jit(solution)/shard_map/reduce_scatter | solution.py:217
  373.6 8.0 %copy-start.46 = (f32[512,768]{1,0:T(8,128)S(1)}, f32[512,768]{1,0:T(8,128)}, u32[]{:S(2)}) copy-start(f32[512,768]{1,0:T(8,128)} %get-tuple-element.175) | copy-start | bytes 4718596
  381.6 6.6 copy-start.33
  381.6 14.6 %slice-start = ((s8[4718592]{0:T(1024)(128)(4,1)}), s8[4194304]{0:T(1024)(128)(4,1)S(1)}, s32[]{:S(2)}) async-start(s8[4718592]{0:T(1024)(128)(4,1)} %bitcast.236), calls=%async_computation.23 | async-start | bytes 8388608
  388.2 8.0 %copy-start.27 = (f32[512,768]{1,0:T(8,128)S(1)}, f32[512,768]{1,0:T(8,128)}, u32[]{:S(2)}) copy-start(f32[512,768]{1,0:T(8,128)} %copy-done.25) | copy-start | bytes 4718596
  388.2 8.0 %slice-start.1 = ((s8[4718592]{0:T(1024)(128)(4,1)}), s8[524288]{0:T(1024)(128)(4,1)S(1)}, s32[]{:S(2)}) async-start(s8[4718592]{0:T(1024)(128)(4,1)} %bitcast.236), calls=%async_computation.24 | async-start | bytes 1048576
  414.2 7.7 %copy-start.10 = (bf16[512,768]{0,1:T(8,128)(2,1)S(1)}, bf16[512,768]{0,1:T(8,128)(2,1)}, u32[]{:S(2)}) copy-start(bf16[512,768]{0,1:T(8,128)(2,1)} %copy.190) | copy-start | bytes 2359300
  421.9 7.7 %copy-start.6 = (bf16[2,1,512,768]{3,2,1,0:T(8,128)(2,1)S(1)}, bf16[2,1,512,768]{3,2,1,0:T(8,128)(2,1)}, u32[]{:S(2)}) copy-start(bf16[2,1,512,768]{3,2,1,0:T(8,128)(2,1)} %param.13) | copy-start | bytes 4718596
  429.6 122.5 %reduce-scatter.11.cloned.1.call-start = ((), (), s32[]{:S(2)}) async-start(), calls=%async_computation.19 | async-start | bytes 1474560 | tf_op jit(solution)/shard_map/reduce_scatter | solution.py:214
  433.5 12.6 %copy-start.12 = (bf16[512,768]{0,1:T(8,128)(2,1)S(1)}, bf16[512,768]{0,1:T(8,128)(2,1)}, u32[]{:S(2)}) copy-start(bf16[512,768]{0,1:T(8,128)(2,1)} %copy-done.11) | copy-start | bytes 2359300
  433.5 12.6 %copy-start.36 = (bf16[512,768]{0,1:T(8,128)(2,1)S(1)}, bf16[512,768]{0,1:T(8,128)(2,1)}, u32[]{:S(2)}) copy-start(bf16[512,768]{0,1:T(8,128)(2,1)} %copy.186) | copy-start | bytes 2359300
  455.1 98.1 %reduce-scatter.9.cloned.1.call-start = ((), (), s32[]{:S(2)}) async-start(), calls=%async_computation.18 | async-start | bytes 1474560 | tf_op jit(solution)/shard_map/reduce_scatter | solution.py:211
  455.2 11.1 %copy-start.18 = (bf16[512,768]{0,1:T(8,128)(2,1)S(1)}, bf16[512,768]{0,1:T(8,128)(2,1)}, u32[]{:S(2)}) copy-start(bf16[512,768]{0,1:T(8,128)(2,1)} %copy.177) | copy-start | bytes 2359300
  455.2 14.8 %copy-start.4 = (f32[12,512,512]{1,2,0:T(8,128)S(1)}, f32[12,512,512]{1,2,0:T(8,128)}, u32[]{:S(2)}) copy-start(f32[12,512,512]{1,2,0:T(8,128)} %get-tuple-element.188) | copy-start | bytes 37748740
  470.0 7.0 %copy-start.17 = (bf16[512,768]{0,1:T(8,128)(2,1)S(1)}, bf16[512,768]{0,1:T(8,128)(2,1)}, u32[]{:S(2)}) copy-start(bf16[512,768]{0,1:T(8,128)(2,1)} %copy.187) | copy-start | bytes 2359300
  482.4 72.8 %reduce-scatter.7.cloned.1.call-start = ((), (), s32[]{:S(2)}) async-start(), calls=%async_computation.17 | async-start | bytes 1474560 | tf_op jit(solution)/shard_map/reduce_scatter | solution.py:208
  495.7 93.1 %reduce-scatter.15.cloned.1.call-start = ((), (), s32[]{:S(2)}) async-start(), calls=%async_computation.21 | async-start | bytes 5898240 | tf_op jit(solution)/shard_map/reduce_scatter | solution.py:220
  517.8 9.9 %all-to-all-start.4 = ((bf16[8,4,96]{2,1,0:T(4,128)(2,1)}), bf16[8,4,96]{2,1,0:T(4,128)(2,1)S(1)}, u32[]{:S(2)}, u32[]{:S(2)}) async-start(bf16[8,4,96]{2,1,0:T(4,128)(2,1)} %copy.205), calls=%async_computation.10 | async-start | bytes 16384 | tf_op jit(solution)/shard_map/all_to_all | solution.py:20
  527.7 9.8 %all-to-all-start.3 = ((bf16[8,2,192]{2,1,0:T(2,128)(2,1)}), bf16[8,2,192]{2,1,0:T(2,128)(2,1)S(1)}, u32[]{:S(2)}, u32[]{:S(2)}) async-start(bf16[8,2,192]{2,1,0:T(2,128)(2,1)} %reshape.300), calls=%async_computation.9 | async-start | bytes 16384 | tf_op jit(solution)/shard_map/all_to_all | solution.py:20
  537.5 9.8 %copy-start.56 = (bf16[8,2,192]{2,1,0:T(2,128)(2,1)}, bf16[8,2,192]{2,1,0:T(2,128)(2,1)S(1)}, u32[]{:S(2)}) copy-start(bf16[8,2,192]{2,1,0:T(2,128)(2,1)S(1)} %all-to-all-done.3) | copy-start | bytes 18436
  537.5 9.8 %all-to-all-start.2 = ((bf16[8,4,96]{2,1,0:T(4,128)(2,1)}), bf16[8,4,96]{2,1,0:T(4,128)(2,1)S(1)}, u32[]{:S(2)}, u32[]{:S(2)}) async-start(bf16[8,4,96]{2,1,0:T(4,128)(2,1)} %copy.203), calls=%async_computation.8 | async-start | bytes 16384 | tf_op jit(solution)/shard_map/all_to_all | solution.py:20
  547.3 46.7 %all-to-all-start.1 = ((bf16[8,384,192]{1,2,0:T(8,128)(2,1)}), bf16[8,384,192]{1,2,0:T(8,128)(2,1)S(1)}, u32[]{:S(2)}, u32[]{:S(2)}) async-start(bf16[8,384,192]{1,2,0:T(8,128)(2,1)} %bitcast.211), calls=%async_computation.7 | async-start | bytes 2359296 | tf_op jit(solution)/shard_map/all_to_all | solution.py:20
  594.0 59.9 %all-to-all-start = ((bf16[8,96,1536]{2,1,0:T(8,128)(2,1)}), bf16[8,96,1536]{2,1,0:T(8,128)(2,1)}, u32[]{:S(2)}, u32[]{:S(2)}) async-start(bf16[8,96,1536]{2,1,0:T(8,128)(2,1)} %bitcast.194), calls=%async_computation.5 | async-start | bytes 4718592 | tf_op jit(solution)/shard_map/all_to_all | solution.py:20
  (49 other events, 124.6 us)
Sparse Core Ops, SparseCore 0:
  16.1 42.5 all-gather.12
  61.4 39.8 all-gather.14
  104.1 39.7 all-gather.10
  146.5 39.8 all-gather.16
  188.4 78.6 all-gather.18
  269.0 79.1 all-gather.20
  372.4 46.0 reduce-scatter.16
  429.7 23.4 reduce-scatter.12
  455.8 25.7 reduce-scatter.10
  484.1 25.7 reduce-scatter.8
  512.4 25.8 reduce-scatter.6
  540.9 47.8 reduce-scatter.14
where the time goes:
time: 669 us; the launch traced here: 665 us
  waiting for transfers between devices  203 us (30%)
  matrix products  193 us (29%)
  blocking collectives  132 us (20%)
  local copies, waits for them, and re-layouts  58.2 us (9%)
  other arithmetic  41.3 us (6%)
  starting transfers between devices  20.3 us (3%)
  between operations  15.7 us (2%)
    all_gather x1, waiting for transfers between devices, gather_forward(): lax.all_gather(column_full[4], 'dp', axis=0, tiled=True)  64.6 us
    all_to_all x5, waiting for transfers between devices, sum_at_owner(): parts = lax.all_to_all(split_up(value, dim, size), axis, 0, 0, tiled=True)  54 us
    all_gather x1, waiting for transfers between devices, gather_forward(): lax.all_gather(column_full[5], 'dp', axis=0, tiled=True)  41.4 us
    dot_general x2, matrix products, layer_step(): jnp.dot(middle_low, inner_full, preferred_element_type=jnp.float32)  37 us
    dot_general x12, matrix products, back_product(): lax.dot_general(upward, weight, (((1,), (1,)), ((), ())), preferred_eleme...  35.1 us
    reduce_scatter x1, waiting for transfers between devices, reduce_grads(): lax.psum_scatter(inner_grad.astype(jnp.bfloat16), 'fsdp', scatter_dimensi...  31.7 us
    dot_general x12, matrix products, outer_sum(): lax.dot_general(left, right, (((0,), (0,)), ((), ())), preferred_element_...  30.8 us
    all_gather x1, blocking collectives, gather_forward(): lax.all_gather(hidden_part, 'dp', axis=0, tiled=True)  26.2 us
  transfers between devices with their start and end apart: 17, of which 8 were waited for; matrix products, arithmetic and copies ran while one was open for 37% of the time, Pallas kernels for 0%

commit v1 on v0

--- a/solution.py
+++ b/solution.py
@@ -1,6 +1,9 @@
+import functools
 import jax
 import jax.numpy as jnp
 from jax import lax
+from jax.experimental import pallas as pl
+from jax.experimental.pallas import tpu as pltpu
 from jax.sharding import PartitionSpec as P
 
 HEADS = 12
@@ -8,6 +11,174 @@
 
 EPSILON = 1e-12
 MASKED = -1000000000.0
+SMALL_ROWS = 16
+
+
+def swap(value, axis, bit):
+    size = lax.axis_size(axis)
+    return lax.ppermute(value, axis, [(i, i ^ (1 << bit)) for i in range(size)])
+
+
+def stage_orders(mesh):
+    dp_bits = mesh.shape["dp"].bit_length() - 1
+    fsdp_bits = mesh.shape["fsdp"].bit_length() - 1
+    far = [("dp", b) for b in range(dp_bits - 1, 0, -1)]
+    across = [("fsdp", b) for b in range(fsdp_bits - 1, 0, -1)]
+    return (far + across + [("dp", 0)], far + [("dp", 0)] + across)
+
+
+def fits(mesh, row_counts, width):
+    sizes = (mesh.shape["dp"], mesh.shape["fsdp"])
+    powers = all(s >= 2 and s & (s - 1) == 0 for s in sizes)
+    return powers and all(r % 32 == 0 for r in row_counts) and width % 64 == 0
+
+
+def true_index(stages, place, mine, pair_flip):
+    index = {"dp": mine["dp"], "fsdp": mine["fsdp"] ^ pair_flip}
+    for s, (axis, bit) in enumerate(stages):
+        index[axis] = index[axis] ^ (((place >> s) & 1) << bit)
+    return index["dp"], index["fsdp"]
+
+
+def gather_part(piece, stages):
+    current = piece[None]
+    for axis, bit in stages:
+        current = jnp.concatenate([current, swap(current, axis, bit)], axis=0)
+    return current, swap(current, "fsdp", 0)
+
+
+def copy_list(stages, rows, mine, with_small, blocks):
+    copies = []
+    for flip in range(2):
+        for place in range(1 << len(stages)):
+            dp, fsdp = true_index(stages, place, mine, flip)
+            at = 0
+            for w, half in enumerate(rows):
+                row = pl.multiple_of((dp * 2 + (fsdp & 1)) * half, 16)
+                copies.append((flip, place, at, half, w, row, fsdp >> 1))
+                at += half
+            if with_small and (flip == 0 or blocks):
+                copies.append((flip, place, at, SMALL_ROWS, len(rows), dp, None))
+    return copies
+
+
+def place_kernel(stages, rows, width, with_small, me_ref, *refs):
+    sources, outs, sems = refs[:2], refs[2:-1], refs[-1]
+    mine = {"dp": me_ref[0], "fsdp": me_ref[1]}
+    seen, started = set(), []
+    for flip, place, at, count, w, row, column in copy_list(stages, rows, mine, with_small, False):
+        source = sources[flip].at[place, pl.ds(at, count), :]
+        if column is None:
+            across = any((place >> s) & 1 for s, (axis, _) in enumerate(stages) if axis == "fsdp")
+            if across:
+                continue
+            target = outs[w].at[row]
+        else:
+            target = outs[w].at[pl.ds(row, count), pl.ds(pl.multiple_of(column * width, 128), width)]
+        copy = pltpu.make_async_copy(source, target, sems.at[len(started)])
+        copy.start()
+        started.append(copy)
+    for copy in started:
+        copy.wait()
+
+
+def place_part(mesh, own, other, me, stages, rows, with_small):
+    width = own.shape[-1]
+    dp, across = mesh.shape["dp"], mesh.shape["fsdp"] // 2
+    shapes = [jax.ShapeDtypeStruct((dp * 2 * h, across * width), own.dtype) for h in rows]
+    if with_small:
+        shapes.append(jax.ShapeDtypeStruct((dp, SMALL_ROWS, width), own.dtype))
+    anywhere = pl.BlockSpec(memory_space=pl.ANY)
+    return pl.pallas_call(
+        functools.partial(place_kernel, stages, rows, width, with_small),
+        out_shape=tuple(shapes),
+        in_specs=[pl.BlockSpec(memory_space=pltpu.SMEM), anywhere, anywhere],
+        out_specs=(anywhere,) * len(shapes),
+        scratch_shapes=[pltpu.SemaphoreType.DMA((2 * (1 << len(stages)) * (len(rows) + 1),))],
+        name="place",
+    )(me, own, other)
+
+
+def cut_kernel(stages, rows, width, with_small, me_ref, *refs):
+    count_in = len(rows) + with_small
+    sources, outs, sems = refs[:count_in], refs[count_in:-1], refs[-1]
+    mine = {"dp": me_ref[0], "fsdp": me_ref[1]}
+    started = []
+    for flip, place, at, count, w, row, column in copy_list(stages, rows, mine, with_small, True):
+        target = outs[flip].at[place, pl.ds(at, count), :]
+        if column is None:
+            source = sources[w].at[row]
+        else:
+            source = sources[w].at[pl.ds(row, count), pl.ds(pl.multiple_of(column * width, 128), width)]
+        copy = pltpu.make_async_copy(source, target, sems.at[len(started)])
+        copy.start()
+        started.append(copy)
+    for copy in started:
+        copy.wait()
+
+
+def cut_part(mesh, arrays, small, me, stages, rows, width):
+    total = sum(rows) + (SMALL_ROWS if small is not None else 0)
+    places = 1 << len(stages)
+    shape = jax.ShapeDtypeStruct((places, total, width), jnp.bfloat16)
+    anywhere = pl.BlockSpec(memory_space=pl.ANY)
+    operands = list(arrays) + ([small] if small is not None else [])
+    return pl.pallas_call(
+        functools.partial(cut_kernel, stages, rows, width, small is not None),
+        out_shape=(shape, shape),
+        in_specs=[pl.BlockSpec(memory_space=pltpu.SMEM)] + [anywhere] * len(operands),
+        out_specs=(anywhere, anywhere),
+        scratch_shapes=[pltpu.SemaphoreType.DMA((2 * places * (len(rows) + 1),))],
+        name="cut",
+    )(me, *operands)
+
+
+def total_of(left, right, kind):
+    return (left.astype(jnp.float32) + right.astype(jnp.float32)).astype(kind)
+
+
+def scatter_part(keep, send, stages):
+    received = swap(send, "fsdp", 0)
+    for axis, bit in reversed(stages):
+        half = keep.shape[0] // 2
+        send = total_of(keep[half:], received[half:], jnp.bfloat16)
+        arriving = swap(send, axis, bit)
+        keep = total_of(keep[:half], received[:half], jnp.bfloat16)
+        received = arriving
+    return total_of(keep, received, jnp.float32)[0]
+
+
+def settle(total, rows):
+    width = total.shape[-1] // 2
+    count = sum(rows)
+    second = lax.axis_index("fsdp") & 1
+    own = jnp.where(second == 0, total[:count, :width], total[:count, width:])
+    away = jnp.where(second == 0, total[:count, width:], total[:count, :width])
+    came = swap(away.astype(jnp.bfloat16), "fsdp", 0).astype(jnp.float32)
+    first, last = jnp.where(second == 0, own, came), jnp.where(second == 0, came, own)
+    outs, at = [], 0
+    for half in rows:
+        outs.append(jnp.concatenate([first[at : at + half], last[at : at + half]], axis=0))
+        at += half
+    return outs
+
+
+def pair_up(shards):
+    second = lax.axis_index("fsdp") & 1
+    outs = []
+    for shard in shards:
+        half = shard.shape[0] // 2
+        mine = jnp.where(second == 0, shard[:half], shard[half:])
+        away = jnp.where(second == 0, shard[half:], shard[:half])
+        came = swap(away, "fsdp", 0)
+        outs.append(
+            jnp.where(
+                second == 0,
+                jnp.concatenate([mine, came], axis=1),
+                jnp.concatenate([came, mine], axis=1),
+            )
+        )
+    return outs
 
 
 def split_up(value, dim, size):
@@ -150,41 +321,6 @@
     )
 
 
-def gather_backward(shards):
-    (
-        query_part,
-        key_part,
-        value_part,
-        output_part,
-        inner_part,
-        outer_part,
-        bias_part,
-        hidden_part,
-        gain_part,
-        shift_part,
-    ) = shards
-    column_full = (
-        lax.all_gather(query_part, "fsdp", axis=1, tiled=True),
-        lax.all_gather(key_part, "fsdp", axis=1, tiled=True),
-        lax.all_gather(value_part, "fsdp", axis=1, tiled=True),
-        lax.all_gather(output_part, "fsdp", axis=1, tiled=True),
-        lax.all_gather(inner_part, "fsdp", axis=1, tiled=True),
-        lax.all_gather(outer_part, "fsdp", axis=1, tiled=True),
-    )
-    return (
-        lax.all_gather(column_full[0], "dp", axis=0, tiled=True),
-        lax.all_gather(column_full[1], "dp", axis=0, tiled=True),
-        lax.all_gather(column_full[2], "dp", axis=0, tiled=True),
-        lax.all_gather(column_full[3], "dp", axis=0, tiled=True),
-        lax.all_gather(column_full[4], "dp", axis=0, tiled=True),
-        lax.all_gather(column_full[5], "dp", axis=0, tiled=True),
-        lax.all_gather(bias_part, "dp", axis=1, tiled=True),
-        lax.all_gather(hidden_part, "dp", axis=0, tiled=True),
-        lax.all_gather(gain_part, "dp", axis=1, tiled=True),
-        lax.all_gather(shift_part, "dp", axis=1, tiled=True),
-    )
-
-
 def reduce_grads(grads):
     (
         query_grad,
@@ -246,7 +382,7 @@
     )
 
 
-def layer_step(inputs, length_row, upstream, forward_weights, backward_weights):
+def layer_step(inputs, length_row, upstream, forward_weights):
     (
         query_full,
         key_full,
@@ -259,7 +395,7 @@
         gain_full,
         shift_full,
     ) = forward_weights
-    query_back, key_back, value_back, output_back, inner_back, outer_back = backward_weights[:6]
+    query_back, key_back, value_back, output_back, inner_back, outer_back = forward_weights[:6]
     seq_count, seq_len, model_width = inputs.shape
     row_count = seq_count * seq_len
     flat_rows = inputs.reshape(row_count, model_width)
@@ -364,69 +500,111 @@
     )
 
 
+def pack_small(bias, hidden, gains, shifts, width):
+    columns = bias.shape[-1]
+    rows = jnp.concatenate([bias, hidden.reshape(-1, columns), gains, shifts], axis=0)
+    return jnp.pad(rows, ((0, SMALL_ROWS - rows.shape[0]), (0, width - columns)))
+
+
+def unpack_small(packed, columns, hidden_count):
+    split = 4 + hidden_count // columns
+    lined = packed[:, :, :columns]
+    whole = jnp.moveaxis(lined, 0, 1).reshape(packed.shape[1], -1)
+    hidden = lined[:, 4:split].reshape(-1)
+    return whole[:4], hidden, whole[split : split + 2], whole[split + 2 : split + 4]
+
+
+def spread_small(bias, hidden, gains, shifts, parts, width):
+    columns = bias.shape[-1] // parts
+
+    def cut(v):
+        return jnp.moveaxis(v.reshape(v.shape[0], parts, columns), 1, 0)
+
+    rows = jnp.concatenate(
+        [cut(bias), hidden.reshape(parts, -1, columns), cut(gains), cut(shifts)], axis=1
+    )
+    rows = rows.astype(jnp.bfloat16)
+    return jnp.pad(rows, ((0, 0), (0, SMALL_ROWS - rows.shape[1]), (0, width - columns)))
+
+
+def exchange_gather(mesh, shards, me):
+    query, key, value, output, inner, outer, bias, hidden, gains, shifts = shards
+    order_one, order_two = stage_orders(mesh)
+    half, half_outer = query.shape[0] // 2, outer.shape[0] // 2
+    width = 2 * query.shape[1]
+    count = query.shape[0]
+    small = pack_small(bias, hidden, gains, shifts, width)
+    (first,) = pair_up((jnp.stack([query, key]).reshape(2, 2, half, -1).swapaxes(0, 1).reshape(4 * half, -1),))
+    (second,) = pair_up((jnp.stack([value, output]).reshape(2, 2, half, -1).swapaxes(0, 1).reshape(4 * half, -1),))
+    (third,) = pair_up((inner,))
+    (fourth,) = pair_up((outer,))
+    first = jnp.concatenate([first, small], axis=0)
+    own, other = gather_part(first, order_one)
+    query_full, key_full, small_full = place_part(mesh, own, other, me, order_one, (half, half), True)
+    own, other = gather_part(second, order_two)
+    value_full, output_full = place_part(mesh, own, other, me, order_two, (half, half), False)
+    own, other = gather_part(third, order_one)
+    (inner_full,) = place_part(mesh, own, other, me, order_one, (half,), False)
+    own, other = gather_part(fourth, order_two)
+    (outer_full,) = place_part(mesh, own, other, me, order_two, (half_outer,), False)
+    vectors = unpack_small(small_full, bias.shape[1], hidden.shape[0])
+    return (query_full, key_full, value_full, output_full, inner_full, outer_full, *vectors)
+
+
+def exchange_scatter(mesh, grads, me, shards):
+    query, key, value, output, inner, outer, bias, hidden, gains, shifts = grads
+    order_one, order_two = stage_orders(mesh)
+    half, half_outer = shards[0].shape[0] // 2, shards[5].shape[0] // 2
+    width = 2 * shards[0].shape[1]
+    columns = shards[6].shape[1]
+    low = jnp.bfloat16
+    keep, send = cut_part(mesh, (outer.astype(low),), None, me, order_two, (half_outer,), width)
+    outer_sum_ = settle(scatter_part(keep, send, order_two), (half_outer,))[0]
+    keep, send = cut_part(mesh, (inner.astype(low),), None, me, order_one, (half,), 2 * shards[4].shape[1])
+    inner_sum = settle(scatter_part(keep, send, order_one), (half,))[0]
+    keep, send = cut_part(
+        mesh, (value.astype(low), output.astype(low)), None, me, order_two, (half, half), width
+    )
+    value_sum, output_sum = settle(scatter_part(keep, send, order_two), (half, half))
+    small = spread_small(bias, hidden, gains, shifts, mesh.shape["dp"], width)
+    keep, send = cut_part(
+        mesh, (query.astype(low), key.astype(low)), small, me, order_one, (half, half), width
+    )
+    total = scatter_part(keep, send, order_one)
+    query_sum, key_sum = settle(total, (half, half))
+    rows = total[2 * half :, :columns]
+    split = 4 + shards[7].shape[0] // columns
+    return (
+        query_sum,
+        key_sum,
+        value_sum,
+        output_sum,
+        inner_sum,
+        outer_sum_,
+        rows[:4],
+        rows[4:split].reshape(-1),
+        rows[split : split + 2],
+        rows[split + 2 : split + 4],
+    )
+
+
 def on_device(
+    mesh,
     tokens,
     lengths,
     cotangent,
-    query_weight,
-    key_weight,
-    value_weight,
-    output_weight,
-    inner_weight,
-    outer_weight,
-    bias_vectors,
-    bias_hidden,
-    norm_gains,
-    norm_shifts,
+    *shards,
 ):
-    shards = (
-        query_weight,
-        key_weight,
-        value_weight,
-        output_weight,
-        inner_weight,
-        outer_weight,
-        bias_vectors,
-        bias_hidden,
-        norm_gains,
-        norm_shifts,
-    )
-    totals = None
-    out_list = []
-    grad_list = []
-    for micro_batch in range(tokens.shape[0]):
-        forward_weights = gather_forward(shards)
-        backward_weights = gather_backward(shards)
-        outputs, grad_inputs, step_grads = layer_step(
-            tokens[micro_batch],
-            lengths[micro_batch],
-            cotangent[micro_batch],
-            forward_weights,
-            backward_weights,
-        )
-        out_list.append(outputs)
-        grad_list.append(grad_inputs)
-        if totals is None:
-            totals = step_grads
-        else:
-            totals = jax.tree.map(jnp.add, totals, step_grads)
-    totals = reduce_grads(totals)
-    activations = jnp.stack(out_list)
-    input_grad = jnp.stack(grad_list)
-    return (
-        activations,
-        input_grad,
-        totals[0],
-        totals[1],
-        totals[2],
-        totals[3],
-        totals[4],
-        totals[5],
-        totals[6],
-        totals[7],
-        totals[8],
-        totals[9],
-    )
+    me = jnp.stack([lax.axis_index("dp"), lax.axis_index("fsdp")]).astype(jnp.int32)
+    rows = (shards[0].shape[0], shards[5].shape[0])
+    direct = fits(mesh, rows, shards[0].shape[1])
+    weights = exchange_gather(mesh, shards, me) if direct else gather_forward(shards)
+    shape = (-1, *tokens.shape[2:])
+    outputs, grad_inputs, grads = layer_step(
+        tokens.reshape(shape), lengths.reshape(-1), cotangent.reshape(shape), weights
+    )
+    totals = exchange_scatter(mesh, grads, me, shards) if direct else reduce_grads(grads)
+    return (outputs.reshape(tokens.shape), grad_inputs.reshape(tokens.shape), *totals)
 
 
 def solution(mesh):
@@ -446,7 +624,7 @@
         P(None, "dp"),
     )
     return jax.shard_map(
-        on_device,
+        functools.partial(on_device, mesh),
         mesh=mesh,
         in_specs=placed,
         out_specs=(

time: 669 us -> 1410 us (2.11)
  Pallas kernels: 0 us -> 893 us
  blocking collectives: 132 us -> 0 us
  waiting for transfers between devices: 203 us -> 122 us
  starting transfers between devices: 20.3 us -> 57 us
  other arithmetic: 41.3 us -> 62.5 us
    pallas_call x0 -> x8, Pallas kernels: none -> 893 us  [the longest x4 451 us: cut_part(): pl.pallas_call(functools.partial(cut_kernel, stages, rows, width, small i...]
    ppermute x0 -> x48, waiting for transfers between devices: none -> 122 us  [swap(): return lax.ppermute(value, axis, [(i, i ^ 1 << bit) for i in range(size)])]
    all_gather x10 -> x0, blocking collectives: 122 us -> none  [the longest x1 26.2 us: gather_forward(): lax.all_gather(hidden_part, 'dp', axis=0, tiled=True)]
    all_gather x6 -> x0, waiting for transfers between devices: 118 us -> none  [the longest x1 64.6 us: gather_forward(): lax.all_gather(column_full[4], 'dp', axis=0, tiled=True)]
    ppermute x0 -> x48, starting transfers between devices: none -> 57 us  [swap(): return lax.ppermute(value, axis, [(i, i ^ 1 << bit) for i in range(size)])]
    all_to_all x5 -> x0, waiting for transfers between devices: 54 us -> none  [sum_at_owner(): parts = lax.all_to_all(split_up(value, dim, size), axis, 0, 0, tiled=True)]
    reduce_scatter x6 -> x0, waiting for transfers between devices: 31.8 us -> none  [the longest x1 31.7 us: reduce_grads(): lax.psum_scatter(inner_grad.astype(jnp.bfloat16), 'fsdp', scatter_dimensi...]
    all_to_all x5 -> x0, starting transfers between devices: 19.6 us -> none  [sum_at_owner(): parts = lax.all_to_all(split_up(value, dim, size), axis, 0, 0, tiled=True)]
  transfers between devices with their start and end apart: 17 -> 48, of which waited for: 8 -> 27; matrix products, arithmetic and copies ran while one was open for 37% -> 12% of each run, Pallas kernels for 0% -> 48%
where the time goes in v1:
time: 1410 us; the launch traced here: 1400 us
  Pallas kernels  893 us (63%)
  matrix products  206 us (15%)
  waiting for transfers between devices  122 us (9%)
  other arithmetic  62.5 us (4%)
  starting transfers between devices  57 us (4%)
  local copies, waits for them, and re-layouts  55.2 us (4%)
    pallas_call x4, Pallas kernels, cut_part(): pl.pallas_call(functools.partial(cut_kernel, stages, rows, width, small i...  451 us
    pallas_call x4, Pallas kernels, place_part(): pl.pallas_call(functools.partial(place_kernel, stages, rows, width, with_...  442 us
    ppermute x48, waiting for transfers between devices, swap(): return lax.ppermute(value, axis, [(i, i ^ 1 << bit) for i in range(size)])  122 us
    ppermute x48, starting transfers between devices, swap(): return lax.ppermute(value, axis, [(i, i ^ 1 << bit) for i in range(size)])  57 us
    dot_general x1, matrix products, layer_step(): jnp.dot(middle_low, inner_full, preferred_element_type=jnp.float32)  37.4 us
    dot_general x6, matrix products, outer_sum(): lax.dot_general(left, right, (((0,), (0,)), ((), ())), preferred_element_...  33.5 us
    dot_general x6, matrix products, back_product(): lax.dot_general(upward, weight, (((1,), (1,)), ((), ())), preferred_eleme...  29.8 us
  transfers between devices with their start and end apart: 48, of which 27 were waited for; matrix products, arithmetic and copies ran while one was open for 12% of the time, Pallas kernels for 48%

profile of v1, /device:TPU:0, one launch (start us, length us, event | category | flops | bytes accessed | tf_op | source)
XLA Modules:
  0.0 1398.7 jit_solution(6441819103573278771)
XLA Ops:
  10.0 4.1 collective-permute-start.1
  18.8 8.4 collective-permute-start.2
  43.2 4.5 collective-permute-done.20
  49.6 4.4 collective-permute-done.14
  58.3 5.8 collective-permute-done.21
  66.0 4.3 collective-permute-done.15
  72.2 6.6 collective-permute-done.10
  79.1 3.9 collective-permute-done.4
  87.1 20.2 %collective-permute-done.22 = bf16[8,192,384]{2,1,0:T(8,128)(2,1)S(1)} collective-permute-done((bf16[8,192,384]{2,1,0:T(8,128)(2,1)S(1)}, bf16[8,192,384]{2,1,0:T(8,128)(2,1)S(1)}, u32[]{:S(2)}, u32[]{:S(2)}) %collective-permute-start.22) | collective-permute-done | bytes 1179680 | tf_op jit(solution)/shard_map/ppermute | solution.py:19
  110.2 74.1 %place.4 = (bf16[768,768]{1,0:T(8,128)(2,1)}, bf16[768,768]{1,0:T(8,128)(2,1)}) custom-call(s32[2]{0:T(128)} %pad_add_fusion.me_ref, bf16[16,96,384]{2,1,0:T(8,128)(2,1)} %copy-done.21, bf16[16,96,384]{2,1,0:T(8,128)(2,1)} %collective-permute-done.5.refs_1_), custom_call_target="tpu_custom_call" | custom-call | tf_op jit(solution)/shard_map/place/pallas_call | solution.py:92
  185.4 77.1 %place.5 = (bf16[768,768]{1,0:T(8,128)(2,1)}, bf16[768,768]{1,0:T(8,128)(2,1)}, bf16[8,16,384]{2,1,0:T(8,128)(2,1)}) custom-call(s32[2]{0:T(128)} %pad_add_fusion.me_ref, bf16[16,112,384]{2,1,0:T(8,128)(2,1)} %copy-done.18, bf16[16,112,384]{2,1,0:T(8,128)(2,1)} %copy-done.20), custom_call_target="tpu_custom_call" | custom-call | tf_op jit(solution)/shard_map/place/pallas_call | solution.py:92
  284.0 27.6 %while.26 = (s32[]{:T(128)}, bf16[2,512,768]{2,1,0:T(8,128)(2,1)}, f32[2,12,512]{2,1,0:T(8,128)}, bf16[2,512,12,64]{1,3,2,0:T(8,128)(2,1)}, s32[2]{0:T(128)}, /*...) while((s32[]{:T(128)}, bf16[2,512,768]{2,1,0:T(8,128)(2,1)}, ...), condition=%wide.region_3.4_spmd, body=%wide.region_0.3_spmd.sunk | while | flops 843049472 | bytes 50557060 | solution.py:419
  286.0 4.1 fusion.155
  299.7 4.1 fusion.155
  321.7 145.3 %place.6 = bf16[768,3072]{1,0:T(8,128)(2,1)} custom-call(s32[2]{0:T(128)} %pad_add_fusion.me_ref, bf16[16,48,1536]{2,1,0:T(8,128)(2,1)} %constant_dynamic-update-slice_fusion.14.refs_0_, bf16[16,48,1536]{2,1,0:T(8,128)(2,1)} %collective-permute-done.17.refs_1_), custom_call_target="tpu_custom_call" | custom-call | tf_op jit(solution)/shard_map/place/pallas_call | solution.py:92
  467.0 37.4 %fusion.38 = (bf16[1024,3072]{1,0:T(8,128)(2,1)}, f32[1024,3072]{1,0:T(8,128)}) fusion(f32[3072]{0:T(1024)S(1)} %reshape.447, bf16[768,3072]{1,0:T(8,128)(2,1)} %place.6, f32[1024,768]{1,0:T(8,128)} %copy-done.4, f32[768]{0:T(1024)S(1)} %add.254, f32[768]{0:T(1024)S(1)} %mul.182, f32[1024]{0:T(1024)S(1)} %add_rsqrt_fusion.1, ...), kind=kOutput, calls=%fused_computation.56 | convolution fusion | flops 5043388416 | bytes 26765312 | tf_op jit(solution)/shard_map/dot_general | solution.py:429
  504.4 145.3 %place.7 = bf16[3072,768]{1,0:T(8,128)(2,1)} custom-call(s32[2]{0:T(128)} %pad_add_fusion.me_ref, bf16[16,192,384]{2,1,0:T(8,128)(2,1)} %constant_dynamic-update-slice_fusion.19.refs_0_, bf16[16,192,384]{2,1,0:T(8,128)(2,1)} %collective-permute-done.23.refs_1_), custom_call_target="tpu_custom_call" | custom-call | tf_op jit(solution)/shard_map/place/pallas_call | solution.py:92
  649.7 9.3 fusion.101
  666.0 13.5 fusion.102
  679.6 6.6 multiply_reduce_fusion.2
  696.9 100.7 %while.27 = (s32[]{:T(128)}, bf16[2,512,768]{2,1,0:T(8,128)(2,1)}, bf16[2,512,768]{2,1,0:T(8,128)(2,1)}, bf16[2,512,768]{2,1,0:T(8,128)(2,1)}, bf16[2,512,12,64]...) while((s32[]{:T(128)}, bf16[2,512,768]{2,1,0:T(8,128)(2,1)}, ...), condition=%wide.region_14.15_spmd, body=%wide.region_12.14_spmd.sunk | while | flops 2062019072 | bytes 184399216 | solution.py:453
  697.1 7.7 fusion.167
  706.4 11.4 multiply_reduce_fusion.10
  719.3 7.1 multiply_convert_fusion.3
  730.7 8.4 fusion.168
  741.8 4.2 convolution_multiply_fusion.4
  747.2 7.7 fusion.167
  756.6 11.4 multiply_reduce_fusion.10
  769.4 7.1 multiply_convert_fusion.3
  780.8 8.4 fusion.168
  792.0 4.2 convolution_multiply_fusion.4
  797.6 4.5 fusion.60.refs_0_
  802.1 74.2 %cut.5 = (bf16[16,96,384]{2,1,0:T(8,128)(2,1)}, bf16[16,96,384]{2,1,0:T(8,128)(2,1)}) custom-call(s32[2]{0:T(128)} %pad_add_fusion.me_ref, bf16[768,768]{1,0:T(8,128)(2,1)} %fusion.60.refs_0_, bf16[768,768]{1,0:T(8,128)(2,1)} %convolution_convert_fusion.4.refs_1_), custom_call_target="tpu_custom_call" | custom-call | tf_op jit(solution)/shard_map/cut/pallas_call | solution.py:126
  877.7 4.0 fusion.58.refs_0_
  885.1 86.0 %cut.4 = (bf16[16,112,384]{2,1,0:T(8,128)(2,1)}, bf16[16,112,384]{2,1,0:T(8,128)(2,1)}) custom-call(s32[2]{0:T(128)} %pad_add_fusion.me_ref, bf16[768,768]{1,0:T(8,128)(2,1)} %fusion.58.refs_0_, bf16[768,768]{1,0:T(8,128)(2,1)} %fusion.59.refs_1_, bf16[8,16,384]{2,1,0:T(8,128)(2,1)} %fusion.69.refs_2_), custom_call_target="tpu_custom_call" | custom-call | tf_op jit(solution)/shard_map/cut/pallas_call | solution.py:126
  971.7 9.6 convolution_convert_fusion.refs_0_
  985.8 10.2 convolution_convert_fusion.1.refs_0_
  996.0 145.3 %cut.7 = (bf16[16,192,384]{2,1,0:T(8,128)(2,1)}, bf16[16,192,384]{2,1,0:T(8,128)(2,1)}) custom-call(s32[2]{0:T(128)} %pad_add_fusion.me_ref, bf16[3072,768]{1,0:T(8,128)(2,1)} %convolution_convert_fusion.refs_0_), custom_call_target="tpu_custom_call" | custom-call | tf_op jit(solution)/shard_map/cut/pallas_call | solution.py:126
  1141.4 145.3 %cut.6 = (bf16[16,48,1536]{2,1,0:T(8,128)(2,1)}, bf16[16,48,1536]{2,1,0:T(8,128)(2,1)}) custom-call(s32[2]{0:T(128)} %pad_add_fusion.me_ref, bf16[768,3072]{1,0:T(8,128)(2,1)} %convolution_convert_fusion.1.refs_0_), custom_call_target="tpu_custom_call" | custom-call | tf_op jit(solution)/shard_map/cut/pallas_call | solution.py:126
  1294.6 5.8 collective-permute-done.32
  1312.0 6.7 collective-permute-done.25
  1320.7 6.2 collective-permute-done.26
  1332.5 4.1 collective-permute-start.28
  1342.0 14.8 %collective-permute-done.43 = bf16[8,192,384]{2,1,0:T(8,128)(2,1)} collective-permute-done((bf16[8,192,384]{2,1,0:T(8,128)(2,1)}, bf16[8,192,384]{2,1,0:T(8,128)(2,1)}, u32[]{:S(2)}, u32[]{:S(2)}) %collective-permute-start.43) | collective-permute-done | bytes 1179680 | tf_op jit(solution)/shard_map/ppermute | solution.py:19
  1360.0 5.9 collective-permute-done.37
  1379.4 4.0 collective-permute-done.45
  1384.5 3.8 collective-permute-done.39
  1391.9 4.2 collective-permute-done.40
  (404 shorter events, 204.7 us)
Async XLA Ops:
  2.0 12.4 collective-permute-start.18
  3.3 6.6 collective-permute-start
  4.3 9.8 collective-permute-start.6
  5.8 12.3 collective-permute-start.12
  10.0 8.7 collective-permute-start.1
  14.3 14.5 %collective-permute-start.7 = (bf16[1,112,384]{2,1,0:T(8,128)(2,1)S(1)}, bf16[1,112,384]{2,1,0:T(8,128)(2,1)S(1)}, u32[]{:S(2)}, u32[]{:S(2)}) collective-permute-start(bf16[1,112,384]{2,1,0:T(8,128)(2,1)S(1)} %maximum_bitcast_fusion.2), channel_id=1, source_target_pairs={{0,16},{4,20},{8,24},{12,28},{16,0},{20,4},{24,8},{28,12},{1,17},{... | collective-permute-start | bytes 258056 | tf_op jit(solution)/shard_map/ppermute | solution.py:19
  15.1 16.8 %collective-permute-start.19 = (bf16[1,192,384]{2,1,0:T(8,128)(2,1)S(1)}, bf16[1,192,384]{2,1,0:T(8,128)(2,1)S(1)}, u32[]{:S(2)}, u32[]{:S(2)}) collective-permute-start(bf16[1,192,384]{2,1,0:T(8,128)(2,1)S(1)} %get-tuple-element.248), channel_id=1, source_target_pairs={{0,16},{4,20},{8,24},{12,28},{16,0},{20,4},{24,8},{28,12},{1,17},{... | collective-permute-start | bytes 442376 | tf_op jit(solution)/shard_map/ppermute | solution.py:19
  18.8 15.8 %collective-permute-start.13 = (bf16[1,48,1536]{2,1,0:T(8,128)(2,1)S(1)}, bf16[1,48,1536]{2,1,0:T(8,128)(2,1)S(1)}, u32[]{:S(2)}, u32[]{:S(2)}) collective-permute-start(bf16[1,48,1536]{2,1,0:T(8,128)(2,1)S(1)} %get-tuple-element.252), channel_id=1, source_target_pairs={{0,16},{4,20},{8,24},{12,28},{16,0},{20,4},{24,8},{28,12},{1,17},{... | collective-permute-start | bytes 442376 | tf_op jit(solution)/shard_map/ppermute | solution.py:19
  18.8 18.9 %collective-permute-start.2 = (bf16[2,96,384]{2,1,0:T(8,128)(2,1)S(1)}, bf16[2,96,384]{2,1,0:T(8,128)(2,1)S(1)}, u32[]{:S(2)}, u32[]{:S(2)}) collective-permute-start(bf16[2,96,384]{2,1,0:T(8,128)(2,1)S(1)} %pad_maximum_fusion.13), channel_id=1, source_target_pairs={{0,8},{4,12},{8,0},{12,4},{16,24},{20,28},{24,16},{28,20},{1,9},{5... | collective-permute-start | bytes 442376 | tf_op jit(solution)/shard_map/ppermute | solution.py:19
  28.8 12.6 collective-permute-start.8
  32.0 15.7 %collective-permute-start.20 = (bf16[2,192,384]{2,1,0:T(8,128)(2,1)S(1)}, bf16[2,192,384]{2,1,0:T(8,128)(2,1)S(1)}, u32[]{:S(2)}, u32[]{:S(2)}) collective-permute-start(bf16[2,192,384]{2,1,0:T(8,128)(2,1)S(1)} %pad_maximum_fusion.10), channel_id=1, source_target_pairs={{0,8},{4,12},{8,0},{12,4},{16,24},{20,28},{24,16},{28,20},{1,9},{5... | collective-permute-start | bytes 884744 | tf_op jit(solution)/shard_map/ppermute | solution.py:19
  34.6 19.3 %collective-permute-start.14 = (bf16[2,48,1536]{2,1,0:T(8,128)(2,1)S(1)}, bf16[2,48,1536]{2,1,0:T(8,128)(2,1)S(1)}, u32[]{:S(2)}, u32[]{:S(2)}) collective-permute-start(bf16[2,48,1536]{2,1,0:T(8,128)(2,1)S(1)} %pad_maximum_fusion.9), channel_id=1, source_target_pairs={{0,8},{4,12},{8,0},{12,4},{16,24},{20,28},{24,16},{28,20},{1,9},{5... | collective-permute-start | bytes 884744 | tf_op jit(solution)/shard_map/ppermute | solution.py:19
  37.8 19.8 %collective-permute-start.3 = (bf16[4,96,384]{2,1,0:T(8,128)(2,1)S(1)}, bf16[4,96,384]{2,1,0:T(8,128)(2,1)S(1)}, u32[]{:S(2)}, u32[]{:S(2)}) collective-permute-start(bf16[4,96,384]{2,1,0:T(8,128)(2,1)S(1)} %pad_maximum_fusion.8), channel_id=1, source_target_pairs={{0,4},{4,0},{8,12},{12,8},{16,20},{20,16},{24,28},{28,24},{1,5},{5... | collective-permute-start | bytes 884744 | tf_op jit(solution)/shard_map/ppermute | solution.py:19
  41.5 14.4 %collective-permute-start.9 = (bf16[4,112,384]{2,1,0:T(8,128)(2,1)S(1)}, bf16[4,112,384]{2,1,0:T(8,128)(2,1)S(1)}, u32[]{:S(2)}, u32[]{:S(2)}) collective-permute-start(bf16[4,112,384]{2,1,0:T(8,128)(2,1)S(1)} %pad_maximum_fusion.7), channel_id=1, source_target_pairs={{0,2},{1,3},{2,0},{3,1},{4,6},{5,7},{6,4},{7,5},{8,10},{9,11},{10,... | collective-permute-start | bytes 1032200 | tf_op jit(solution)/shard_map/ppermute | solution.py:19
  47.8 16.3 %collective-permute-start.21 = (bf16[4,192,384]{2,1,0:T(8,128)(2,1)S(1)}, bf16[4,192,384]{2,1,0:T(8,128)(2,1)S(1)}, u32[]{:S(2)}, u32[]{:S(2)}) collective-permute-start(bf16[4,192,384]{2,1,0:T(8,128)(2,1)S(1)} %pad_maximum_fusion.5), channel_id=1, source_target_pairs={{0,4},{4,0},{8,12},{12,8},{16,20},{20,16},{24,28},{28,24},{1,5},{5... | collective-permute-start | bytes 1769480 | tf_op jit(solution)/shard_map/ppermute | solution.py:19
  54.0 16.3 %collective-permute-start.15 = (bf16[4,48,1536]{2,1,0:T(8,128)(2,1)S(1)}, bf16[4,48,1536]{2,1,0:T(8,128)(2,1)S(1)}, u32[]{:S(2)}, u32[]{:S(2)}) collective-permute-start(bf16[4,48,1536]{2,1,0:T(8,128)(2,1)S(1)} %pad_maximum_fusion.4), channel_id=1, source_target_pairs={{0,2},{1,3},{2,0},{3,1},{4,6},{5,7},{6,4},{7,5},{8,10},{9,11},{10,... | collective-permute-start | bytes 1769480 | tf_op jit(solution)/shard_map/ppermute | solution.py:19
  55.9 22.9 %collective-permute-start.10 = (bf16[8,112,384]{2,1,0:T(8,128)(2,1)S(1)}, bf16[8,112,384]{2,1,0:T(8,128)(2,1)S(1)}, u32[]{:S(2)}, u32[]{:S(2)}) collective-permute-start(bf16[8,112,384]{2,1,0:T(8,128)(2,1)S(1)} %pad_maximum_fusion.2), channel_id=1, source_target_pairs={{0,4},{4,0},{8,12},{12,8},{16,20},{20,16},{24,28},{28,24},{1,5},{5... | collective-permute-start | bytes 2064392 | tf_op jit(solution)/shard_map/ppermute | solution.py:19
  57.6 25.3 %collective-permute-start.4 = (bf16[8,96,384]{2,1,0:T(8,128)(2,1)S(1)}, bf16[8,96,384]{2,1,0:T(8,128)(2,1)S(1)}, u32[]{:S(2)}, u32[]{:S(2)}) collective-permute-start(bf16[8,96,384]{2,1,0:T(8,128)(2,1)S(1)} %pad_maximum_fusion.3), channel_id=1, source_target_pairs={{0,2},{1,3},{2,0},{3,1},{4,6},{5,7},{6,4},{7,5},{8,10},{9,11},{10,... | collective-permute-start | bytes 1769480 | tf_op jit(solution)/shard_map/ppermute | solution.py:19
  64.2 43.1 %collective-permute-start.22 = (bf16[8,192,384]{2,1,0:T(8,128)(2,1)S(1)}, bf16[8,192,384]{2,1,0:T(8,128)(2,1)S(1)}, u32[]{:S(2)}, u32[]{:S(2)}) collective-permute-start(bf16[8,192,384]{2,1,0:T(8,128)(2,1)S(1)} %pad_maximum_fusion.1), channel_id=1, source_target_pairs={{0,2},{1,3},{2,0},{3,1},{4,6},{5,7},{6,4},{7,5},{8,10},{9,11},{10,... | collective-permute-start | bytes 3538952 | tf_op jit(solution)/shard_map/ppermute | solution.py:19
  70.4 38.1 %collective-permute-start.16 = (bf16[8,48,1536]{2,1,0:T(8,128)(2,1)S(1)}, bf16[8,48,1536]{2,1,0:T(8,128)(2,1)S(1)}, u32[]{:S(2)}, u32[]{:S(2)}) collective-permute-start(bf16[8,48,1536]{2,1,0:T(8,128)(2,1)S(1)} %pad_maximum_fusion), channel_id=1, source_target_pairs={{0,4},{4,0},{8,12},{12,8},{16,20},{20,16},{24,28},{28,24},{1,5},{5... | collective-permute-start | bytes 3538952 | tf_op jit(solution)/shard_map/ppermute | solution.py:19
  78.9 105.3 %collective-permute-start.11 = (bf16[16,112,384]{2,1,0:T(8,128)(2,1)S(1)}, bf16[16,112,384]{2,1,0:T(8,128)(2,1)S(1)}, u32[]{:S(2)}, u32[]{:S(2)}) collective-permute-start(bf16[16,112,384]{2,1,0:T(8,128)(2,1)S(1)} %constant_dynamic-update-slice_fusion.9.refs_0_), channel_id=1, source_target_pairs={{0,1},{1,0},{2,3},{3,2},{4,5},{5,4},{6,7},{7,6},{8,9},{9,8},{10,11... | collective-permute-start | bytes 4128776 | tf_op jit(solution)/shard_map/ppermute | solution.py:19
  83.0 27.1 %collective-permute-start.5 = (bf16[16,96,384]{2,1,0:T(8,128)(2,1)S(1)}, bf16[16,96,384]{2,1,0:T(8,128)(2,1)}, u32[]{:S(2)}, u32[]{:S(2)}) collective-permute-start(bf16[16,96,384]{2,1,0:T(8,128)(2,1)S(1)} %constant_dynamic-update-slice_fusion.4.refs_0_), channel_id=1, source_target_pairs={{0,1},{1,0},{2,3},{3,2},{4,5},{5,4},{6,7},{7,6},{8,9},{9,8},{10,11... | collective-permute-start | bytes 3538952 | tf_op jit(solution)/shard_map/ppermute | solution.py:19
  108.5 395.8 %collective-permute-start.23 = (bf16[16,192,384]{2,1,0:T(8,128)(2,1)}, bf16[16,192,384]{2,1,0:T(8,128)(2,1)}, u32[]{:S(2)}, u32[]{:S(2)}) collective-permute-start(bf16[16,192,384]{2,1,0:T(8,128)(2,1)} %constant_dynamic-update-slice_fusion.19.refs_0_), channel_id=1, source_target_pairs={{0,1},{1,0},{2,3},{3,2},{4,5},{5,4},{6,7},{7,6},{8,9},{9,8},{10,11... | collective-permute-start | bytes 7077896 | tf_op jit(solution)/shard_map/ppermute | solution.py:19
  109.7 212.0 %collective-permute-start.17 = (bf16[16,48,1536]{2,1,0:T(8,128)(2,1)}, bf16[16,48,1536]{2,1,0:T(8,128)(2,1)}, u32[]{:S(2)}, u32[]{:S(2)}) collective-permute-start(bf16[16,48,1536]{2,1,0:T(8,128)(2,1)} %constant_dynamic-update-slice_fusion.14.refs_0_), channel_id=1, source_target_pairs={{0,1},{1,0},{2,3},{3,2},{4,5},{5,4},{6,7},{7,6},{8,9},{9,8},{10,11... | collective-permute-start | bytes 7077896 | tf_op jit(solution)/shard_map/ppermute | solution.py:19
  876.3 105.0 %collective-permute-start.30 = (bf16[16,96,384]{2,1,0:T(8,128)(2,1)}, bf16[16,96,384]{2,1,0:T(8,128)(2,1)}, u32[]{:S(2)}, u32[]{:S(2)}) collective-permute-start(bf16[16,96,384]{2,1,0:T(8,128)(2,1)} %get-tuple-element.130), channel_id=1, source_target_pairs={{0,1},{1,0},{2,3},{3,2},{4,5},{5,4},{6,7},{7,6},{8,9},{9,8},{10,11... | collective-permute-start | bytes 3538952 | tf_op jit(solution)/shard_map/ppermute | solution.py:19
  971.1 329.4 %collective-permute-start.24 = (bf16[16,112,384]{2,1,0:T(8,128)(2,1)}, bf16[16,112,384]{2,1,0:T(8,128)(2,1)}, u32[]{:S(2)}, u32[]{:S(2)}) collective-permute-start(bf16[16,112,384]{2,1,0:T(8,128)(2,1)} %get-tuple-element.128), channel_id=1, source_target_pairs={{0,1},{1,0},{2,3},{3,2},{4,5},{5,4},{6,7},{7,6},{8,9},{9,8},{10,11... | collective-permute-start | bytes 4128776 | tf_op jit(solution)/shard_map/ppermute | solution.py:19
  984.1 306.2 %collective-permute-start.31 = (bf16[8,96,384]{2,1,0:T(8,128)(2,1)}, bf16[8,96,384]{2,1,0:T(8,128)(2,1)}, u32[]{:S(2)}, u32[]{:S(2)}) collective-permute-start(bf16[8,96,384]{2,1,0:T(8,128)(2,1)} %get-tuple-element.271), channel_id=1, source_target_pairs={{0,2},{1,3},{2,0},{3,1},{4,6},{5,7},{6,4},{7,5},{8,10},{9,11},{10,... | collective-permute-start | bytes 1769480 | tf_op jit(solution)/shard_map/ppermute | solution.py:19
  1141.3 187.2 %collective-permute-start.42 = (bf16[16,192,384]{2,1,0:T(8,128)(2,1)}, bf16[16,192,384]{2,1,0:T(8,128)(2,1)}, u32[]{:S(2)}, u32[]{:S(2)}) collective-permute-start(bf16[16,192,384]{2,1,0:T(8,128)(2,1)} %get-tuple-element.134), channel_id=1, source_target_pairs={{0,1},{1,0},{2,3},{3,2},{4,5},{5,4},{6,7},{7,6},{8,9},{9,8},{10,11... | collective-permute-start | bytes 7077896 | tf_op jit(solution)/shard_map/ppermute | solution.py:19
  1286.7 49.9 %collective-permute-start.36 = (bf16[16,48,1536]{2,1,0:T(8,128)(2,1)}, bf16[16,48,1536]{2,1,0:T(8,128)(2,1)S(1)}, u32[]{:S(2)}, u32[]{:S(2)}) collective-permute-start(bf16[16,48,1536]{2,1,0:T(8,128)(2,1)} %get-tuple-element.132), channel_id=1, source_target_pairs={{0,1},{1,0},{2,3},{3,2},{4,5},{5,4},{6,7},{7,6},{8,9},{9,8},{10,11... | collective-permute-start | bytes 7077896 | tf_op jit(solution)/shard_map/ppermute | solution.py:19
  1291.5 8.9 collective-permute-start.32
  1300.4 5.2 collective-permute-start.33
  1302.2 16.4 %collective-permute-start.25 = (bf16[8,112,384]{2,1,0:T(8,128)(2,1)S(1)}, bf16[8,112,384]{2,1,0:T(8,128)(2,1)S(1)}, u32[]{:S(2)}, u32[]{:S(2)}) collective-permute-start(bf16[8,112,384]{2,1,0:T(8,128)(2,1)S(1)} %get-tuple-element.265), channel_id=1, source_target_pairs={{0,4},{4,0},{8,12},{12,8},{16,20},{20,16},{24,28},{28,24},{1,5},{5... | collective-permute-start | bytes 2064392 | tf_op jit(solution)/shard_map/ppermute | solution.py:19
  1305.7 6.1 collective-permute-start.34
  1311.9 7.4 collective-permute-start.35
  1318.8 8.1 collective-permute-start.26
  1327.0 5.5 collective-permute-start.27
  1332.0 24.8 %collective-permute-start.43 = (bf16[8,192,384]{2,1,0:T(8,128)(2,1)}, bf16[8,192,384]{2,1,0:T(8,128)(2,1)}, u32[]{:S(2)}, u32[]{:S(2)}) collective-permute-start(bf16[8,192,384]{2,1,0:T(8,128)(2,1)} %get-tuple-element.260), channel_id=1, source_target_pairs={{0,2},{1,3},{2,0},{3,1},{4,6},{5,7},{6,4},{7,5},{8,10},{9,11},{10,... | collective-permute-start | bytes 3538952 | tf_op jit(solution)/shard_map/ppermute | solution.py:19
  1332.5 7.4 collective-permute-start.28
  1338.4 27.5 %collective-permute-start.37 = (bf16[8,48,1536]{2,1,0:T(8,128)(2,1)}, bf16[8,48,1536]{2,1,0:T(8,128)(2,1)}, u32[]{:S(2)}, u32[]{:S(2)}) collective-permute-start(bf16[8,48,1536]{2,1,0:T(8,128)(2,1)} %get-tuple-element.262), channel_id=1, source_target_pairs={{0,4},{4,0},{8,12},{12,8},{16,20},{20,16},{24,28},{28,24},{1,5},{5... | collective-permute-start | bytes 3538952 | tf_op jit(solution)/shard_map/ppermute | solution.py:19
  1340.0 1.9 collective-permute-start.29
  1358.4 15.6 %collective-permute-start.44 = (bf16[4,192,384]{2,1,0:T(8,128)(2,1)S(1)}, bf16[4,192,384]{2,1,0:T(8,128)(2,1)S(1)}, u32[]{:S(2)}, u32[]{:S(2)}) collective-permute-start(bf16[4,192,384]{2,1,0:T(8,128)(2,1)S(1)} %get-tuple-element.267), channel_id=1, source_target_pairs={{0,4},{4,0},{8,12},{12,8},{16,20},{20,16},{24,28},{28,24},{1,5},{5... | collective-permute-start | bytes 1769480 | tf_op jit(solution)/shard_map/ppermute | solution.py:19
  1367.4 10.4 collective-permute-start.38
  1374.1 9.3 collective-permute-start.45
  1377.9 10.4 collective-permute-start.39
  1383.5 8.2 collective-permute-start.46
  1388.4 7.7 collective-permute-start.40
  1391.8 4.4 collective-permute-start.47
  1396.1 1.3 collective-permute-start.41
  (65 other events, 2480.3 us)

commit v2 on v1

--- a/solution.py
+++ b/solution.py
@@ -65,7 +65,7 @@
 def place_kernel(stages, rows, width, with_small, me_ref, *refs):
     sources, outs, sems = refs[:2], refs[2:-1], refs[-1]
     mine = {"dp": me_ref[0], "fsdp": me_ref[1]}
-    seen, started = set(), []
+    started = []
     for flip, place, at, count, w, row, column in copy_list(stages, rows, mine, with_small, False):
         source = sources[flip].at[place, pl.ds(at, count), :]
         if column is None:
@@ -93,7 +93,8 @@
         functools.partial(place_kernel, stages, rows, width, with_small),
         out_shape=tuple(shapes),
         in_specs=[pl.BlockSpec(memory_space=pltpu.SMEM), anywhere, anywhere],
-        out_specs=(anywhere,) * len(shapes),
+        out_specs=(pl.BlockSpec(memory_space=pltpu.VMEM),) * len(shapes),
+        compiler_params=pltpu.CompilerParams(vmem_limit_bytes=VMEM_BYTES),
         scratch_shapes=[pltpu.SemaphoreType.DMA((2 * (1 << len(stages)) * (len(rows) + 1),))],
         name="place",
     )(me, own, other)
@@ -126,8 +127,10 @@
     return pl.pallas_call(
         functools.partial(cut_kernel, stages, rows, width, small is not None),
         out_shape=(shape, shape),
-        in_specs=[pl.BlockSpec(memory_space=pltpu.SMEM)] + [anywhere] * len(operands),
+        in_specs=[pl.BlockSpec(memory_space=pltpu.SMEM)]
+        + [pl.BlockSpec(memory_space=pltpu.VMEM)] * len(operands),
         out_specs=(anywhere, anywhere),
+        compiler_params=pltpu.CompilerParams(vmem_limit_bytes=VMEM_BYTES),
         scratch_shapes=[pltpu.SemaphoreType.DMA((2 * places * (len(rows) + 1),))],
         name="cut",
     )(me, *operands)
@@ -181,6 +184,472 @@
     return outs
 
 
+VMEM_BYTES = 56 << 20
+
+
+def dot(left, right):
+    return jnp.dot(left, right, preferred_element_type=jnp.float32)
+
+
+def dot_last(left, right):
+    return lax.dot_general(
+        left, right, (((1,), (1,)), ((), ())), preferred_element_type=jnp.float32
+    )
+
+
+def dot_first(left, right):
+    return lax.dot_general(
+        left, right, (((0,), (0,)), ((), ())), preferred_element_type=jnp.float32
+    )
+
+
+def normalize(values):
+    centered = values - jnp.mean(values, axis=-1, keepdims=True)
+    variance = jnp.mean(centered * centered, axis=-1, keepdims=True)
+    factor = lax.rsqrt(variance + EPSILON)
+    return (centered * factor, factor)
+
+
+def norm_back(upward, normed, factor):
+    return factor * (
+        upward
+        - jnp.mean(upward, axis=-1, keepdims=True)
+        - normed * jnp.mean(upward * normed, axis=-1, keepdims=True)
+    )
+
+
+def gelu_pair(v):
+    size = jnp.abs(v) * 0.7071067811865476
+    t = 1.0 / (1.0 + 0.3275911 * size)
+    bell = jnp.exp(-size * size)
+    poly = t * (
+        0.254829592
+        + t * (-0.284496736 + t * (1.421413741 + t * (-1.453152027 + t * 1.061405429)))
+    )
+    tail = 0.5 * poly * bell
+    cdf = jnp.where(v >= 0.0, 1.0 - tail, tail)
+    return v * cdf, cdf + v * bell * 0.3989422804014327
+
+
+def three_parts(value):
+    high = value.astype(jnp.bfloat16).astype(jnp.float32)
+    rest = value - high
+    middle = rest.astype(jnp.bfloat16).astype(jnp.float32)
+    return high, middle, rest - middle
+
+
+def head_keys(pair, head, length, with_stats):
+    rows, lanes = pair.shape
+    lane = lax.broadcasted_iota(jnp.int32, (rows, lanes), 1)
+    row = lax.broadcasted_iota(jnp.int32, (rows, lanes), 0)
+    start = lanes // 2 if head == 0 else 0
+    own = lane < lanes // 2 if head == 0 else lane >= lanes // 2
+    hidden = jnp.where((lane == start) & (row >= length), MASKED, 0.0)
+    if with_stats:
+        hidden = jnp.where((lane > start) & (lane < start + 4), 1.0, hidden)
+    return jnp.where(own, pair.astype(jnp.float32), hidden).astype(jnp.bfloat16)
+
+
+def head_values(pair, head):
+    rows, lanes = pair.shape
+    lane = lax.broadcasted_iota(jnp.int32, (rows, lanes), 1)
+    start = lanes // 2 if head == 0 else 0
+    own = lane < lanes // 2 if head == 0 else lane >= lanes // 2
+    ones = jnp.where((lane >= start) & (lane < start + 3), 1.0, 0.0)
+    return jnp.where(own, pair.astype(jnp.float32), ones).astype(jnp.bfloat16)
+
+
+def only_head(pair, head):
+    lane = lax.broadcasted_iota(jnp.int32, pair.shape, 1)
+    own = lane < pair.shape[1] // 2 if head == 0 else lane >= pair.shape[1] // 2
+    return jnp.where(own, pair.astype(jnp.float32), 0.0).astype(jnp.bfloat16)
+
+
+def with_rows(part, head, rows):
+    count, width = part.shape
+    row = lax.broadcasted_iota(jnp.int32, (count, width), 0)
+    extra = jnp.zeros((count, width), jnp.float32)
+    for i, value in enumerate(rows):
+        extra = jnp.where(row == i, value, extra)
+    extra = extra.astype(jnp.bfloat16)
+    return jnp.concatenate([part, extra] if head == 0 else [extra, part], axis=0)
+
+
+def forward_kernel(
+    lengths, x_ref, wq_ref, wk_ref, wv_ref, wo_ref, vec_ref,
+    q_ref, k_ref, v_ref, att_ref, lse_ref, first_ref, qt, vt, ot,
+):
+    length = lengths[pl.program_id(0)]
+    x = x_ref[...]
+    head_size = x.shape[1] // HEADS
+    scale = head_size**-0.5
+    queries = (dot(x, wq_ref[...]) + vec_ref[0:1, :]).astype(jnp.bfloat16)
+    queries = (queries.astype(jnp.float32) * scale).astype(jnp.bfloat16)
+    q_ref[...] = queries
+    qt[...] = queries.T
+    k_ref[...] = dot(x, wk_ref[...]).astype(jnp.bfloat16)
+    values = (dot(x, wv_ref[...]) + vec_ref[1:2, :]).astype(jnp.bfloat16)
+    v_ref[...] = values
+    vt[...] = values.T
+
+    def one_pair(p, carry):
+        base = pl.multiple_of(p * 2 * head_size, 2 * head_size)
+        pair = k_ref[:, pl.ds(base, 2 * head_size)]
+        for head in range(2):
+            at = pl.multiple_of(base + head * head_size, head_size)
+            keys = head_keys(pair, head, length, False)
+            scores = dot(keys, with_rows(qt[pl.ds(at, head_size), :], head, [1.0]))
+            highest = jnp.max(scores, axis=0, keepdims=True)
+            exponent = jnp.exp(scores - highest)
+            total = jnp.sum(exponent, axis=0, keepdims=True)
+            blended = dot(vt[pl.ds(at, head_size), :], exponent.astype(jnp.bfloat16))
+            ot[pl.ds(at, head_size), :] = (blended / total).astype(jnp.bfloat16)
+            lse_ref[p, head : head + 1, :] = highest + jnp.log(total)
+        return carry
+
+    lax.fori_loop(0, HEADS // 2, one_pair, 0)
+    attended = ot[...].T
+    att_ref[...] = attended
+    first_ref[...] = x.astype(jnp.float32) + dot(attended, wo_ref[...]) + vec_ref[2:3, :]
+
+
+def whole(shape):
+    return pl.BlockSpec(shape, lambda *_: (0,) * len(shape))
+
+
+def attend_forward(x, lengths, wq, wk, wv, wo, vectors):
+    seqs, slots, width = x.shape
+    rows = pl.BlockSpec((None, slots, width), lambda i, *_: (i, 0, 0))
+    low = jax.ShapeDtypeStruct(x.shape, jnp.bfloat16)
+    return pl.pallas_call(
+        forward_kernel,
+        grid_spec=pltpu.PrefetchScalarGridSpec(
+            num_scalar_prefetch=1,
+            grid=(seqs,),
+            in_specs=[rows] + [whole((width, width))] * 4 + [whole(vectors.shape)],
+            out_specs=[rows] * 4
+            + [pl.BlockSpec((None, HEADS // 2, 2, slots), lambda i, *_: (i, 0, 0, 0)), rows],
+            scratch_shapes=[pltpu.VMEM((width, slots), jnp.bfloat16)] * 3,
+        ),
+        out_shape=[low] * 4
+        + [
+            jax.ShapeDtypeStruct((seqs, HEADS // 2, 2, slots), jnp.float32),
+            jax.ShapeDtypeStruct(x.shape, jnp.float32),
+        ],
+        compiler_params=pltpu.CompilerParams(vmem_limit_bytes=VMEM_BYTES),
+        name="attend_forward",
+    )(lengths, x, wq, wk, wv, wo, vectors)
+
+
+def feed_kernel(
+    tiles, chunk, lengths, first_ref, cot_ref, wi_ref, wo_ref, hb_ref, vec_ref,
+    out_ref, act_ref, slope_ref, mid_ref, gs_ref, low_ref, sums_ref,
+):
+    step = pl.program_id(0)
+    count = first_ref.shape[0]
+    normed, _ = normalize(first_ref[...])
+    middle = normed * vec_ref[4:5, :] + vec_ref[6:7, :]
+    middle_low = middle.astype(jnp.bfloat16)
+    mid_ref[...] = middle_low
+    second = middle + vec_ref[3:4, :]
+    for at in range(0, wi_ref.shape[1], chunk):
+        here = slice(at, at + chunk)
+        hidden = dot(middle_low, wi_ref[:, here]) + hb_ref[:, here]
+        active, slope = gelu_pair(hidden)
+        active = active.astype(jnp.bfloat16)
+        act_ref[:, here] = active
+        slope_ref[:, here] = slope.astype(jnp.bfloat16)
+        second = second + dot(active, wo_ref[here, :])
+    normed, factor = normalize(second)
+    slot = (step % tiles) * count + lax.broadcasted_iota(jnp.int32, (count, 1), 0)
+    mask = (slot < lengths[step // tiles]).astype(jnp.float32)
+    out_ref[...] = ((normed * vec_ref[5:6, :] + vec_ref[7:8, :]) * mask).astype(jnp.bfloat16)
+    upward = cot_ref[...].astype(jnp.float32) * mask
+    grad = norm_back(upward * vec_ref[5:6, :], normed, factor)
+    gs_ref[...] = grad
+    low = grad.astype(jnp.bfloat16)
+    low_ref[...] = low
+
+    @pl.when(step == 0)
+    def _():
+        sums_ref[...] = jnp.zeros_like(sums_ref)
+
+    sums_ref[0:1, :] += jnp.sum(upward * normed, axis=0, keepdims=True)
+    sums_ref[1:2, :] += jnp.sum(upward, axis=0, keepdims=True)
+    sums_ref[2:3, :] += jnp.sum(low.astype(jnp.float32), axis=0, keepdims=True)
+
+
+def feed_forward(first, cotangent, lengths, wi, wo, hidden_bias, vectors):
+    seqs, slots, width = first.shape
+    inner = wi.shape[1]
+    count = min(256, slots)
+    tiles = slots // count
+    total = seqs * slots
+    rows = pl.BlockSpec((count, width), lambda i, *_: (i, 0))
+    wide = pl.BlockSpec((count, inner), lambda i, *_: (i, 0))
+
+    def shape(columns, kind):
+        return jax.ShapeDtypeStruct((total, columns), kind)
+
+    return pl.pallas_call(
+        functools.partial(feed_kernel, tiles, min(512, inner)),
+        grid_spec=pltpu.PrefetchScalarGridSpec(
+            num_scalar_prefetch=1,
+            grid=(seqs * tiles,),
+            in_specs=[rows, rows, whole(wi.shape), whole(wo.shape), whole((1, inner)), whole(vectors.shape)],
+            out_specs=[rows, wide, wide, rows, rows, rows, whole((8, width))],
+        ),
+        out_shape=[
+            shape(width, jnp.bfloat16),
+            shape(inner, jnp.bfloat16),
+            shape(inner, jnp.bfloat16),
+            shape(width, jnp.bfloat16),
+            shape(width, jnp.float32),
+            shape(width, jnp.bfloat16),
+            jax.ShapeDtypeStruct((8, width), jnp.float32),
+        ],
+        compiler_params=pltpu.CompilerParams(vmem_limit_bytes=VMEM_BYTES),
+        name="feed_forward",
+    )(lengths, first.reshape(total, width), cotangent.reshape(total, width), wi, wo, hidden_bias, vectors)
+
+
+def feed_back_outer_kernel(low_ref, act_ref, slope_ref, wo_ref, hid_ref, grad_ref, sum_ref):
+    low = low_ref[...]
+    up = dot_last(low, wo_ref[...]) * slope_ref[...].astype(jnp.float32)
+    hidden = up.astype(jnp.bfloat16)
+    hid_ref[...] = hidden
+    sum_ref[...] = jnp.sum(hidden.astype(jnp.float32), axis=0, keepdims=True)
+    grad_ref[...] = dot_first(act_ref[...], low).astype(jnp.bfloat16)
+
+
+def feed_back_outer(low, act, slope, wo):
+    total, width = low.shape
+    inner = act.shape[1]
+    chunk = min(512, inner)
+    wide = pl.BlockSpec((total, chunk), lambda i: (0, i))
+    tall = pl.BlockSpec((chunk, width), lambda i: (i, 0))
+    return pl.pallas_call(
+        feed_back_outer_kernel,
+        grid=(inner // chunk,),
+        in_specs=[whole((total, width)), wide, wide, tall],
+        out_specs=[wide, tall, pl.BlockSpec((1, chunk), lambda i: (0, i))],
+        out_shape=[
+            jax.ShapeDtypeStruct((total, inner), jnp.bfloat16),
+            jax.ShapeDtypeStruct((inner, width), jnp.bfloat16),
+            jax.ShapeDtypeStruct((1, inner), jnp.float32),
+        ],
+        compiler_params=pltpu.CompilerParams(vmem_limit_bytes=VMEM_BYTES),
+        name="feed_back_outer",
+    )(low, act, slope, wo)
+
+
+def feed_back_inner_kernel(gs_ref, mid_ref, hid_ref, wi_ref, gm_ref, grad_ref, mid_t):
+    step = pl.program_id(0)
+
+    @pl.when(step == 0)
+    def _():
+        gm_ref[...] = gs_ref[...]
+        mid_t[...] = mid_ref[...].T
+
+    hidden = hid_ref[...]
+    grad_ref[...] = dot(mid_t[...], hidden).astype(jnp.bfloat16)
+    gm_ref[...] += dot_last(hidden, wi_ref[...])
+
+
+def feed_back_inner(gs, mid, hid, wi):
+    total, width = mid.shape
+    inner = hid.shape[1]
+    chunk = min(512, inner)
+    wide = pl.BlockSpec((total, chunk), lambda i: (0, i))
+    flat = pl.BlockSpec((width, chunk), lambda i: (0, i))
+    return pl.pallas_call(
+        feed_back_inner_kernel,
+        grid=(inner // chunk,),
+        in_specs=[whole((total, width)), whole((total, width)), wide, flat],
+        out_specs=[whole((total, width)), flat],
+        out_shape=[
+            jax.ShapeDtypeStruct((total, width), jnp.float32),
+            jax.ShapeDtypeStruct((width, inner), jnp.bfloat16),
+        ],
+        scratch_shapes=[pltpu.VMEM((width, total), jnp.bfloat16)],
+        compiler_params=pltpu.CompilerParams(vmem_limit_bytes=VMEM_BYTES),
+        name="feed_back_inner",
+    )(gs, mid, hid, wi)
+
+
+def backward_kernel(
+    lengths, gm_ref, first_ref, q_ref, k_ref, v_ref, att_ref, lse_ref, wo_ref, vec_ref,
+    gf_ref, dq_ref, dk_ref, dv_ref, og_ref, sums_ref,
+    qt, kt, at_t, do_s, do_t, dq_t, total_s,
+):
+    step = pl.program_id(0)
+    length = lengths[step]
+    slots, width = gm_ref.shape
+    head_size = width // HEADS
+    scale = head_size**-0.5
+    grad_middle = gm_ref[...]
+    normed, factor = normalize(first_ref[...])
+
+    @pl.when(step == 0)
+    def _():
+        sums_ref[...] = jnp.zeros_like(sums_ref)
+        total_s[...] = jnp.zeros_like(total_s)
+
+    sums_ref[0:1, :] += jnp.sum(grad_middle * normed, axis=0, keepdims=True)
+    sums_ref[1:2, :] += jnp.sum(grad_middle, axis=0, keepdims=True)
+    grad_first = norm_back(grad_middle * vec_ref[4:5, :], normed, factor)
+    gf_ref[...] = grad_first
+    branch = grad_first.astype(jnp.bfloat16)
+    sums_ref[2:3, :] += jnp.sum(branch.astype(jnp.float32), axis=0, keepdims=True)
+    at_t[...] = att_ref[...].T
+    total_s[...] += dot(at_t[...], branch)
+
+    @pl.when(step == pl.num_programs(0) - 1)
+    def _():
+        og_ref[...] = total_s[...].astype(jnp.bfloat16)
+
+    upward = dot_last(branch, wo_ref[...]).astype(jnp.bfloat16)
+    do_s[...] = upward
+    do_t[...] = upward.T
+    qt[...] = q_ref[...].T
+    kt[...] = k_ref[...].T
+
+    def one_pair(p, carry):
+        base = pl.multiple_of(p * 2 * head_size, 2 * head_size)
+        here = pl.ds(base, 2 * head_size)
+        key_pair, value_pair = k_ref[:, here], v_ref[:, here]
+        query_pair, up_pair = q_ref[:, here], do_s[:, here]
+        grad_keys = grad_values = None
+        for head in range(2):
+            at = pl.multiple_of(base + head * head_size, head_size)
+            mine = pl.ds(at, head_size)
+            logs = [-part for part in three_parts(lse_ref[p, head : head + 1, :])]
+            keys = head_keys(key_pair, head, length, True)
+            soft = jnp.exp(dot(keys, with_rows(qt[mine, :], head, [1.0] + logs)))
+            up = do_t[mine, :]
+            delta = jnp.sum(
+                up.astype(jnp.float32) * at_t[mine, :].astype(jnp.float32), axis=0, keepdims=True
+            )
+            deltas = [-part for part in three_parts(delta)]
+            grad_soft = dot(head_values(value_pair, head), with_rows(up, head, deltas))
+            scores = (soft * grad_soft).astype(jnp.bfloat16)
+            from_values = dot(soft.astype(jnp.bfloat16), only_head(up_pair, head))
+            from_keys = dot(scores, only_head(query_pair, head))
+            grad_values = from_values if head == 0 else grad_values + from_values
+            grad_keys = from_keys if head == 0 else grad_keys + from_keys
+            dq_t[mine, :] = (dot(kt[mine, :], scores) * scale).astype(jnp.bfloat16)
+        dk_ref[:, here] = grad_keys.astype(jnp.bfloat16)
+        dv_ref[:, here] = grad_values.astype(jnp.bfloat16)
+        return carry
+
+    lax.fori_loop(0, HEADS // 2, one_pair, 0)
+    dq_ref[...] = dq_t[...].T
+
+
+def attend_backward(gm, first, q, k, v, att, lse, lengths, wo, vectors):
+    seqs, slots, width = q.shape
+    rows = pl.BlockSpec((None, slots, width), lambda i, *_: (i, 0, 0))
+    low = jax.ShapeDtypeStruct(q.shape, jnp.bfloat16)
+    turned = pltpu.VMEM((width, slots), jnp.bfloat16)
+    return pl.pallas_call(
+        backward_kernel,
+        grid_spec=pltpu.PrefetchScalarGridSpec(
+            num_scalar_prefetch=1,
+            grid=(seqs,),
+            in_specs=[rows] * 6
+            + [
+                pl.BlockSpec((None, HEADS // 2, 2, slots), lambda i, *_: (i, 0, 0, 0)),
+                whole((width, width)),
+                whole(vectors.shape),
+            ],
+            out_specs=[rows] * 4 + [whole((width, width)), whole((8, width))],
+            scratch_shapes=[
+                turned, turned, turned, pltpu.VMEM((slots, width), jnp.bfloat16), turned, turned,
+                pltpu.VMEM((width, width), jnp.float32),
+            ],
+        ),
+        out_shape=[
+            jax.ShapeDtypeStruct(q.shape, jnp.float32), low, low, low,
+            jax.ShapeDtypeStruct((width, width), jnp.bfloat16),
+            jax.ShapeDtypeStruct((8, width), jnp.float32),
+        ],
+        compiler_params=pltpu.CompilerParams(vmem_limit_bytes=VMEM_BYTES),
+        name="attend_backward",
+    )(lengths, gm, first, q, k, v, att, lse, wo, vectors)
+
+
+def project_grads_kernel(x_ref, dq_ref, dk_ref, dv_ref, gq_ref, gk_ref, gv_ref, sums_ref, xt):
+    xt[...] = x_ref[...].T
+    gq_ref[...] = dot(xt[...], dq_ref[...]).astype(jnp.bfloat16)
+    gk_ref[...] = dot(xt[...], dk_ref[...]).astype(jnp.bfloat16)
+    gv_ref[...] = dot(xt[...], dv_ref[...]).astype(jnp.bfloat16)
+    sums_ref[...] = jnp.zeros_like(sums_ref)
+    sums_ref[0:1, :] = jnp.sum(dq_ref[...].astype(jnp.float32), axis=0, keepdims=True)
+    sums_ref[1:2, :] = jnp.sum(dv_ref[...].astype(jnp.float32), axis=0, keepdims=True)
+
+
+def project_grads(x, dq, dk, dv):
+    total, width = x.shape
+    grad = jax.ShapeDtypeStruct((width, width), jnp.bfloat16)
+    return pl.pallas_call(
+        project_grads_kernel,
+        out_shape=[grad, grad, grad, jax.ShapeDtypeStruct((8, width), jnp.float32)],
+        scratch_shapes=[pltpu.VMEM((width, total), jnp.bfloat16)],
+        compiler_params=pltpu.CompilerParams(vmem_limit_bytes=VMEM_BYTES),
+        name="project_grads",
+    )(x, dq, dk, dv)
+
+
+def input_grad_kernel(gf_ref, dq_ref, dk_ref, dv_ref, wq_ref, wk_ref, wv_ref, out_ref):
+    grad = gf_ref[...] + dot_last(dq_ref[...], wq_ref[...])
+    grad = grad + dot_last(dk_ref[...], wk_ref[...])
+    grad = grad + dot_last(dv_ref[...], wv_ref[...])
+    out_ref[...] = grad.astype(jnp.bfloat16)
+
+
+def input_grads(gf, dq, dk, dv, wq, wk, wv):
+    total, width = dq.shape
+    count = min(256, total)
+    rows = pl.BlockSpec((count, width), lambda i: (i, 0))
+    return pl.pallas_call(
+        input_grad_kernel,
+        grid=(total // count,),
+        in_specs=[rows] * 4 + [whole((width, width))] * 3,
+        out_specs=rows,
+        out_shape=jax.ShapeDtypeStruct((total, width), jnp.bfloat16),
+        compiler_params=pltpu.CompilerParams(vmem_limit_bytes=VMEM_BYTES),
+        name="input_grads",
+    )(gf, dq, dk, dv, wq, wk, wv)
+
+
+def layer_step(inputs, lengths, upstream, weights):
+    wq, wk, wv, wo, wi, wf, bias, hidden, gains, shifts = weights
+    shape = inputs.shape
+    flat = (shape[0] * shape[1], shape[2])
+    vectors = jnp.concatenate([bias, gains, shifts], axis=0).astype(jnp.float32)
+    hidden_bias = hidden.astype(jnp.float32)[None]
+    q, k, v, att, lse, first = attend_forward(inputs, lengths, wq, wk, wv, wo, vectors)
+    outputs, act, slope, mid, gs, low, sums_two = feed_forward(
+        first, upstream, lengths, wi, wf, hidden_bias, vectors
+    )
+    hid, outer_grad, hidden_sum = feed_back_outer(low, act, slope, wf)
+    gm, inner_grad = feed_back_inner(gs, mid, hid, wi)
+    gf, dq, dk, dv, output_grad, sums_one = attend_backward(
+        gm.reshape(shape), first, q, k, v, att, lse, lengths, wo, vectors
+    )
+    dq, dk, dv = dq.reshape(flat), dk.reshape(flat), dv.reshape(flat)
+    query_grad, key_grad, value_grad, sums_in = project_grads(inputs.reshape(flat), dq, dk, dv)
+    input_grad = input_grads(gf.reshape(flat), dq, dk, dv, wq, wk, wv)
+    bias_grad = jnp.concatenate([sums_in[:2], sums_one[2:3], sums_two[2:3]], axis=0)
+    gain_grad = jnp.concatenate([sums_one[:1], sums_two[:1]], axis=0)
+    shift_grad = jnp.concatenate([sums_one[1:2], sums_two[1:2]], axis=0)
+    grads = (
+        query_grad, key_grad, value_grad, output_grad, inner_grad, outer_grad,
+        bias_grad, hidden_sum[0], gain_grad, shift_grad,
+    )
+    return outputs.reshape(shape), input_grad.reshape(shape), grads
+
+
 def split_up(value, dim, size):
     before, after = (value.shape[:dim], value.shape[dim + 1 :])
     return jnp.moveaxis(value.reshape(*before, size, -1, *after), dim, 0)
@@ -199,91 +668,6 @@
         ends.append(at)
     both = jnp.concatenate(arrays, axis=along)
     return tuple(jnp.split(sum_at_owner(both, axis, dim), ends, axis=along))
-
-
-def normalize(values):
-    centered = values - jnp.mean(values, axis=-1, keepdims=True)
-    variance = jnp.mean(centered * centered, axis=-1, keepdims=True)
-    factor = lax.rsqrt(variance + EPSILON)
-    return (centered * factor, factor)
-
-
-def norm_back(upward, normed, factor):
-    return factor * (
-        upward
-        - jnp.mean(upward, axis=-1, keepdims=True)
-        - normed * jnp.mean(upward * normed, axis=-1, keepdims=True)
-    )
-
-
-def gelu_slope(hidden_pre):
-    cumulative = 0.5 * (1.0 + lax.erf(hidden_pre * 0.7071067811865476))
-    return cumulative + hidden_pre * jnp.exp(-0.5 * hidden_pre * hidden_pre) * 0.3989422804014327
-
-
-def outer_sum(left, right):
-    return lax.dot_general(
-        left, right, (((0,), (0,)), ((), ())), preferred_element_type=jnp.float32
-    )
-
-
-def back_product(upward, weight):
-    return lax.dot_general(
-        upward, weight, (((1,), (1,)), ((), ())), preferred_element_type=jnp.float32
-    )
-
-
-def column_sums(values):
-    return jnp.sum(values.astype(jnp.float32), axis=0)
-
-
-def masked_scores(queries, keys_seq, length):
-    factor = queries.shape[-1] ** (-0.5)
-    scores = (
-        jnp.einsum("qhd,khd->hqk", queries, keys_seq, preferred_element_type=jnp.float32) * factor
-    )
-    visible = lax.broadcasted_iota(jnp.int32, scores.shape, 2) < length
-    return (jnp.where(visible, scores, MASKED), factor)
-
-
-def attend_forward(inputs):
-    queries, keys_seq, values_seq, length = inputs
-    scores, factor = masked_scores(queries, keys_seq, length)
-    highest = jnp.max(scores, axis=-1, keepdims=True)
-    exponent = jnp.exp(scores - highest)
-    row_total = jnp.sum(exponent, axis=-1, keepdims=True)
-    soft_low = (exponent / row_total).astype(jnp.bfloat16)
-    blended = jnp.einsum("hqk,khd->qhd", soft_low, values_seq, preferred_element_type=jnp.float32)
-    return (blended.reshape(blended.shape[0], -1), (highest + jnp.log(row_total))[..., 0])
-
-
-def attend_backward(inputs):
-    queries, keys_seq, values_seq, upward, logsum, length = inputs
-    scores, factor = masked_scores(queries, keys_seq, length)
-    soft = jnp.exp(scores - logsum[..., None])
-    soft_low = soft.astype(jnp.bfloat16)
-    upward_heads = upward.reshape(queries.shape)
-    grad_soft = jnp.einsum(
-        "qhd,khd->hqk", upward_heads, values_seq, preferred_element_type=jnp.float32
-    )
-    grad_values = jnp.einsum(
-        "hqk,qhd->khd", soft_low, upward_heads, preferred_element_type=jnp.float32
-    )
-    inner = jnp.sum(soft * grad_soft, axis=-1, keepdims=True)
-    scores_low = (soft * (grad_soft - inner)).astype(jnp.bfloat16)
-    grad_queries = (
-        jnp.einsum("hqk,khd->qhd", scores_low, keys_seq, preferred_element_type=jnp.float32)
-        * factor
-    )
-    grad_keys = (
-        jnp.einsum("hqk,qhd->khd", scores_low, queries, preferred_element_type=jnp.float32) * factor
-    )
-    row_count = queries.shape[0]
-    return (
-        grad_queries.reshape(row_count, -1),
-        grad_keys.reshape(row_count, -1),
-        grad_values.reshape(row_count, -1),
-    )
 
 
 def gather_forward(shards):
@@ -379,124 +763,6 @@
         *side_by_side(
             (gain_grad.astype(jnp.bfloat16), shift_grad.astype(jnp.bfloat16)), "dp", 1, 0
         ),
-    )
-
-
-def layer_step(inputs, length_row, upstream, forward_weights):
-    (
-        query_full,
-        key_full,
-        value_full,
-        output_full,
-        inner_full,
-        outer_full,
-        bias_full,
-        hidden_full,
-        gain_full,
-        shift_full,
-    ) = forward_weights
-    query_back, key_back, value_back, output_back, inner_back, outer_back = forward_weights[:6]
-    seq_count, seq_len, model_width = inputs.shape
-    row_count = seq_count * seq_len
-    flat_rows = inputs.reshape(row_count, model_width)
-    row_mask = lax.broadcasted_iota(jnp.int32, (seq_count, seq_len), 1) < length_row[:, None]
-    row_mask = row_mask.astype(jnp.float32).reshape(row_count, 1)
-    bias_rows = bias_full.astype(jnp.float32)
-    gain_rows = gain_full.astype(jnp.float32)
-    shift_rows = shift_full.astype(jnp.float32)
-    hidden_bias = hidden_full.astype(jnp.float32)
-    shape_heads = (seq_count, seq_len, HEADS, model_width // HEADS)
-    queries = (
-        jnp.dot(flat_rows, query_full, preferred_element_type=jnp.float32) + bias_rows[0]
-    ).astype(jnp.bfloat16)
-    keys_all = jnp.dot(flat_rows, key_full, preferred_element_type=jnp.float32).astype(jnp.bfloat16)
-    values_all = (
-        jnp.dot(flat_rows, value_full, preferred_element_type=jnp.float32) + bias_rows[1]
-    ).astype(jnp.bfloat16)
-    query_heads = queries.reshape(shape_heads)
-    key_heads = keys_all.reshape(shape_heads)
-    value_heads = values_all.reshape(shape_heads)
-    blended, logsum = lax.map(attend_forward, (query_heads, key_heads, value_heads, length_row))
-    attended = blended.reshape(row_count, model_width).astype(jnp.bfloat16)
-    first_sum = (
-        flat_rows.astype(jnp.float32)
-        + jnp.dot(attended, output_full, preferred_element_type=jnp.float32)
-        + bias_rows[2]
-    )
-    normed_one, factor_one = normalize(first_sum)
-    middle = normed_one * gain_rows[0] + shift_rows[0]
-    middle_low = middle.astype(jnp.bfloat16)
-    hidden_pre = jnp.dot(middle_low, inner_full, preferred_element_type=jnp.float32) + hidden_bias
-    activated = jax.nn.gelu(hidden_pre, approximate=False).astype(jnp.bfloat16)
-    second = (
-        middle + jnp.dot(activated, outer_full, preferred_element_type=jnp.float32) + bias_rows[3]
-    )
-    normed_two, factor_two = normalize(second)
-    outputs = ((normed_two * gain_rows[1] + shift_rows[1]) * row_mask).astype(jnp.bfloat16)
-    upward = upstream.reshape(row_count, model_width).astype(jnp.float32) * row_mask
-    gain_two = jnp.sum(upward * normed_two, axis=0)
-    shift_two = jnp.sum(upward, axis=0)
-    grad_second = norm_back(upward * gain_rows[1], normed_two, factor_two)
-    second_low = grad_second.astype(jnp.bfloat16)
-    outer_grad = outer_sum(activated, second_low)
-    hidden_low = (back_product(second_low, outer_back) * gelu_slope(hidden_pre)).astype(
-        jnp.bfloat16
-    )
-    inner_grad = outer_sum(middle_low, hidden_low)
-    grad_middle = grad_second + back_product(hidden_low, inner_back)
-    gain_one = jnp.sum(grad_middle * normed_one, axis=0)
-    shift_one = jnp.sum(grad_middle, axis=0)
-    grad_first = norm_back(grad_middle * gain_rows[0], normed_one, factor_one)
-    branch_low = grad_first.astype(jnp.bfloat16)
-    output_grad = outer_sum(attended, branch_low)
-    attended_low = back_product(branch_low, output_back).astype(jnp.bfloat16)
-    grad_queries, grad_keys, grad_values = lax.map(
-        attend_backward,
-        (
-            query_heads,
-            key_heads,
-            value_heads,
-            attended_low.reshape(seq_count, seq_len, model_width),
-            logsum,
-            length_row,
-        ),
-    )
-    queries_low = grad_queries.reshape(row_count, model_width).astype(jnp.bfloat16)
-    keys_low = grad_keys.reshape(row_count, model_width).astype(jnp.bfloat16)
-    values_low = grad_values.reshape(row_count, model_width).astype(jnp.bfloat16)
-    query_grad = outer_sum(flat_rows, queries_low)
-    key_grad = outer_sum(flat_rows, keys_low)
-    value_grad = outer_sum(flat_rows, values_low)
-    grad_inputs = (
-        grad_first
-        + back_product(queries_low, query_back)
-        + back_product(keys_low, key_back)
-        + back_product(values_low, value_back)
-    )
-    bias_grad = jnp.stack(
-        [
-            column_sums(queries_low),
-            column_sums(values_low),
-            column_sums(branch_low),
-            column_sums(second_low),
-        ]
-    )
-    grads = (
-        query_grad,
-        key_grad,
-        value_grad,
-        output_grad,
-        inner_grad,
-        outer_grad,
-        bias_grad,
-        column_sums(hidden_low),
-        jnp.stack([gain_one, gain_two]),
-        jnp.stack([shift_one, shift_two]),
-    )
-    return (
-        outputs.reshape(inputs.shape),
-        grad_inputs.astype(jnp.bfloat16).reshape(inputs.shape),
-        grads,
     )
 
 

time: 1410 us -> 405 us (0.29)
  Pallas kernels: 893 us -> 176 us
  matrix products: 206 us -> 0 us
  local copies, waits for them, and re-layouts: 55.2 us -> 14.7 us
  other arithmetic: 62.5 us -> 24.6 us
  waiting for transfers between devices: 122 us -> 138 us
    pallas_call x4, Pallas kernels: 451 us -> 18.3 us  [cut_part(): pl.pallas_call(functools.partial(cut_kernel, stages, rows, width, small i...]
    pallas_call x4, Pallas kernels: 442 us -> 20.7 us  [place_part(): pl.pallas_call(functools.partial(place_kernel, stages, rows, width, with_...]
    dot_general x32 -> x0, matrix products: 206 us -> none  [the longest x1 37.4 us: layer_step(): jnp.dot(middle_low, inner_full, preferred_element_type=jnp.float32)]
    pallas_call x0 -> x7, Pallas kernels: none -> 137 us  [the longest x1 32.3 us: feed_forward(): pl.pallas_call(functools.partial(feed_kernel, tiles, min(512, inner)), gr...]
    reduce_sum x10 -> x0, other arithmetic: 16.2 us -> none  [the longest x2 5.2 us: attend_forward(): row_total = jnp.sum(exponent, axis=-1, keepdims=True)]
    ppermute x48, waiting for transfers between devices: 122 us -> 138 us  [swap(): return lax.ppermute(value, axis, [(i, i ^ 1 << bit) for i in range(size)])]
    convert_element_type x6 -> x2, other arithmetic: 16.3 us -> 1.36 us  [the longest x1 0.73 us: layer_step(): hidden_bias = hidden.astype(jnp.float32)[None]]
  transfers between devices with their start and end apart: 48 -> 48, of which waited for: 27 -> 25; matrix products, arithmetic and copies ran while one was open for 12% -> 9% of each run, Pallas kernels for 48% -> 16%
where the time goes in v2:
time: 405 us; the launch traced here: 404 us
  Pallas kernels  176 us (43%)
  waiting for transfers between devices  138 us (34%)
  starting transfers between devices  49 us (12%)
  other arithmetic  24.6 us (6%)
  local copies, waits for them, and re-layouts  14.7 us (4%)
    ppermute x48, waiting for transfers between devices, swap(): return lax.ppermute(value, axis, [(i, i ^ 1 << bit) for i in range(size)])  138 us
    ppermute x48, starting transfers between devices, swap(): return lax.ppermute(value, axis, [(i, i ^ 1 << bit) for i in range(size)])  49 us
    pallas_call x1, Pallas kernels, feed_forward(): pl.pallas_call(functools.partial(feed_kernel, tiles, min(512, inner)), gr...  32.3 us
    pallas_call x1, Pallas kernels, attend_backward(): pl.pallas_call(backward_kernel, grid_spec=pltpu.PrefetchScalarGridSpec(nu...  31.7 us
    pallas_call x1, Pallas kernels, attend_forward(): pl.pallas_call(forward_kernel, grid_spec=pltpu.PrefetchScalarGridSpec(num...  24.9 us
    pallas_call x4, Pallas kernels, place_part(): pl.pallas_call(functools.partial(place_kernel, stages, rows, width, with_...  20.7 us
    pallas_call x4, Pallas kernels, cut_part(): pl.pallas_call(functools.partial(cut_kernel, stages, rows, width, small i...  18.3 us
    pallas_call x1, Pallas kernels, feed_back_inner(): pl.pallas_call(feed_back_inner_kernel, grid=(inner // chunk,), in_specs=[...  16.4 us
  transfers between devices with their start and end apart: 48, of which 25 were waited for; matrix products, arithmetic and copies ran while one was open for 9% of the time, Pallas kernels for 16%

profile of v2, /device:TPU:0, one launch (start us, length us, event | category | flops | bytes accessed | tf_op | source)
XLA Modules:
  0.0 403.5 jit_solution(15860382536898479516)
XLA Ops:
  7.4 4.1 %collective-permute-start.1 = (bf16[1,112,384]{2,1,0:T(8,128)(2,1)S(1)}, bf16[1,112,384]{2,1,0:T(8,128)(2,1)S(1)}, u32[]{:S(2)}, u32[]{:S(2)}) collective-permute-start(bf16[1,112,384]{2,1,0:T(8,128)(2,1)S(1)} %maximum_bitcast_fusion.2), channel_id=1, source_target_pairs={{0,16},{4,20},{8,24},{12,28},{16,0},{20,4},{24,8},{28,12},{1,17},{... | collective-permute-start | bytes 258056 | tf_op jit(solution)/shard_map/ppermute | solution.py:19
  14.1 3.0 collective-permute-start.19
  17.1 1.7 constant_dynamic-update-slice_fusion.14
  18.8 7.3 %collective-permute-done.7 = bf16[1,96,384]{2,1,0:T(8,128)(2,1)S(1)} collective-permute-done((bf16[1,96,384]{2,1,0:T(8,128)(2,1)S(1)}, bf16[1,96,384]{2,1,0:T(8,128)(2,1)S(1)}, u32[]{:S(2)}, u32[]{:S(2)}) %collective-permute-start.7) | collective-permute-done | bytes 73760 | tf_op jit(solution)/shard_map/ppermute | solution.py:19
  26.5 1.9 collective-permute-start.2
  29.0 2.9 collective-permute-done.13
  34.8 10.3 %collective-permute-done.14 = bf16[2,48,1536]{2,1,0:T(8,128)(2,1)S(1)} collective-permute-done((bf16[2,48,1536]{2,1,0:T(8,128)(2,1)S(1)}, bf16[2,48,1536]{2,1,0:T(8,128)(2,1)S(1)}, u32[]{:S(2)}, u32[]{:S(2)}) %collective-permute-start.14) | collective-permute-done | bytes 294944 | tf_op jit(solution)/shard_map/ppermute | solution.py:19
  48.5 2.9 collective-permute-done.20
  51.4 1.7 collective-permute-start.21
  54.7 6.7 %collective-permute-done.15 = bf16[4,48,1536]{2,1,0:T(8,128)(2,1)S(1)} collective-permute-done((bf16[4,48,1536]{2,1,0:T(8,128)(2,1)S(1)}, bf16[4,48,1536]{2,1,0:T(8,128)(2,1)S(1)}, u32[]{:S(2)}, u32[]{:S(2)}) %collective-permute-start.15) | collective-permute-done | bytes 589856 | tf_op jit(solution)/shard_map/ppermute | solution.py:19
  61.6 1.7 collective-permute-start.16
  63.9 5.6 %collective-permute-done.21 = bf16[4,192,384]{2,1,0:T(8,128)(2,1)S(1)} collective-permute-done((bf16[4,192,384]{2,1,0:T(8,128)(2,1)S(1)}, bf16[4,192,384]{2,1,0:T(8,128)(2,1)S(1)}, u32[]{:S(2)}, u32[]{:S(2)}) %collective-permute-start.21) | collective-permute-done | bytes 589856 | tf_op jit(solution)/shard_map/ppermute | solution.py:19
  70.6 2.1 collective-permute-start.10
  75.3 19.5 %collective-permute-done.16 = bf16[8,48,1536]{2,1,0:T(8,128)(2,1)S(1)} collective-permute-done((bf16[8,48,1536]{2,1,0:T(8,128)(2,1)S(1)}, bf16[8,48,1536]{2,1,0:T(8,128)(2,1)S(1)}, u32[]{:S(2)}, u32[]{:S(2)}) %collective-permute-start.16) | collective-permute-done | bytes 1179680 | tf_op jit(solution)/shard_map/ppermute | solution.py:19
  95.9 2.7 collective-permute-done.22
  99.9 8.3 %collective-permute-done.4 = bf16[8,112,384]{2,1,0:T(8,128)(2,1)S(1)} collective-permute-done((bf16[8,112,384]{2,1,0:T(8,128)(2,1)S(1)}, bf16[8,112,384]{2,1,0:T(8,128)(2,1)S(1)}, u32[]{:S(2)}, u32[]{:S(2)}) %collective-permute-start.4) | collective-permute-done | bytes 688160 | tf_op jit(solution)/shard_map/ppermute | solution.py:19
  110.4 3.6 collective-permute-done.11.refs_1_
  114.0 4.6 %place.5 = (bf16[768,768]{1,0:T(8,128)(2,1)}, bf16[768,768]{1,0:T(8,128)(2,1)}) custom-call(s32[2]{0:T(128)} %pad_add_fusion.me_ref, bf16[16,96,384]{2,1,0:T(8,128)(2,1)} %copy-done.4, bf16[16,96,384]{2,1,0:T(8,128)(2,1)} %collective-permute-done.11.refs_1_), custom_call_target="tpu_custom_call" | custom-call | tf_op jit(solution)/shard_map/place/pallas_call | solution.py:92
  118.6 4.6 %place.4 = (bf16[768,768]{1,0:T(8,128)(2,1)}, bf16[768,768]{1,0:T(8,128)(2,1)}, bf16[8,16,384]{2,1,0:T(8,128)(2,1)}) custom-call(s32[2]{0:T(128)} %pad_add_fusion.me_ref, bf16[16,112,384]{2,1,0:T(8,128)(2,1)} %constant_dynamic-update-slice_fusion.refs_0_, bf16[16,112,384]{2,1,0:T(8,128)(2,1)} %collective-permute-done.5.refs_1_), custom_call_target="tpu_custom_call" | custom-call | tf_op jit(solution)/shard_map/place/pallas_call | solution.py:92
  126.3 24.9 %attend_forward.1 = (bf16[2,512,768]{2,1,0:T(8,128)(2,1)}, bf16[2,512,768]{2,1,0:T(8,128)(2,1)}, bf16[2,512,768]{2,1,0:T(8,128)(2,1)}, bf16[2,512,768]{2,1,0:T(8...) custom-call(s32[2]{0:T(128)} %bitcast.94, bf16[2,512,768]{2,1,0:T(8,128)(2,1)} %bitcast.75, ...), custom_call_target="tpu_custom_call" | custom-call | tf_op jit(solution)/shard_map/attend_forward/pallas_call | solution.py:324
  151.3 5.8 %place.6.wi_ref = bf16[768,3072]{1,0:T(8,128)(2,1)} custom-call(s32[2]{0:T(128)} %pad_add_fusion.me_ref, bf16[16,48,1536]{2,1,0:T(8,128)(2,1)} %constant_dynamic-update-slice_fusion.10.refs_0_, bf16[16,48,1536]{2,1,0:T(8,128)(2,1)} %collective-permute-done.17.refs_1_), custom_call_target="tpu_custom_call" | custom-call | tf_op jit(solution)/shard_map/place/pallas_call | solution.py:92
  157.1 5.7 %place.7.wo_ref = bf16[3072,768]{1,0:T(8,128)(2,1)} custom-call(s32[2]{0:T(128)} %pad_add_fusion.me_ref, bf16[16,192,384]{2,1,0:T(8,128)(2,1)} %copy-done, bf16[16,192,384]{2,1,0:T(8,128)(2,1)} %collective-permute-done.23.refs_1_), custom_call_target="tpu_custom_call" | custom-call | tf_op jit(solution)/shard_map/place/pallas_call | solution.py:92
  162.9 32.3 %feed_forward.1 = (bf16[1024,768]{1,0:T(8,128)(2,1)}, bf16[1024,3072]{1,0:T(8,128)(2,1)}, bf16[1024,3072]{1,0:T(8,128)(2,1)}, bf16[1024,768]{1,0:T(8,128)(2,1)},...) custom-call(s32[2]{0:T(128)} %bitcast.95, f32[1024,768]{1,0:T(8,128)} %bitcast.68, ...), custom_call_target="tpu_custom_call" | custom-call | tf_op jit(solution)/shard_map/feed_forward/pallas_call | solution.py:394
  195.1 15.2 %feed_back_outer.1 = (bf16[1024,3072]{1,0:T(8,128)(2,1)}, bf16[3072,768]{1,0:T(8,128)(2,1)}, f32[1,3072]{1,0:T(1,128)}) custom-call(bf16[1024,768]{1,0:T(8,128)(2,1)} %get-tuple-element.62.low_ref, bf16[1024,3072]{1,0:T(8,128)(2,1)} %get-tuple-element.63.act_ref, bf16[1024,3072]{1,0:T(8,128)(2,1)} %get-tuple-element.64.slope_ref, bf16[3072,768]{1,0:T(8,128)(2,1)} %place.7.wo_ref), custom_call_target="tpu_custom_call" | custom-call | tf_op jit(solution)/shard_map/feed_back_outer/pallas_call | solution.py:431
  210.3 16.4 %feed_back_inner.1 = (f32[1024,768]{1,0:T(8,128)}, bf16[768,3072]{1,0:T(8,128)(2,1)}) custom-call(f32[1024,768]{1,0:T(8,128)} %get-tuple-element.60.gs_ref, bf16[1024,768]{1,0:T(8,128)(2,1)} %get-tuple-element.61.mid_ref, bf16[1024,3072]{1,0:T(8,128)(2,1)} %get-tuple-element.65.hid_ref, bf16[768,3072]{1,0:T(8,128)(2,1)} %place.6.wi_ref), custom_call_target="tpu_custom_call" | custom-call | tf_op jit(solution)/shard_map/feed_back_inner/pallas_call | solution.py:465
  226.8 31.7 %attend_backward.1 = (f32[2,512,768]{2,1,0:T(8,128)}, bf16[2,512,768]{2,1,0:T(8,128)(2,1)}, bf16[2,512,768]{2,1,0:T(8,128)(2,1)}, bf16[2,512,768]{2,1,0:T(8,128)...) custom-call(s32[2]{0:T(128)} %bitcast.96, f32[2,512,768]{2,1,0:T(8,128)} %bitcast.78, ...), custom_call_target="tpu_custom_call" | custom-call | tf_op jit(solution)/shard_map/attend_backward/pallas_call | solution.py:554
  258.5 7.8 %project_grads.1 = (bf16[768,768]{1,0:T(8,128)(2,1)}, bf16[768,768]{1,0:T(8,128)(2,1)}, bf16[768,768]{1,0:T(8,128)(2,1)}, f32[8,768]{1,0:T(8,128)}) custom-call(bf16[1024,768]{1,0:T(8,128)(2,1)} %bitcast.76, bf16[1024,768]{1,0:T(8,128)(2,1)} %bitcast.69, bf16[1024,768]{1,0:T(8,128)(2,1)} %bitcast.71, bf16[1024,768]{1,0:T(8,128)(2,1)} %bitcast.73), custom_call_target="tpu_custom_call" | custom-call | tf_op jit(solution)/shard_map/project_grads/pallas_call | solution.py:594
  266.2 4.0 cut.5
  276.1 4.0 cut.4
  280.2 10.1 %collective-permute-done.31 = bf16[8,96,384]{2,1,0:T(8,128)(2,1)S(1)} collective-permute-done((bf16[8,96,384]{2,1,0:T(8,128)(2,1)S(1)}, bf16[8,96,384]{2,1,0:T(8,128)(2,1)S(1)}, u32[]{:S(2)}, u32[]{:S(2)}) %collective-permute-start.31) | collective-permute-done | bytes 589856 | tf_op jit(solution)/shard_map/ppermute | solution.py:19
  292.1 5.2 %cut.6 = (bf16[16,48,1536]{2,1,0:T(8,128)(2,1)}, bf16[16,48,1536]{2,1,0:T(8,128)(2,1)}) custom-call(s32[2]{0:T(128)} %pad_add_fusion.me_ref, bf16[768,3072]{1,0:T(8,128)(2,1)} %get-tuple-element.88.refs_0_), custom_call_target="tpu_custom_call" | custom-call | tf_op jit(solution)/shard_map/cut/pallas_call | solution.py:127
  300.9 3.2 collective-permute-done.33
  304.1 2.1 collective-permute-start.34
  306.2 8.6 %input_grads.1 = bf16[1024,768]{1,0:T(8,128)(2,1)} custom-call(f32[1024,768]{1,0:T(8,128)} %bitcast.77, bf16[1024,768]{1,0:T(8,128)(2,1)} %bitcast.70, bf16[1024,768]{1,0:T(8,128)(2,1)} %bitcast.72, bf16[1024,768]{1,0:T(8,128)(2,1)} %bitcast.74, bf16[768,768]{1,0:T(8,128)(2,1)} %get-tuple-element.53.wq_ref, bf16[768,768]{1,0:T(8,128)(2,1)} %get-tuple-element.54.wk_ref, ...), custom_call_target="tpu_custom_call" | custom-call | tf_op jit(solution)/shard_map/input_grads/pallas_call | solution.py:614
  314.7 5.1 %cut.7 = (bf16[16,192,384]{2,1,0:T(8,128)(2,1)}, bf16[16,192,384]{2,1,0:T(8,128)(2,1)}) custom-call(s32[2]{0:T(128)} %pad_add_fusion.me_ref, bf16[3072,768]{1,0:T(8,128)(2,1)} %get-tuple-element.91.refs_0_), custom_call_target="tpu_custom_call" | custom-call | tf_op jit(solution)/shard_map/cut/pallas_call | solution.py:127
  321.4 2.7 collective-permute-done.35
  325.6 5.3 %collective-permute-done.26 = bf16[4,112,384]{2,1,0:T(8,128)(2,1)S(1)} collective-permute-done((bf16[4,112,384]{2,1,0:T(8,128)(2,1)S(1)}, bf16[4,112,384]{2,1,0:T(8,128)(2,1)S(1)}, u32[]{:S(2)}, u32[]{:S(2)}) %collective-permute-start.26) | collective-permute-done | bytes 344096 | tf_op jit(solution)/shard_map/ppermute | solution.py:19
  330.9 2.1 collective-permute-start.27
  333.0 1.7 add_convert_fusion.3
  337.5 1.7 add_convert_fusion.1
  339.6 2.6 collective-permute-done.28
  344.3 20.9 %collective-permute-done.43 = bf16[8,192,384]{2,1,0:T(8,128)(2,1)} collective-permute-done((bf16[8,192,384]{2,1,0:T(8,128)(2,1)}, bf16[8,192,384]{2,1,0:T(8,128)(2,1)}, u32[]{:S(2)}, u32[]{:S(2)}) %collective-permute-start.43) | collective-permute-done | bytes 1179680 | tf_op jit(solution)/shard_map/ppermute | solution.py:19
  366.8 1.7 collective-permute-start.44
  371.2 7.9 %collective-permute-done.44 = bf16[4,192,384]{2,1,0:T(8,128)(2,1)S(1)} collective-permute-done((bf16[4,192,384]{2,1,0:T(8,128)(2,1)S(1)}, bf16[4,192,384]{2,1,0:T(8,128)(2,1)S(1)}, u32[]{:S(2)}, u32[]{:S(2)}) %collective-permute-start.44) | collective-permute-done | bytes 589856 | tf_op jit(solution)/shard_map/ppermute | solution.py:19
  384.0 5.0 %collective-permute-done.45 = bf16[2,192,384]{2,1,0:T(8,128)(2,1)S(1)} collective-permute-done((bf16[2,192,384]{2,1,0:T(8,128)(2,1)S(1)}, bf16[2,192,384]{2,1,0:T(8,128)(2,1)S(1)}, u32[]{:S(2)}, u32[]{:S(2)}) %collective-permute-start.45) | collective-permute-done | bytes 294944 | tf_op jit(solution)/shard_map/ppermute | solution.py:19
  389.1 3.3 collective-permute-start.46
  393.5 3.7 collective-permute-start.40
  397.4 4.0 collective-permute-done.40
  (204 shorter events, 62.5 us)
Async XLA Ops:
  1.6 5.7 %collective-permute-start = (bf16[96,192]{1,0:T(8,128)(2,1)S(1)}, bf16[96,192]{1,0:T(8,128)(2,1)S(1)}, u32[]{:S(2)}, u32[]{:S(2)}) collective-permute-start(bf16[96,192]{1,0:T(8,128)(2,1)S(1)} %bitcast.89), channel_id=1, source_target_pairs={{0,1},{1,0},{2,3},{3,2},{4,5},{5,4},{6,7},{7,6},{8,9},{9,8},{10,11... | collective-permute-start | bytes 110600 | tf_op jit(solution)/shard_map/ppermute | solution.py:19
  3.0 8.5 %collective-permute-start.6 = (bf16[96,192]{1,0:T(8,128)(2,1)S(1)}, bf16[96,192]{1,0:T(8,128)(2,1)S(1)}, u32[]{:S(2)}, u32[]{:S(2)}) collective-permute-start(bf16[96,192]{1,0:T(8,128)(2,1)S(1)} %bitcast.88), channel_id=1, source_target_pairs={{0,1},{1,0},{2,3},{3,2},{4,5},{5,4},{6,7},{7,6},{8,9},{9,8},{10,11... | collective-permute-start | bytes 110600 | tf_op jit(solution)/shard_map/ppermute | solution.py:19
  4.7 12.4 %collective-permute-start.12 = (bf16[48,768]{1,0:T(8,128)(2,1)}, bf16[48,768]{1,0:T(8,128)(2,1)}, u32[]{:S(2)}, u32[]{:S(2)}) collective-permute-start(bf16[48,768]{1,0:T(8,128)(2,1)} %get-tuple-element.164), channel_id=1, source_target_pairs={{0,1},{1,0},{2,3},{3,2},{4,5},{5,4},{6,7},{7,6},{8,9},{9,8},{10,11... | collective-permute-start | bytes 221192 | tf_op jit(solution)/shard_map/ppermute | solution.py:19
  7.1 5.3 %collective-permute-start.18 = (bf16[192,192]{1,0:T(8,128)(2,1)S(1)}, bf16[192,192]{1,0:T(8,128)(2,1)S(1)}, u32[]{:S(2)}, u32[]{:S(2)}) collective-permute-start(bf16[192,192]{1,0:T(8,128)(2,1)S(1)} %get-tuple-element.156), channel_id=1, source_target_pairs={{0,1},{1,0},{2,3},{3,2},{4,5},{5,4},{6,7},{7,6},{8,9},{9,8},{10,11... | collective-permute-start | bytes 221192 | tf_op jit(solution)/shard_map/ppermute | solution.py:19
  7.4 19.1 %collective-permute-start.1 = (bf16[1,112,384]{2,1,0:T(8,128)(2,1)S(1)}, bf16[1,112,384]{2,1,0:T(8,128)(2,1)S(1)}, u32[]{:S(2)}, u32[]{:S(2)}) collective-permute-start(bf16[1,112,384]{2,1,0:T(8,128)(2,1)S(1)} %maximum_bitcast_fusion.2), channel_id=1, source_target_pairs={{0,16},{4,20},{8,24},{12,28},{16,0},{20,4},{24,8},{28,12},{1,17},{... | collective-permute-start | bytes 258056 | tf_op jit(solution)/shard_map/ppermute | solution.py:19
  11.6 14.6 %collective-permute-start.7 = (bf16[1,96,384]{2,1,0:T(8,128)(2,1)S(1)}, bf16[1,96,384]{2,1,0:T(8,128)(2,1)S(1)}, u32[]{:S(2)}, u32[]{:S(2)}) collective-permute-start(bf16[1,96,384]{2,1,0:T(8,128)(2,1)S(1)} %get-tuple-element.123), channel_id=1, source_target_pairs={{0,16},{4,20},{8,24},{12,28},{16,0},{20,4},{24,8},{28,12},{1,17},{... | collective-permute-start | bytes 221192 | tf_op jit(solution)/shard_map/ppermute | solution.py:19
  14.1 18.6 %collective-permute-start.19 = (bf16[1,192,384]{2,1,0:T(8,128)(2,1)S(1)}, bf16[1,192,384]{2,1,0:T(8,128)(2,1)S(1)}, u32[]{:S(2)}, u32[]{:S(2)}) collective-permute-start(bf16[1,192,384]{2,1,0:T(8,128)(2,1)S(1)} %get-tuple-element.119), channel_id=1, source_target_pairs={{0,16},{4,20},{8,24},{12,28},{16,0},{20,4},{24,8},{28,12},{1,17},{... | collective-permute-start | bytes 442376 | tf_op jit(solution)/shard_map/ppermute | solution.py:19
  18.8 13.1 %collective-permute-start.13 = (bf16[1,48,1536]{2,1,0:T(8,128)(2,1)S(1)}, bf16[1,48,1536]{2,1,0:T(8,128)(2,1)S(1)}, u32[]{:S(2)}, u32[]{:S(2)}) collective-permute-start(bf16[1,48,1536]{2,1,0:T(8,128)(2,1)S(1)} %get-tuple-element.121), channel_id=1, source_target_pairs={{0,16},{4,20},{8,24},{12,28},{16,0},{20,4},{24,8},{28,12},{1,17},{... | collective-permute-start | bytes 442376 | tf_op jit(solution)/shard_map/ppermute | solution.py:19
  26.2 20.7 %collective-permute-start.8 = (bf16[2,96,384]{2,1,0:T(8,128)(2,1)S(1)}, bf16[2,96,384]{2,1,0:T(8,128)(2,1)S(1)}, u32[]{:S(2)}, u32[]{:S(2)}) collective-permute-start(bf16[2,96,384]{2,1,0:T(8,128)(2,1)S(1)} %pad_maximum_fusion.13), channel_id=1, source_target_pairs={{0,8},{4,12},{8,0},{12,4},{16,24},{20,28},{24,16},{28,20},{1,9},{5... | collective-permute-start | bytes 442376 | tf_op jit(solution)/shard_map/ppermute | solution.py:19
  26.5 26.6 %collective-permute-start.2 = (bf16[2,112,384]{2,1,0:T(8,128)(2,1)S(1)}, bf16[2,112,384]{2,1,0:T(8,128)(2,1)S(1)}, u32[]{:S(2)}, u32[]{:S(2)}) collective-permute-start(bf16[2,112,384]{2,1,0:T(8,128)(2,1)S(1)} %pad_maximum_fusion.12), channel_id=1, source_target_pairs={{0,8},{4,12},{8,0},{12,4},{16,24},{20,28},{24,16},{28,20},{1,9},{5... | collective-permute-start | bytes 516104 | tf_op jit(solution)/shard_map/ppermute | solution.py:19
  32.0 13.1 %collective-permute-start.14 = (bf16[2,48,1536]{2,1,0:T(8,128)(2,1)S(1)}, bf16[2,48,1536]{2,1,0:T(8,128)(2,1)S(1)}, u32[]{:S(2)}, u32[]{:S(2)}) collective-permute-start(bf16[2,48,1536]{2,1,0:T(8,128)(2,1)S(1)} %pad_maximum_fusion.9), channel_id=1, source_target_pairs={{0,8},{4,12},{8,0},{12,4},{16,24},{20,28},{24,16},{28,20},{1,9},{5... | collective-permute-start | bytes 884744 | tf_op jit(solution)/shard_map/ppermute | solution.py:19
  32.7 18.6 %collective-permute-start.20 = (bf16[2,192,384]{2,1,0:T(8,128)(2,1)S(1)}, bf16[2,192,384]{2,1,0:T(8,128)(2,1)S(1)}, u32[]{:S(2)}, u32[]{:S(2)}) collective-permute-start(bf16[2,192,384]{2,1,0:T(8,128)(2,1)S(1)} %pad_maximum_fusion.10), channel_id=1, source_target_pairs={{0,8},{4,12},{8,0},{12,4},{16,24},{20,28},{24,16},{28,20},{1,9},{5... | collective-permute-start | bytes 884744 | tf_op jit(solution)/shard_map/ppermute | solution.py:19
  45.2 16.3 %collective-permute-start.15 = (bf16[4,48,1536]{2,1,0:T(8,128)(2,1)S(1)}, bf16[4,48,1536]{2,1,0:T(8,128)(2,1)S(1)}, u32[]{:S(2)}, u32[]{:S(2)}) collective-permute-start(bf16[4,48,1536]{2,1,0:T(8,128)(2,1)S(1)} %pad_maximum_fusion.4), channel_id=1, source_target_pairs={{0,2},{1,3},{2,0},{3,1},{4,6},{5,7},{6,4},{7,5},{8,10},{9,11},{10,... | collective-permute-start | bytes 1769480 | tf_op jit(solution)/shard_map/ppermute | solution.py:19
  46.9 23.7 %collective-permute-start.9 = (bf16[4,96,384]{2,1,0:T(8,128)(2,1)S(1)}, bf16[4,96,384]{2,1,0:T(8,128)(2,1)S(1)}, u32[]{:S(2)}, u32[]{:S(2)}) collective-permute-start(bf16[4,96,384]{2,1,0:T(8,128)(2,1)S(1)} %pad_maximum_fusion.8), channel_id=1, source_target_pairs={{0,4},{4,0},{8,12},{12,8},{16,20},{20,16},{24,28},{28,24},{1,5},{5... | collective-permute-start | bytes 884744 | tf_op jit(solution)/shard_map/ppermute | solution.py:19
  51.4 18.1 %collective-permute-start.21 = (bf16[4,192,384]{2,1,0:T(8,128)(2,1)S(1)}, bf16[4,192,384]{2,1,0:T(8,128)(2,1)S(1)}, u32[]{:S(2)}, u32[]{:S(2)}) collective-permute-start(bf16[4,192,384]{2,1,0:T(8,128)(2,1)S(1)} %pad_maximum_fusion.5), channel_id=1, source_target_pairs={{0,4},{4,0},{8,12},{12,8},{16,20},{20,16},{24,28},{28,24},{1,5},{5... | collective-permute-start | bytes 1769480 | tf_op jit(solution)/shard_map/ppermute | solution.py:19
  53.2 19.5 %collective-permute-start.3 = (bf16[4,112,384]{2,1,0:T(8,128)(2,1)S(1)}, bf16[4,112,384]{2,1,0:T(8,128)(2,1)S(1)}, u32[]{:S(2)}, u32[]{:S(2)}) collective-permute-start(bf16[4,112,384]{2,1,0:T(8,128)(2,1)S(1)} %pad_maximum_fusion.7), channel_id=1, source_target_pairs={{0,2},{1,3},{2,0},{3,1},{4,6},{5,7},{6,4},{7,5},{8,10},{9,11},{10,... | collective-permute-start | bytes 1032200 | tf_op jit(solution)/shard_map/ppermute | solution.py:19
  61.6 33.2 %collective-permute-start.16 = (bf16[8,48,1536]{2,1,0:T(8,128)(2,1)S(1)}, bf16[8,48,1536]{2,1,0:T(8,128)(2,1)S(1)}, u32[]{:S(2)}, u32[]{:S(2)}) collective-permute-start(bf16[8,48,1536]{2,1,0:T(8,128)(2,1)S(1)} %pad_maximum_fusion), channel_id=1, source_target_pairs={{0,4},{4,0},{8,12},{12,8},{16,20},{20,16},{24,28},{28,24},{1,5},{5... | collective-permute-start | bytes 3538952 | tf_op jit(solution)/shard_map/ppermute | solution.py:19
  69.7 29.0 %collective-permute-start.22 = (bf16[8,192,384]{2,1,0:T(8,128)(2,1)S(1)}, bf16[8,192,384]{2,1,0:T(8,128)(2,1)S(1)}, u32[]{:S(2)}, u32[]{:S(2)}) collective-permute-start(bf16[8,192,384]{2,1,0:T(8,128)(2,1)S(1)} %pad_maximum_fusion.1), channel_id=1, source_target_pairs={{0,2},{1,3},{2,0},{3,1},{4,6},{5,7},{6,4},{7,5},{8,10},{9,11},{10,... | collective-permute-start | bytes 3538952 | tf_op jit(solution)/shard_map/ppermute | solution.py:19
  70.6 38.5 %collective-permute-start.10 = (bf16[8,96,384]{2,1,0:T(8,128)(2,1)S(1)}, bf16[8,96,384]{2,1,0:T(8,128)(2,1)S(1)}, u32[]{:S(2)}, u32[]{:S(2)}) collective-permute-start(bf16[8,96,384]{2,1,0:T(8,128)(2,1)S(1)} %pad_maximum_fusion.3), channel_id=1, source_target_pairs={{0,2},{1,3},{2,0},{3,1},{4,6},{5,7},{6,4},{7,5},{8,10},{9,11},{10,... | collective-permute-start | bytes 1769480 | tf_op jit(solution)/shard_map/ppermute | solution.py:19
  72.8 35.4 %collective-permute-start.4 = (bf16[8,112,384]{2,1,0:T(8,128)(2,1)S(1)}, bf16[8,112,384]{2,1,0:T(8,128)(2,1)S(1)}, u32[]{:S(2)}, u32[]{:S(2)}) collective-permute-start(bf16[8,112,384]{2,1,0:T(8,128)(2,1)S(1)} %pad_maximum_fusion.2), channel_id=1, source_target_pairs={{0,4},{4,0},{8,12},{12,8},{16,20},{20,16},{24,28},{28,24},{1,5},{5... | collective-permute-start | bytes 2064392 | tf_op jit(solution)/shard_map/ppermute | solution.py:19
  95.9 55.4 %collective-permute-start.17 = (bf16[16,48,1536]{2,1,0:T(8,128)(2,1)}, bf16[16,48,1536]{2,1,0:T(8,128)(2,1)}, u32[]{:S(2)}, u32[]{:S(2)}) collective-permute-start(bf16[16,48,1536]{2,1,0:T(8,128)(2,1)} %constant_dynamic-update-slice_fusion.10.refs_0_), channel_id=1, source_target_pairs={{0,1},{1,0},{2,3},{3,2},{4,5},{5,4},{6,7},{7,6},{8,9},{9,8},{10,11... | collective-permute-start | bytes 7077896 | tf_op jit(solution)/shard_map/ppermute | solution.py:19
  98.9 58.2 %collective-permute-start.23 = (bf16[16,192,384]{2,1,0:T(8,128)(2,1)S(1)}, bf16[16,192,384]{2,1,0:T(8,128)(2,1)}, u32[]{:S(2)}, u32[]{:S(2)}) collective-permute-start(bf16[16,192,384]{2,1,0:T(8,128)(2,1)S(1)} %constant_dynamic-update-slice_fusion.15.refs_0_), channel_id=1, source_target_pairs={{0,1},{1,0},{2,3},{3,2},{4,5},{5,4},{6,7},{7,6},{8,9},{9,8},{10,11... | collective-permute-start | bytes 7077896 | tf_op jit(solution)/shard_map/ppermute | solution.py:19
  109.1 9.5 %collective-permute-start.5 = (bf16[16,112,384]{2,1,0:T(8,128)(2,1)}, bf16[16,112,384]{2,1,0:T(8,128)(2,1)}, u32[]{:S(2)}, u32[]{:S(2)}) collective-permute-start(bf16[16,112,384]{2,1,0:T(8,128)(2,1)} %constant_dynamic-update-slice_fusion.refs_0_), channel_id=1, source_target_pairs={{0,1},{1,0},{2,3},{3,2},{4,5},{5,4},{6,7},{7,6},{8,9},{9,8},{10,11... | collective-permute-start | bytes 4128776 | tf_op jit(solution)/shard_map/ppermute | solution.py:19
  109.3 4.8 %collective-permute-start.11 = (bf16[16,96,384]{2,1,0:T(8,128)(2,1)S(1)}, bf16[16,96,384]{2,1,0:T(8,128)(2,1)}, u32[]{:S(2)}, u32[]{:S(2)}) collective-permute-start(bf16[16,96,384]{2,1,0:T(8,128)(2,1)S(1)} %constant_dynamic-update-slice_fusion.5.refs_0_), channel_id=1, source_target_pairs={{0,1},{1,0},{2,3},{3,2},{4,5},{5,4},{6,7},{7,6},{8,9},{9,8},{10,11... | collective-permute-start | bytes 3538952 | tf_op jit(solution)/shard_map/ppermute | solution.py:19
  270.2 3.1 collective-permute-start.30
  274.9 15.4 %collective-permute-start.31 = (bf16[8,96,384]{2,1,0:T(8,128)(2,1)S(1)}, bf16[8,96,384]{2,1,0:T(8,128)(2,1)S(1)}, u32[]{:S(2)}, u32[]{:S(2)}) collective-permute-start(bf16[8,96,384]{2,1,0:T(8,128)(2,1)S(1)} %get-tuple-element.135), channel_id=1, source_target_pairs={{0,2},{1,3},{2,0},{3,1},{4,6},{5,7},{6,4},{7,5},{8,10},{9,11},{10,... | collective-permute-start | bytes 1769480 | tf_op jit(solution)/shard_map/ppermute | solution.py:19
  280.1 18.8 %collective-permute-start.24 = (bf16[16,112,384]{2,1,0:T(8,128)(2,1)}, bf16[16,112,384]{2,1,0:T(8,128)(2,1)S(1)}, u32[]{:S(2)}, u32[]{:S(2)}) collective-permute-start(bf16[16,112,384]{2,1,0:T(8,128)(2,1)} %get-tuple-element.83), channel_id=1, source_target_pairs={{0,1},{1,0},{2,3},{3,2},{4,5},{5,4},{6,7},{7,6},{8,9},{9,8},{10,11... | collective-permute-start | bytes 4128776 | tf_op jit(solution)/shard_map/ppermute | solution.py:19
  290.5 8.3 %collective-permute-start.32 = (bf16[4,96,384]{2,1,0:T(8,128)(2,1)S(1)}, bf16[4,96,384]{2,1,0:T(8,128)(2,1)S(1)}, u32[]{:S(2)}, u32[]{:S(2)}) collective-permute-start(bf16[4,96,384]{2,1,0:T(8,128)(2,1)S(1)} %get-tuple-element.143), channel_id=1, source_target_pairs={{0,4},{4,0},{8,12},{12,8},{16,20},{20,16},{24,28},{28,24},{1,5},{5... | collective-permute-start | bytes 884744 | tf_op jit(solution)/shard_map/ppermute | solution.py:19
  297.3 35.7 %collective-permute-start.36 = (bf16[16,48,1536]{2,1,0:T(8,128)(2,1)}, bf16[16,48,1536]{2,1,0:T(8,128)(2,1)S(1)}, u32[]{:S(2)}, u32[]{:S(2)}) collective-permute-start(bf16[16,48,1536]{2,1,0:T(8,128)(2,1)} %get-tuple-element.90), channel_id=1, source_target_pairs={{0,1},{1,0},{2,3},{3,2},{4,5},{5,4},{6,7},{7,6},{8,9},{9,8},{10,11... | collective-permute-start | bytes 7077896 | tf_op jit(solution)/shard_map/ppermute | solution.py:19
  298.8 5.2 %collective-permute-start.33 = (bf16[2,96,384]{2,1,0:T(8,128)(2,1)S(1)}, bf16[2,96,384]{2,1,0:T(8,128)(2,1)S(1)}, u32[]{:S(2)}, u32[]{:S(2)}) collective-permute-start(bf16[2,96,384]{2,1,0:T(8,128)(2,1)S(1)} %get-tuple-element.147), channel_id=1, source_target_pairs={{0,8},{4,12},{8,0},{12,4},{16,24},{20,28},{24,16},{28,20},{1,9},{5... | collective-permute-start | bytes 442376 | tf_op jit(solution)/shard_map/ppermute | solution.py:19
  299.3 21.3 %collective-permute-start.25 = (bf16[8,112,384]{2,1,0:T(8,128)(2,1)S(1)}, bf16[8,112,384]{2,1,0:T(8,128)(2,1)S(1)}, u32[]{:S(2)}, u32[]{:S(2)}) collective-permute-start(bf16[8,112,384]{2,1,0:T(8,128)(2,1)S(1)} %get-tuple-element.129), channel_id=1, source_target_pairs={{0,4},{4,0},{8,12},{12,8},{16,20},{20,16},{24,28},{28,24},{1,5},{5... | collective-permute-start | bytes 2064392 | tf_op jit(solution)/shard_map/ppermute | solution.py:19
  304.1 15.9 %collective-permute-start.34 = (bf16[1,96,384]{2,1,0:T(8,128)(2,1)S(1)}, bf16[1,96,384]{2,1,0:T(8,128)(2,1)S(1)}, u32[]{:S(2)}, u32[]{:S(2)}) collective-permute-start(bf16[1,96,384]{2,1,0:T(8,128)(2,1)S(1)} %add_convert_fusion.30), channel_id=1, source_target_pairs={{0,16},{4,20},{8,24},{12,28},{16,0},{20,4},{24,8},{28,12},{1,17},{... | collective-permute-start | bytes 221192 | tf_op jit(solution)/shard_map/ppermute | solution.py:19
  319.8 17.6 %collective-permute-start.42 = (bf16[16,192,384]{2,1,0:T(8,128)(2,1)}, bf16[16,192,384]{2,1,0:T(8,128)(2,1)S(1)}, u32[]{:S(2)}, u32[]{:S(2)}) collective-permute-start(bf16[16,192,384]{2,1,0:T(8,128)(2,1)} %get-tuple-element.93), channel_id=1, source_target_pairs={{0,1},{1,0},{2,3},{3,2},{4,5},{5,4},{6,7},{7,6},{8,9},{9,8},{10,11... | collective-permute-start | bytes 7077896 | tf_op jit(solution)/shard_map/ppermute | solution.py:19
  320.1 4.1 %collective-permute-start.35 = (bf16[96,192]{1,0:T(8,128)(2,1)S(1)}, bf16[96,192]{1,0:T(8,128)(2,1)S(1)}, u32[]{:S(2)}, u32[]{:S(2)}) collective-permute-start(bf16[96,192]{1,0:T(8,128)(2,1)S(1)} %select_convert_fusion.2), channel_id=1, source_target_pairs={{0,1},{1,0},{2,3},{3,2},{4,5},{5,4},{6,7},{7,6},{8,9},{9,8},{10,11... | collective-permute-start | bytes 110600 | tf_op jit(solution)/shard_map/ppermute | solution.py:19
  320.8 10.1 %collective-permute-start.26 = (bf16[4,112,384]{2,1,0:T(8,128)(2,1)S(1)}, bf16[4,112,384]{2,1,0:T(8,128)(2,1)S(1)}, u32[]{:S(2)}, u32[]{:S(2)}) collective-permute-start(bf16[4,112,384]{2,1,0:T(8,128)(2,1)S(1)} %get-tuple-element.137), channel_id=1, source_target_pairs={{0,2},{1,3},{2,0},{3,1},{4,6},{5,7},{6,4},{7,5},{8,10},{9,11},{10,... | collective-permute-start | bytes 1032200 | tf_op jit(solution)/shard_map/ppermute | solution.py:19
  330.9 5.8 %collective-permute-start.27 = (bf16[2,112,384]{2,1,0:T(8,128)(2,1)S(1)}, bf16[2,112,384]{2,1,0:T(8,128)(2,1)S(1)}, u32[]{:S(2)}, u32[]{:S(2)}) collective-permute-start(bf16[2,112,384]{2,1,0:T(8,128)(2,1)S(1)} %get-tuple-element.145), channel_id=1, source_target_pairs={{0,8},{4,12},{8,0},{12,4},{16,24},{20,28},{24,16},{28,20},{1,9},{5... | collective-permute-start | bytes 516104 | tf_op jit(solution)/shard_map/ppermute | solution.py:19
  334.8 33.7 %collective-permute-start.37 = (bf16[8,48,1536]{2,1,0:T(8,128)(2,1)}, bf16[8,48,1536]{2,1,0:T(8,128)(2,1)}, u32[]{:S(2)}, u32[]{:S(2)}) collective-permute-start(bf16[8,48,1536]{2,1,0:T(8,128)(2,1)} %get-tuple-element.127), channel_id=1, source_target_pairs={{0,4},{4,0},{8,12},{12,8},{16,20},{20,16},{24,28},{28,24},{1,5},{5... | collective-permute-start | bytes 3538952 | tf_op jit(solution)/shard_map/ppermute | solution.py:19
  336.8 5.4 %collective-permute-start.28 = (bf16[1,112,384]{2,1,0:T(8,128)(2,1)S(1)}, bf16[1,112,384]{2,1,0:T(8,128)(2,1)S(1)}, u32[]{:S(2)}, u32[]{:S(2)}) collective-permute-start(bf16[1,112,384]{2,1,0:T(8,128)(2,1)S(1)} %add_convert_fusion.28), channel_id=1, source_target_pairs={{0,16},{4,20},{8,24},{12,28},{16,0},{20,4},{24,8},{28,12},{1,17},{... | collective-permute-start | bytes 258056 | tf_op jit(solution)/shard_map/ppermute | solution.py:19
  339.2 26.1 %collective-permute-start.43 = (bf16[8,192,384]{2,1,0:T(8,128)(2,1)}, bf16[8,192,384]{2,1,0:T(8,128)(2,1)}, u32[]{:S(2)}, u32[]{:S(2)}) collective-permute-start(bf16[8,192,384]{2,1,0:T(8,128)(2,1)} %get-tuple-element.125), channel_id=1, source_target_pairs={{0,2},{1,3},{2,0},{3,1},{4,6},{5,7},{6,4},{7,5},{8,10},{9,11},{10,... | collective-permute-start | bytes 3538952 | tf_op jit(solution)/shard_map/ppermute | solution.py:19
  342.3 1.9 collective-permute-start.29
  366.8 12.3 %collective-permute-start.44 = (bf16[4,192,384]{2,1,0:T(8,128)(2,1)S(1)}, bf16[4,192,384]{2,1,0:T(8,128)(2,1)S(1)}, u32[]{:S(2)}, u32[]{:S(2)}) collective-permute-start(bf16[4,192,384]{2,1,0:T(8,128)(2,1)S(1)} %get-tuple-element.131), channel_id=1, source_target_pairs={{0,4},{4,0},{8,12},{12,8},{16,20},{20,16},{24,28},{28,24},{1,5},{5... | collective-permute-start | bytes 1769480 | tf_op jit(solution)/shard_map/ppermute | solution.py:19
  370.0 12.1 %collective-permute-start.38 = (bf16[4,48,1536]{2,1,0:T(8,128)(2,1)S(1)}, bf16[4,48,1536]{2,1,0:T(8,128)(2,1)S(1)}, u32[]{:S(2)}, u32[]{:S(2)}) collective-permute-start(bf16[4,48,1536]{2,1,0:T(8,128)(2,1)S(1)} %get-tuple-element.133), channel_id=1, source_target_pairs={{0,2},{1,3},{2,0},{3,1},{4,6},{5,7},{6,4},{7,5},{8,10},{9,11},{10,... | collective-permute-start | bytes 1769480 | tf_op jit(solution)/shard_map/ppermute | solution.py:19
  379.2 9.8 %collective-permute-start.45 = (bf16[2,192,384]{2,1,0:T(8,128)(2,1)S(1)}, bf16[2,192,384]{2,1,0:T(8,128)(2,1)S(1)}, u32[]{:S(2)}, u32[]{:S(2)}) collective-permute-start(bf16[2,192,384]{2,1,0:T(8,128)(2,1)S(1)} %get-tuple-element.139), channel_id=1, source_target_pairs={{0,8},{4,12},{8,0},{12,4},{16,24},{20,28},{24,16},{28,20},{1,9},{5... | collective-permute-start | bytes 884744 | tf_op jit(solution)/shard_map/ppermute | solution.py:19
  382.2 11.2 %collective-permute-start.39 = (bf16[2,48,1536]{2,1,0:T(8,128)(2,1)S(1)}, bf16[2,48,1536]{2,1,0:T(8,128)(2,1)S(1)}, u32[]{:S(2)}, u32[]{:S(2)}) collective-permute-start(bf16[2,48,1536]{2,1,0:T(8,128)(2,1)S(1)} %get-tuple-element.141), channel_id=1, source_target_pairs={{0,8},{4,12},{8,0},{12,4},{16,24},{20,28},{24,16},{28,20},{1,9},{5... | collective-permute-start | bytes 884744 | tf_op jit(solution)/shard_map/ppermute | solution.py:19
  389.1 8.1 %collective-permute-start.46 = (bf16[1,192,384]{2,1,0:T(8,128)(2,1)S(1)}, bf16[1,192,384]{2,1,0:T(8,128)(2,1)S(1)}, u32[]{:S(2)}, u32[]{:S(2)}) collective-permute-start(bf16[1,192,384]{2,1,0:T(8,128)(2,1)S(1)} %add_convert_fusion.22), channel_id=1, source_target_pairs={{0,16},{4,20},{8,24},{12,28},{16,0},{20,4},{24,8},{28,12},{1,17},{... | collective-permute-start | bytes 442376 | tf_op jit(solution)/shard_map/ppermute | solution.py:19
  393.5 7.9 %collective-permute-start.40 = (bf16[1,48,1536]{2,1,0:T(8,128)(2,1)S(1)}, bf16[1,48,1536]{2,1,0:T(8,128)(2,1)S(1)}, u32[]{:S(2)}, u32[]{:S(2)}) collective-permute-start(bf16[1,48,1536]{2,1,0:T(8,128)(2,1)S(1)} %add_convert_fusion.24), channel_id=1, source_target_pairs={{0,16},{4,20},{8,24},{12,28},{16,0},{20,4},{24,8},{28,12},{1,17},{... | collective-permute-start | bytes 442376 | tf_op jit(solution)/shard_map/ppermute | solution.py:19
  397.3 4.2 %collective-permute-start.47 = (bf16[192,192]{1,0:T(8,128)(2,1)S(1)}, bf16[192,192]{1,0:T(8,128)(2,1)S(1)}, u32[]{:S(2)}, u32[]{:S(2)}) collective-permute-start(bf16[192,192]{1,0:T(8,128)(2,1)S(1)} %select_convert_fusion), channel_id=1, source_target_pairs={{0,1},{1,0},{2,3},{3,2},{4,5},{5,4},{6,7},{7,6},{8,9},{9,8},{10,11... | collective-permute-start | bytes 221192 | tf_op jit(solution)/shard_map/ppermute | solution.py:19
  401.4 1.3 collective-permute-start.41
  (13 other events, 79.9 us)

commit v3 on v2

--- a/solution.py
+++ b/solution.py
@@ -38,13 +38,6 @@
     for s, (axis, bit) in enumerate(stages):
         index[axis] = index[axis] ^ (((place >> s) & 1) << bit)
     return index["dp"], index["fsdp"]
-
-
-def gather_part(piece, stages):
-    current = piece[None]
-    for axis, bit in stages:
-        current = jnp.concatenate([current, swap(current, axis, bit)], axis=0)
-    return current, swap(current, "fsdp", 0)
 
 
 def copy_list(stages, rows, mine, with_small, blocks):
@@ -96,59 +89,68 @@
         out_specs=(pl.BlockSpec(memory_space=pltpu.VMEM),) * len(shapes),
         compiler_params=pltpu.CompilerParams(vmem_limit_bytes=VMEM_BYTES),
         scratch_shapes=[pltpu.SemaphoreType.DMA((2 * (1 << len(stages)) * (len(rows) + 1),))],
+        cost_estimate=estimate(5),
         name="place",
     )(me, own, other)
 
 
-def cut_kernel(stages, rows, width, with_small, me_ref, *refs):
-    count_in = len(rows) + with_small
-    sources, outs, sems = refs[:count_in], refs[count_in:-1], refs[-1]
-    mine = {"dp": me_ref[0], "fsdp": me_ref[1]}
-    started = []
-    for flip, place, at, count, w, row, column in copy_list(stages, rows, mine, with_small, True):
-        target = outs[flip].at[place, pl.ds(at, count), :]
-        if column is None:
-            source = sources[w].at[row]
-        else:
-            source = sources[w].at[pl.ds(row, count), pl.ds(pl.multiple_of(column * width, 128), width)]
-        copy = pltpu.make_async_copy(source, target, sems.at[len(started)])
+def place_of(stages, dp, fsdp, me_ref):
+    index = {"dp": dp ^ me_ref[0], "fsdp": fsdp ^ me_ref[1]}
+    place = 0
+    for s, (axis, bit) in enumerate(stages):
+        place = place + (((index[axis] >> bit) & 1) << s)
+    return place
+
+
+def piece_copies(source, outs, sems, me_ref, stages, first_dp, count_dp, half, at, columns, width):
+    copies = []
+    for i in range(count_dp):
+        dp = first_dp + i
+        for flip in range(2):
+            fsdp = (me_ref[1] & 1) ^ flip
+            row = pl.multiple_of((2 * i + fsdp) * half, 16)
+            for start, pair, into, count in columns:
+                place = place_of(stages, dp, 2 * pair + fsdp, me_ref)
+                copies.append(
+                    pltpu.make_async_copy(
+                        source.at[pl.ds(row, half), pl.ds(start, count)],
+                        outs[flip].at[place, pl.ds(at, half), pl.ds(into, count)],
+                        sems.at[len(copies)],
+                    )
+                )
+    return copies
+
+
+def small_copies(source, outs, sems, me_ref, stages, at, dp_size, pairs):
+    copies = []
+    for dp in range(dp_size):
+        for flip in range(2):
+            fsdp = (me_ref[1] & 1) ^ flip
+            for pair in range(pairs):
+                place = place_of(stages, dp, 2 * pair + fsdp, me_ref)
+                copies.append(
+                    pltpu.make_async_copy(
+                        source.at[dp],
+                        outs[flip].at[place, pl.ds(at, SMALL_ROWS), :],
+                        sems.at[len(copies)],
+                    )
+                )
+    return copies
+
+
+def run_all(copies):
+    for copy in copies:
         copy.start()
-        started.append(copy)
-    for copy in started:
+    return copies
+
+
+def wait_all(copies):
+    for copy in copies:
         copy.wait()
-
-
-def cut_part(mesh, arrays, small, me, stages, rows, width):
-    total = sum(rows) + (SMALL_ROWS if small is not None else 0)
-    places = 1 << len(stages)
-    shape = jax.ShapeDtypeStruct((places, total, width), jnp.bfloat16)
-    anywhere = pl.BlockSpec(memory_space=pl.ANY)
-    operands = list(arrays) + ([small] if small is not None else [])
-    return pl.pallas_call(
-        functools.partial(cut_kernel, stages, rows, width, small is not None),
-        out_shape=(shape, shape),
-        in_specs=[pl.BlockSpec(memory_space=pltpu.SMEM)]
-        + [pl.BlockSpec(memory_space=pltpu.VMEM)] * len(operands),
-        out_specs=(anywhere, anywhere),
-        compiler_params=pltpu.CompilerParams(vmem_limit_bytes=VMEM_BYTES),
-        scratch_shapes=[pltpu.SemaphoreType.DMA((2 * places * (len(rows) + 1),))],
-        name="cut",
-    )(me, *operands)
 
 
 def total_of(left, right, kind):
     return (left.astype(jnp.float32) + right.astype(jnp.float32)).astype(kind)
-
-
-def scatter_part(keep, send, stages):
-    received = swap(send, "fsdp", 0)
-    for axis, bit in reversed(stages):
-        half = keep.shape[0] // 2
-        send = total_of(keep[half:], received[half:], jnp.bfloat16)
-        arriving = swap(send, axis, bit)
-        keep = total_of(keep[:half], received[:half], jnp.bfloat16)
-        received = arriving
-    return total_of(keep, received, jnp.float32)[0]
 
 
 def settle(total, rows):
@@ -187,6 +189,10 @@
 VMEM_BYTES = 56 << 20
 
 
+def estimate(micros):
+    return pl.CostEstimate(flops=micros * 1000000000, bytes_accessed=micros * 1000000, transcendentals=0)
+
+
 def dot(left, right):
     return jnp.dot(left, right, preferred_element_type=jnp.float32)
 
@@ -276,10 +282,10 @@
 
 
 def forward_kernel(
-    lengths, x_ref, wq_ref, wk_ref, wv_ref, wo_ref, vec_ref,
+    seq, lengths, x_ref, wq_ref, wk_ref, wv_ref, wo_ref, vec_ref,
     q_ref, k_ref, v_ref, att_ref, lse_ref, first_ref, qt, vt, ot,
 ):
-    length = lengths[pl.program_id(0)]
+    length = lengths[seq]
     x = x_ref[...]
     head_size = x.shape[1] // HEADS
     scale = head_size**-0.5
@@ -317,18 +323,26 @@
     return pl.BlockSpec(shape, lambda *_: (0,) * len(shape))
 
 
-def attend_forward(x, lengths, wq, wk, wv, wo, vectors):
+def skip_refs(kernel, first, count, *refs):
+    kernel(*refs[:first], *refs[first + count :])
+
+
+def attend_forward(seq, x, lengths, wq, wk, wv, wo, vectors, before):
     seqs, slots, width = x.shape
-    rows = pl.BlockSpec((None, slots, width), lambda i, *_: (i, 0, 0))
+    rows = pl.BlockSpec((None, slots, width), lambda i, *_: (seq, 0, 0))
     low = jax.ShapeDtypeStruct(x.shape, jnp.bfloat16)
+    inputs = (lengths, x, wq, wk, wv, wo, vectors)
     return pl.pallas_call(
-        forward_kernel,
+        functools.partial(skip_refs, functools.partial(forward_kernel, seq), len(inputs), len(before)),
         grid_spec=pltpu.PrefetchScalarGridSpec(
             num_scalar_prefetch=1,
-            grid=(seqs,),
-            in_specs=[rows] + [whole((width, width))] * 4 + [whole(vectors.shape)],
+            grid=(1,),
+            in_specs=[rows]
+            + [whole((width, width))] * 4
+            + [whole(vectors.shape)]
+            + [pl.BlockSpec(memory_space=pl.ANY)] * len(before),
             out_specs=[rows] * 4
-            + [pl.BlockSpec((None, HEADS // 2, 2, slots), lambda i, *_: (i, 0, 0, 0)), rows],
+            + [pl.BlockSpec((None, HEADS // 2, 2, slots), lambda i, *_: (seq, 0, 0, 0)), rows],
             scratch_shapes=[pltpu.VMEM((width, slots), jnp.bfloat16)] * 3,
         ),
         out_shape=[low] * 4
@@ -336,9 +350,11 @@
             jax.ShapeDtypeStruct((seqs, HEADS // 2, 2, slots), jnp.float32),
             jax.ShapeDtypeStruct(x.shape, jnp.float32),
         ],
+        input_output_aliases={len(inputs) + i: i for i in range(len(before))},
         compiler_params=pltpu.CompilerParams(vmem_limit_bytes=VMEM_BYTES),
+        cost_estimate=estimate(12),
         name="attend_forward",
-    )(lengths, x, wq, wk, wv, wo, vectors)
+    )(*inputs, *before)
 
 
 def feed_kernel(
@@ -409,42 +425,93 @@
             jax.ShapeDtypeStruct((8, width), jnp.float32),
         ],
         compiler_params=pltpu.CompilerParams(vmem_limit_bytes=VMEM_BYTES),
+        cost_estimate=estimate(32),
         name="feed_forward",
     )(lengths, first.reshape(total, width), cotangent.reshape(total, width), wi, wo, hidden_bias, vectors)
 
 
-def feed_back_outer_kernel(low_ref, act_ref, slope_ref, wo_ref, hid_ref, grad_ref, sum_ref):
+def feed_back_outer_kernel(cut, me_ref, low_ref, act_ref, slope_ref, wo_ref, hid_ref, sum_ref, *rest):
     low = low_ref[...]
     up = dot_last(low, wo_ref[...]) * slope_ref[...].astype(jnp.float32)
     hidden = up.astype(jnp.bfloat16)
     hid_ref[...] = hidden
     sum_ref[...] = jnp.sum(hidden.astype(jnp.float32), axis=0, keepdims=True)
-    grad_ref[...] = dot_first(act_ref[...], low).astype(jnp.bfloat16)
-
-
-def feed_back_outer(low, act, slope, wo):
+    grad = dot_first(act_ref[...], low).astype(jnp.bfloat16)
+    if cut is None:
+        rest[0][...] = grad
+        return
+    outs, held, sems = rest[:2], rest[2], rest[3]
+    step = pl.program_id(0)
+    slot = step % 2
+    chunk = grad.shape[0]
+    blocks = chunk // (2 * cut.half)
+    width = outs[0].shape[2]
+    columns = [(p * width, p, 0, width) for p in range(grad.shape[1] // width)]
+
+    def copies(at_step):
+        return piece_copies(
+            held.at[at_step % 2], outs, sems.at[at_step % 2], me_ref, cut.stages,
+            at_step * blocks, blocks, cut.half, 0, columns, width,
+        )
+
+    @pl.when(step >= 2)
+    def _():
+        wait_all(copies(step - 2))
+
+    held[slot] = grad
+    run_all(copies(step))
+
+    @pl.when(step == pl.num_programs(0) - 1)
+    def _():
+        if pl.num_programs(0) > 1:
+            wait_all(copies(step - 1))
+        wait_all(copies(step))
+
+
+class Cut:
+    def __init__(self, stages, half, rows, width):
+        self.stages, self.half, self.rows, self.width = tuple(stages), half, rows, width
+        self.places = 1 << len(stages)
+
+    def shapes(self):
+        return [jax.ShapeDtypeStruct((self.places, self.rows, self.width), jnp.bfloat16)] * 2
+
+
+ANYWHERE = pl.BlockSpec(memory_space=pl.ANY)
+SCALARS = pl.BlockSpec(memory_space=pltpu.SMEM)
+
+
+def feed_back_outer(me, low, act, slope, wo, cut):
     total, width = low.shape
     inner = act.shape[1]
-    chunk = min(512, inner)
+    chunk = min(768, inner)
     wide = pl.BlockSpec((total, chunk), lambda i: (0, i))
     tall = pl.BlockSpec((chunk, width), lambda i: (i, 0))
+    direct = cut is not None
+    grads = cut.shapes() if direct else [jax.ShapeDtypeStruct((inner, width), jnp.bfloat16)]
+    copies = 2 * (chunk // (2 * cut.half)) * (width // cut.width) if direct else 1
+    scratch = [pltpu.VMEM((2, chunk, width), jnp.bfloat16), pltpu.SemaphoreType.DMA((2, copies))]
     return pl.pallas_call(
-        feed_back_outer_kernel,
+        functools.partial(feed_back_outer_kernel, cut),
         grid=(inner // chunk,),
-        in_specs=[whole((total, width)), wide, wide, tall],
-        out_specs=[wide, tall, pl.BlockSpec((1, chunk), lambda i: (0, i))],
+        in_specs=[SCALARS, whole((total, width)), wide, wide, tall],
+        out_specs=[wide, pl.BlockSpec((1, chunk), lambda i: (0, i))]
+        + ([ANYWHERE] * 2 if direct else [tall]),
         out_shape=[
             jax.ShapeDtypeStruct((total, inner), jnp.bfloat16),
-            jax.ShapeDtypeStruct((inner, width), jnp.bfloat16),
             jax.ShapeDtypeStruct((1, inner), jnp.float32),
+            *grads,
         ],
+        scratch_shapes=scratch if direct else [],
         compiler_params=pltpu.CompilerParams(vmem_limit_bytes=VMEM_BYTES),
+        cost_estimate=estimate(15),
         name="feed_back_outer",
-    )(low, act, slope, wo)
-
-
-def feed_back_inner_kernel(gs_ref, mid_ref, hid_ref, wi_ref, gm_ref, grad_ref, mid_t):
+    )(me, low, act, slope, wo)
+
+
+def feed_back_inner_kernel(cut, me_ref, gs_ref, mid_ref, hid_ref, wi_ref, gm_ref, *rest):
     step = pl.program_id(0)
+    mid_t = rest[-1]
 
     @pl.when(step == 0)
     def _():
@@ -452,49 +519,77 @@
         mid_t[...] = mid_ref[...].T
 
     hidden = hid_ref[...]
-    grad_ref[...] = dot(mid_t[...], hidden).astype(jnp.bfloat16)
+    grad = dot(mid_t[...], hidden).astype(jnp.bfloat16)
+    if cut is None:
+        rest[0][...] = grad
+        gm_ref[...] += dot_last(hidden, wi_ref[...])
+        return
+    outs, held, sems = rest[:2], rest[2], rest[3]
+    rows, chunk = grad.shape
+    parts = cut.width // chunk
+    blocks = rows // (2 * cut.half)
+
+    def copies(at_step):
+        columns = [(0, at_step // parts, pl.multiple_of(at_step % parts * chunk, 128), chunk)]
+        return piece_copies(
+            held.at[at_step % 2], outs, sems.at[at_step % 2], me_ref, cut.stages,
+            0, blocks, cut.half, 0, columns, chunk,
+        )
+
+    @pl.when(step >= 2)
+    def _():
+        wait_all(copies(step - 2))
+
+    held[step % 2] = grad
+    run_all(copies(step))
     gm_ref[...] += dot_last(hidden, wi_ref[...])
 
-
-def feed_back_inner(gs, mid, hid, wi):
+    @pl.when(step == pl.num_programs(0) - 1)
+    def _():
+        if pl.num_programs(0) > 1:
+            wait_all(copies(step - 1))
+        wait_all(copies(step))
+
+
+def feed_back_inner(me, gs, mid, hid, wi, cut):
     total, width = mid.shape
     inner = hid.shape[1]
-    chunk = min(512, inner)
+    chunk = min(768, inner)
     wide = pl.BlockSpec((total, chunk), lambda i: (0, i))
     flat = pl.BlockSpec((width, chunk), lambda i: (0, i))
+    direct = cut is not None
+    grads = cut.shapes() if direct else [jax.ShapeDtypeStruct((width, inner), jnp.bfloat16)]
+    scratch = [
+        pltpu.VMEM((2, width, chunk), jnp.bfloat16),
+        pltpu.SemaphoreType.DMA((2, width // cut.half if direct else 1)),
+    ]
     return pl.pallas_call(
-        feed_back_inner_kernel,
+        functools.partial(feed_back_inner_kernel, cut),
         grid=(inner // chunk,),
-        in_specs=[whole((total, width)), whole((total, width)), wide, flat],
-        out_specs=[whole((total, width)), flat],
-        out_shape=[
-            jax.ShapeDtypeStruct((total, width), jnp.float32),
-            jax.ShapeDtypeStruct((width, inner), jnp.bfloat16),
-        ],
-        scratch_shapes=[pltpu.VMEM((width, total), jnp.bfloat16)],
+        in_specs=[SCALARS, whole((total, width)), whole((total, width)), wide, flat],
+        out_specs=[whole((total, width))] + ([ANYWHERE] * 2 if direct else [flat]),
+        out_shape=[jax.ShapeDtypeStruct((total, width), jnp.float32), *grads],
+        scratch_shapes=(scratch if direct else []) + [pltpu.VMEM((width, total), jnp.bfloat16)],
         compiler_params=pltpu.CompilerParams(vmem_limit_bytes=VMEM_BYTES),
+        cost_estimate=estimate(16),
         name="feed_back_inner",
-    )(gs, mid, hid, wi)
+    )(me, gs, mid, hid, wi)
 
 
 def backward_kernel(
-    lengths, gm_ref, first_ref, q_ref, k_ref, v_ref, att_ref, lse_ref, wo_ref, vec_ref,
-    gf_ref, dq_ref, dk_ref, dv_ref, og_ref, sums_ref,
-    qt, kt, at_t, do_s, do_t, dq_t, total_s,
+    seq, lengths, gm_ref, first_ref, q_ref, k_ref, v_ref, att_ref, lse_ref, wo_ref, vec_ref,
+    *rest,
 ):
-    step = pl.program_id(0)
-    length = lengths[step]
+    gf_ref, dq_ref, dk_ref, dv_ref, og_ref, sums_ref, qt, kt, at_t, do_s, do_t, dq_t = rest[-12:]
+    totals_before = rest[:-12]
+    length = lengths[seq]
     slots, width = gm_ref.shape
     head_size = width // HEADS
     scale = head_size**-0.5
     grad_middle = gm_ref[...]
     normed, factor = normalize(first_ref[...])
 
-    @pl.when(step == 0)
-    def _():
-        sums_ref[...] = jnp.zeros_like(sums_ref)
-        total_s[...] = jnp.zeros_like(total_s)
-
+    sums_ref[...] = totals_before[1][...] if totals_before else jnp.zeros_like(sums_ref)
     sums_ref[0:1, :] += jnp.sum(grad_middle * normed, axis=0, keepdims=True)
     sums_ref[1:2, :] += jnp.sum(grad_middle, axis=0, keepdims=True)
     grad_first = norm_back(grad_middle * vec_ref[4:5, :], normed, factor)
@@ -502,12 +597,8 @@
     branch = grad_first.astype(jnp.bfloat16)
     sums_ref[2:3, :] += jnp.sum(branch.astype(jnp.float32), axis=0, keepdims=True)
     at_t[...] = att_ref[...].T
-    total_s[...] += dot(at_t[...], branch)
-
-    @pl.when(step == pl.num_programs(0) - 1)
-    def _():
-        og_ref[...] = total_s[...].astype(jnp.bfloat16)
-
+    output_grad = dot(at_t[...], branch)
+    og_ref[...] = totals_before[0][...] + output_grad if totals_before else output_grad
     upward = dot_last(branch, wo_ref[...]).astype(jnp.bfloat16)
     do_s[...] = upward
     do_t[...] = upward.T
@@ -544,60 +635,105 @@
 
     lax.fori_loop(0, HEADS // 2, one_pair, 0)
     dq_ref[...] = dq_t[...].T
-
-
-def attend_backward(gm, first, q, k, v, att, lse, lengths, wo, vectors):
+    sums_ref[3:4, :] += jnp.sum(dq_ref[...].astype(jnp.float32), axis=0, keepdims=True)
+    sums_ref[4:5, :] += jnp.sum(dv_ref[...].astype(jnp.float32), axis=0, keepdims=True)
+
+
+def attend_backward(seq, gm, first, q, k, v, att, lse, lengths, wo, vectors, totals, before):
     seqs, slots, width = q.shape
-    rows = pl.BlockSpec((None, slots, width), lambda i, *_: (i, 0, 0))
+    rows = pl.BlockSpec((None, slots, width), lambda i, *_: (seq, 0, 0))
     low = jax.ShapeDtypeStruct(q.shape, jnp.bfloat16)
     turned = pltpu.VMEM((width, slots), jnp.bfloat16)
+    inputs = (lengths, gm, first, q, k, v, att, lse, wo, vectors, *totals)
     return pl.pallas_call(
-        backward_kernel,
+        functools.partial(skip_refs, functools.partial(backward_kernel, seq), len(inputs), len(before)),
         grid_spec=pltpu.PrefetchScalarGridSpec(
             num_scalar_prefetch=1,
-            grid=(seqs,),
+            grid=(1,),
             in_specs=[rows] * 6
             + [
-                pl.BlockSpec((None, HEADS // 2, 2, slots), lambda i, *_: (i, 0, 0, 0)),
+                pl.BlockSpec((None, HEADS // 2, 2, slots), lambda i, *_: (seq, 0, 0, 0)),
                 whole((width, width)),
                 whole(vectors.shape),
-            ],
+            ]
+            + ([whole((width, width)), whole((8, width))] if totals else [])
+            + [pl.BlockSpec(memory_space=pl.ANY)] * len(before),
             out_specs=[rows] * 4 + [whole((width, width)), whole((8, width))],
             scratch_shapes=[
                 turned, turned, turned, pltpu.VMEM((slots, width), jnp.bfloat16), turned, turned,
-                pltpu.VMEM((width, width), jnp.float32),
             ],
         ),
         out_shape=[
             jax.ShapeDtypeStruct(q.shape, jnp.float32), low, low, low,
-            jax.ShapeDtypeStruct((width, width), jnp.bfloat16),
+            jax.ShapeDtypeStruct((width, width), jnp.float32),
             jax.ShapeDtypeStruct((8, width), jnp.float32),
         ],
+        input_output_aliases={len(inputs) + i: i for i in range(len(before))},
         compiler_params=pltpu.CompilerParams(vmem_limit_bytes=VMEM_BYTES),
+        cost_estimate=estimate(16),
         name="attend_backward",
-    )(lengths, gm, first, q, k, v, att, lse, wo, vectors)
-
-
-def project_grads_kernel(x_ref, dq_ref, dk_ref, dv_ref, gq_ref, gk_ref, gv_ref, sums_ref, xt):
+    )(*inputs, *before)
+
+
+def project_grads_kernel(cuts, dp_size, me_ref, x_ref, dq_ref, dk_ref, dv_ref, og_ref, small_ref, *rest):
+    xt, held, sems = rest[-3:]
+    outs = rest[:-3]
     xt[...] = x_ref[...].T
-    gq_ref[...] = dot(xt[...], dq_ref[...]).astype(jnp.bfloat16)
-    gk_ref[...] = dot(xt[...], dk_ref[...]).astype(jnp.bfloat16)
-    gv_ref[...] = dot(xt[...], dv_ref[...]).astype(jnp.bfloat16)
-    sums_ref[...] = jnp.zeros_like(sums_ref)
-    sums_ref[0:1, :] = jnp.sum(dq_ref[...].astype(jnp.float32), axis=0, keepdims=True)
-    sums_ref[1:2, :] = jnp.sum(dv_ref[...].astype(jnp.float32), axis=0, keepdims=True)
-
-
-def project_grads(x, dq, dk, dv):
+    held[0] = og_ref[...].astype(jnp.bfloat16)
+    started = []
+
+    def emit(which, cut, refs, at):
+        pairs = held.shape[2] // cut.width
+        columns = [(p * cut.width, p, 0, cut.width) for p in range(pairs)]
+        started.extend(
+            run_all(
+                piece_copies(
+                    held.at[which], refs, sems.at[which], me_ref, cut.stages, 0, dp_size,
+                    cut.half, at, columns, cut.width,
+                )
+            )
+        )
+
+    if cuts is not None:
+        emit(0, cuts[1], outs[2:4], cuts[1].half)
+        small = small_copies(
+            small_ref, outs[:2], sems.at[4], me_ref, cuts[0].stages, 2 * cuts[0].half, dp_size,
+            held.shape[2] // cuts[0].width,
+        )
+        started.extend(run_all(small))
+    for which, ref in ((1, dv_ref), (2, dq_ref), (3, dk_ref)):
+        held[which] = dot(xt[...], ref[...]).astype(jnp.bfloat16)
+        if cuts is not None:
+            cut, refs, at = (
+                (cuts[1], outs[2:4], 0) if which == 1 else (cuts[0], outs[:2], (which - 2) * cuts[0].half)
+            )
+            emit(which, cut, refs, at)
+    if cuts is None:
+        for out, which in zip(outs, (2, 3, 1, 0)):
+            out[...] = held[which]
+    wait_all(started)
+
+
+def project_grads(me, x, dq, dk, dv, og, small, cuts, dp_size):
     total, width = x.shape
     grad = jax.ShapeDtypeStruct((width, width), jnp.bfloat16)
+    here = pl.BlockSpec(memory_space=pltpu.VMEM)
+    direct = cuts is not None
+    copies = 2 * dp_size * (width // cuts[0].width) if direct else 1
     return pl.pallas_call(
-        project_grads_kernel,
-        out_shape=[grad, grad, grad, jax.ShapeDtypeStruct((8, width), jnp.float32)],
-        scratch_shapes=[pltpu.VMEM((width, total), jnp.bfloat16)],
+        functools.partial(project_grads_kernel, cuts, dp_size),
+        in_specs=[SCALARS] + [here] * 6,
+        out_specs=[ANYWHERE] * 4 if direct else [here] * 4,
+        out_shape=[*cuts[0].shapes(), *cuts[1].shapes()] if direct else [grad] * 4,
+        scratch_shapes=[
+            pltpu.VMEM((width, total), jnp.bfloat16),
+            pltpu.VMEM((4, width, width), jnp.bfloat16),
+            pltpu.SemaphoreType.DMA((5, copies)),
+        ],
         compiler_params=pltpu.CompilerParams(vmem_limit_bytes=VMEM_BYTES),
+        cost_estimate=estimate(8),
         name="project_grads",
-    )(x, dq, dk, dv)
+    )(me, x, dq, dk, dv, og, small)
 
 
 def input_grad_kernel(gf_ref, dq_ref, dk_ref, dv_ref, wq_ref, wk_ref, wv_ref, out_ref):
@@ -618,36 +754,74 @@
         out_specs=rows,
         out_shape=jax.ShapeDtypeStruct((total, width), jnp.bfloat16),
         compiler_params=pltpu.CompilerParams(vmem_limit_bytes=VMEM_BYTES),
+        cost_estimate=estimate(8),
         name="input_grads",
     )(gf, dq, dk, dv, wq, wk, wv)
 
 
-def layer_step(inputs, lengths, upstream, weights):
-    wq, wk, wv, wo, wi, wf, bias, hidden, gains, shifts = weights
+def after(values, *others):
+    return lax.optimization_barrier((values, others))[0]
+
+
+class Attention:
+    def __init__(self, inputs, lengths, weights, vectors):
+        self.inputs, self.lengths, self.vectors = inputs, lengths, vectors
+        self.weights, self.state, self.back = weights, (), ()
+        self.totals = ()
+
+    def forward(self, seq):
+        self.state = tuple(
+            attend_forward(seq, self.inputs, self.lengths, *self.weights, self.vectors, self.state)
+        )
+
+    def backward(self, seq, gm):
+        q, k, v, att, lse, first = self.state
+        results = attend_backward(
+            seq, gm, first, q, k, v, att, lse, self.lengths, self.weights[3], self.vectors,
+            self.totals, self.back,
+        )
+        self.back, self.totals = tuple(results[:4]), tuple(results[4:])
+
+
+def layer_step(inputs, lengths, upstream, gather, scatter):
     shape = inputs.shape
     flat = (shape[0] * shape[1], shape[2])
+    seqs = shape[0]
+    wq, wk, wv, wo, bias, hidden, gains, shifts = gather.first()
     vectors = jnp.concatenate([bias, gains, shifts], axis=0).astype(jnp.float32)
     hidden_bias = hidden.astype(jnp.float32)[None]
-    q, k, v, att, lse, first = attend_forward(inputs, lengths, wq, wk, wv, wo, vectors)
+    attention = Attention(inputs, lengths, (wq, wk, wv, wo), vectors)
+    for seq in range(seqs):
+        attention.inputs = gather.before(seq, attention.inputs)
+        attention.forward(seq)
+        attention.state = gather.after(seq, attention.state)
+    wi, wf = gather.second()
+    first = attention.state[5]
     outputs, act, slope, mid, gs, low, sums_two = feed_forward(
         first, upstream, lengths, wi, wf, hidden_bias, vectors
     )
-    hid, outer_grad, hidden_sum = feed_back_outer(low, act, slope, wf)
-    gm, inner_grad = feed_back_inner(gs, mid, hid, wi)
-    gf, dq, dk, dv, output_grad, sums_one = attend_backward(
-        gm.reshape(shape), first, q, k, v, att, lse, lengths, wo, vectors
-    )
+    me = gather.me
+    hid, hidden_sum, *outer_grad = feed_back_outer(me, low, act, slope, wf, scatter.cuts["outer"])
+    mid = scatter.outer(outer_grad, mid)
+    gm, *inner_grad = feed_back_inner(me, gs, mid, hid, wi, scatter.cuts["inner"])
+    gm = scatter.inner(inner_grad, gm)
+    for seq in range(seqs):
+        attention.backward(seq, gm.reshape(shape))
+        attention.back = scatter.step(seq, attention.back)
+    gf, dq, dk, dv = attention.back
+    output_grad, sums_one = attention.totals
     dq, dk, dv = dq.reshape(flat), dk.reshape(flat), dv.reshape(flat)
-    query_grad, key_grad, value_grad, sums_in = project_grads(inputs.reshape(flat), dq, dk, dv)
-    input_grad = input_grads(gf.reshape(flat), dq, dk, dv, wq, wk, wv)
-    bias_grad = jnp.concatenate([sums_in[:2], sums_one[2:3], sums_two[2:3]], axis=0)
+    bias_grad = jnp.concatenate([sums_one[3:5], sums_one[2:3], sums_two[2:3]], axis=0)
     gain_grad = jnp.concatenate([sums_one[:1], sums_two[:1]], axis=0)
     shift_grad = jnp.concatenate([sums_one[1:2], sums_two[1:2]], axis=0)
-    grads = (
-        query_grad, key_grad, value_grad, output_grad, inner_grad, outer_grad,
-        bias_grad, hidden_sum[0], gain_grad, shift_grad,
-    )
-    return outputs.reshape(shape), input_grad.reshape(shape), grads
+    small = scatter.small((bias_grad, hidden_sum[0], gain_grad, shift_grad))
+    packed = small if scatter.cuts["first"] else jnp.zeros((1, 8, 128), jnp.bfloat16)
+    results = project_grads(
+        me, inputs.reshape(flat), dq, dk, dv, output_grad, packed, scatter.cuts["first"], scatter.dp_size
+    )
+    gf = scatter.last(results, small, gf)
+    input_grad = input_grads(gf.reshape(flat), dq, dk, dv, wq, wk, wv)
+    return outputs.reshape(shape), input_grad.reshape(shape), scatter.totals()
 
 
 def split_up(value, dim, size):
@@ -793,65 +967,232 @@
     return jnp.pad(rows, ((0, 0), (0, SMALL_ROWS - rows.shape[1]), (0, width - columns)))
 
 
-def exchange_gather(mesh, shards, me):
-    query, key, value, output, inner, outer, bias, hidden, gains, shifts = shards
-    order_one, order_two = stage_orders(mesh)
-    half, half_outer = query.shape[0] // 2, outer.shape[0] // 2
-    width = 2 * query.shape[1]
-    count = query.shape[0]
-    small = pack_small(bias, hidden, gains, shifts, width)
-    (first,) = pair_up((jnp.stack([query, key]).reshape(2, 2, half, -1).swapaxes(0, 1).reshape(4 * half, -1),))
-    (second,) = pair_up((jnp.stack([value, output]).reshape(2, 2, half, -1).swapaxes(0, 1).reshape(4 * half, -1),))
-    (third,) = pair_up((inner,))
-    (fourth,) = pair_up((outer,))
-    first = jnp.concatenate([first, small], axis=0)
-    own, other = gather_part(first, order_one)
-    query_full, key_full, small_full = place_part(mesh, own, other, me, order_one, (half, half), True)
-    own, other = gather_part(second, order_two)
-    value_full, output_full = place_part(mesh, own, other, me, order_two, (half, half), False)
-    own, other = gather_part(third, order_one)
-    (inner_full,) = place_part(mesh, own, other, me, order_one, (half,), False)
-    own, other = gather_part(fourth, order_two)
-    (outer_full,) = place_part(mesh, own, other, me, order_two, (half_outer,), False)
-    vectors = unpack_small(small_full, bias.shape[1], hidden.shape[0])
-    return (query_full, key_full, value_full, output_full, inner_full, outer_full, *vectors)
-
-
-def exchange_scatter(mesh, grads, me, shards):
-    query, key, value, output, inner, outer, bias, hidden, gains, shifts = grads
-    order_one, order_two = stage_orders(mesh)
-    half, half_outer = shards[0].shape[0] // 2, shards[5].shape[0] // 2
-    width = 2 * shards[0].shape[1]
-    columns = shards[6].shape[1]
-    low = jnp.bfloat16
-    keep, send = cut_part(mesh, (outer.astype(low),), None, me, order_two, (half_outer,), width)
-    outer_sum_ = settle(scatter_part(keep, send, order_two), (half_outer,))[0]
-    keep, send = cut_part(mesh, (inner.astype(low),), None, me, order_one, (half,), 2 * shards[4].shape[1])
-    inner_sum = settle(scatter_part(keep, send, order_one), (half,))[0]
-    keep, send = cut_part(
-        mesh, (value.astype(low), output.astype(low)), None, me, order_two, (half, half), width
-    )
-    value_sum, output_sum = settle(scatter_part(keep, send, order_two), (half, half))
-    small = spread_small(bias, hidden, gains, shifts, mesh.shape["dp"], width)
-    keep, send = cut_part(
-        mesh, (query.astype(low), key.astype(low)), small, me, order_one, (half, half), width
-    )
-    total = scatter_part(keep, send, order_one)
-    query_sum, key_sum = settle(total, (half, half))
-    rows = total[2 * half :, :columns]
-    split = 4 + shards[7].shape[0] // columns
-    return (
-        query_sum,
-        key_sum,
-        value_sum,
-        output_sum,
-        inner_sum,
-        outer_sum_,
-        rows[:4],
-        rows[4:split].reshape(-1),
-        rows[split : split + 2],
-        rows[split + 2 : split + 4],
-    )
+class Gather:
+    def __init__(self, mesh, shards, me):
+        self.mesh, self.shards, self.me = mesh, shards, me
+        self.orders = stage_orders(mesh)
+
+    def prepare(self):
+        query, key, value, output, inner, outer, bias, hidden, gains, shifts = self.shards
+        half = query.shape[0] // 2
+        small = pack_small(bias, hidden, gains, shifts, 2 * query.shape[1])
+
+        def both(left, right):
+            parts = [left[:half], right[:half], left[half:], right[half:]]
+            return jnp.concatenate(parts, axis=0)
+
+        parts = pair_up((both(query, key), both(value, output)))
+        self.one = [jnp.concatenate([parts[0], small], axis=0)[None], parts[1][None]]
+        self.two = [part[None] for part in pair_up((inner, outer))]
+
+    def send(self, parts, stage):
+        return [swap(part, *self.orders[i][stage]) for i, part in enumerate(parts)]
+
+    def join(self, parts, received):
+        return [jnp.concatenate(pair, axis=0) for pair in zip(parts, received)]
+
+    def first(self):
+        self.prepare()
+        count = len(self.orders[0])
+        far = sum(1 for axis, bit in self.orders[0] if axis == "dp" and bit > 0)
+        for stage in range(count):
+            arriving = self.send(self.one, stage)
+            if 0 < stage <= far:
+                self.two = self.join(self.two, self.send(self.two, stage - 1))
+            self.one = self.join(self.one, arriving)
+            if stage < far:
+                self.two = after(self.two, self.one)
+        self.stage = far
+        self.two = after(self.two, self.one)
+        others = [swap(part, "fsdp", 0) for part in self.one]
+        half = self.shards[0].shape[0] // 2
+        wq, wk, small = place_part(
+            self.mesh, self.one[0], others[0], self.me, self.orders[0], (half, half), True
+        )
+        wv, wo = place_part(
+            self.mesh, self.one[1], others[1], self.me, self.orders[1], (half, half), False
+        )
+        bias, hidden = self.shards[6:8]
+        return (wq, wk, wv, wo, *unpack_small(small, bias.shape[1], hidden.shape[0]))
+
+    def before(self, seq, inputs):
+        if self.stage == len(self.orders[0]):
+            return inputs
+        self.arriving = self.send(self.two, self.stage)
+        self.stage += 1
+        return after(inputs, self.two)
+
+    def after(self, seq, state):
+        if self.arriving is None:
+            return state
+        arriving = after(self.arriving, state)
+        self.two, self.arriving = self.join(self.two, arriving), None
+        return state
+
+    def second(self):
+        while self.stage < len(self.orders[0]):
+            self.two = self.join(self.two, self.send(self.two, self.stage))
+            self.stage += 1
+        others = [swap(part, "fsdp", 0) for part in self.two]
+        half, half_outer = self.shards[4].shape[0] // 2, self.shards[5].shape[0] // 2
+        (wi,) = place_part(
+            self.mesh, self.two[0], others[0], self.me, self.orders[0], (half,), False
+        )
+        (wf,) = place_part(
+            self.mesh, self.two[1], others[1], self.me, self.orders[1], (half_outer,), False
+        )
+        return wi, wf
+
+
+class Part:
+    def __init__(self, keep, send, stages):
+        self.keep, self.stages = keep, list(stages)
+        self.arriving = swap(send, "fsdp", 0)
+
+    def step(self):
+        axis, bit = self.stages.pop()
+        half = self.keep.shape[0] // 2
+        send = total_of(self.keep[half:], self.arriving[half:], jnp.bfloat16)
+        arriving = swap(send, axis, bit)
+        self.keep = total_of(self.keep[:half], self.arriving[:half], jnp.bfloat16)
+        self.arriving = arriving
+        return send
+
+    def finish(self):
+        while self.stages:
+            self.step()
+        return total_of(self.keep, self.arriving, jnp.float32)[0]
+
+
+class Scatter:
+    def __init__(self, mesh, shards, me):
+        self.shards = shards
+        one, two = stage_orders(mesh)
+        width = 2 * shards[0].shape[1]
+        half, half_outer = shards[0].shape[0] // 2, shards[5].shape[0] // 2
+        self.dp_size = mesh.shape["dp"]
+        self.cuts = {
+            "outer": Cut(two, half_outer, half_outer, width),
+            "inner": Cut(one, half, half, 2 * shards[4].shape[1]),
+            "first": (Cut(one, half, 2 * half + SMALL_ROWS, width), Cut(two, half, 2 * half, width)),
+        }
+
+    def outer(self, grad, passing):
+        self.outer_part = Part(*grad, self.cuts["outer"].stages)
+        return after(passing, grad)
+
+    def inner(self, grad, passing):
+        self.inner_part = Part(*grad, self.cuts["inner"].stages)
+        return after(passing, grad, self.outer_part.step())
+
+    def step(self, seq, state):
+        if seq == 0:
+            self.inner_part.arriving = after(self.inner_part.arriving, state)
+            sent = [self.inner_part.step()]
+        else:
+            self.outer_part.arriving = after(self.outer_part.arriving, state)
+            self.inner_part.arriving = after(self.inner_part.arriving, state)
+            sent = [self.outer_part.step(), self.inner_part.step()]
+        return after(state, sent)
+
+    def small(self, small):
+        return spread_small(*small, self.dp_size, self.cuts["first"][0].width)
+
+    def last(self, results, small, passing):
+        cuts = self.cuts["first"]
+        self.first_part = Part(*results[:2], cuts[0].stages)
+        self.second_part = Part(*results[2:], cuts[1].stages)
+        late, early = self.early(), [self.first_part, self.second_part]
+        for part in late:
+            part.arriving = after(part.arriving, results)
+        sent = [part.step() for part in late]
+        for part in early:
+            part.arriving = after(part.arriving, sent)
+        sent = [part.step() for part in early]
+        return after(passing, sent)
+
+    def early(self):
+        return [self.outer_part, self.inner_part]
+
+    def together(self, parts):
+        values = after([(part.keep, part.arriving) for part in parts])
+        for part, (keep, arriving) in zip(parts, values):
+            part.keep, part.arriving = keep, arriving
+
+    def totals(self):
+        half, half_outer = self.shards[0].shape[0] // 2, self.shards[5].shape[0] // 2
+        columns = self.shards[6].shape[1]
+        front, behind = [self.first_part, self.second_part], self.early()
+        for part in behind:
+            if part.stages:
+                part.step()
+        done = []
+        while any(part.stages for part in front + behind):
+            self.together(front)
+            for part in front:
+                if part.stages:
+                    part.step()
+            for part in behind:
+                part.arriving = after(part.arriving, [p.keep for p in front])
+                if part.stages:
+                    part.step()
+        (outer,) = settle(behind[0].finish(), (half_outer,))
+        (inner,) = settle(behind[1].finish(), (half,))
+        value, output = settle(front[1].finish(), (half, half))
+        total = front[0].finish()
+        query, key = settle(total, (half, half))
+        rows = total[2 * half :, :columns]
+        split = 4 + self.shards[7].shape[0] // columns
+        return (
+            query, key, value, output, inner, outer,
+            rows[:4], rows[4:split].reshape(-1), rows[split : split + 2], rows[split + 2 : split + 4],
+        )
+
+
+class PlainGather:
+    def __init__(self, mesh, shards, me):
+        self.shards, self.me = shards, me
+
+    def first(self):
+        whole_ = gather_forward(self.shards)
+        self.rest = whole_[4:6]
+        return (*whole_[:4], *whole_[6:])
+
+    def before(self, seq, inputs):
+        return inputs
+
+    def after(self, seq, state):
+        return state
+
+    def second(self):
+        return self.rest
+
+
+class PlainScatter:
+    def __init__(self, mesh, shards, me):
+        self.cuts = {"outer": None, "inner": None, "first": None}
+        self.dp_size = mesh.shape["dp"]
+
+    def outer(self, grad, passing):
+        self.outer_grad = grad[0]
+        return passing
+
+    def inner(self, grad, passing):
+        self.inner_grad = grad[0]
+        return passing
+
+    def step(self, seq, state):
+        return state
+
+    def small(self, small):
+        return small
+
+    def last(self, results, small, passing):
+        self.grads = (*results, self.inner_grad, self.outer_grad, *small)
+        return passing
+
+    def totals(self):
+        return reduce_grads(self.grads)
 
 
 def on_device(
@@ -864,12 +1205,12 @@
     me = jnp.stack([lax.axis_index("dp"), lax.axis_index("fsdp")]).astype(jnp.int32)
     rows = (shards[0].shape[0], shards[5].shape[0])
     direct = fits(mesh, rows, shards[0].shape[1])
-    weights = exchange_gather(mesh, shards, me) if direct else gather_forward(shards)
+    gather = (Gather if direct else PlainGather)(mesh, shards, me)
+    scatter = (Scatter if direct else PlainScatter)(mesh, shards, me)
     shape = (-1, *tokens.shape[2:])
-    outputs, grad_inputs, grads = layer_step(
-        tokens.reshape(shape), lengths.reshape(-1), cotangent.reshape(shape), weights
-    )
-    totals = exchange_scatter(mesh, grads, me, shards) if direct else reduce_grads(grads)
+    outputs, grad_inputs, totals = layer_step(
+        tokens.reshape(shape), lengths.reshape(-1), cotangent.reshape(shape), gather, scatter
+    )
     return (outputs.reshape(tokens.shape), grad_inputs.reshape(tokens.shape), *totals)
 
 

time: 405 us -> 360 us (0.89); the launches traced: 404 us -> 354 us
  waiting for transfers between devices: 138 us -> 77.9 us
  local copies, waits for them, and re-layouts: 14.7 us -> 28.2 us
  starting transfers between devices: 49 us -> 43.2 us
    ppermute x48, waiting for transfers between devices: 138 us -> 77.9 us  [swap(): return lax.ppermute(value, axis, [(i, i ^ 1 << bit) for i in range(size)])]
    ppermute x48, starting transfers between devices: 49 us -> 43.2 us  [swap(): return lax.ppermute(value, axis, [(i, i ^ 1 << bit) for i in range(size)])]
    unnamed x41 -> x39, local copies, waits for them, and re-layouts: 6.51 us -> 11.7 us
    pallas_call x9 -> x7, Pallas kernels: 114 us -> 115 us  [the longest x2 35.5 us: attend_backward(): pl.pallas_call(functools.partial(skip_refs, functools.partial(backward_ke...]
  transfers between devices with their start and end apart: 48 -> 48, of which waited for: 25 -> 17; matrix products, arithmetic and copies ran while one was open for 9% -> 13% of each run, Pallas kernels for 16% -> 31%
where the time goes in v3:
time: 360 us; the launch traced here: 354 us
  Pallas kernels  177 us (49%)
  waiting for transfers between devices  77.9 us (22%)
  starting transfers between devices  43.2 us (12%)
  local copies, waits for them, and re-layouts  28.2 us (8%)
  other arithmetic  26.1 us (7%)
    ppermute x48, waiting for transfers between devices, swap(): return lax.ppermute(value, axis, [(i, i ^ 1 << bit) for i in range(size)])  77.9 us
    ppermute x48, starting transfers between devices, swap(): return lax.ppermute(value, axis, [(i, i ^ 1 << bit) for i in range(size)])  43.2 us
    pallas_call x2, Pallas kernels, attend_backward(): pl.pallas_call(functools.partial(skip_refs, functools.partial(backward_ke...  35.5 us
    pallas_call x1, Pallas kernels, feed_forward(): pl.pallas_call(functools.partial(feed_kernel, tiles, min(512, inner)), gr...  32.4 us
    pallas_call x2, Pallas kernels, attend_forward(): pl.pallas_call(functools.partial(skip_refs, functools.partial(forward_ker...  29.4 us
    pallas_call x1, Pallas kernels, feed_back_inner(): pl.pallas_call(functools.partial(feed_back_inner_kernel, cut), grid=(inne...  22.1 us
    pallas_call x4, Pallas kernels, place_part(): pl.pallas_call(functools.partial(place_kernel, stages, rows, width, with_...  20.8 us
    pallas_call x1, Pallas kernels, feed_back_outer(): pl.pallas_call(functools.partial(feed_back_outer_kernel, cut), grid=(inne...  17.8 us
  transfers between devices with their start and end apart: 48, of which 17 were waited for; matrix products, arithmetic and copies ran while one was open for 13% of the time, Pallas kernels for 31%

profile of v3, /device:TPU:0, one launch (start us, length us, event | category | flops | bytes accessed | tf_op | source)
XLA Modules:
  0.0 353.9 jit_solution(1026114124977848060)
XLA Ops:
  6.1 4.1 %collective-permute-start.3 = (bf16[1,112,384]{2,1,0:T(8,128)(2,1)S(1)}, bf16[1,112,384]{2,1,0:T(8,128)(2,1)S(1)}, u32[]{:S(2)}, u32[]{:S(2)}) collective-permute-start(bf16[1,112,384]{2,1,0:T(8,128)(2,1)S(1)} %maximum_bitcast_fusion), channel_id=1, source_target_pairs={{0,16},{4,20},{8,24},{12,28},{16,0},{20,4},{24,8},{28,12},{1,17},{... | collective-permute-start | bytes 258056 | tf_op jit(solution)/shard_map/ppermute | solution.py:19
  11.8 6.1 %collective-permute-done.5 = bf16[1,96,384]{2,1,0:T(8,128)(2,1)S(1)} collective-permute-done((bf16[1,96,384]{2,1,0:T(8,128)(2,1)S(1)}, bf16[1,96,384]{2,1,0:T(8,128)(2,1)S(1)}, u32[]{:S(2)}, u32[]{:S(2)}) %collective-permute-start.5) | collective-permute-done | bytes 73760 | tf_op jit(solution)/shard_map/ppermute | solution.py:19
  20.8 2.2 collective-permute-start.6
  23.7 6.8 %collective-permute-done.9 = bf16[2,96,384]{2,1,0:T(8,128)(2,1)S(1)} collective-permute-done((bf16[2,96,384]{2,1,0:T(8,128)(2,1)S(1)}, bf16[2,96,384]{2,1,0:T(8,128)(2,1)S(1)}, u32[]{:S(2)}, u32[]{:S(2)}) %collective-permute-start.9) | collective-permute-done | bytes 147488 | tf_op jit(solution)/shard_map/ppermute | solution.py:19
  30.6 1.5 collective-permute-start.14
  32.8 1.6 collective-permute-start.12
  35.0 2.3 collective-permute-done.14
  37.4 1.5 collective-permute-start.15
  39.0 4.9 %collective-permute-done.12 = bf16[4,112,384]{2,1,0:T(8,128)(2,1)S(1)} collective-permute-done((bf16[4,112,384]{2,1,0:T(8,128)(2,1)S(1)}, bf16[4,112,384]{2,1,0:T(8,128)(2,1)S(1)}, u32[]{:S(2)}, u32[]{:S(2)}) %collective-permute-start.12) | collective-permute-done | bytes 344096 | tf_op jit(solution)/shard_map/ppermute | solution.py:19
  43.9 1.5 collective-permute-start.13
  45.6 2.0 collective-permute-start.11
  48.3 5.8 %collective-permute-done.15 = bf16[8,96,384]{2,1,0:T(8,128)(2,1)S(1)} collective-permute-done((bf16[8,96,384]{2,1,0:T(8,128)(2,1)S(1)}, bf16[8,96,384]{2,1,0:T(8,128)(2,1)S(1)}, u32[]{:S(2)}, u32[]{:S(2)}) %collective-permute-start.15) | collective-permute-done | bytes 589856 | tf_op jit(solution)/shard_map/ppermute | solution.py:19
  58.6 1.5 collective-permute-start.16
  60.1 1.5 collective-permute-start.17
  63.7 4.6 %place.5 = (bf16[768,768]{1,0:T(8,128)(2,1)}, bf16[768,768]{1,0:T(8,128)(2,1)}) custom-call(s32[2]{0:T(128)} %pad_add_fusion.me_ref, bf16[16,96,384]{2,1,0:T(8,128)(2,1)} %constant_dynamic-update-slice_fusion.5.refs_0_, bf16[16,96,384]{2,1,0:T(8,128)(2,1)} %collective-permute-done.19.refs_1_), custom_call_target="tpu_custom_call" | custom-call | flops 5000000000 | bytes 5000000 | tf_op jit(solution)/shard_map/place/pallas_call | solution.py:85
  68.2 4.6 %place.4 = (bf16[768,768]{1,0:T(8,128)(2,1)}, bf16[768,768]{1,0:T(8,128)(2,1)}, bf16[8,16,384]{2,1,0:T(8,128)(2,1)}) custom-call(s32[2]{0:T(128)} %pad_add_fusion.me_ref, bf16[16,112,384]{2,1,0:T(8,128)(2,1)} %constant_dynamic-update-slice_fusion.refs_0_, bf16[16,112,384]{2,1,0:T(8,128)(2,1)} %collective-permute-done.18.refs_1_), custom_call_target="tpu_custom_call" | custom-call | flops 5000000000 | bytes 5000000 | tf_op jit(solution)/shard_map/place/pallas_call | solution.py:85
  77.1 15.0 %attend_forward.2 = (bf16[2,512,768]{2,1,0:T(8,128)(2,1)}, bf16[2,512,768]{2,1,0:T(8,128)(2,1)}, bf16[2,512,768]{2,1,0:T(8,128)(2,1)}, bf16[2,512,768]{2,1,0:T(8...) custom-call(s32[2]{0:T(128)} %bitcast.60, bf16[2,512,768]{2,1,0:T(8,128)(2,1)} %bitcast.57, ...), custom_call_target="tpu_custom_call" | custom-call | flops 12000000000 | bytes 12000000 | tf_op jit(solution)/shard_map/attend_forward/pallas_call | solution.py:335
  95.1 14.4 %attend_forward.3 = (bf16[2,512,768]{2,1,0:T(8,128)(2,1)}, bf16[2,512,768]{2,1,0:T(8,128)(2,1)}, bf16[2,512,768]{2,1,0:T(8,128)(2,1)}, bf16[2,512,768]{2,1,0:T(8...) custom-call(s32[2]{0:T(128)} %bitcast.61, ...), custom_call_target="tpu_custom_call", output_to_operand_aliasing={{0}: (7, {}), {1}: (8, {}), {2}: (9, {}), {3}: (10, {}), {4... | custom-call | flops 12000000000 | bytes 12000000 | tf_op jit(solution)/shard_map/attend_forward/pallas_call | solution.py:335
  109.5 11.1 %collective-permute-done.21 = bf16[8,192,384]{2,1,0:T(8,128)(2,1)S(1)} collective-permute-done((bf16[8,192,384]{2,1,0:T(8,128)(2,1)S(1)}, bf16[8,192,384]{2,1,0:T(8,128)(2,1)S(1)}, u32[]{:S(2)}, u32[]{:S(2)}) %collective-permute-start.21) | collective-permute-done | bytes 1179680 | tf_op jit(solution)/shard_map/ppermute | solution.py:19
  125.0 4.4 %collective-permute-done.23.refs_1_ = bf16[16,192,384]{2,1,0:T(8,128)(2,1)} collective-permute-done((bf16[16,192,384]{2,1,0:T(8,128)(2,1)}, bf16[16,192,384]{2,1,0:T(8,128)(2,1)}, u32[]{:S(2)}, u32[]{:S(2)}) %collective-permute-start.23) | collective-permute-done | bytes 2359328 | tf_op jit(solution)/shard_map/ppermute | solution.py:19
  129.5 5.8 %place.7.wo_ref = bf16[3072,768]{1,0:T(8,128)(2,1)} custom-call(s32[2]{0:T(128)} %pad_add_fusion.me_ref, bf16[16,192,384]{2,1,0:T(8,128)(2,1)} %constant_dynamic-update-slice_fusion.17.refs_0_, bf16[16,192,384]{2,1,0:T(8,128)(2,1)} %collective-permute-done.23.refs_1_), custom_call_target="tpu_custom_call" | custom-call | flops 5000000000 | bytes 5000000 | tf_op jit(solution)/shard_map/place/pallas_call | solution.py:85
  135.3 5.8 %place.6.wi_ref = bf16[768,3072]{1,0:T(8,128)(2,1)} custom-call(s32[2]{0:T(128)} %pad_add_fusion.me_ref, bf16[16,48,1536]{2,1,0:T(8,128)(2,1)} %copy-done.6, bf16[16,48,1536]{2,1,0:T(8,128)(2,1)} %collective-permute-done.22.refs_1_), custom_call_target="tpu_custom_call" | custom-call | flops 5000000000 | bytes 5000000 | tf_op jit(solution)/shard_map/place/pallas_call | solution.py:85
  141.1 32.4 %feed_forward.1 = (bf16[1024,768]{1,0:T(8,128)(2,1)}, bf16[1024,3072]{1,0:T(8,128)(2,1)}, bf16[1024,3072]{1,0:T(8,128)(2,1)}, bf16[1024,768]{1,0:T(8,128)(2,1)},...) custom-call(s32[2]{0:T(128)} %bitcast.62, f32[1024,768]{1,0:T(8,128)} %bitcast.67, ...), custom_call_target="tpu_custom_call" | custom-call | flops 32000000000 | bytes 32000000 | tf_op jit(solution)/shard_map/feed_forward/pallas_call | solution.py:410
  173.6 17.8 %feed_back_outer.1 = (bf16[1024,3072]{1,0:T(8,128)(2,1)}, f32[1,3072]{1,0:T(1,128)}, bf16[16,192,384]{2,1,0:T(8,128)(2,1)}, bf16[16,192,384]{2,1,0:T(8,128)(2,1)}) custom-call(s32[2]{0:T(128)} %pad_add_fusion.me_ref, bf16[1024,768]{1,0:T(8,128)(2,1)} %get-tuple-element.139.low_ref, bf16[1024,3072]{1,0:T(8,128)(2,1)} %get-tuple-element.140.act_ref, ...), custom_call_target="tpu_custom_call" | custom-call | flops 15000000512 | bytes 15000000 | tf_op jit(solution)/shard_map/feed_back_outer/pallas_call | solution.py:494
  191.6 22.1 %feed_back_inner.1 = (f32[1024,768]{1,0:T(8,128)}, bf16[16,48,1536]{2,1,0:T(8,128)(2,1)}, bf16[16,48,1536]{2,1,0:T(8,128)(2,1)}) custom-call(s32[2]{0:T(128)} %pad_add_fusion.me_ref, f32[1024,768]{1,0:T(8,128)} %get-tuple-element.137.gs_ref, bf16[1024,768]{1,0:T(8,128)(2,1)} %get-tuple-element.144.mid_ref, bf16[1024,3072]{1,0:T(8,128)(2,1)} %get-tuple-element.145.hid_ref, ...), custom_call_target="tpu_custom_call" | custom-call | flops 16000000000 | bytes 16000000 | tf_op jit(solution)/shard_map/feed_back_inner/pallas_call | solution.py:566
  214.9 4.1 %add_convert_fusion.1 = (bf16[8,192,384]{2,1,0:T(8,128)(2,1)S(1)}, bf16[8,192,384]{2,1,0:T(8,128)(2,1)}) fusion(bf16[16,192,384]{2,1,0:T(8,128)(2,1)} %collective-permute-done.24, bf16[16,192,384]{2,1,0:T(8,128)(2,1)} %get-tuple-element.142), kind=kLoop, calls=%fused_computation.1 | loop fusion | flops 4718592 | bytes 7077888 | tf_op jit(solution)/shard_map/convert_element_type | solution.py:153
  218.9 1.5 collective-permute-start.26
  220.5 17.6 %attend_backward.2 = (f32[2,512,768]{2,1,0:T(8,128)}, bf16[2,512,768]{2,1,0:T(8,128)(2,1)}, bf16[2,512,768]{2,1,0:T(8,128)(2,1)}, bf16[2,512,768]{2,1,0:T(8,128)...) custom-call(s32[2]{0:T(128)} %bitcast.63, f32[2,512,768]{2,1,0:T(8,128)} %bitcast.65, ...), custom_call_target="tpu_custom_call" | custom-call | flops 16000000000 | bytes 16000000 | tf_op jit(solution)/shard_map/attend_backward/pallas_call | solution.py:648
  238.1 1.4 copy-done.1
  239.5 3.3 add_convert_fusion
  243.2 18.0 %attend_backward.3 = (f32[2,512,768]{2,1,0:T(8,128)}, bf16[2,512,768]{2,1,0:T(8,128)(2,1)}, bf16[2,512,768]{2,1,0:T(8,128)(2,1)}, bf16[2,512,768]{2,1,0:T(8,128)...) custom-call(s32[2]{0:T(128)} %bitcast.64, ...), custom_call_target="tpu_custom_call", output_to_operand_aliasing={{0}: (12, {}), {1}: (13, {}), {2}: (14, {}), {3}: (15, {})} | custom-call | flops 16000000000 | bytes 16000000 | tf_op jit(solution)/shard_map/attend_backward/pallas_call | solution.py:648
  269.8 1.4 fusion.8.small_ref
  271.2 1.5 add_convert_fusion.9
  273.0 10.1 %project_grads.1 = (bf16[16,112,384]{2,1,0:T(8,128)(2,1)}, bf16[16,112,384]{2,1,0:T(8,128)(2,1)}, bf16[16,96,384]{2,1,0:T(8,128)(2,1)}, bf16[16,96,384]{2,1,0:T(8,128)(2,1)}) custom-call(s32[2]{0:T(128)} %pad_add_fusion.me_ref, bf16[1024,768]{1,0:T(8,128)(2,1)} %bitcast.59, bf16[1024,768]{1,0:T(8,128)(2,1)} %bitcast.71, bf16[1024,768]{1,0:T(8,128)(2,1)} %bitcast.73, ...), custom_call_target="tpu_custom_call" | custom-call | flops 8000000000 | bytes 8000000 | tf_op jit(solution)/shard_map/project_grads/pallas_call | solution.py:723
  284.0 1.4 collective-permute-start.29
  285.4 13.6 %collective-permute-done.30 = bf16[4,48,1536]{2,1,0:T(8,128)(2,1)S(1)} collective-permute-done((bf16[4,48,1536]{2,1,0:T(8,128)(2,1)S(1)}, bf16[4,48,1536]{2,1,0:T(8,128)(2,1)S(1)}, u32[]{:S(2)}, u32[]{:S(2)}) %collective-permute-start.30) | collective-permute-done | bytes 589856 | tf_op jit(solution)/shard_map/ppermute | solution.py:19
  301.1 1.5 collective-permute-start.32
  302.8 1.6 collective-permute-start.33
  304.4 2.0 collective-permute-start.42
  306.5 9.5 %collective-permute-done.45 = bf16[2,192,384]{2,1,0:T(8,128)(2,1)S(1)} collective-permute-done((bf16[2,192,384]{2,1,0:T(8,128)(2,1)S(1)}, bf16[2,192,384]{2,1,0:T(8,128)(2,1)S(1)}, u32[]{:S(2)}, u32[]{:S(2)}) %collective-permute-start.45) | collective-permute-done | bytes 294944 | tf_op jit(solution)/shard_map/ppermute | solution.py:19
  318.0 1.4 collective-permute-start.34
  319.5 1.7 collective-permute-start.35
  321.7 4.9 %collective-permute-done.35 = bf16[4,96,384]{2,1,0:T(8,128)(2,1)S(1)} collective-permute-done((bf16[4,96,384]{2,1,0:T(8,128)(2,1)S(1)}, bf16[4,96,384]{2,1,0:T(8,128)(2,1)S(1)}, u32[]{:S(2)}, u32[]{:S(2)}) %collective-permute-start.35) | collective-permute-done | bytes 294944 | tf_op jit(solution)/shard_map/ppermute | solution.py:19
  326.9 2.1 collective-permute-start.37
  329.0 8.6 %input_grads.1 = bf16[1024,768]{1,0:T(8,128)(2,1)} custom-call(f32[1024,768]{1,0:T(8,128)} %bitcast.68, bf16[1024,768]{1,0:T(8,128)(2,1)} %bitcast.72, bf16[1024,768]{1,0:T(8,128)(2,1)} %bitcast.74, bf16[1024,768]{1,0:T(8,128)(2,1)} %bitcast.76, bf16[768,768]{1,0:T(8,128)(2,1)} %get-tuple-element.114.refs_2_.wq_ref, ...), custom_call_target="tpu_custom_call" | custom-call | flops 8000000000 | bytes 8000000 | tf_op jit(solution)/shard_map/input_grads/pallas_call | solution.py:750
  338.7 2.1 collective-permute-start.38
  340.7 3.4 collective-permute-done.40
  344.3 1.6 collective-permute-done.38
  (200 shorter events, 56.7 us)
Async XLA Ops:
  1.5 4.5 %collective-permute-start.2 = (bf16[96,192]{1,0:T(8,128)(2,1)S(1)}, bf16[96,192]{1,0:T(8,128)(2,1)S(1)}, u32[]{:S(2)}, u32[]{:S(2)}) collective-permute-start(bf16[96,192]{1,0:T(8,128)(2,1)S(1)} %get-tuple-element.293), channel_id=1, source_target_pairs={{0,1},{1,0},{2,3},{3,2},{4,5},{5,4},{6,7},{7,6},{8,9},{9,8},{10,11... | collective-permute-start | bytes 110600 | tf_op jit(solution)/shard_map/ppermute | solution.py:19
  2.9 7.4 %collective-permute-start.4 = (bf16[96,192]{1,0:T(8,128)(2,1)S(1)}, bf16[96,192]{1,0:T(8,128)(2,1)S(1)}, u32[]{:S(2)}, u32[]{:S(2)}) collective-permute-start(bf16[96,192]{1,0:T(8,128)(2,1)S(1)} %get-tuple-element.290), channel_id=1, source_target_pairs={{0,1},{1,0},{2,3},{3,2},{4,5},{5,4},{6,7},{7,6},{8,9},{9,8},{10,11... | collective-permute-start | bytes 110600 | tf_op jit(solution)/shard_map/ppermute | solution.py:19
  3.9 7.7 %collective-permute-start = (bf16[48,768]{1,0:T(8,128)(2,1)S(1)}, bf16[48,768]{1,0:T(8,128)(2,1)S(1)}, u32[]{:S(2)}, u32[]{:S(2)}) collective-permute-start(bf16[48,768]{1,0:T(8,128)(2,1)S(1)} %get-tuple-element.281), channel_id=1, source_target_pairs={{0,1},{1,0},{2,3},{3,2},{4,5},{5,4},{6,7},{7,6},{8,9},{9,8},{10,11... | collective-permute-start | bytes 221192 | tf_op jit(solution)/shard_map/ppermute | solution.py:19
  5.8 5.9 %collective-permute-start.1 = (bf16[192,192]{1,0:T(8,128)(2,1)S(1)}, bf16[192,192]{1,0:T(8,128)(2,1)S(1)}, u32[]{:S(2)}, u32[]{:S(2)}) collective-permute-start(bf16[192,192]{1,0:T(8,128)(2,1)S(1)} %get-tuple-element.273), channel_id=1, source_target_pairs={{0,1},{1,0},{2,3},{3,2},{4,5},{5,4},{6,7},{7,6},{8,9},{9,8},{10,11... | collective-permute-start | bytes 221192 | tf_op jit(solution)/shard_map/ppermute | solution.py:19
  6.1 13.3 %collective-permute-start.3 = (bf16[1,112,384]{2,1,0:T(8,128)(2,1)S(1)}, bf16[1,112,384]{2,1,0:T(8,128)(2,1)S(1)}, u32[]{:S(2)}, u32[]{:S(2)}) collective-permute-start(bf16[1,112,384]{2,1,0:T(8,128)(2,1)S(1)} %maximum_bitcast_fusion), channel_id=1, source_target_pairs={{0,16},{4,20},{8,24},{12,28},{16,0},{20,4},{24,8},{28,12},{1,17},{... | collective-permute-start | bytes 258056 | tf_op jit(solution)/shard_map/ppermute | solution.py:19
  11.0 7.0 %collective-permute-start.5 = (bf16[1,96,384]{2,1,0:T(8,128)(2,1)S(1)}, bf16[1,96,384]{2,1,0:T(8,128)(2,1)S(1)}, u32[]{:S(2)}, u32[]{:S(2)}) collective-permute-start(bf16[1,96,384]{2,1,0:T(8,128)(2,1)S(1)} %get-tuple-element.231), channel_id=1, source_target_pairs={{0,16},{4,20},{8,24},{12,28},{16,0},{20,4},{24,8},{28,12},{1,17},{... | collective-permute-start | bytes 221192 | tf_op jit(solution)/shard_map/ppermute | solution.py:19
  18.0 12.5 %collective-permute-start.9 = (bf16[2,96,384]{2,1,0:T(8,128)(2,1)S(1)}, bf16[2,96,384]{2,1,0:T(8,128)(2,1)S(1)}, u32[]{:S(2)}, u32[]{:S(2)}) collective-permute-start(bf16[2,96,384]{2,1,0:T(8,128)(2,1)S(1)} %pad_maximum_fusion.11), channel_id=1, source_target_pairs={{0,8},{4,12},{8,0},{12,4},{16,24},{20,28},{24,16},{28,20},{1,9},{5... | collective-permute-start | bytes 442376 | tf_op jit(solution)/shard_map/ppermute | solution.py:19
  19.4 13.3 %collective-permute-start.8 = (bf16[2,112,384]{2,1,0:T(8,128)(2,1)S(1)}, bf16[2,112,384]{2,1,0:T(8,128)(2,1)S(1)}, u32[]{:S(2)}, u32[]{:S(2)}) collective-permute-start(bf16[2,112,384]{2,1,0:T(8,128)(2,1)S(1)} %pad_maximum_fusion.10), channel_id=1, source_target_pairs={{0,8},{4,12},{8,0},{12,4},{16,24},{20,28},{24,16},{28,20},{1,9},{5... | collective-permute-start | bytes 516104 | tf_op jit(solution)/shard_map/ppermute | solution.py:19
  20.8 24.6 %collective-permute-start.6 = (bf16[1,48,1536]{2,1,0:T(8,128)(2,1)S(1)}, bf16[1,48,1536]{2,1,0:T(8,128)(2,1)S(1)}, u32[]{:S(2)}, u32[]{:S(2)}) collective-permute-start(bf16[1,48,1536]{2,1,0:T(8,128)(2,1)S(1)} %maximum_select_fusion), channel_id=1, source_target_pairs={{0,16},{4,20},{8,24},{12,28},{16,0},{20,4},{24,8},{28,12},{1,17},{... | collective-permute-start | bytes 442376 | tf_op jit(solution)/shard_map/ppermute | solution.py:19
  23.0 16.0 %collective-permute-start.7 = (bf16[1,192,384]{2,1,0:T(8,128)(2,1)S(1)}, bf16[1,192,384]{2,1,0:T(8,128)(2,1)S(1)}, u32[]{:S(2)}, u32[]{:S(2)}) collective-permute-start(bf16[1,192,384]{2,1,0:T(8,128)(2,1)S(1)} %maximum_select_fusion.1), channel_id=1, source_target_pairs={{0,16},{4,20},{8,24},{12,28},{16,0},{20,4},{24,8},{28,12},{1,17},{... | collective-permute-start | bytes 442376 | tf_op jit(solution)/shard_map/ppermute | solution.py:19
  30.6 6.8 %collective-permute-start.14 = (bf16[4,96,384]{2,1,0:T(8,128)(2,1)S(1)}, bf16[4,96,384]{2,1,0:T(8,128)(2,1)S(1)}, u32[]{:S(2)}, u32[]{:S(2)}) collective-permute-start(bf16[4,96,384]{2,1,0:T(8,128)(2,1)S(1)} %pad_maximum_fusion.8), channel_id=1, source_target_pairs={{0,4},{4,0},{8,12},{12,8},{16,20},{20,16},{24,28},{28,24},{1,5},{5... | collective-permute-start | bytes 884744 | tf_op jit(solution)/shard_map/ppermute | solution.py:19
  32.8 11.1 %collective-permute-start.12 = (bf16[4,112,384]{2,1,0:T(8,128)(2,1)S(1)}, bf16[4,112,384]{2,1,0:T(8,128)(2,1)S(1)}, u32[]{:S(2)}, u32[]{:S(2)}) collective-permute-start(bf16[4,112,384]{2,1,0:T(8,128)(2,1)S(1)} %pad_maximum_fusion.5), channel_id=1, source_target_pairs={{0,2},{1,3},{2,0},{3,1},{4,6},{5,7},{6,4},{7,5},{8,10},{9,11},{10,... | collective-permute-start | bytes 1032200 | tf_op jit(solution)/shard_map/ppermute | solution.py:19
  37.4 16.6 %collective-permute-start.15 = (bf16[8,96,384]{2,1,0:T(8,128)(2,1)S(1)}, bf16[8,96,384]{2,1,0:T(8,128)(2,1)S(1)}, u32[]{:S(2)}, u32[]{:S(2)}) collective-permute-start(bf16[8,96,384]{2,1,0:T(8,128)(2,1)S(1)} %pad_maximum_fusion.3), channel_id=1, source_target_pairs={{0,2},{1,3},{2,0},{3,1},{4,6},{5,7},{6,4},{7,5},{8,10},{9,11},{10,... | collective-permute-start | bytes 1769480 | tf_op jit(solution)/shard_map/ppermute | solution.py:19
  43.9 12.7 %collective-permute-start.13 = (bf16[8,112,384]{2,1,0:T(8,128)(2,1)S(1)}, bf16[8,112,384]{2,1,0:T(8,128)(2,1)S(1)}, u32[]{:S(2)}, u32[]{:S(2)}) collective-permute-start(bf16[8,112,384]{2,1,0:T(8,128)(2,1)S(1)} %pad_maximum_fusion), channel_id=1, source_target_pairs={{0,4},{4,0},{8,12},{12,8},{16,20},{20,16},{24,28},{28,24},{1,5},{5... | collective-permute-start | bytes 2064392 | tf_op jit(solution)/shard_map/ppermute | solution.py:19
  45.5 13.0 %collective-permute-start.10 = (bf16[2,48,1536]{2,1,0:T(8,128)(2,1)S(1)}, bf16[2,48,1536]{2,1,0:T(8,128)(2,1)S(1)}, u32[]{:S(2)}, u32[]{:S(2)}) collective-permute-start(bf16[2,48,1536]{2,1,0:T(8,128)(2,1)S(1)} %pad_maximum_fusion.6), channel_id=1, source_target_pairs={{0,8},{4,12},{8,0},{12,4},{16,24},{20,28},{24,16},{28,20},{1,9},{5... | collective-permute-start | bytes 884744 | tf_op jit(solution)/shard_map/ppermute | solution.py:19
  45.6 12.9 %collective-permute-start.11 = (bf16[2,192,384]{2,1,0:T(8,128)(2,1)S(1)}, bf16[2,192,384]{2,1,0:T(8,128)(2,1)S(1)}, u32[]{:S(2)}, u32[]{:S(2)}) collective-permute-start(bf16[2,192,384]{2,1,0:T(8,128)(2,1)S(1)} %pad_maximum_fusion.7), channel_id=1, source_target_pairs={{0,8},{4,12},{8,0},{12,4},{16,24},{20,28},{24,16},{28,20},{1,9},{5... | collective-permute-start | bytes 884744 | tf_op jit(solution)/shard_map/ppermute | solution.py:19
  55.0 8.7 %collective-permute-start.19 = (bf16[16,96,384]{2,1,0:T(8,128)(2,1)}, bf16[16,96,384]{2,1,0:T(8,128)(2,1)}, u32[]{:S(2)}, u32[]{:S(2)}) collective-permute-start(bf16[16,96,384]{2,1,0:T(8,128)(2,1)} %constant_dynamic-update-slice_fusion.5.refs_0_), channel_id=1, source_target_pairs={{0,1},{1,0},{2,3},{3,2},{4,5},{5,4},{6,7},{7,6},{8,9},{9,8},{10,11... | collective-permute-start | bytes 3538952 | tf_op jit(solution)/shard_map/ppermute | solution.py:19
  57.6 10.7 %collective-permute-start.18 = (bf16[16,112,384]{2,1,0:T(8,128)(2,1)}, bf16[16,112,384]{2,1,0:T(8,128)(2,1)}, u32[]{:S(2)}, u32[]{:S(2)}) collective-permute-start(bf16[16,112,384]{2,1,0:T(8,128)(2,1)} %constant_dynamic-update-slice_fusion.refs_0_), channel_id=1, source_target_pairs={{0,1},{1,0},{2,3},{3,2},{4,5},{5,4},{6,7},{7,6},{8,9},{9,8},{10,11... | collective-permute-start | bytes 4128776 | tf_op jit(solution)/shard_map/ppermute | solution.py:19
  58.6 33.5 %collective-permute-start.16 = (bf16[4,48,1536]{2,1,0:T(8,128)(2,1)S(1)}, bf16[4,48,1536]{2,1,0:T(8,128)(2,1)S(1)}, u32[]{:S(2)}, u32[]{:S(2)}) collective-permute-start(bf16[4,48,1536]{2,1,0:T(8,128)(2,1)S(1)} %pad_maximum_fusion.1), channel_id=1, source_target_pairs={{0,2},{1,3},{2,0},{3,1},{4,6},{5,7},{6,4},{7,5},{8,10},{9,11},{10,... | collective-permute-start | bytes 1769480 | tf_op jit(solution)/shard_map/ppermute | solution.py:19
  60.1 32.0 %collective-permute-start.17 = (bf16[4,192,384]{2,1,0:T(8,128)(2,1)S(1)}, bf16[4,192,384]{2,1,0:T(8,128)(2,1)S(1)}, u32[]{:S(2)}, u32[]{:S(2)}) collective-permute-start(bf16[4,192,384]{2,1,0:T(8,128)(2,1)S(1)} %pad_maximum_fusion.2), channel_id=1, source_target_pairs={{0,4},{4,0},{8,12},{12,8},{16,20},{20,16},{24,28},{28,24},{1,5},{5... | collective-permute-start | bytes 1769480 | tf_op jit(solution)/shard_map/ppermute | solution.py:19
  93.0 27.6 %collective-permute-start.21 = (bf16[8,192,384]{2,1,0:T(8,128)(2,1)S(1)}, bf16[8,192,384]{2,1,0:T(8,128)(2,1)S(1)}, u32[]{:S(2)}, u32[]{:S(2)}) collective-permute-start(bf16[8,192,384]{2,1,0:T(8,128)(2,1)S(1)} %get-tuple-element.257), channel_id=1, source_target_pairs={{0,2},{1,3},{2,0},{3,1},{4,6},{5,7},{6,4},{7,5},{8,10},{9,11},{10,... | collective-permute-start | bytes 3538952 | tf_op jit(solution)/shard_map/ppermute | solution.py:19
  94.5 27.3 %collective-permute-start.20 = (bf16[8,48,1536]{2,1,0:T(8,128)(2,1)S(1)}, bf16[8,48,1536]{2,1,0:T(8,128)(2,1)S(1)}, u32[]{:S(2)}, u32[]{:S(2)}) collective-permute-start(bf16[8,48,1536]{2,1,0:T(8,128)(2,1)S(1)} %get-tuple-element.261), channel_id=1, source_target_pairs={{0,4},{4,0},{8,12},{12,8},{16,20},{20,16},{24,28},{28,24},{1,5},{5... | collective-permute-start | bytes 3538952 | tf_op jit(solution)/shard_map/ppermute | solution.py:19
  122.9 6.6 %collective-permute-start.23 = (bf16[16,192,384]{2,1,0:T(8,128)(2,1)}, bf16[16,192,384]{2,1,0:T(8,128)(2,1)}, u32[]{:S(2)}, u32[]{:S(2)}) collective-permute-start(bf16[16,192,384]{2,1,0:T(8,128)(2,1)} %constant_dynamic-update-slice_fusion.17.refs_0_), channel_id=1, source_target_pairs={{0,1},{1,0},{2,3},{3,2},{4,5},{5,4},{6,7},{7,6},{8,9},{9,8},{10,11... | collective-permute-start | bytes 7077896 | tf_op jit(solution)/shard_map/ppermute | solution.py:19
  123.0 12.3 %collective-permute-start.22 = (bf16[16,48,1536]{2,1,0:T(8,128)(2,1)S(1)}, bf16[16,48,1536]{2,1,0:T(8,128)(2,1)}, u32[]{:S(2)}, u32[]{:S(2)}) collective-permute-start(bf16[16,48,1536]{2,1,0:T(8,128)(2,1)S(1)} %constant_dynamic-update-slice_fusion.14.refs_0_), channel_id=1, source_target_pairs={{0,1},{1,0},{2,3},{3,2},{4,5},{5,4},{6,7},{7,6},{8,9},{9,8},{10,11... | collective-permute-start | bytes 7077896 | tf_op jit(solution)/shard_map/ppermute | solution.py:19
  191.4 23.5 %collective-permute-start.24 = (bf16[16,192,384]{2,1,0:T(8,128)(2,1)}, bf16[16,192,384]{2,1,0:T(8,128)(2,1)}, u32[]{:S(2)}, u32[]{:S(2)}) collective-permute-start(bf16[16,192,384]{2,1,0:T(8,128)(2,1)} %get-tuple-element.143), channel_id=1, source_target_pairs={{0,1},{1,0},{2,3},{3,2},{4,5},{5,4},{6,7},{7,6},{8,9},{9,8},{10,11... | collective-permute-start | bytes 7077896 | tf_op jit(solution)/shard_map/ppermute | solution.py:19
  213.7 24.3 %collective-permute-start.25 = (bf16[16,48,1536]{2,1,0:T(8,128)(2,1)}, bf16[16,48,1536]{2,1,0:T(8,128)(2,1)S(1)}, u32[]{:S(2)}, u32[]{:S(2)}) collective-permute-start(bf16[16,48,1536]{2,1,0:T(8,128)(2,1)} %get-tuple-element.148), channel_id=1, source_target_pairs={{0,1},{1,0},{2,3},{3,2},{4,5},{5,4},{6,7},{7,6},{8,9},{9,8},{10,11... | collective-permute-start | bytes 7077896 | tf_op jit(solution)/shard_map/ppermute | solution.py:19
  218.9 52.3 %collective-permute-start.26 = (bf16[8,192,384]{2,1,0:T(8,128)(2,1)}, bf16[8,192,384]{2,1,0:T(8,128)(2,1)}, u32[]{:S(2)}, u32[]{:S(2)}) collective-permute-start(bf16[8,192,384]{2,1,0:T(8,128)(2,1)} %get-tuple-element.235), channel_id=1, source_target_pairs={{0,2},{1,3},{2,0},{3,1},{4,6},{5,7},{6,4},{7,5},{8,10},{9,11},{10,... | collective-permute-start | bytes 3538952 | tf_op jit(solution)/shard_map/ppermute | solution.py:19
  242.8 28.4 %collective-permute-start.27 = (bf16[8,48,1536]{2,1,0:T(8,128)(2,1)}, bf16[8,48,1536]{2,1,0:T(8,128)(2,1)S(1)}, u32[]{:S(2)}, u32[]{:S(2)}) collective-permute-start(bf16[8,48,1536]{2,1,0:T(8,128)(2,1)} %get-tuple-element.233), channel_id=1, source_target_pairs={{0,4},{4,0},{8,12},{12,8},{16,20},{20,16},{24,28},{28,24},{1,5},{5... | collective-permute-start | bytes 3538952 | tf_op jit(solution)/shard_map/ppermute | solution.py:19
  283.1 16.6 %collective-permute-start.28 = (bf16[16,112,384]{2,1,0:T(8,128)(2,1)}, bf16[16,112,384]{2,1,0:T(8,128)(2,1)S(1)}, u32[]{:S(2)}, u32[]{:S(2)}) collective-permute-start(bf16[16,112,384]{2,1,0:T(8,128)(2,1)} %get-tuple-element.176), channel_id=1, source_target_pairs={{0,1},{1,0},{2,3},{3,2},{4,5},{5,4},{6,7},{7,6},{8,9},{9,8},{10,11... | collective-permute-start | bytes 4128776 | tf_op jit(solution)/shard_map/ppermute | solution.py:19
  283.2 15.7 %collective-permute-start.30 = (bf16[4,48,1536]{2,1,0:T(8,128)(2,1)S(1)}, bf16[4,48,1536]{2,1,0:T(8,128)(2,1)S(1)}, u32[]{:S(2)}, u32[]{:S(2)}) collective-permute-start(bf16[4,48,1536]{2,1,0:T(8,128)(2,1)S(1)} %get-tuple-element.241), channel_id=1, source_target_pairs={{0,2},{1,3},{2,0},{3,1},{4,6},{5,7},{6,4},{7,5},{8,10},{9,11},{10,... | collective-permute-start | bytes 1769480 | tf_op jit(solution)/shard_map/ppermute | solution.py:19
  284.0 15.4 %collective-permute-start.29 = (bf16[4,192,384]{2,1,0:T(8,128)(2,1)S(1)}, bf16[4,192,384]{2,1,0:T(8,128)(2,1)S(1)}, u32[]{:S(2)}, u32[]{:S(2)}) collective-permute-start(bf16[4,192,384]{2,1,0:T(8,128)(2,1)S(1)} %get-tuple-element.243), channel_id=1, source_target_pairs={{0,4},{4,0},{8,12},{12,8},{16,20},{20,16},{24,28},{28,24},{1,5},{5... | collective-permute-start | bytes 1769480 | tf_op jit(solution)/shard_map/ppermute | solution.py:19
  285.4 14.3 %collective-permute-start.31 = (bf16[16,96,384]{2,1,0:T(8,128)(2,1)}, bf16[16,96,384]{2,1,0:T(8,128)(2,1)S(1)}, u32[]{:S(2)}, u32[]{:S(2)}) collective-permute-start(bf16[16,96,384]{2,1,0:T(8,128)(2,1)} %get-tuple-element.178), channel_id=1, source_target_pairs={{0,1},{1,0},{2,3},{3,2},{4,5},{5,4},{6,7},{7,6},{8,9},{9,8},{10,11... | collective-permute-start | bytes 3538952 | tf_op jit(solution)/shard_map/ppermute | solution.py:19
  301.1 16.7 %collective-permute-start.32 = (bf16[8,112,384]{2,1,0:T(8,128)(2,1)S(1)}, bf16[8,112,384]{2,1,0:T(8,128)(2,1)S(1)}, u32[]{:S(2)}, u32[]{:S(2)}) collective-permute-start(bf16[8,112,384]{2,1,0:T(8,128)(2,1)S(1)} %get-tuple-element.237), channel_id=1, source_target_pairs={{0,4},{4,0},{8,12},{12,8},{16,20},{20,16},{24,28},{28,24},{1,5},{5... | collective-permute-start | bytes 2064392 | tf_op jit(solution)/shard_map/ppermute | solution.py:19
  302.8 14.5 %collective-permute-start.33 = (bf16[8,96,384]{2,1,0:T(8,128)(2,1)S(1)}, bf16[8,96,384]{2,1,0:T(8,128)(2,1)S(1)}, u32[]{:S(2)}, u32[]{:S(2)}) collective-permute-start(bf16[8,96,384]{2,1,0:T(8,128)(2,1)S(1)} %get-tuple-element.239), channel_id=1, source_target_pairs={{0,2},{1,3},{2,0},{3,1},{4,6},{5,7},{6,4},{7,5},{8,10},{9,11},{10,... | collective-permute-start | bytes 1769480 | tf_op jit(solution)/shard_map/ppermute | solution.py:19
  304.4 11.5 %collective-permute-start.45 = (bf16[2,192,384]{2,1,0:T(8,128)(2,1)S(1)}, bf16[2,192,384]{2,1,0:T(8,128)(2,1)S(1)}, u32[]{:S(2)}, u32[]{:S(2)}) collective-permute-start(bf16[2,192,384]{2,1,0:T(8,128)(2,1)S(1)} %get-tuple-element.247), channel_id=1, source_target_pairs={{0,8},{4,12},{8,0},{12,4},{16,24},{20,28},{24,16},{28,20},{1,9},{5... | collective-permute-start | bytes 884744 | tf_op jit(solution)/shard_map/ppermute | solution.py:19
  304.4 16.8 %collective-permute-start.42 = (bf16[2,48,1536]{2,1,0:T(8,128)(2,1)S(1)}, bf16[2,48,1536]{2,1,0:T(8,128)(2,1)S(1)}, u32[]{:S(2)}, u32[]{:S(2)}) collective-permute-start(bf16[2,48,1536]{2,1,0:T(8,128)(2,1)S(1)} %get-tuple-element.249), channel_id=1, source_target_pairs={{0,8},{4,12},{8,0},{12,4},{16,24},{20,28},{24,16},{28,20},{1,9},{5... | collective-permute-start | bytes 884744 | tf_op jit(solution)/shard_map/ppermute | solution.py:19
  316.0 21.6 %collective-permute-start.46 = (bf16[1,192,384]{2,1,0:T(8,128)(2,1)S(1)}, bf16[1,192,384]{2,1,0:T(8,128)(2,1)S(1)}, u32[]{:S(2)}, u32[]{:S(2)}) collective-permute-start(bf16[1,192,384]{2,1,0:T(8,128)(2,1)S(1)} %add_convert_fusion.22), channel_id=1, source_target_pairs={{0,16},{4,20},{8,24},{12,28},{16,0},{20,4},{24,8},{28,12},{1,17},{... | collective-permute-start | bytes 442376 | tf_op jit(solution)/shard_map/ppermute | solution.py:19
  318.0 8.7 %collective-permute-start.34 = (bf16[4,112,384]{2,1,0:T(8,128)(2,1)S(1)}, bf16[4,112,384]{2,1,0:T(8,128)(2,1)S(1)}, u32[]{:S(2)}, u32[]{:S(2)}) collective-permute-start(bf16[4,112,384]{2,1,0:T(8,128)(2,1)S(1)} %get-tuple-element.244), channel_id=1, source_target_pairs={{0,2},{1,3},{2,0},{3,1},{4,6},{5,7},{6,4},{7,5},{8,10},{9,11},{10,... | collective-permute-start | bytes 1032200 | tf_op jit(solution)/shard_map/ppermute | solution.py:19
  319.5 7.1 %collective-permute-start.35 = (bf16[4,96,384]{2,1,0:T(8,128)(2,1)S(1)}, bf16[4,96,384]{2,1,0:T(8,128)(2,1)S(1)}, u32[]{:S(2)}, u32[]{:S(2)}) collective-permute-start(bf16[4,96,384]{2,1,0:T(8,128)(2,1)S(1)} %get-tuple-element.250), channel_id=1, source_target_pairs={{0,4},{4,0},{8,12},{12,8},{16,20},{20,16},{24,28},{28,24},{1,5},{5... | collective-permute-start | bytes 884744 | tf_op jit(solution)/shard_map/ppermute | solution.py:19
  321.3 16.3 %collective-permute-start.43 = (bf16[1,48,1536]{2,1,0:T(8,128)(2,1)S(1)}, bf16[1,48,1536]{2,1,0:T(8,128)(2,1)S(1)}, u32[]{:S(2)}, u32[]{:S(2)}) collective-permute-start(bf16[1,48,1536]{2,1,0:T(8,128)(2,1)S(1)} %add_convert_fusion.24), channel_id=1, source_target_pairs={{0,16},{4,20},{8,24},{12,28},{16,0},{20,4},{24,8},{28,12},{1,17},{... | collective-permute-start | bytes 442376 | tf_op jit(solution)/shard_map/ppermute | solution.py:19
  326.7 10.8 %collective-permute-start.36 = (bf16[2,112,384]{2,1,0:T(8,128)(2,1)S(1)}, bf16[2,112,384]{2,1,0:T(8,128)(2,1)S(1)}, u32[]{:S(2)}, u32[]{:S(2)}) collective-permute-start(bf16[2,112,384]{2,1,0:T(8,128)(2,1)S(1)} %get-tuple-element.252), channel_id=1, source_target_pairs={{0,8},{4,12},{8,0},{12,4},{16,24},{20,28},{24,16},{28,20},{1,9},{5... | collective-permute-start | bytes 516104 | tf_op jit(solution)/shard_map/ppermute | solution.py:19
  326.9 10.7 %collective-permute-start.37 = (bf16[2,96,384]{2,1,0:T(8,128)(2,1)S(1)}, bf16[2,96,384]{2,1,0:T(8,128)(2,1)S(1)}, u32[]{:S(2)}, u32[]{:S(2)}) collective-permute-start(bf16[2,96,384]{2,1,0:T(8,128)(2,1)S(1)} %get-tuple-element.254), channel_id=1, source_target_pairs={{0,8},{4,12},{8,0},{12,4},{16,24},{20,28},{24,16},{28,20},{1,9},{5... | collective-permute-start | bytes 442376 | tf_op jit(solution)/shard_map/ppermute | solution.py:19
  337.6 6.4 %collective-permute-start.40 = (bf16[1,96,384]{2,1,0:T(8,128)(2,1)S(1)}, bf16[1,96,384]{2,1,0:T(8,128)(2,1)S(1)}, u32[]{:S(2)}, u32[]{:S(2)}) collective-permute-start(bf16[1,96,384]{2,1,0:T(8,128)(2,1)S(1)} %add_convert_fusion.30), channel_id=1, source_target_pairs={{0,16},{4,20},{8,24},{12,28},{16,0},{20,4},{24,8},{28,12},{1,17},{... | collective-permute-start | bytes 221192 | tf_op jit(solution)/shard_map/ppermute | solution.py:19
  338.7 7.3 %collective-permute-start.38 = (bf16[1,112,384]{2,1,0:T(8,128)(2,1)S(1)}, bf16[1,112,384]{2,1,0:T(8,128)(2,1)S(1)}, u32[]{:S(2)}, u32[]{:S(2)}) collective-permute-start(bf16[1,112,384]{2,1,0:T(8,128)(2,1)S(1)} %add_convert_fusion.28), channel_id=1, source_target_pairs={{0,16},{4,20},{8,24},{12,28},{16,0},{20,4},{24,8},{28,12},{1,17},{... | collective-permute-start | bytes 258056 | tf_op jit(solution)/shard_map/ppermute | solution.py:19
  344.2 4.6 %collective-permute-start.41 = (bf16[96,192]{1,0:T(8,128)(2,1)S(1)}, bf16[96,192]{1,0:T(8,128)(2,1)S(1)}, u32[]{:S(2)}, u32[]{:S(2)}) collective-permute-start(bf16[96,192]{1,0:T(8,128)(2,1)S(1)} %select_convert_fusion.2), channel_id=1, source_target_pairs={{0,1},{1,0},{2,3},{3,2},{4,5},{5,4},{6,7},{7,6},{8,9},{9,8},{10,11... | collective-permute-start | bytes 110600 | tf_op jit(solution)/shard_map/ppermute | solution.py:19
  347.8 2.3 collective-permute-start.39
  347.9 4.7 %collective-permute-start.44 = (bf16[48,768]{1,0:T(8,128)(2,1)S(1)}, bf16[48,768]{1,0:T(8,128)(2,1)S(1)}, u32[]{:S(2)}, u32[]{:S(2)}) collective-permute-start(bf16[48,768]{1,0:T(8,128)(2,1)S(1)} %select_convert_fusion.1), channel_id=1, source_target_pairs={{0,1},{1,0},{2,3},{3,2},{4,5},{5,4},{6,7},{7,6},{8,9},{9,8},{10,11... | collective-permute-start | bytes 221192 | tf_op jit(solution)/shard_map/ppermute | solution.py:19
  348.7 3.0 collective-permute-start.47
  (13 other events, 131.7 us)

commit v4 on v3

v4 whole, which is shorter than its diff:
```python
import functools
import jax
import jax.numpy as jnp
from jax import lax
from jax.experimental import pallas as pl
from jax.experimental.pallas import tpu as pltpu
from jax.sharding import PartitionSpec as P

HEADS = 12


EPSILON = 1e-12
MASKED = -1000000000.0
SMALL_ROWS = 16


def swap(value, axis, bit):
    size = lax.axis_size(axis)
    return lax.ppermute(value, axis, [(i, i ^ (1 << bit)) for i in range(size)])


def stage_orders(mesh):
    dp_bits = mesh.shape["dp"].bit_length() - 1
    fsdp_bits = mesh.shape["fsdp"].bit_length() - 1
    far = [("dp", b) for b in range(dp_bits - 1, 0, -1)]
    across = [("fsdp", b) for b in range(fsdp_bits - 1, 0, -1)]
    near = [("dp", 0)]
    return (far + across + near, far + near + across, across + near + far)


def fits(mesh, rows, width, hidden):
    sizes = (mesh.shape["dp"], mesh.shape["fsdp"])
    powers = all(s >= 2 and s & (s - 1) == 0 for s in sizes)
    return powers and all(r % 32 == 0 for r in rows) and width % 64 == 0 and hidden % 128 == 0 and 32 < rows[0] <= 128


def place_of(stages, dp, fsdp, me_ref):
    index = {"dp": dp ^ me_ref[0], "fsdp": fsdp ^ me_ref[1]}
    place = 0
    for s, (axis, bit) in enumerate(stages):
        place = place + (((index[axis] >> bit) & 1) << s)
    return place


def piece_copies(source, outs, sems, me_ref, stages, first_dp, count_dp, half, span, columns):
    copies = []
    offset, rows, at = span
    for i in range(count_dp):
        dp = first_dp + i
        for flip in range(2):
            fsdp = (me_ref[1] & 1) ^ flip
            row = pl.multiple_of((2 * i + fsdp) * half + offset, 16)
            for start, pair, into, count in columns:
                place = place_of(stages, dp, 2 * pair + fsdp, me_ref)
                copies.append(
                    pltpu.make_async_copy(
                        source.at[pl.ds(row, rows), pl.ds(start, count)],
                        outs[flip].at[place, pl.ds(at, rows), pl.ds(into, count)],
                        sems.at[len(copies)],
                    )
                )
    return copies


class Source:
    def __init__(self, operands, stages=(), spots=(), dp_size=0, small_at=None):
        self.operands, self.stages, self.spots = tuple(operands), stages, spots
        self.dp_size, self.small_at = dp_size, small_at

    def count(self, shape):
        if not self.spots:
            return 1
        return 2 * self.dp_size * max(shape[1] // width * len(spans) for _, width, spans in self.spots)

    def copies(self, which, refs, target, sems, me_ref):
        if not self.spots:
            return [pltpu.make_async_copy(refs[which], target, sems.at[0])]
        half, width, spans = self.spots[which]
        copies = []
        for part, at, offset, rows, column in spans:
            count = self.operands[2 * part].shape[2]
            for dp in range(self.dp_size):
                for flip in range(2):
                    fsdp = (me_ref[1] & 1) ^ flip
                    row = pl.multiple_of((2 * dp + fsdp) * half + offset, 16)
                    for pair in range(target.shape[1] // width):
                        place = place_of(self.stages[part], dp, 2 * pair + fsdp, me_ref)
                        copies.append(
                            pltpu.make_async_copy(
                                refs[2 * part + flip].at[place, pl.ds(at, rows), :],
                                target.at[pl.ds(row, rows), pl.ds(pair * width + column, count)],
                                sems.at[len(copies)],
                            )
                        )
        return copies

    def small_copies(self, refs, target, sems, me_ref):
        copies = []
        for dp in range(self.dp_size):
            place = place_of(self.stages[0], dp, me_ref[1], me_ref)
            source = refs[0].at[place, pl.ds(self.small_at, SMALL_ROWS), :]
            copies.append(pltpu.make_async_copy(source, target.at[dp], sems.at[dp]))
        return copies

    def pick(self, which):
        if not self.spots:
            return Source([self.operands[i] for i in which])
        return Source(self.operands, self.stages, [self.spots[i] for i in which], self.dp_size)


def lay_vectors(small, columns, hidden_count, vec_ref, hb_ref):
    lanes = min(128, small.shape[2])
    width = vec_ref.shape[1]
    parts = small.shape[0]

    def chosen(to, start):
        row = lax.broadcasted_iota(jnp.int32, (lanes, to), 0)
        column = lax.broadcasted_iota(jnp.int32, (lanes, to), 1)
        return ((column - start == row) & (row < columns)).astype(jnp.float32).astype(jnp.bfloat16)

    total = jnp.zeros((SMALL_ROWS, width), jnp.float32)
    for dp in range(parts):
        total = total + dot(small[dp, :, :lanes], chosen(width, dp * columns))
    share = hidden_count // parts
    rows = share // columns
    vec_ref[0:4, :] = total[0:4]
    vec_ref[4:8, :] = total[4 + rows : 8 + rows]
    flat = small[:, :, :lanes].reshape(parts * SMALL_ROWS, lanes)
    spread = [dot(flat, chosen(share, k * columns)) for k in range(rows)]
    for dp in range(parts):
        at = dp * SMALL_ROWS + 4
        hb_ref[:, dp * share : (dp + 1) * share] = sum(
            spread[k][at + k : at + k + 1] for k in range(rows)
        )


def small_copies(source, outs, sems, me_ref, stages, at, dp_size, pairs):
    copies = []
    for dp in range(dp_size):
        for flip in range(2):
            fsdp = (me_ref[1] & 1) ^ flip
            for pair in range(pairs):
                place = place_of(stages, dp, 2 * pair + fsdp, me_ref)
                copies.append(
                    pltpu.make_async_copy(
                        source.at[dp],
                        outs[flip].at[place, pl.ds(at, SMALL_ROWS), :],
                        sems.at[len(copies)],
                    )
                )
    return copies


def run_all(copies):
    for copy in copies:
        copy.start()
    return copies


def wait_all(copies):
    for copy in copies:
        copy.wait()


def total_of(left, right, kind):
    return (left.astype(jnp.float32) + right.astype(jnp.float32)).astype(kind)


def settle(total, rows):
    width = total.shape[-1] // 2
    count = sum(rows)
    second = lax.axis_index("fsdp") & 1
    own = jnp.where(second == 0, total[:count, :width], total[:count, width:])
    away = jnp.where(second == 0, total[:count, width:], total[:count, :width])
    came = swap(away.astype(jnp.bfloat16), "fsdp", 0).astype(jnp.float32)
    first, last = jnp.where(second == 0, own, came), jnp.where(second == 0, came, own)
    outs, at = [], 0
    for half in rows:
        outs.append(jnp.concatenate([first[at : at + half], last[at : at + half]], axis=0))
        at += half
    return outs


def pair_up(shards):
    second = lax.axis_index("fsdp") & 1
    outs = []
    for shard in shards:
        half = shard.shape[0] // 2
        mine = jnp.where(second == 0, shard[:half], shard[half:])
        away = jnp.where(second == 0, shard[half:], shard[:half])
        came = swap(away, "fsdp", 0)
        outs.append(
            jnp.where(
                second == 0,
                jnp.concatenate([mine, came], axis=1),
                jnp.concatenate([came, mine], axis=1),
            )
        )
    return outs


VMEM_BYTES = 56 << 20
FEED_BYTES = 60 << 20


def estimate(micros):
    return pl.CostEstimate(flops=micros * 1000000000, bytes_accessed=micros * 1000000, transcendentals=0)


def dot(left, right):
    return jnp.dot(left, right, preferred_element_type=jnp.float32)


def dot_last(left, right):
    return lax.dot_general(
        left, right, (((1,), (1,)), ((), ())), preferred_element_type=jnp.float32
    )


def dot_first(left, right):
    return lax.dot_general(
        left, right, (((0,), (0,)), ((), ())), preferred_element_type=jnp.float32
    )


def normalize(values):
    centered = values - jnp.mean(values, axis=-1, keepdims=True)
    variance = jnp.mean(centered * centered, axis=-1, keepdims=True)
    factor = lax.rsqrt(variance + EPSILON)
    return (centered * factor, factor)


def norm_back(upward, normed, factor):
    return factor * (
        upward
        - jnp.mean(upward, axis=-1, keepdims=True)
        - normed * jnp.mean(upward * normed, axis=-1, keepdims=True)
    )


def gelu_pair(v):
    size = jnp.abs(v) * 0.7071067811865476
    t = 1.0 / (1.0 + 0.3275911 * size)
    bell = jnp.exp(-size * size)
    poly = t * (
        0.254829592
        + t * (-0.284496736 + t * (1.421413741 + t * (-1.453152027 + t * 1.061405429)))
    )
    tail = 0.5 * poly * bell
    cdf = jnp.where(v >= 0.0, 1.0 - tail, tail)
    return v * cdf, cdf + v * bell * 0.3989422804014327


def three_parts(value):
    high = value.astype(jnp.bfloat16).astype(jnp.float32)
    rest = value - high
    middle = rest.astype(jnp.bfloat16).astype(jnp.float32)
    return high, middle, rest - middle


def head_keys(pair, head, length, with_stats):
    rows, lanes = pair.shape
    lane = lax.broadcasted_iota(jnp.int32, (rows, lanes), 1)
    row = lax.broadcasted_iota(jnp.int32, (rows, lanes), 0)
    start = lanes // 2 if head == 0 else 0
    own = lane < lanes // 2 if head == 0 else lane >= lanes // 2
    hidden = jnp.where((lane == start) & (row >= length), MASKED, 0.0)
    if with_stats:
        hidden = jnp.where((lane > start) & (lane < start + 4), 1.0, hidden)
    return jnp.where(own, pair.astype(jnp.float32), hidden).astype(jnp.bfloat16)


def head_values(pair, head):
    rows, lanes = pair.shape
    lane = lax.broadcasted_iota(jnp.int32, (rows, lanes), 1)
    start = lanes // 2 if head == 0 else 0
    own = lane < lanes // 2 if head == 0 else lane >= lanes // 2
    ones = jnp.where((lane >= start) & (lane < start + 3), 1.0, 0.0)
    return jnp.where(own, pair.astype(jnp.float32), ones).astype(jnp.bfloat16)


def only_head(pair, head):
    lane = lax.broadcasted_iota(jnp.int32, pair.shape, 1)
    own = lane < pair.shape[1] // 2 if head == 0 else lane >= pair.shape[1] // 2
    return jnp.where(own, pair.astype(jnp.float32), 0.0).astype(jnp.bfloat16)


def with_rows(part, head, rows):
    count, width = part.shape
    row = lax.broadcasted_iota(jnp.int32, (count, width), 0)
    extra = jnp.zeros((count, width), jnp.float32)
    for i, value in enumerate(rows):
        extra = jnp.where(row == i, value, extra)
    extra = extra.astype(jnp.bfloat16)
    return jnp.concatenate([part, extra] if head == 0 else [extra, part], axis=0)


def forward_kernel(seq, source, columns, count_in, lengths, me_ref, x_ref, *refs):
    inputs, refs = refs[:count_in], refs[count_in:]
    q_ref, k_ref, v_ref, att_ref, lse_ref, vec_ref, hb_ref = refs[:7]
    qt, vt, ot, weights, sems, small, small_sems = refs[7:]
    length = lengths[seq]
    started = []
    for which in range(3):
        started.append(
            run_all(source.copies(which, inputs, weights.at[which], sems.at[which], me_ref))
        )
    wq_ref, wk_ref, wv_ref = (weights.at[i] for i in range(3))
    if source.spots:
        wait_all(run_all(source.small_copies(inputs, small, small_sems, me_ref)))
        lay_vectors(small[...], columns, hb_ref.shape[1], vec_ref, hb_ref)
    else:
        vec_ref[...] = inputs[-2][...]
        hb_ref[...] = inputs[-1][...]
    for copies in started:
        wait_all(copies)
    x = x_ref[...]
    head_size = x.shape[1] // HEADS
    scale = head_size**-0.5
    queries = (dot(x, wq_ref[...]) + vec_ref[0:1, :]).astype(jnp.bfloat16)
    queries = (queries.astype(jnp.float32) * scale).astype(jnp.bfloat16)
    q_ref[...] = queries
    qt[...] = queries.T
    k_ref[...] = dot(x, wk_ref[...]).astype(jnp.bfloat16)
    values = (dot(x, wv_ref[...]) + vec_ref[1:2, :]).astype(jnp.bfloat16)
    v_ref[...] = values
    vt[...] = values.T

    def one_pair(p, carry):
        base = pl.multiple_of(p * 2 * head_size, 2 * head_size)
        pair = k_ref[:, pl.ds(base, 2 * head_size)]
        for head in range(2):
            at = pl.multiple_of(base + head * head_size, head_size)
            keys = head_keys(pair, head, length, False)
            scores = dot(keys, with_rows(qt[pl.ds(at, head_size), :], head, [1.0]))
            highest = jnp.max(scores, axis=0, keepdims=True)
            exponent = jnp.exp(scores - highest)
            total = jnp.sum(exponent, axis=0, keepdims=True)
            blended = dot(vt[pl.ds(at, head_size), :], exponent.astype(jnp.bfloat16))
            ot[pl.ds(at, head_size), :] = (blended / total).astype(jnp.bfloat16)
            lse_ref[p, head : head + 1, :] = highest + jnp.log(total)
        return carry

    lax.fori_loop(0, HEADS // 2, one_pair, 0)
    att_ref[...] = ot[...].T


def whole(shape):
    return pl.BlockSpec(shape, lambda *_: (0,) * len(shape))


def skip_refs(kernel, first, count, *refs):
    kernel(*refs[:first], *refs[first + count :])


def attend_forward(seq, me, x, lengths, source, vectors, columns, hidden_count, before):
    seqs, slots, width = x.shape
    rows = pl.BlockSpec((None, slots, width), lambda i, *_: (seq, 0, 0))
    low = jax.ShapeDtypeStruct(x.shape, jnp.bfloat16)
    given = (*source.operands, *vectors)
    kernel = functools.partial(forward_kernel, seq, source, columns, len(given))
    known = 3 + len(given)
    small = (max(source.dp_size, 1), SMALL_ROWS, source.spots[0][1] if source.spots else 128)
    return pl.pallas_call(
        functools.partial(skip_refs, kernel, known, len(before)),
        grid_spec=pltpu.PrefetchScalarGridSpec(
            num_scalar_prefetch=2,
            grid=(1,),
            in_specs=[rows]
            + [ANYWHERE] * len(source.operands)
            + [whole(v.shape) for v in vectors]
            + [ANYWHERE] * len(before),
            out_specs=[rows] * 4
            + [
                pl.BlockSpec((None, HEADS // 2, 2, slots), lambda i, *_: (seq, 0, 0, 0)),
                whole((8, width)),
                whole((1, hidden_count)),
            ],
            scratch_shapes=[pltpu.VMEM((width, slots), jnp.bfloat16)] * 3
            + [
                pltpu.VMEM((3, width, width), jnp.bfloat16),
                pltpu.SemaphoreType.DMA((3, source.count((width, width)))),
                pltpu.VMEM(small, jnp.bfloat16),
                pltpu.SemaphoreType.DMA((small[0],)),
            ],
        ),
        out_shape=[low] * 4
        + [
            jax.ShapeDtypeStruct((seqs, HEADS // 2, 2, slots), jnp.float32),
            jax.ShapeDtypeStruct((8, width), jnp.float32),
            jax.ShapeDtypeStruct((1, hidden_count), jnp.float32),
        ],
        input_output_aliases={known + i: i for i in range(len(before))},
        compiler_params=pltpu.CompilerParams(vmem_limit_bytes=VMEM_BYTES),
        cost_estimate=estimate(14),
        name="attend_forward",
    )(lengths, me, x, *given, *before)


def feed_kernel(
    source, cuts, slots, lengths, me_ref, x_ref, att_ref, cot_ref, hb_ref, vec_ref, *refs
):
    count_in = len(source.operands)
    inputs, refs = refs[:count_in], refs[count_in:]
    out_ref, gf_ref, do_ref, hsum_ref, sums_ref = refs[:5]
    (
        wi, wf, wo, act, slope_s, first, mid, mid_t, low_s, held_i, held_o, held_a,
        load_a, load_i, load_o, sems, sems_a,
    ) = refs[-17:]
    grads = refs[5:-17]
    loads = [
        run_all(source.copies(which, inputs, target, sem, me_ref))
        for which, target, sem in ((0, wo, load_a), (1, wi, load_i), (2, wf, load_o))
    ]
    total, width = x_ref.shape
    inner = wi.shape[1]
    tile = min(256, slots)
    piece = min(1024, inner)
    sums_ref[...] = jnp.zeros_like(sums_ref)
    wait_all(loads[0])
    first[...] = x_ref[...].astype(jnp.float32) + dot(att_ref[...], wo[...]) + vec_ref[2:3, :]
    for copies in loads[1:]:
        wait_all(copies)

    def forward(t, carry):
        rows = pl.ds(pl.multiple_of(t * tile, tile), tile)
        normed, _ = normalize(first[rows, :])
        middle = normed * vec_ref[4:5, :] + vec_ref[6:7, :]
        middle_low = middle.astype(jnp.bfloat16)
        mid[rows, :] = middle_low
        second = middle + vec_ref[3:4, :]
        for at in range(0, inner, piece):
            here = slice(at, at + piece)
            hidden = dot(middle_low, wi[:, here]) + hb_ref[:, here]
            active, slope = gelu_pair(hidden)
            active = active.astype(jnp.bfloat16)
            act[rows, here] = active
            slope_s[rows, here] = slope.astype(jnp.bfloat16)
            second = second + dot(active, wf[here, :])
        normed, factor = normalize(second)
        start = t * tile
        slot = start % slots + lax.broadcasted_iota(jnp.int32, (tile, 1), 0)
        mask = (slot < lengths[start // slots]).astype(jnp.float32)
        out_ref[rows, :] = ((normed * vec_ref[5:6, :] + vec_ref[7:8, :]) * mask).astype(jnp.bfloat16)
        upward = cot_ref[rows, :].astype(jnp.float32) * mask
        grad = norm_back(upward * vec_ref[5:6, :], normed, factor)
        gf_ref[rows, :] = grad
        low = grad.astype(jnp.bfloat16)
        low_s[rows, :] = low
        sums_ref[0:1, :] += jnp.sum(upward * normed, axis=0, keepdims=True)
        sums_ref[1:2, :] += jnp.sum(upward, axis=0, keepdims=True)
        sums_ref[2:3, :] += jnp.sum(low.astype(jnp.float32), axis=0, keepdims=True)
        return carry

    lax.fori_loop(0, total // tile, forward, 0)
    mid_t[...] = mid[...].T
    chunk = held_i.shape[2]
    steps = inner // chunk

    def copies(step):
        slot = step % 2
        if cuts is None:
            start = pl.multiple_of(step * chunk, chunk)
            return [
                pltpu.make_async_copy(
                    held_o.at[slot], grads[2].at[pl.ds(start, chunk), :], sems.at[slot, 0]
                ),
                pltpu.make_async_copy(
                    held_i.at[slot], grads[1].at[:, pl.ds(start, chunk)], sems.at[slot, 1]
                ),
            ]
        made, split = [], cuts.split
        blocks = chunk // (2 * split.half_outer)
        for cut, outs, span, columns in cuts.outer(grads, width):
            made += piece_copies(
                held_o.at[slot], outs, sems.at[slot, pl.ds(len(made), 2 * blocks * len(columns))],
                me_ref, cut.stages, step * blocks, blocks, split.half_outer, span, columns,
            )
        for cut, outs, span, columns in cuts.inner(grads, step, chunk):
            made += piece_copies(
                held_i.at[slot], outs, sems.at[slot, pl.ds(len(made), width // split.half)],
                me_ref, cut.stages, 0, width // (2 * split.half), split.half, span, columns,
            )
        return made

    def backward(step, carry):
        here = pl.ds(pl.multiple_of(step * chunk, chunk), chunk)
        low = low_s[...]
        up = dot_last(low, wf[here, :]) * slope_s[:, here].astype(jnp.float32)
        hidden = up.astype(jnp.bfloat16)
        hsum_ref[:, here] = jnp.sum(hidden.astype(jnp.float32), axis=0, keepdims=True)

        @pl.when(step >= 2)
        def _():
            wait_all(copies(step - 2))

        held_o[step % 2] = dot_first(act[:, here], low).astype(jnp.bfloat16)
        held_i[step % 2] = dot(mid_t[...], hidden).astype(jnp.bfloat16)
        run_all(copies(step))
        gf_ref[...] += dot_last(hidden, wi[:, here])
        return carry

    lax.fori_loop(0, steps, backward, 0, unroll=2)

    def finish(t, carry):
        rows = pl.ds(pl.multiple_of(t * tile, tile), tile)
        grad_middle = gf_ref[rows, :]
        normed, factor = normalize(first[rows, :])
        sums_ref[3:4, :] += jnp.sum(grad_middle * normed, axis=0, keepdims=True)
        sums_ref[4:5, :] += jnp.sum(grad_middle, axis=0, keepdims=True)
        grad_first = norm_back(grad_middle * vec_ref[4:5, :], normed, factor)
        gf_ref[rows, :] = grad_first
        branch = grad_first.astype(jnp.bfloat16)
        low_s[rows, :] = branch
        sums_ref[5:6, :] += jnp.sum(branch.astype(jnp.float32), axis=0, keepdims=True)
        do_ref[rows, :] = dot_last(branch, wo[...]).astype(jnp.bfloat16)
        return carry

    lax.fori_loop(0, total // tile, finish, 0)
    held_a[...] = dot_first(att_ref[...], low_s[...]).astype(jnp.bfloat16)
    if cuts is None:
        last = [pltpu.make_async_copy(held_a, grads[0], sems_a.at[0])]
    else:
        cut, outs, span, columns = cuts.output(grads, width)
        half = cuts.split.half
        last = piece_copies(
            held_a, outs, sems_a, me_ref, cut.stages, 0, width // (2 * half), half, span, columns
        )
    run_all(last)
    for step in range(max(0, steps - 2), steps):
        wait_all(copies(step))
    wait_all(last)


class Cut:
    def __init__(self, stages, rows, width):
        self.stages, self.rows, self.width = tuple(stages), rows, width
        self.places = 1 << len(stages)

    def shapes(self):
        return [jax.ShapeDtypeStruct((self.places, self.rows, self.width), jnp.bfloat16)] * 2


class FeedSplit:
    def __init__(self, half, half_outer, width, width_inner):
        self.half, self.half_outer, self.width, self.width_inner = half, half_outer, width, width_inner
        self.groups = width_inner // width
        self.extra = 0
        self.most = max(16, half_outer // 6 * 5 // 16 * 16)
        self.rest = half_outer - self.most
        self.folded = half + self.rest

    def spots(self):
        kept = self.half - self.extra
        folds = [
            (2, self.folded + g * self.extra, kept, self.extra, g * self.width)
            for g in range(self.groups if self.extra else 0)
        ]
        return [
            (self.half, self.width, [(2, 0, 0, self.half, 0)]),
            (self.half, self.width_inner, [(0, 0, 0, kept, 0)] + folds),
            (
                self.half_outer,
                self.width,
                [(1, 0, 0, self.most, 0), (2, self.half, self.most, self.rest, 0)],
            ),
        ]


class FeedCuts:
    def __init__(self, orders, split):
        self.split = split
        rows = (split.half - split.extra, split.most, split.folded + split.groups * split.extra)
        widths = (split.width_inner, split.width, split.width)
        self.cuts = [Cut(*sizes) for sizes in zip(orders, rows, widths)]

    def shapes(self):
        return [shape for cut in self.cuts for shape in cut.shapes()]

    def inner(self, grads, step, chunk):
        split = self.split
        kept = split.half - split.extra
        parts = split.width_inner // chunk
        into = pl.multiple_of(step % parts * chunk, 128)
        listed = [(self.cuts[0], grads[0:2], (0, kept, 0), [(0, step // parts, into, chunk)])]
        for g in range(chunk // split.width if split.extra else 0):
            group = step % parts * (chunk // split.width) + g
            at = pl.multiple_of(split.folded + group * split.extra, 16)
            columns = [(g * split.width, step // parts, 0, split.width)]
            listed.append((self.cuts[2], grads[4:6], (kept, split.extra, at), columns))
        return listed

    def outer(self, grads, width):
        split = self.split
        columns = [(p * split.width, p, 0, split.width) for p in range(width // split.width)]
        listed = [(self.cuts[1], grads[2:4], (0, split.most, 0), columns)]
        if split.rest:
            listed.append((self.cuts[2], grads[4:6], (split.most, split.rest, split.half), columns))
        return listed

    def output(self, grads, width):
        split = self.split
        columns = [(p * split.width, p, 0, split.width) for p in range(width // split.width)]
        return self.cuts[2], grads[4:6], (0, split.half, 0), columns


ANYWHERE = pl.BlockSpec(memory_space=pl.ANY)
SCALARS = pl.BlockSpec(memory_space=pltpu.SMEM)
HERE = pl.BlockSpec(memory_space=pltpu.VMEM)


def feed(me, lengths, x, att, cotangent, hidden_bias, vectors, source, cuts):
    seqs, slots, width = x.shape
    inner = hidden_bias.shape[1]
    total = seqs * slots
    chunk = min(768, inner)
    low = jnp.bfloat16
    if cuts is None:
        shapes = ((width, width), (width, inner), (inner, width))
        grads = [jax.ShapeDtypeStruct(shape, low) for shape in shapes]
        copies, copies_last = 2, 1
    else:
        grads = cuts.shapes()
        split = cuts.split
        pairs = width // split.width
        copies = 2 * (chunk // split.half_outer) * pairs
        copies += width // split.half * (1 + chunk // split.width)
        copies_last = width // split.half * pairs
    return pl.pallas_call(
        functools.partial(feed_kernel, source, cuts, slots),
        in_specs=[SCALARS, SCALARS] + [HERE] * 5 + [ANYWHERE] * len(source.operands),
        out_specs=[HERE] * 5 + [ANYWHERE] * len(grads),
        out_shape=[
            jax.ShapeDtypeStruct((total, width), low),
            jax.ShapeDtypeStruct((total, width), jnp.float32),
            jax.ShapeDtypeStruct((total, width), low),
            jax.ShapeDtypeStruct((1, inner), jnp.float32),
            jax.ShapeDtypeStruct((8, width), jnp.float32),
            *grads,
        ],
        scratch_shapes=[
            pltpu.VMEM((width, inner), low),
            pltpu.VMEM((inner, width), low),
            pltpu.VMEM((width, width), low),
            pltpu.VMEM((total, inner), low),
            pltpu.VMEM((total, inner), low),
            pltpu.VMEM((total, width), jnp.float32),
            pltpu.VMEM((total, width), low),
            pltpu.VMEM((width, total), low),
            pltpu.VMEM((total, width), low),
            pltpu.VMEM((2, width, chunk), low),
            pltpu.VMEM((2, chunk, width), low),
            pltpu.VMEM((width, width), low),
            pltpu.SemaphoreType.DMA((source.pick([0]).count((width, width)),)),
            pltpu.SemaphoreType.DMA((source.pick([1]).count((width, inner)),)),
            pltpu.SemaphoreType.DMA((source.pick([2]).count((inner, width)),)),
            pltpu.SemaphoreType.DMA((2, copies)),
            pltpu.SemaphoreType.DMA((copies_last,)),
        ],
        compiler_params=pltpu.CompilerParams(vmem_limit_bytes=FEED_BYTES),
        cost_estimate=estimate(60),
        name="feed",
    )(
        lengths, me, x.reshape(total, width), att.reshape(total, width),
        cotangent.reshape(total, width), hidden_bias, vectors, *source.operands,
    )


def backward_kernel(
    seq, head_size, lengths, do_ref, q_ref, k_ref, v_ref, att_ref, lse_ref, *rest
):
    dq_ref, dk_ref, dv_ref, qt, kt, at_t, do_t, dq_t = rest
    length = lengths[seq]
    width = q_ref.shape[1]
    scale = head_size**-0.5
    at_t[...] = att_ref[...].T
    do_t[...] = do_ref[...].T
    qt[...] = q_ref[...].T
    kt[...] = k_ref[...].T

    def one_pair(p, carry):
        base = pl.multiple_of(p * 2 * head_size, 2 * head_size)
        here = pl.ds(base, 2 * head_size)
        key_pair, value_pair = k_ref[:, here], v_ref[:, here]
        query_pair, up_pair = q_ref[:, here], do_ref[:, here]
        grad_keys = grad_values = None
        for head in range(2):
            at = pl.multiple_of(base + head * head_size, head_size)
            mine = pl.ds(at, head_size)
            logs = [-part for part in three_parts(lse_ref[p, head : head + 1, :])]
            keys = head_keys(key_pair, head, length, True)
            soft = jnp.exp(dot(keys, with_rows(qt[mine, :], head, [1.0] + logs)))
            up = do_t[mine, :]
            delta = jnp.sum(
                up.astype(jnp.float32) * at_t[mine, :].astype(jnp.float32), axis=0, keepdims=True
            )
            deltas = [-part for part in three_parts(delta)]
            grad_soft = dot(head_values(value_pair, head), with_rows(up, head, deltas))
            scores = (soft * grad_soft).astype(jnp.bfloat16)
            from_values = dot(soft.astype(jnp.bfloat16), only_head(up_pair, head))
            from_keys = dot(scores, only_head(query_pair, head))
            grad_values = from_values if head == 0 else grad_values + from_values
            grad_keys = from_keys if head == 0 else grad_keys + from_keys
            dq_t[mine, :] = (dot(kt[mine, :], scores) * scale).astype(jnp.bfloat16)
        dk_ref[:, here] = grad_keys.astype(jnp.bfloat16)
        dv_ref[:, here] = grad_values.astype(jnp.bfloat16)
        return carry

    lax.fori_loop(0, width // (2 * head_size), one_pair, 0)
    dq_ref[...] = dq_t[...].T


def attend_backward(seq, part, parts, do, q, k, v, att, lse, lengths, before):
    seqs, slots, width = q.shape
    count = width // parts
    pairs = HEADS // 2 // parts
    rows = pl.BlockSpec((None, slots, count), lambda i, *_: (seq, 0, part))
    low = jax.ShapeDtypeStruct(q.shape, jnp.bfloat16)
    inputs = (lengths, do, q, k, v, att, lse)
    kernel = functools.partial(backward_kernel, seq, width // HEADS)
    return pl.pallas_call(
        functools.partial(skip_refs, kernel, len(inputs), len(before)),
        grid_spec=pltpu.PrefetchScalarGridSpec(
            num_scalar_prefetch=1,
            grid=(1,),
            in_specs=[rows] * 5
            + [pl.BlockSpec((None, pairs, 2, slots), lambda i, *_: (seq, part, 0, 0))]
            + [ANYWHERE] * len(before),
            out_specs=[rows] * 3,
            scratch_shapes=[pltpu.VMEM((count, slots), jnp.bfloat16)] * 5,
        ),
        out_shape=[low, low, low],
        input_output_aliases={len(inputs) + i: i for i in range(len(before))},
        compiler_params=pltpu.CompilerParams(vmem_limit_bytes=VMEM_BYTES),
        cost_estimate=estimate(14 // parts),
        name="attend_backward",
    )(*inputs, *before)


def pack_gradients(sums_feed, sums_in, hsum, small, columns):
    parts, _, lanes = small.shape
    lanes = min(128, lanes)
    width, share = sums_feed.shape[1], hsum.shape[1] // parts
    rows = share // columns

    def chosen(count, start):
        row = lax.broadcasted_iota(jnp.int32, (count, lanes), 0)
        column = lax.broadcasted_iota(jnp.int32, (count, lanes), 1)
        return ((row - start == column) & (column < columns)).astype(jnp.float32).astype(jnp.bfloat16)

    small[...] = jnp.zeros_like(small)
    listed = (
        [*sums_in, sums_feed[5:6], sums_feed[2:3]]
        + [jnp.zeros((rows, width), jnp.float32)]
        + [sums_feed[3:4], sums_feed[0:1], sums_feed[4:5], sums_feed[1:2]]
    )
    pad = SMALL_ROWS - 8 - rows
    lined = jnp.concatenate(listed + [jnp.zeros((pad, width), jnp.float32)], axis=0)
    lined = lined.astype(jnp.bfloat16)
    hidden = [hsum[:, dp * share : (dp + 1) * share] for dp in range(parts)]
    hidden = jnp.concatenate(hidden, axis=0).astype(jnp.bfloat16)
    spread = [dot(hidden, chosen(share, k * columns)) for k in range(rows)]
    for dp in range(parts):
        here = dot(lined, chosen(width, dp * columns))
        own = [spread[k][dp : dp + 1] for k in range(rows)]
        here = jnp.concatenate([here[:4]] + own + [here[4 + rows :]], axis=0)
        small[dp, :, 0:lanes] = here.astype(jnp.bfloat16)


def project_grads_kernel(
    cuts, columns, me_ref, x_ref, dq_ref, dk_ref, dv_ref, sums_feed, hsum, *rest
):
    xt, held, small, sems = rest[-4:]
    outs = rest[:-4]
    xt[...] = x_ref[...].T
    started = []
    for which, ref in enumerate((dq_ref, dk_ref, dv_ref)):
        held[which] = dot(xt[...], ref[...]).astype(jnp.bfloat16)
        if cuts is None:
            outs[which][...] = held[which]
            continue
        width, half, third = held.shape[2], (cuts[0].rows + cuts[1].rows - SMALL_ROWS) // 3, 0
        third = cuts[0].rows - SMALL_ROWS - half
        spans = [(0, 0, half, 0)], [(1, 0, half, 0)], [(0, 0, third, half), (1, third, half - third, half)]
        used = 0
        for i, offset, count, at in spans[which]:
            if count == 0:
                continue
            cut = cuts[i]
            ends = [(p * cut.width, p, 0, cut.width) for p in range(width // cut.width)]
            made = piece_copies(
                held.at[which], outs[2 * i : 2 * i + 2],
                sems.at[which, pl.ds(used, width // half * len(ends))],
                me_ref, cut.stages, 0, width // (2 * half), half, (offset, count, at), ends,
            )
            used += len(made)
            started += run_all(made)
    if cuts is not None:
        sums_in = [
            jnp.sum(ref[...].astype(jnp.float32), axis=0, keepdims=True) for ref in (dq_ref, dv_ref)
        ]
        pack_gradients(sums_feed[...], sums_in, hsum[...], small, columns)
        started += run_all(
            small_copies(
                small, outs[:2], sems.at[3], me_ref, cuts[0].stages, cuts[0].rows - SMALL_ROWS, small.shape[0],
                held.shape[2] // cuts[0].width,
            )
        )
    wait_all(started)


def project_grads(me, x, dq, dk, dv, sums, cuts, dp_size, columns):
    total, width = x.shape
    grad = jax.ShapeDtypeStruct((width, width), jnp.bfloat16)
    direct = cuts is not None
    copies = 4 * dp_size * (width // cuts[0].width) if direct else 1
    piece = cuts[0].width if direct else 128
    return pl.pallas_call(
        functools.partial(project_grads_kernel, cuts, columns),
        in_specs=[SCALARS] + [HERE] * 6,
        out_specs=[ANYWHERE] * 4 if direct else [HERE] * 3,
        out_shape=[shape for cut in cuts for shape in cut.shapes()] if direct else [grad] * 3,
        scratch_shapes=[
            pltpu.VMEM((width, total), jnp.bfloat16),
            pltpu.VMEM((3, width, width), jnp.bfloat16),
            pltpu.VMEM((dp_size if direct else 1, SMALL_ROWS, piece), jnp.bfloat16),
            pltpu.SemaphoreType.DMA((4, copies)),
        ],
        compiler_params=pltpu.CompilerParams(vmem_limit_bytes=VMEM_BYTES),
        cost_estimate=estimate(8),
        name="project_grads",
    )(me, x, dq, dk, dv, *sums)


def input_grad_kernel(source, me_ref, gf_ref, dq_ref, dk_ref, dv_ref, *refs):
    inputs, (out_ref, weights, sems) = refs[:-3], refs[-3:]
    started = [
        run_all(source.copies(i, inputs, weights.at[i], sems.at[i], me_ref)) for i in range(3)
    ]
    grad = gf_ref[...]
    for i, ref in enumerate((dq_ref, dk_ref, dv_ref)):
        wait_all(started[i])
        grad = grad + dot_last(ref[...], weights[i])
    out_ref[...] = grad.astype(jnp.bfloat16)


def input_grads(me, gf, dq, dk, dv, source):
    total, width = dq.shape
    return pl.pallas_call(
        functools.partial(input_grad_kernel, source),
        in_specs=[SCALARS] + [HERE] * 4 + [ANYWHERE] * len(source.operands),
        out_specs=HERE,
        out_shape=jax.ShapeDtypeStruct((total, width), jnp.bfloat16),
        scratch_shapes=[
            pltpu.VMEM((3, width, width), jnp.bfloat16),
            pltpu.SemaphoreType.DMA((3, source.count((width, width)))),
        ],
        compiler_params=pltpu.CompilerParams(vmem_limit_bytes=VMEM_BYTES),
        cost_estimate=estimate(8),
        name="input_grads",
    )(me, gf, dq, dk, dv, *source.operands)


def after(values, *others):
    return lax.optimization_barrier((values, others))[0]


def meet(values, parts):
    values, arriving = lax.optimization_barrier((values, [part.arriving for part in parts]))
    for part, value in zip(parts, arriving):
        part.arriving = value
    return values


class Attention:
    def __init__(self, me, inputs, lengths, source, given, columns, hidden_count):
        self.me, self.inputs, self.lengths, self.source = me, inputs, lengths, source
        self.given, self.sizes = given, (columns, hidden_count)
        self.state, self.back = (), ()

    def forward(self, seq):
        *state, self.vectors, self.hidden_bias = attend_forward(
            seq, self.me, self.inputs, self.lengths, self.source, self.given, *self.sizes, self.state
        )
        self.state = tuple(state)

    def backward(self, seq, part, parts, do):
        self.back = tuple(
            attend_backward(seq, part, parts, do, *self.state, self.lengths, self.back)
        )


def layer_step(inputs, lengths, upstream, gather, scatter):
    shape = inputs.shape
    flat = (shape[0] * shape[1], shape[2])
    seqs = shape[0]
    source, given = gather.first()
    bias, hidden = gather.shards[6:8]
    me = gather.me
    columns = bias.shape[1]
    attention = Attention(
        me, inputs, lengths, source, given, columns, hidden.shape[0] * scatter.dp_size
    )
    for seq in range(seqs):
        attention.inputs = gather.before(seq, attention.inputs)
        attention.forward(seq)
        attention.state = gather.after(seq, attention.state)
    outputs, gf, do, hidden_sum, sums_feed, *grads = feed(
        me, lengths, inputs, attention.state[3], upstream, attention.hidden_bias,
        attention.vectors, gather.second(), scatter.feed_cuts,
    )
    parts = 2
    scatter.feed(grads)
    for at in range(seqs * parts):
        attention.backward(at // parts, at % parts, parts, do.reshape(shape))
        attention.back = scatter.step(at, attention.back)
    dq, dk, dv = (grad.reshape(flat) for grad in attention.back)
    sums = (sums_feed, hidden_sum)
    scatter.ends = (dq, dv)
    results = project_grads(
        me, inputs.reshape(flat), dq, dk, dv, sums, scatter.first_cuts, scatter.dp_size, columns
    )
    gf = scatter.last(results, sums, gf)
    input_grad = input_grads(me, gf, dq, dk, dv, source)
    input_grad, totals = scatter.totals(input_grad)
    return outputs.reshape(shape), input_grad.reshape(shape), totals


def split_up(value, dim, size):
    before, after = (value.shape[:dim], value.shape[dim + 1 :])
    return jnp.moveaxis(value.reshape(*before, size, -1, *after), dim, 0)


def sum_at_owner(value, axis, dim):
    size = lax.axis_size(axis)
    parts = lax.all_to_all(split_up(value, dim, size), axis, 0, 0, tiled=True)
    return jnp.sum(parts.astype(jnp.float32), axis=0)


def side_by_side(arrays, axis, dim, along):
    ends, at = ([], 0)
    for a in arrays[:-1]:
        at += a.shape[along]
        ends.append(at)
    both = jnp.concatenate(arrays, axis=along)
    return tuple(jnp.split(sum_at_owner(both, axis, dim), ends, axis=along))


def gather_forward(shards):
    (
        query_part,
        key_part,
        value_part,
        output_part,
        inner_part,
        outer_part,
        bias_part,
        hidden_part,
        gain_part,
        shift_part,
    ) = shards
    column_full = (
        lax.all_gather(query_part, "fsdp", axis=1, tiled=True),
        lax.all_gather(key_part, "fsdp", axis=1, tiled=True),
        lax.all_gather(value_part, "fsdp", axis=1, tiled=True),
        lax.all_gather(output_part, "fsdp", axis=1, tiled=True),
        lax.all_gather(inner_part, "fsdp", axis=1, tiled=True),
        lax.all_gather(outer_part, "fsdp", axis=1, tiled=True),
    )
    return (
        lax.all_gather(column_full[0], "dp", axis=0, tiled=True),
        lax.all_gather(column_full[1], "dp", axis=0, tiled=True),
        lax.all_gather(column_full[2], "dp", axis=0, tiled=True),
        lax.all_gather(column_full[3], "dp", axis=0, tiled=True),
        lax.all_gather(column_full[4], "dp", axis=0, tiled=True),
        lax.all_gather(column_full[5], "dp", axis=0, tiled=True),
        lax.all_gather(bias_part, "dp", axis=1, tiled=True),
        lax.all_gather(hidden_part, "dp", axis=0, tiled=True),
        lax.all_gather(gain_part, "dp", axis=1, tiled=True),
        lax.all_gather(shift_part, "dp", axis=1, tiled=True),
    )


def reduce_grads(grads):
    (
        query_grad,
        key_grad,
        value_grad,
        output_grad,
        inner_grad,
        outer_grad,
        bias_grad,
        hidden_grad,
        gain_grad,
        shift_grad,
    ) = grads
    bias_grad, hidden_grad, gain_grad, shift_grad = (
        lax.psum(bias_grad.astype(jnp.bfloat16), "fsdp").astype(jnp.float32),
        lax.psum(hidden_grad.astype(jnp.bfloat16), "fsdp").astype(jnp.float32),
        lax.psum(gain_grad.astype(jnp.bfloat16), "fsdp").astype(jnp.float32),
        lax.psum(shift_grad.astype(jnp.bfloat16), "fsdp").astype(jnp.float32),
    )
    narrow = (
        lax.psum_scatter(
            query_grad.astype(jnp.bfloat16), "fsdp", scatter_dimension=1, tiled=True
        ).astype(jnp.float32),
        lax.psum_scatter(
            key_grad.astype(jnp.bfloat16), "fsdp", scatter_dimension=1, tiled=True
        ).astype(jnp.float32),
        lax.psum_scatter(
            value_grad.astype(jnp.bfloat16), "fsdp", scatter_dimension=1, tiled=True
        ).astype(jnp.float32),
        lax.psum_scatter(
            output_grad.astype(jnp.bfloat16), "fsdp", scatter_dimension=1, tiled=True
        ).astype(jnp.float32),
        lax.psum_scatter(
            inner_grad.astype(jnp.bfloat16), "fsdp", scatter_dimension=1, tiled=True
        ).astype(jnp.float32),
        lax.psum_scatter(
            outer_grad.astype(jnp.bfloat16), "fsdp", scatter_dimension=1, tiled=True
        ).astype(jnp.float32),
    )
    return (
        *side_by_side(
            (
                narrow[0].astype(jnp.bfloat16),
                narrow[1].astype(jnp.bfloat16),
                narrow[2].astype(jnp.bfloat16),
                narrow[3].astype(jnp.bfloat16),
                narrow[4].astype(jnp.bfloat16),
            ),
            "dp",
            0,
            1,
        ),
        sum_at_owner(narrow[5].astype(jnp.bfloat16), "dp", 0),
        sum_at_owner(bias_grad.astype(jnp.bfloat16), "dp", 1),
        sum_at_owner(hidden_grad.astype(jnp.bfloat16), "dp", 0),
        *side_by_side(
            (gain_grad.astype(jnp.bfloat16), shift_grad.astype(jnp.bfloat16)), "dp", 1, 0
        ),
    )


def pack_small(bias, hidden, gains, shifts, width):
    columns = bias.shape[-1]
    rows = jnp.concatenate([bias, hidden.reshape(-1, columns), gains, shifts], axis=0)
    return jnp.pad(rows, ((0, SMALL_ROWS - rows.shape[0]), (0, width - columns)))


class Gather:
    def __init__(self, mesh, shards, me):
        self.mesh, self.shards, self.me = mesh, shards, me
        self.orders = stage_orders(mesh)

    def prepare(self):
        query, key, value, output, inner, outer, bias, hidden, gains, shifts = self.shards
        half, half_outer = query.shape[0] // 2, outer.shape[0] // 2
        small = pack_small(bias, hidden, gains, shifts, 2 * query.shape[1])

        def both(*arrays):
            halves = [array[: array.shape[0] // 2] for array in arrays]
            halves += [array[array.shape[0] // 2 :] for array in arrays]
            return jnp.concatenate(halves, axis=0)

        one, rest, inner = pair_up((both(query, key, value), both(output, outer), inner))
        self.one = [
            jnp.concatenate([one[:half], small], axis=0)[None],
            one[half : 2 * half][None],
            one[2 * half :][None],
        ]
        split = self.split = FeedSplit(half, half_outer, 2 * query.shape[1], inner.shape[1])
        folded = inner[half - split.extra :].reshape(split.extra, split.groups, split.width)
        folded = folded.swapaxes(0, 1).reshape(split.groups * split.extra, split.width)
        self.two = [
            inner[: half - split.extra][None],
            rest[half : half + split.most][None],
            jnp.concatenate([rest[:half], rest[half + split.most :], folded], axis=0)[None],
        ]

    def send(self, parts, stage):
        return [swap(part, *self.orders[i][stage]) for i, part in enumerate(parts)]

    def join(self, parts, received):
        return [jnp.concatenate(pair, axis=0) for pair in zip(parts, received)]

    def first(self):
        self.prepare()
        count = len(self.orders[0])
        self.stage = 0
        for stage in range(count):
            arriving = self.send(self.one, stage)
            ahead = None
            if stage >= count - 2:
                self.two = after(self.two, self.one)
                ahead = self.send(self.two, self.stage)
                self.stage += 1
            self.one = self.join(self.one, arriving)
            if ahead is not None:
                self.two = self.join(self.two, after(ahead, self.one))
        self.two = after(self.two, self.one)
        others = [swap(part, "fsdp", 0) for part in self.one]
        half, width = self.shards[0].shape[0] // 2, self.one[0].shape[2]
        spots = [(half, width, [(i, 0, 0, half, 0)]) for i in range(3)]
        operands = [array for pair in zip(self.one, others) for array in pair]
        return Source(operands, self.orders, spots, self.mesh.shape["dp"], half), ()

    def before(self, seq, inputs):
        if self.stage == len(self.orders[0]):
            return inputs
        self.arriving = self.send(self.two, self.stage)
        self.stage += 1
        return after(inputs, self.two)

    def after(self, seq, state):
        if self.arriving is None:
            return state
        arriving = after(self.arriving, state)
        self.two, self.arriving = self.join(self.two, arriving), None
        return state

    def second(self):
        while self.stage < len(self.orders[0]):
            self.two = self.join(self.two, self.send(self.two, self.stage))
            self.stage += 1
        others = [swap(part, "fsdp", 0) for part in self.two]
        operands = [array for pair in zip(self.two, others) for array in pair]
        return Source(operands, self.orders, self.split.spots(), self.mesh.shape["dp"])


class Part:
    def __init__(self, keep, send, stages):
        self.keep, self.stages = keep, list(stages)
        self.arriving = swap(send, "fsdp", 0)

    def step(self):
        axis, bit = self.stages.pop()
        half = self.keep.shape[0] // 2
        send = total_of(self.keep[half:], self.arriving[half:], jnp.bfloat16)
        arriving = swap(send, axis, bit)
        self.keep = total_of(self.keep[:half], self.arriving[:half], jnp.bfloat16)
        self.arriving = arriving
        return send

    def finish(self):
        while self.stages:
            self.step()
        return total_of(self.keep, self.arriving, jnp.float32)[0]


class Scatter:
    def __init__(self, mesh, shards, me):
        self.shards = shards
        self.orders = stage_orders(mesh)
        width, width_inner = 2 * shards[0].shape[1], 2 * shards[4].shape[1]
        half, half_outer = shards[0].shape[0] // 2, shards[5].shape[0] // 2
        self.dp_size = mesh.shape["dp"]
        self.split = FeedSplit(half, half_outer, width, width_inner)
        self.feed_cuts = FeedCuts(self.orders, self.split)
        self.third = half // 3 // 16 * 16
        rows = (half + self.third + SMALL_ROWS, 2 * half - self.third)
        self.first_cuts = [Cut(order, r, width) for order, r in zip(self.orders, rows)]

    def feed(self, grads):
        self.behind = [
            Part(*grads[2 * i : 2 * i + 2], cut.stages) for i, cut in enumerate(self.feed_cuts.cuts)
        ]

    def step(self, at, state):
        parts = {0: self.behind, 2: self.behind[2:], 3: self.behind}.get(at, [])
        if not parts:
            return state
        state = meet(state, parts)
        return after(state, [part.step() for part in parts])

    def last(self, results, sums, passing):
        results = meet(results, self.behind)
        self.front = [
            Part(*results[2 * i : 2 * i + 2], cut.stages) for i, cut in enumerate(self.first_cuts)
        ]
        sent = [part.step() for part in self.behind]
        meet((), self.front)
        sent += [part.step() for part in self.front]
        return after(passing, sent)

    def totals(self, passing):
        half, half_outer = self.shards[0].shape[0] // 2, self.shards[5].shape[0] // 2
        columns = self.shards[6].shape[1]
        parts = self.front + self.behind
        passing = meet(passing, parts)
        while any(part.stages for part in parts):
            for part in parts:
                if part.stages:
                    part.step()
            meet((), parts)
        one, two = [part.finish() for part in self.front]
        third = self.third
        inner, outer, rest = [part.finish() for part in self.behind]
        thirds = [one[half : half + third], two[half:]]
        query, key, value = settle(jnp.concatenate([one[:half], two[:half], *thirds]), (half,) * 3)
        split = self.split
        folded = rest[split.folded :].reshape(split.groups, split.extra, split.width)
        folded = folded.swapaxes(0, 1).reshape(split.extra, split.width_inner)
        (inner,) = settle(jnp.concatenate([inner, folded], axis=0), (half,))
        outer = jnp.concatenate([outer, rest[half : split.folded]], axis=0)
        output, outer = settle(jnp.concatenate([rest[:half], outer]), (half, half_outer))
        rows = one[half + third :, :columns]
        split = 4 + self.shards[7].shape[0] // columns
        return passing, (
            query, key, value, output, inner, outer,
            rows[:4], rows[4:split].reshape(-1), rows[split : split + 2], rows[split + 2 : split + 4],
        )


class PlainGather:
    def __init__(self, mesh, shards, me):
        self.shards, self.me = shards, me

    def first(self):
        arrays = gather_forward(self.shards)
        self.rest = arrays[3:6]
        bias, hidden, gains, shifts = arrays[6:]
        vectors = jnp.concatenate([bias, gains, shifts], axis=0).astype(jnp.float32)
        return Source(arrays[:3]), (vectors, hidden.astype(jnp.float32)[None])

    def before(self, seq, inputs):
        return inputs

    def after(self, seq, state):
        return state

    def second(self):
        return Source(self.rest)


class PlainScatter:
    def __init__(self, mesh, shards, me):
        self.feed_cuts = self.first_cuts = None
        self.dp_size = mesh.shape["dp"]

    def feed(self, grads):
        self.grads = grads

    def step(self, at, state):
        return state

    def last(self, results, sums, passing):
        (feed, hidden), (dq, dv) = sums, self.ends
        ends = [jnp.sum(d.astype(jnp.float32), axis=0, keepdims=True) for d in (dq, dv)]
        bias = jnp.concatenate([*ends, feed[5:6], feed[2:3]], axis=0)
        gains = jnp.concatenate([feed[3:4], feed[:1]], axis=0)
        shifts = jnp.concatenate([feed[4:5], feed[1:2]], axis=0)
        self.grads = (*results, *self.grads, bias, hidden[0], gains, shifts)
        return passing

    def totals(self, passing):
        return passing, reduce_grads(self.grads)


def on_device(
    mesh,
    tokens,
    lengths,
    cotangent,
    *shards,
):
    me = jnp.stack([lax.axis_index("dp"), lax.axis_index("fsdp")]).astype(jnp.int32)
    rows = (shards[0].shape[0], shards[5].shape[0])
    direct = fits(mesh, rows, shards[0].shape[1], shards[7].shape[0])
    gather = (Gather if direct else PlainGather)(mesh, shards, me)
    scatter = (Scatter if direct else PlainScatter)(mesh, shards, me)
    shape = (-1, *tokens.shape[2:])
    outputs, grad_inputs, totals = layer_step(
        tokens.reshape(shape), lengths.reshape(-1), cotangent.reshape(shape), gather, scatter
    )
    return (outputs.reshape(tokens.shape), grad_inputs.reshape(tokens.shape), *totals)


def solution(mesh):
    placed = (
        P(None, ("dp", "fsdp"), None, None),
        P(None, ("dp", "fsdp")),
        P(None, ("dp", "fsdp"), None, None),
        P("dp", "fsdp"),
        P("dp", "fsdp"),
        P("dp", "fsdp"),
        P("dp", "fsdp"),
        P("dp", "fsdp"),
        P("dp", "fsdp"),
        P(None, "dp"),
        P("dp"),
        P(None, "dp"),
        P(None, "dp"),
    )
    return jax.shard_map(
        functools.partial(on_device, mesh),
        mesh=mesh,
        in_specs=placed,
        out_specs=(
            P(None, ("dp", "fsdp"), None, None),
            P(None, ("dp", "fsdp"), None, None),
            P("dp", "fsdp"),
            P("dp", "fsdp"),
            P("dp", "fsdp"),
            P("dp", "fsdp"),
            P("dp", "fsdp"),
            P("dp", "fsdp"),
            P(None, "dp"),
            P("dp"),
            P(None, "dp"),
            P(None, "dp"),
        ),
        check_vma=False,
    )
```

time: 360 us -> 314 us (0.87)
  Pallas kernels: 177 us -> 153 us
  starting transfers between devices: 43.2 us -> 64.6 us
  waiting for transfers between devices: 77.9 us -> 58.5 us
  other arithmetic: 26.1 us -> 12.7 us
  local copies, waits for them, and re-layouts: 28.2 us -> 16.8 us
    pallas_call x13 -> x9, Pallas kernels: 177 us -> 153 us  [the longest x1 66.4 us: feed(): pl.pallas_call(functools.partial(feed_kernel, source, cuts, slots), in_sp...]
    ppermute x48 -> x61, starting transfers between devices: 43.2 us -> 64.6 us  [swap(): return lax.ppermute(value, axis, [(i, i ^ 1 << bit) for i in range(size)])]
    ppermute x48 -> x61, waiting for transfers between devices: 77.9 us -> 58.5 us  [swap(): return lax.ppermute(value, axis, [(i, i ^ 1 << bit) for i in range(size)])]
    concatenate x4 -> x2, other arithmetic: 4.57 us -> 0.04 us  [the longest x1 0.02 us: totals(): jnp.concatenate([rest[:half], outer])]
    convert_element_type x16 -> x20, other arithmetic: 10.8 us -> 6.26 us  [total_of(): return (left.astype(jnp.float32) + right.astype(jnp.float32)).astype(kind)]
    unnamed x39 -> x55, local copies, waits for them, and re-layouts: 11.7 us -> 9.06 us
  transfers between devices with their start and end apart: 48 -> 61, of which waited for: 17 -> 23; matrix products, arithmetic and copies ran while one was open for 13% -> 6% of each run, Pallas kernels for 31% -> 28%
where the time goes in v4:
time: 314 us; the launch traced here: 308 us
  Pallas kernels  153 us (49%)
  starting transfers between devices  64.6 us (21%)
  waiting for transfers between devices  58.5 us (19%)
  local copies, waits for them, and re-layouts  16.8 us (5%)
  other arithmetic  12.7 us (4%)
    pallas_call x1, Pallas kernels, feed(): pl.pallas_call(functools.partial(feed_kernel, source, cuts, slots), in_sp...  66.4 us
    ppermute x61, starting transfers between devices, swap(): return lax.ppermute(value, axis, [(i, i ^ 1 << bit) for i in range(size)])  64.6 us
    ppermute x61, waiting for transfers between devices, swap(): return lax.ppermute(value, axis, [(i, i ^ 1 << bit) for i in range(size)])  58.5 us
    pallas_call x4, Pallas kernels, attend_backward(): pl.pallas_call(functools.partial(skip_refs, kernel, len(inputs), len(befo...  32.6 us
    pallas_call x2, Pallas kernels, attend_forward(): pl.pallas_call(functools.partial(skip_refs, kernel, known, len(before)),...  31.2 us
    pallas_call x1, Pallas kernels, input_grads(): pl.pallas_call(functools.partial(input_grad_kernel, source), in_specs=[SC...  12.5 us
    pallas_call x1, Pallas kernels, project_grads(): pl.pallas_call(functools.partial(project_grads_kernel, cuts, columns), in...  10.5 us
    unnamed x55, local copies, waits for them, and re-layouts  9.06 us
  transfers between devices with their start and end apart: 61, of which 23 were waited for; matrix products, arithmetic and copies ran while one was open for 6% of the time, Pallas kernels for 28%

profile of v4, /device:TPU:0, one launch (start us, length us, event | category | flops | bytes accessed | tf_op | source)
XLA Modules:
  0.0 307.8 jit_solution(7748776048570492936)
XLA Ops:
  7.4 2.6 collective-permute-start.7
  10.0 2.6 collective-permute-start.5
  13.2 1.6 collective-permute-start.8
  15.2 1.9 collective-permute-start.6
  19.3 2.3 collective-permute-start.14
  21.6 1.6 collective-permute-start.13
  24.8 1.5 collective-permute-start.11
  26.3 2.2 collective-permute-start.10
  28.5 2.3 collective-permute-done.14
  30.8 8.0 %collective-permute-start.20 = (bf16[8,48,384]{2,1,0:T(8,128)(2,1)S(1)}, bf16[8,48,384]{2,1,0:T(8,128)(2,1)S(1)}, u32[]{:S(2)}, u32[]{:S(2)}) collective-permute-start(bf16[8,48,384]{2,1,0:T(8,128)(2,1)S(1)} %pad_maximum_fusion.6), channel_id=1, source_target_pairs={{0,8},{4,12},{8,0},{12,4},{16,24},{20,28},{24,16},{28,20},{1,9},{5... | collective-permute-start | bytes 884744 | tf_op jit(solution)/shard_map/ppermute | solution.py:19
  39.6 1.6 collective-permute-start.18
  41.9 1.6 collective-permute-start.16
  43.5 2.2 collective-permute-done.19
  46.0 1.5 collective-permute-done.18
  48.8 2.4 collective-permute-done.16
  51.2 4.1 %collective-permute-done.15 = bf16[2,48,1536]{2,1,0:T(8,128)(2,1)S(1)} collective-permute-done((bf16[2,48,1536]{2,1,0:T(8,128)(2,1)S(1)}, bf16[2,48,1536]{2,1,0:T(8,128)(2,1)S(1)}, u32[]{:S(2)}, u32[]{:S(2)}) %collective-permute-start.15) | collective-permute-done | bytes 294944 | tf_op jit(solution)/shard_map/ppermute | solution.py:19
  55.4 2.4 collective-permute-start.23
  57.8 1.5 collective-permute-start.22
  63.4 15.7 %attend_forward.2 = (bf16[2,512,768]{2,1,0:T(8,128)(2,1)}, bf16[2,512,768]{2,1,0:T(8,128)(2,1)}, bf16[2,512,768]{2,1,0:T(8,128)(2,1)}, bf16[2,512,768]{2,1,0:T(8...) custom-call(s32[2]{0:T(128)} %bitcast.61, s32[2]{0:T(128)} %pad_add_fusion.refs_1_.me_ref, ...), custom_call_target="tpu_custom_call" | custom-call | flops 14000000000 | bytes 14000000 | tf_op jit(solution)/shard_map/attend_forward/pallas_call | solution.py:364
  79.9 2.5 collective-permute-start.29
  83.2 1.5 collective-permute-start.28
  85.4 15.4 %attend_forward.3 = (bf16[2,512,768]{2,1,0:T(8,128)(2,1)}, bf16[2,512,768]{2,1,0:T(8,128)(2,1)}, bf16[2,512,768]{2,1,0:T(8,128)(2,1)}, bf16[2,512,768]{2,1,0:T(8...) custom-call(s32[2]{0:T(128)} %bitcast.62, ...), custom_call_target="tpu_custom_call", output_to_operand_aliasing={{0}: (9, {}), {1}: (10, {}), {2}: (11, {}), {3}: (12, {}), ... | custom-call | flops 14000000000 | bytes 14000000 | tf_op jit(solution)/shard_map/attend_forward/pallas_call | solution.py:364
  100.9 3.1 %collective-permute-done.28 = bf16[8,160,384]{2,1,0:T(8,128)(2,1)S(1)} collective-permute-done((bf16[8,160,384]{2,1,0:T(8,128)(2,1)S(1)}, bf16[8,160,384]{2,1,0:T(8,128)(2,1)S(1)}, u32[]{:S(2)}, u32[]{:S(2)}) %collective-permute-start.28) | collective-permute-done | bytes 983072 | tf_op jit(solution)/shard_map/ppermute | solution.py:19
  104.0 5.6 %collective-permute-done.27 = bf16[8,48,1536]{2,1,0:T(8,128)(2,1)S(1)} collective-permute-done((bf16[8,48,1536]{2,1,0:T(8,128)(2,1)S(1)}, bf16[8,48,1536]{2,1,0:T(8,128)(2,1)S(1)}, u32[]{:S(2)}, u32[]{:S(2)}) %collective-permute-start.27) | collective-permute-done | bytes 1179680 | tf_op jit(solution)/shard_map/ppermute | solution.py:19
  112.4 6.3 %collective-permute-done.32.refs_5_ = bf16[16,80,384]{2,1,0:T(8,128)(2,1)S(1)} collective-permute-done((bf16[16,80,384]{2,1,0:T(8,128)(2,1)}, bf16[16,80,384]{2,1,0:T(8,128)(2,1)S(1)}, u32[]{:S(2)}, u32[]{:S(2)}) %collective-permute-start.32) | collective-permute-done | bytes 983072 | tf_op jit(solution)/shard_map/ppermute | solution.py:19
  118.7 2.0 copy-done.13
  121.0 66.4 %feed.1 = (bf16[1024,768]{1,0:T(8,128)(2,1)}, f32[1024,768]{1,0:T(8,128)}, bf16[1024,768]{1,0:T(8,128)(2,1)}, f32[1,3072]{1,0:T(1,128)}, f32[8,768]{1,0:T(8,128)...) custom-call(s32[2]{0:T(128)} %bitcast.63, ...), custom_call_target="tpu_custom_call" | custom-call | flops 60000002048 | bytes 60000000 | tf_op jit(solution)/shard_map/feed/pallas_call | solution.py:629
  188.1 8.2 %attend_backward.4 = (bf16[2,512,768]{2,1,0:T(8,128)(2,1)}, bf16[2,512,768]{2,1,0:T(8,128)(2,1)}, bf16[2,512,768]{2,1,0:T(8,128)(2,1)}) custom-call(s32[2]{0:T(128)} %bitcast.64, bf16[2,512,768]{2,1,0:T(8,128)(2,1)} %bitcast.70, bf16[2,512,768]{2,1,0:T(8,128)(2,1)} %get-tuple-element.158.refs_2_, bf16[2,512,768]{2,1,0:T(8,128)(2,1)} %get-tuple-element.159.refs_3_, ...), custom_call_target="tpu_custom_call" | custom-call | flops 7000000000 | bytes 7000000 | tf_op jit(solution)/shard_map/attend_backward/pallas_call | solution.py:721
  198.1 1.5 add_convert_fusion.2
  201.4 8.1 %attend_backward.5 = (bf16[2,512,768]{2,1,0:T(8,128)(2,1)}, bf16[2,512,768]{2,1,0:T(8,128)(2,1)}, bf16[2,512,768]{2,1,0:T(8,128)(2,1)}) custom-call(s32[2]{0:T(128)} %bitcast.65, bf16[2,512,768]{2,1,0:T(8,128)(2,1)} %bitcast.71, bf16[2,512,768]{2,1,0:T(8,128)(2,1)} %get-tuple-element.158.refs_2_, ...), custom_call_target="tpu_custom_call", output_to_operand_aliasing={{0}: (7, {}), {1}: (8, {}), {2}: (9, {})} | custom-call | flops 7000000000 | bytes 7000000 | tf_op jit(solution)/shard_map/attend_backward/pallas_call | solution.py:721
  209.5 8.0 %attend_backward.6 = (bf16[2,512,768]{2,1,0:T(8,128)(2,1)}, bf16[2,512,768]{2,1,0:T(8,128)(2,1)}, bf16[2,512,768]{2,1,0:T(8,128)(2,1)}) custom-call(s32[2]{0:T(128)} %bitcast.66, bf16[2,512,768]{2,1,0:T(8,128)(2,1)} %bitcast.72, bf16[2,512,768]{2,1,0:T(8,128)(2,1)} %get-tuple-element.158.refs_2_, ...), custom_call_target="tpu_custom_call", output_to_operand_aliasing={{0}: (7, {}), {1}: (8, {}), {2}: (9, {})} | custom-call | flops 7000000000 | bytes 7000000 | tf_op jit(solution)/shard_map/attend_backward/pallas_call | solution.py:721
  219.2 8.2 %attend_backward.7 = (bf16[2,512,768]{2,1,0:T(8,128)(2,1)}, bf16[2,512,768]{2,1,0:T(8,128)(2,1)}, bf16[2,512,768]{2,1,0:T(8,128)(2,1)}) custom-call(s32[2]{0:T(128)} %bitcast.67, bf16[2,512,768]{2,1,0:T(8,128)(2,1)} %bitcast.73, bf16[2,512,768]{2,1,0:T(8,128)(2,1)} %get-tuple-element.158.refs_2_, ...), custom_call_target="tpu_custom_call", output_to_operand_aliasing={{0}: (7, {}), {1}: (8, {}), {2}: (9, {})} | custom-call | flops 7000000000 | bytes 7000000 | tf_op jit(solution)/shard_map/attend_backward/pallas_call | solution.py:721
  227.4 5.5 %collective-permute-done.39 = bf16[4,80,384]{2,1,0:T(8,128)(2,1)S(1)} collective-permute-done((bf16[4,80,384]{2,1,0:T(8,128)(2,1)S(1)}, bf16[4,80,384]{2,1,0:T(8,128)(2,1)S(1)}, u32[]{:S(2)}, u32[]{:S(2)}) %collective-permute-start.39) | collective-permute-done | bytes 245792 | tf_op jit(solution)/shard_map/ppermute | solution.py:19
  232.9 1.6 collective-permute-start.42
  235.6 1.3 collective-permute-start.40
  236.9 10.5 %project_grads.1 = (bf16[16,80,384]{2,1,0:T(8,128)(2,1)}, bf16[16,80,384]{2,1,0:T(8,128)(2,1)}, bf16[16,80,384]{2,1,0:T(8,128)(2,1)}, bf16[16,80,384]{2,1,0:T(8,128)(2,1)}) custom-call(s32[2]{0:T(128)} %pad_add_fusion.refs_1_.me_ref, bf16[1024,768]{1,0:T(8,128)(2,1)} %bitcast.60, bf16[1024,768]{1,0:T(8,128)(2,1)} %bitcast.75, bf16[1024,768]{1,0:T(8,128)(2,1)} %bitcast.77, ...), custom_call_target="tpu_custom_call" | custom-call | flops 8000000000 | bytes 8000000 | tf_op jit(solution)/shard_map/project_grads/pallas_call | solution.py:818
  248.4 1.5 collective-permute-done.40
  252.0 2.1 collective-permute-start.47
  255.9 1.6 collective-permute-start.45
  257.5 12.5 %input_grads.1 = bf16[1024,768]{1,0:T(8,128)(2,1)} custom-call(s32[2]{0:T(128)} %pad_add_fusion.refs_1_.me_ref, f32[1024,768]{1,0:T(8,128)} %get-tuple-element.226.gf_ref, bf16[1024,768]{1,0:T(8,128)(2,1)} %bitcast.76, bf16[1024,768]{1,0:T(8,128)(2,1)} %bitcast.78, bf16[1024,768]{1,0:T(8,128)(2,1)} %bitcast.80, bf16[16,64,384]{2,1,0:T(8,128)(2,1)} %copy-done.6, ...), custom_call_target="tpu_custom_call" | custom-call | flops 8000000000 | bytes 8000000 | tf_op jit(solution)/shard_map/input_grads/pallas_call | solution.py:849
  271.9 3.0 collective-permute-start.53
  274.9 8.5 %collective-permute-done.53 = bf16[1,160,384]{2,1,0:T(8,128)(2,1)S(1)} collective-permute-done((bf16[1,160,384]{2,1,0:T(8,128)(2,1)S(1)}, bf16[1,160,384]{2,1,0:T(8,128)(2,1)S(1)}, u32[]{:S(2)}, u32[]{:S(2)}) %collective-permute-start.53) | collective-permute-done | bytes 122912 | tf_op jit(solution)/shard_map/ppermute | solution.py:19
  283.7 2.1 collective-permute-start.54
  285.7 4.1 %collective-permute-done.55 = bf16[2,80,384]{2,1,0:T(8,128)(2,1)S(1)} collective-permute-done((bf16[2,80,384]{2,1,0:T(8,128)(2,1)S(1)}, bf16[2,80,384]{2,1,0:T(8,128)(2,1)S(1)}, u32[]{:S(2)}, u32[]{:S(2)}) %collective-permute-start.55) | collective-permute-done | bytes 122912 | tf_op jit(solution)/shard_map/ppermute | solution.py:19
  289.8 1.4 collective-permute-done.54
  292.5 1.9 collective-permute-start.56
  294.3 3.4 %collective-permute-done.57 = bf16[1,80,384]{2,1,0:T(8,128)(2,1)S(1)} collective-permute-done((bf16[1,80,384]{2,1,0:T(8,128)(2,1)S(1)}, bf16[1,80,384]{2,1,0:T(8,128)(2,1)S(1)}, u32[]{:S(2)}, u32[]{:S(2)}) %collective-permute-start.57) | collective-permute-done | bytes 61472 | tf_op jit(solution)/shard_map/ppermute | solution.py:19
  297.7 1.3 collective-permute-done.56
  (233 shorter events, 47.2 us)
Async XLA Ops:
  3.8 9.1 %collective-permute-start = (bf16[48,768]{1,0:T(8,128)(2,1)S(1)}, bf16[48,768]{1,0:T(8,128)(2,1)S(1)}, u32[]{:S(2)}, u32[]{:S(2)}) collective-permute-start(bf16[48,768]{1,0:T(8,128)(2,1)S(1)} %get-tuple-element.321), channel_id=1, source_target_pairs={{0,1},{1,0},{2,3},{3,2},{4,5},{5,4},{6,7},{7,6},{8,9},{9,8},{10,11... | collective-permute-start | bytes 221192 | tf_op jit(solution)/shard_map/ppermute | solution.py:19
  6.0 7.0 %collective-permute-start.1 = (bf16[240,192]{1,0:T(8,128)(2,1)S(1)}, bf16[240,192]{1,0:T(8,128)(2,1)S(1)}, u32[]{:S(2)}, u32[]{:S(2)}) collective-permute-start(bf16[240,192]{1,0:T(8,128)(2,1)S(1)} %get-tuple-element.309), channel_id=1, source_target_pairs={{0,1},{1,0},{2,3},{3,2},{4,5},{5,4},{6,7},{7,6},{8,9},{9,8},{10,11... | collective-permute-start | bytes 276488 | tf_op jit(solution)/shard_map/ppermute | solution.py:19
  19.3 11.5 %collective-permute-start.14 = (bf16[4,48,384]{2,1,0:T(8,128)(2,1)S(1)}, bf16[4,48,384]{2,1,0:T(8,128)(2,1)S(1)}, u32[]{:S(2)}, u32[]{:S(2)}) collective-permute-start(bf16[4,48,384]{2,1,0:T(8,128)(2,1)S(1)} %pad_maximum_fusion.14), channel_id=1, source_target_pairs={{0,16},{4,20},{8,24},{12,28},{16,0},{20,4},{24,8},{28,12},{1,17},{... | collective-permute-start | bytes 442376 | tf_op jit(solution)/shard_map/ppermute | solution.py:19
  21.6 9.2 %collective-permute-start.13 = (bf16[4,48,384]{2,1,0:T(8,128)(2,1)S(1)}, bf16[4,48,384]{2,1,0:T(8,128)(2,1)S(1)}, u32[]{:S(2)}, u32[]{:S(2)}) collective-permute-start(bf16[4,48,384]{2,1,0:T(8,128)(2,1)S(1)} %pad_maximum_fusion.13), channel_id=1, source_target_pairs={{0,4},{4,0},{8,12},{12,8},{16,20},{20,16},{24,28},{28,24},{1,5},{5... | collective-permute-start | bytes 442376 | tf_op jit(solution)/shard_map/ppermute | solution.py:19
  24.2 14.7 %collective-permute-start.12 = (bf16[4,64,384]{2,1,0:T(8,128)(2,1)S(1)}, bf16[4,64,384]{2,1,0:T(8,128)(2,1)S(1)}, u32[]{:S(2)}, u32[]{:S(2)}) collective-permute-start(bf16[4,64,384]{2,1,0:T(8,128)(2,1)S(1)} %pad_maximum_fusion.12), channel_id=1, source_target_pairs={{0,2},{1,3},{2,0},{3,1},{4,6},{5,7},{6,4},{7,5},{8,10},{9,11},{10,... | collective-permute-start | bytes 589832 | tf_op jit(solution)/shard_map/ppermute | solution.py:19
  24.8 14.8 %collective-permute-start.11 = (bf16[1,80,384]{2,1,0:T(8,128)(2,1)S(1)}, bf16[1,80,384]{2,1,0:T(8,128)(2,1)S(1)}, u32[]{:S(2)}, u32[]{:S(2)}) collective-permute-start(bf16[1,80,384]{2,1,0:T(8,128)(2,1)S(1)} %maximum_bitcast_fusion), channel_id=1, source_target_pairs={{0,2},{1,3},{2,0},{3,1},{4,6},{5,7},{6,4},{7,5},{8,10},{9,11},{10,... | collective-permute-start | bytes 184328 | tf_op jit(solution)/shard_map/ppermute | solution.py:19
  26.3 14.9 %collective-permute-start.10 = (bf16[1,160,384]{2,1,0:T(8,128)(2,1)S(1)}, bf16[1,160,384]{2,1,0:T(8,128)(2,1)S(1)}, u32[]{:S(2)}, u32[]{:S(2)}) collective-permute-start(bf16[1,160,384]{2,1,0:T(8,128)(2,1)S(1)} %slice_bitcast_fusion), channel_id=1, source_target_pairs={{0,16},{4,20},{8,24},{12,28},{16,0},{20,4},{24,8},{28,12},{1,17},{... | collective-permute-start | bytes 368648 | tf_op jit(solution)/shard_map/ppermute | solution.py:19
  30.8 10.4 %collective-permute-start.9 = (bf16[1,48,1536]{2,1,0:T(8,128)(2,1)S(1)}, bf16[1,48,1536]{2,1,0:T(8,128)(2,1)S(1)}, u32[]{:S(2)}, u32[]{:S(2)}) collective-permute-start(bf16[1,48,1536]{2,1,0:T(8,128)(2,1)S(1)} %maximum_select_fusion.1), channel_id=1, source_target_pairs={{0,16},{4,20},{8,24},{12,28},{16,0},{20,4},{24,8},{28,12},{1,17},{... | collective-permute-start | bytes 442376 | tf_op jit(solution)/shard_map/ppermute | solution.py:19
  30.8 15.0 %collective-permute-start.20 = (bf16[8,48,384]{2,1,0:T(8,128)(2,1)S(1)}, bf16[8,48,384]{2,1,0:T(8,128)(2,1)S(1)}, u32[]{:S(2)}, u32[]{:S(2)}) collective-permute-start(bf16[8,48,384]{2,1,0:T(8,128)(2,1)S(1)} %pad_maximum_fusion.6), channel_id=1, source_target_pairs={{0,8},{4,12},{8,0},{12,4},{16,24},{20,28},{24,16},{28,20},{1,9},{5... | collective-permute-start | bytes 884744 | tf_op jit(solution)/shard_map/ppermute | solution.py:19
  38.9 6.8 %collective-permute-start.19 = (bf16[8,48,384]{2,1,0:T(8,128)(2,1)S(1)}, bf16[8,48,384]{2,1,0:T(8,128)(2,1)S(1)}, u32[]{:S(2)}, u32[]{:S(2)}) collective-permute-start(bf16[8,48,384]{2,1,0:T(8,128)(2,1)S(1)} %pad_maximum_fusion.5), channel_id=1, source_target_pairs={{0,2},{1,3},{2,0},{3,1},{4,6},{5,7},{6,4},{7,5},{8,10},{9,11},{10,... | collective-permute-start | bytes 884744 | tf_op jit(solution)/shard_map/ppermute | solution.py:19
  39.6 7.8 %collective-permute-start.18 = (bf16[8,64,384]{2,1,0:T(8,128)(2,1)S(1)}, bf16[8,64,384]{2,1,0:T(8,128)(2,1)S(1)}, u32[]{:S(2)}, u32[]{:S(2)}) collective-permute-start(bf16[8,64,384]{2,1,0:T(8,128)(2,1)S(1)} %pad_maximum_fusion.2), channel_id=1, source_target_pairs={{0,4},{4,0},{8,12},{12,8},{16,20},{20,16},{24,28},{28,24},{1,5},{5... | collective-permute-start | bytes 1179656 | tf_op jit(solution)/shard_map/ppermute | solution.py:19
  41.3 7.5 %collective-permute-start.17 = (bf16[2,80,384]{2,1,0:T(8,128)(2,1)S(1)}, bf16[2,80,384]{2,1,0:T(8,128)(2,1)S(1)}, u32[]{:S(2)}, u32[]{:S(2)}) collective-permute-start(bf16[2,80,384]{2,1,0:T(8,128)(2,1)S(1)} %pad_maximum_fusion.17), channel_id=1, source_target_pairs={{0,4},{4,0},{8,12},{12,8},{16,20},{20,16},{24,28},{28,24},{1,5},{5... | collective-permute-start | bytes 368648 | tf_op jit(solution)/shard_map/ppermute | solution.py:19
  41.9 9.3 %collective-permute-start.16 = (bf16[2,160,384]{2,1,0:T(8,128)(2,1)S(1)}, bf16[2,160,384]{2,1,0:T(8,128)(2,1)S(1)}, u32[]{:S(2)}, u32[]{:S(2)}) collective-permute-start(bf16[2,160,384]{2,1,0:T(8,128)(2,1)S(1)} %pad_maximum_fusion.9), channel_id=1, source_target_pairs={{0,8},{4,12},{8,0},{12,4},{16,24},{20,28},{24,16},{28,20},{1,9},{5... | collective-permute-start | bytes 737288 | tf_op jit(solution)/shard_map/ppermute | solution.py:19
  45.7 9.5 %collective-permute-start.15 = (bf16[2,48,1536]{2,1,0:T(8,128)(2,1)S(1)}, bf16[2,48,1536]{2,1,0:T(8,128)(2,1)S(1)}, u32[]{:S(2)}, u32[]{:S(2)}) collective-permute-start(bf16[2,48,1536]{2,1,0:T(8,128)(2,1)S(1)} %pad_maximum_fusion.7), channel_id=1, source_target_pairs={{0,8},{4,12},{8,0},{12,4},{16,24},{20,28},{24,16},{28,20},{1,9},{5... | collective-permute-start | bytes 884744 | tf_op jit(solution)/shard_map/ppermute | solution.py:19
  45.9 15.1 %collective-permute-start.25 = (bf16[16,48,384]{2,1,0:T(8,128)(2,1)S(1)}, bf16[16,48,384]{2,1,0:T(8,128)(2,1)}, u32[]{:S(2)}, u32[]{:S(2)}) collective-permute-start(bf16[16,48,384]{2,1,0:T(8,128)(2,1)S(1)} %constant_dynamic-update-slice_fusion.5.refs_5_.refs_2_), channel_id=1, source_target_pairs={{0,1},{1,0},{2,3},{3,2},{4,5},{5,4},{6,7},{7,6},{8,9},{9,8},{10,11... | collective-permute-start | bytes 1769480 | tf_op jit(solution)/shard_map/ppermute | solution.py:19
  47.4 14.2 %collective-permute-start.26 = (bf16[16,48,384]{2,1,0:T(8,128)(2,1)S(1)}, bf16[16,48,384]{2,1,0:T(8,128)(2,1)S(1)}, u32[]{:S(2)}, u32[]{:S(2)}) collective-permute-start(bf16[16,48,384]{2,1,0:T(8,128)(2,1)S(1)} %constant_dynamic-update-slice_fusion.10.refs_7_.refs_4_), channel_id=1, source_target_pairs={{0,1},{1,0},{2,3},{3,2},{4,5},{5,4},{6,7},{7,6},{8,9},{9,8},{10,11... | collective-permute-start | bytes 1769480 | tf_op jit(solution)/shard_map/ppermute | solution.py:19
  48.8 12.9 %collective-permute-start.24 = (bf16[16,64,384]{2,1,0:T(8,128)(2,1)S(1)}, bf16[16,64,384]{2,1,0:T(8,128)(2,1)S(1)}, u32[]{:S(2)}, u32[]{:S(2)}) collective-permute-start(bf16[16,64,384]{2,1,0:T(8,128)(2,1)S(1)} %constant_dynamic-update-slice_fusion.refs_3_.refs_0_), channel_id=1, source_target_pairs={{0,1},{1,0},{2,3},{3,2},{4,5},{5,4},{6,7},{7,6},{8,9},{9,8},{10,11... | collective-permute-start | bytes 2359304 | tf_op jit(solution)/shard_map/ppermute | solution.py:19
  55.4 23.7 %collective-permute-start.23 = (bf16[4,80,384]{2,1,0:T(8,128)(2,1)S(1)}, bf16[4,80,384]{2,1,0:T(8,128)(2,1)S(1)}, u32[]{:S(2)}, u32[]{:S(2)}) collective-permute-start(bf16[4,80,384]{2,1,0:T(8,128)(2,1)S(1)} %pad_maximum_fusion.10), channel_id=1, source_target_pairs={{0,16},{4,20},{8,24},{12,28},{16,0},{20,4},{24,8},{28,12},{1,17},{... | collective-permute-start | bytes 737288 | tf_op jit(solution)/shard_map/ppermute | solution.py:19
  57.8 21.4 %collective-permute-start.22 = (bf16[4,160,384]{2,1,0:T(8,128)(2,1)S(1)}, bf16[4,160,384]{2,1,0:T(8,128)(2,1)S(1)}, u32[]{:S(2)}, u32[]{:S(2)}) collective-permute-start(bf16[4,160,384]{2,1,0:T(8,128)(2,1)S(1)} %pad_maximum_fusion.1), channel_id=1, source_target_pairs={{0,4},{4,0},{8,12},{12,8},{16,20},{20,16},{24,28},{28,24},{1,5},{5... | collective-permute-start | bytes 1474568 | tf_op jit(solution)/shard_map/ppermute | solution.py:19
  61.0 18.1 %collective-permute-start.21 = (bf16[4,48,1536]{2,1,0:T(8,128)(2,1)S(1)}, bf16[4,48,1536]{2,1,0:T(8,128)(2,1)S(1)}, u32[]{:S(2)}, u32[]{:S(2)}) collective-permute-start(bf16[4,48,1536]{2,1,0:T(8,128)(2,1)S(1)} %pad_maximum_fusion), channel_id=1, source_target_pairs={{0,2},{1,3},{2,0},{3,1},{4,6},{5,7},{6,4},{7,5},{8,10},{9,11},{10,... | collective-permute-start | bytes 1769480 | tf_op jit(solution)/shard_map/ppermute | solution.py:19
  79.9 20.9 %collective-permute-start.29 = (bf16[8,80,384]{2,1,0:T(8,128)(2,1)S(1)}, bf16[8,80,384]{2,1,0:T(8,128)(2,1)S(1)}, u32[]{:S(2)}, u32[]{:S(2)}) collective-permute-start(bf16[8,80,384]{2,1,0:T(8,128)(2,1)S(1)} %get-tuple-element.305), channel_id=1, source_target_pairs={{0,8},{4,12},{8,0},{12,4},{16,24},{20,28},{24,16},{28,20},{1,9},{5... | collective-permute-start | bytes 1474568 | tf_op jit(solution)/shard_map/ppermute | solution.py:19
  83.2 20.7 %collective-permute-start.28 = (bf16[8,160,384]{2,1,0:T(8,128)(2,1)S(1)}, bf16[8,160,384]{2,1,0:T(8,128)(2,1)S(1)}, u32[]{:S(2)}, u32[]{:S(2)}) collective-permute-start(bf16[8,160,384]{2,1,0:T(8,128)(2,1)S(1)} %get-tuple-element.297), channel_id=1, source_target_pairs={{0,2},{1,3},{2,0},{3,1},{4,6},{5,7},{6,4},{7,5},{8,10},{9,11},{10,... | collective-permute-start | bytes 2949128 | tf_op jit(solution)/shard_map/ppermute | solution.py:19
  84.8 24.7 %collective-permute-start.27 = (bf16[8,48,1536]{2,1,0:T(8,128)(2,1)S(1)}, bf16[8,48,1536]{2,1,0:T(8,128)(2,1)S(1)}, u32[]{:S(2)}, u32[]{:S(2)}) collective-permute-start(bf16[8,48,1536]{2,1,0:T(8,128)(2,1)S(1)} %get-tuple-element.285), channel_id=1, source_target_pairs={{0,4},{4,0},{8,12},{12,8},{16,20},{20,16},{24,28},{28,24},{1,5},{5... | collective-permute-start | bytes 3538952 | tf_op jit(solution)/shard_map/ppermute | solution.py:19
  109.7 9.0 %collective-permute-start.30 = (bf16[16,48,1536]{2,1,0:T(8,128)(2,1)S(1)}, bf16[16,48,1536]{2,1,0:T(8,128)(2,1)S(1)}, u32[]{:S(2)}, u32[]{:S(2)}) collective-permute-start(bf16[16,48,1536]{2,1,0:T(8,128)(2,1)S(1)} %constant_dynamic-update-slice_fusion.21.refs_0_), channel_id=1, source_target_pairs={{0,1},{1,0},{2,3},{3,2},{4,5},{5,4},{6,7},{7,6},{8,9},{9,8},{10,11... | collective-permute-start | bytes 7077896 | tf_op jit(solution)/shard_map/ppermute | solution.py:19
  111.0 7.7 %collective-permute-start.31 = (bf16[16,160,384]{2,1,0:T(8,128)(2,1)}, bf16[16,160,384]{2,1,0:T(8,128)(2,1)S(1)}, u32[]{:S(2)}, u32[]{:S(2)}) collective-permute-start(bf16[16,160,384]{2,1,0:T(8,128)(2,1)} %constant_dynamic-update-slice_fusion.24.refs_2_), channel_id=1, source_target_pairs={{0,1},{1,0},{2,3},{3,2},{4,5},{5,4},{6,7},{7,6},{8,9},{9,8},{10,11... | collective-permute-start | bytes 5898248 | tf_op jit(solution)/shard_map/ppermute | solution.py:19
  112.2 6.5 %collective-permute-start.32 = (bf16[16,80,384]{2,1,0:T(8,128)(2,1)}, bf16[16,80,384]{2,1,0:T(8,128)(2,1)S(1)}, u32[]{:S(2)}, u32[]{:S(2)}) collective-permute-start(bf16[16,80,384]{2,1,0:T(8,128)(2,1)} %constant_dynamic-update-slice_fusion.27.refs_4_), channel_id=1, source_target_pairs={{0,1},{1,0},{2,3},{3,2},{4,5},{5,4},{6,7},{7,6},{8,9},{9,8},{10,11... | collective-permute-start | bytes 2949128 | tf_op jit(solution)/shard_map/ppermute | solution.py:19
  187.4 9.0 %collective-permute-start.33 = (bf16[16,48,1536]{2,1,0:T(8,128)(2,1)}, bf16[16,48,1536]{2,1,0:T(8,128)(2,1)S(1)}, u32[]{:S(2)}, u32[]{:S(2)}) collective-permute-start(bf16[16,48,1536]{2,1,0:T(8,128)(2,1)} %get-tuple-element.172), channel_id=1, source_target_pairs={{0,1},{1,0},{2,3},{3,2},{4,5},{5,4},{6,7},{7,6},{8,9},{9,8},{10,11... | collective-permute-start | bytes 7077896 | tf_op jit(solution)/shard_map/ppermute | solution.py:19
  187.6 8.8 %collective-permute-start.34 = (bf16[16,160,384]{2,1,0:T(8,128)(2,1)}, bf16[16,160,384]{2,1,0:T(8,128)(2,1)S(1)}, u32[]{:S(2)}, u32[]{:S(2)}) collective-permute-start(bf16[16,160,384]{2,1,0:T(8,128)(2,1)} %get-tuple-element.173), channel_id=1, source_target_pairs={{0,1},{1,0},{2,3},{3,2},{4,5},{5,4},{6,7},{7,6},{8,9},{9,8},{10,11... | collective-permute-start | bytes 5898248 | tf_op jit(solution)/shard_map/ppermute | solution.py:19
  188.0 8.5 %collective-permute-start.35 = (bf16[16,80,384]{2,1,0:T(8,128)(2,1)}, bf16[16,80,384]{2,1,0:T(8,128)(2,1)S(1)}, u32[]{:S(2)}, u32[]{:S(2)}) collective-permute-start(bf16[16,80,384]{2,1,0:T(8,128)(2,1)} %get-tuple-element.174), channel_id=1, source_target_pairs={{0,1},{1,0},{2,3},{3,2},{4,5},{5,4},{6,7},{7,6},{8,9},{9,8},{10,11... | collective-permute-start | bytes 2949128 | tf_op jit(solution)/shard_map/ppermute | solution.py:19
  197.5 20.1 %collective-permute-start.36 = (bf16[8,80,384]{2,1,0:T(8,128)(2,1)}, bf16[8,80,384]{2,1,0:T(8,128)(2,1)}, u32[]{:S(2)}, u32[]{:S(2)}) collective-permute-start(bf16[8,80,384]{2,1,0:T(8,128)(2,1)} %get-tuple-element.273), channel_id=1, source_target_pairs={{0,8},{4,12},{8,0},{12,4},{16,24},{20,28},{24,16},{28,20},{1,9},{5... | collective-permute-start | bytes 1474568 | tf_op jit(solution)/shard_map/ppermute | solution.py:19
  199.5 33.3 %collective-permute-start.38 = (bf16[8,160,384]{2,1,0:T(8,128)(2,1)}, bf16[8,160,384]{2,1,0:T(8,128)(2,1)S(1)}, u32[]{:S(2)}, u32[]{:S(2)}) collective-permute-start(bf16[8,160,384]{2,1,0:T(8,128)(2,1)} %get-tuple-element.263), channel_id=1, source_target_pairs={{0,2},{1,3},{2,0},{3,1},{4,6},{5,7},{6,4},{7,5},{8,10},{9,11},{10,... | collective-permute-start | bytes 2949128 | tf_op jit(solution)/shard_map/ppermute | solution.py:19
  200.8 32.1 %collective-permute-start.37 = (bf16[8,48,1536]{2,1,0:T(8,128)(2,1)S(1)}, bf16[8,48,1536]{2,1,0:T(8,128)(2,1)S(1)}, u32[]{:S(2)}, u32[]{:S(2)}) collective-permute-start(bf16[8,48,1536]{2,1,0:T(8,128)(2,1)S(1)} %get-tuple-element.260), channel_id=1, source_target_pairs={{0,4},{4,0},{8,12},{12,8},{16,20},{20,16},{24,28},{28,24},{1,5},{5... | collective-permute-start | bytes 3538952 | tf_op jit(solution)/shard_map/ppermute | solution.py:19
  218.7 14.2 %collective-permute-start.39 = (bf16[4,80,384]{2,1,0:T(8,128)(2,1)S(1)}, bf16[4,80,384]{2,1,0:T(8,128)(2,1)S(1)}, u32[]{:S(2)}, u32[]{:S(2)}) collective-permute-start(bf16[4,80,384]{2,1,0:T(8,128)(2,1)S(1)} %get-tuple-element.283), channel_id=1, source_target_pairs={{0,16},{4,20},{8,24},{12,28},{16,0},{20,4},{24,8},{28,12},{1,17},{... | collective-permute-start | bytes 737288 | tf_op jit(solution)/shard_map/ppermute | solution.py:19
  232.9 14.5 %collective-permute-start.42 = (bf16[2,80,384]{2,1,0:T(8,128)(2,1)S(1)}, bf16[2,80,384]{2,1,0:T(8,128)(2,1)S(1)}, u32[]{:S(2)}, u32[]{:S(2)}) collective-permute-start(bf16[2,80,384]{2,1,0:T(8,128)(2,1)S(1)} %get-tuple-element.295), channel_id=1, source_target_pairs={{0,4},{4,0},{8,12},{12,8},{16,20},{20,16},{24,28},{28,24},{1,5},{5... | collective-permute-start | bytes 368648 | tf_op jit(solution)/shard_map/ppermute | solution.py:19
  234.8 13.7 %collective-permute-start.41 = (bf16[4,160,384]{2,1,0:T(8,128)(2,1)S(1)}, bf16[4,160,384]{2,1,0:T(8,128)(2,1)S(1)}, u32[]{:S(2)}, u32[]{:S(2)}) collective-permute-start(bf16[4,160,384]{2,1,0:T(8,128)(2,1)S(1)} %get-tuple-element.271), channel_id=1, source_target_pairs={{0,4},{4,0},{8,12},{12,8},{16,20},{20,16},{24,28},{28,24},{1,5},{5... | collective-permute-start | bytes 1474568 | tf_op jit(solution)/shard_map/ppermute | solution.py:19
  235.6 14.2 %collective-permute-start.40 = (bf16[4,48,1536]{2,1,0:T(8,128)(2,1)S(1)}, bf16[4,48,1536]{2,1,0:T(8,128)(2,1)S(1)}, u32[]{:S(2)}, u32[]{:S(2)}) collective-permute-start(bf16[4,48,1536]{2,1,0:T(8,128)(2,1)S(1)} %get-tuple-element.264), channel_id=1, source_target_pairs={{0,2},{1,3},{2,0},{3,1},{4,6},{5,7},{6,4},{7,5},{8,10},{9,11},{10,... | collective-permute-start | bytes 1769480 | tf_op jit(solution)/shard_map/ppermute | solution.py:19
  250.4 19.5 %collective-permute-start.49 = (bf16[1,80,384]{2,1,0:T(8,128)(2,1)S(1)}, bf16[1,80,384]{2,1,0:T(8,128)(2,1)S(1)}, u32[]{:S(2)}, u32[]{:S(2)}) collective-permute-start(bf16[1,80,384]{2,1,0:T(8,128)(2,1)S(1)} %add_convert_fusion.39), channel_id=1, source_target_pairs={{0,2},{1,3},{2,0},{3,1},{4,6},{5,7},{6,4},{7,5},{8,10},{9,11},{10,... | collective-permute-start | bytes 184328 | tf_op jit(solution)/shard_map/ppermute | solution.py:19
  251.8 18.2 %collective-permute-start.48 = (bf16[2,160,384]{2,1,0:T(8,128)(2,1)S(1)}, bf16[2,160,384]{2,1,0:T(8,128)(2,1)S(1)}, u32[]{:S(2)}, u32[]{:S(2)}) collective-permute-start(bf16[2,160,384]{2,1,0:T(8,128)(2,1)S(1)} %get-tuple-element.279), channel_id=1, source_target_pairs={{0,8},{4,12},{8,0},{12,4},{16,24},{20,28},{24,16},{28,20},{1,9},{5... | collective-permute-start | bytes 737288 | tf_op jit(solution)/shard_map/ppermute | solution.py:19
  252.0 17.9 %collective-permute-start.47 = (bf16[2,48,1536]{2,1,0:T(8,128)(2,1)S(1)}, bf16[2,48,1536]{2,1,0:T(8,128)(2,1)S(1)}, u32[]{:S(2)}, u32[]{:S(2)}) collective-permute-start(bf16[2,48,1536]{2,1,0:T(8,128)(2,1)S(1)} %get-tuple-element.275), channel_id=1, source_target_pairs={{0,8},{4,12},{8,0},{12,4},{16,24},{20,28},{24,16},{28,20},{1,9},{5... | collective-permute-start | bytes 884744 | tf_op jit(solution)/shard_map/ppermute | solution.py:19
  254.4 15.6 %collective-permute-start.46 = (bf16[8,80,384]{2,1,0:T(8,128)(2,1)S(1)}, bf16[8,80,384]{2,1,0:T(8,128)(2,1)S(1)}, u32[]{:S(2)}, u32[]{:S(2)}) collective-permute-start(bf16[8,80,384]{2,1,0:T(8,128)(2,1)S(1)} %get-tuple-element.267), channel_id=1, source_target_pairs={{0,2},{1,3},{2,0},{3,1},{4,6},{5,7},{6,4},{7,5},{8,10},{9,11},{10,... | collective-permute-start | bytes 1474568 | tf_op jit(solution)/shard_map/ppermute | solution.py:19
  255.9 14.1 %collective-permute-start.45 = (bf16[8,80,384]{2,1,0:T(8,128)(2,1)S(1)}, bf16[8,80,384]{2,1,0:T(8,128)(2,1)S(1)}, u32[]{:S(2)}, u32[]{:S(2)}) collective-permute-start(bf16[8,80,384]{2,1,0:T(8,128)(2,1)S(1)} %get-tuple-element.269), channel_id=1, source_target_pairs={{0,4},{4,0},{8,12},{12,8},{16,20},{20,16},{24,28},{28,24},{1,5},{5... | collective-permute-start | bytes 1474568 | tf_op jit(solution)/shard_map/ppermute | solution.py:19
  270.0 13.4 %collective-permute-start.52 = (bf16[1,48,1536]{2,1,0:T(8,128)(2,1)S(1)}, bf16[1,48,1536]{2,1,0:T(8,128)(2,1)S(1)}, u32[]{:S(2)}, u32[]{:S(2)}) collective-permute-start(bf16[1,48,1536]{2,1,0:T(8,128)(2,1)S(1)} %add_convert_fusion.25), channel_id=1, source_target_pairs={{0,16},{4,20},{8,24},{12,28},{16,0},{20,4},{24,8},{28,12},{1,17},{... | collective-permute-start | bytes 442376 | tf_op jit(solution)/shard_map/ppermute | solution.py:19
  270.2 13.2 %collective-permute-start.51 = (bf16[4,80,384]{2,1,0:T(8,128)(2,1)S(1)}, bf16[4,80,384]{2,1,0:T(8,128)(2,1)S(1)}, u32[]{:S(2)}, u32[]{:S(2)}) collective-permute-start(bf16[4,80,384]{2,1,0:T(8,128)(2,1)S(1)} %get-tuple-element.277), channel_id=1, source_target_pairs={{0,4},{4,0},{8,12},{12,8},{16,20},{20,16},{24,28},{28,24},{1,5},{5... | collective-permute-start | bytes 737288 | tf_op jit(solution)/shard_map/ppermute | solution.py:19
  270.9 12.5 %collective-permute-start.50 = (bf16[4,80,384]{2,1,0:T(8,128)(2,1)S(1)}, bf16[4,80,384]{2,1,0:T(8,128)(2,1)S(1)}, u32[]{:S(2)}, u32[]{:S(2)}) collective-permute-start(bf16[4,80,384]{2,1,0:T(8,128)(2,1)S(1)} %get-tuple-element.280), channel_id=1, source_target_pairs={{0,2},{1,3},{2,0},{3,1},{4,6},{5,7},{6,4},{7,5},{8,10},{9,11},{10,... | collective-permute-start | bytes 737288 | tf_op jit(solution)/shard_map/ppermute | solution.py:19
  271.9 11.5 %collective-permute-start.53 = (bf16[1,160,384]{2,1,0:T(8,128)(2,1)S(1)}, bf16[1,160,384]{2,1,0:T(8,128)(2,1)S(1)}, u32[]{:S(2)}, u32[]{:S(2)}) collective-permute-start(bf16[1,160,384]{2,1,0:T(8,128)(2,1)S(1)} %add_convert_fusion.31), channel_id=1, source_target_pairs={{0,16},{4,20},{8,24},{12,28},{16,0},{20,4},{24,8},{28,12},{1,17},{... | collective-permute-start | bytes 368648 | tf_op jit(solution)/shard_map/ppermute | solution.py:19
  283.7 7.6 %collective-permute-start.54 = (bf16[2,80,384]{2,1,0:T(8,128)(2,1)S(1)}, bf16[2,80,384]{2,1,0:T(8,128)(2,1)S(1)}, u32[]{:S(2)}, u32[]{:S(2)}) collective-permute-start(bf16[2,80,384]{2,1,0:T(8,128)(2,1)S(1)} %get-tuple-element.292), channel_id=1, source_target_pairs={{0,8},{4,12},{8,0},{12,4},{16,24},{20,28},{24,16},{28,20},{1,9},{5... | collective-permute-start | bytes 368648 | tf_op jit(solution)/shard_map/ppermute | solution.py:19
  291.3 6.4 %collective-permute-start.57 = (bf16[1,80,384]{2,1,0:T(8,128)(2,1)S(1)}, bf16[1,80,384]{2,1,0:T(8,128)(2,1)S(1)}, u32[]{:S(2)}, u32[]{:S(2)}) collective-permute-start(bf16[1,80,384]{2,1,0:T(8,128)(2,1)S(1)} %add_convert_fusion.36), channel_id=1, source_target_pairs={{0,16},{4,20},{8,24},{12,28},{16,0},{20,4},{24,8},{28,12},{1,17},{... | collective-permute-start | bytes 184328 | tf_op jit(solution)/shard_map/ppermute | solution.py:19
  292.5 6.5 %collective-permute-start.56 = (bf16[1,80,384]{2,1,0:T(8,128)(2,1)S(1)}, bf16[1,80,384]{2,1,0:T(8,128)(2,1)S(1)}, u32[]{:S(2)}, u32[]{:S(2)}) collective-permute-start(bf16[1,80,384]{2,1,0:T(8,128)(2,1)S(1)} %add_convert_fusion.37), channel_id=1, source_target_pairs={{0,16},{4,20},{8,24},{12,28},{16,0},{20,4},{24,8},{28,12},{1,17},{... | collective-permute-start | bytes 184328 | tf_op jit(solution)/shard_map/ppermute | solution.py:19
  (31 other events, 156.1 us)

commit v5 on v4

--- a/solution.py
+++ b/solution.py
@@ -28,10 +28,18 @@
     return (far + across + near, far + near + across, across + near + far)
 
 
+def far_stages(mesh):
+    return mesh.shape["dp"].bit_length() - 2
+
+
+def third_of(half):
+    return half // 3 // 16 * 16
+
+
 def fits(mesh, rows, width, hidden):
     sizes = (mesh.shape["dp"], mesh.shape["fsdp"])
     powers = all(s >= 2 and s & (s - 1) == 0 for s in sizes)
-    return powers and all(r % 32 == 0 for r in rows) and width % 64 == 0 and hidden % 128 == 0 and 32 < rows[0] <= 128
+    return powers and all(r % 32 == 0 for r in rows) and width % 64 == 0 and hidden % 128 == 0 and 96 <= rows[0] <= 128
 
 
 def place_of(stages, dp, fsdp, me_ref):
@@ -415,7 +423,7 @@
     total, width = x_ref.shape
     inner = wi.shape[1]
     tile = min(256, slots)
-    piece = min(1024, inner)
+    piece = min(512, inner)
     sums_ref[...] = jnp.zeros_like(sums_ref)
     wait_all(loads[0])
     first[...] = x_ref[...].astype(jnp.float32) + dot(att_ref[...], wo[...]) + vec_ref[2:3, :]
@@ -429,14 +437,19 @@
         middle_low = middle.astype(jnp.bfloat16)
         mid[rows, :] = middle_low
         second = middle + vec_ref[3:4, :]
+        def ahead(at):
+            return dot(middle_low, wi[:, at : at + piece]) + hb_ref[:, at : at + piece]
+
+        hidden = ahead(0)
         for at in range(0, inner, piece):
             here = slice(at, at + piece)
-            hidden = dot(middle_low, wi[:, here]) + hb_ref[:, here]
+            following = ahead(at + piece) if at + piece < inner else None
             active, slope = gelu_pair(hidden)
             active = active.astype(jnp.bfloat16)
             act[rows, here] = active
             slope_s[rows, here] = slope.astype(jnp.bfloat16)
             second = second + dot(active, wf[here, :])
+            hidden = following
         normed, factor = normalize(second)
         start = t * tile
         slot = start % slots + lax.broadcasted_iota(jnp.int32, (tile, 1), 0)
@@ -452,7 +465,7 @@
         sums_ref[2:3, :] += jnp.sum(low.astype(jnp.float32), axis=0, keepdims=True)
         return carry
 
-    lax.fori_loop(0, total // tile, forward, 0)
+    lax.fori_loop(0, total // tile, forward, 0, unroll=2)
     mid_t[...] = mid[...].T
     chunk = held_i.shape[2]
     steps = inner // chunk
@@ -500,7 +513,7 @@
         gf_ref[...] += dot_last(hidden, wi[:, here])
         return carry
 
-    lax.fori_loop(0, steps, backward, 0, unroll=2)
+    lax.fori_loop(0, steps, backward, 0, unroll=4)
 
     def finish(t, carry):
         rows = pl.ds(pl.multiple_of(t * tile, tile), tile)
@@ -516,7 +529,7 @@
         do_ref[rows, :] = dot_last(branch, wo[...]).astype(jnp.bfloat16)
         return carry
 
-    lax.fori_loop(0, total // tile, finish, 0)
+    lax.fori_loop(0, total // tile, finish, 0, unroll=4)
     held_a[...] = dot_first(att_ref[...], low_s[...]).astype(jnp.bfloat16)
     if cuts is None:
         last = [pltpu.make_async_copy(held_a, grads[0], sems_a.at[0])]
@@ -544,21 +557,14 @@
 class FeedSplit:
     def __init__(self, half, half_outer, width, width_inner):
         self.half, self.half_outer, self.width, self.width_inner = half, half_outer, width, width_inner
-        self.groups = width_inner // width
-        self.extra = 0
         self.most = max(16, half_outer // 6 * 5 // 16 * 16)
         self.rest = half_outer - self.most
         self.folded = half + self.rest
 
     def spots(self):
-        kept = self.half - self.extra
-        folds = [
-            (2, self.folded + g * self.extra, kept, self.extra, g * self.width)
-            for g in range(self.groups if self.extra else 0)
-        ]
         return [
             (self.half, self.width, [(2, 0, 0, self.half, 0)]),
-            (self.half, self.width_inner, [(0, 0, 0, kept, 0)] + folds),
+            (self.half, self.width_inner, [(0, 0, 0, self.half, 0)]),
             (
                 self.half_outer,
                 self.width,
@@ -570,7 +576,7 @@
 class FeedCuts:
     def __init__(self, orders, split):
         self.split = split
-        rows = (split.half - split.extra, split.most, split.folded + split.groups * split.extra)
+        rows = (split.half, split.most, split.folded)
         widths = (split.width_inner, split.width, split.width)
         self.cuts = [Cut(*sizes) for sizes in zip(orders, rows, widths)]
 
@@ -579,16 +585,9 @@
 
     def inner(self, grads, step, chunk):
         split = self.split
-        kept = split.half - split.extra
         parts = split.width_inner // chunk
         into = pl.multiple_of(step % parts * chunk, 128)
-        listed = [(self.cuts[0], grads[0:2], (0, kept, 0), [(0, step // parts, into, chunk)])]
-        for g in range(chunk // split.width if split.extra else 0):
-            group = step % parts * (chunk // split.width) + g
-            at = pl.multiple_of(split.folded + group * split.extra, 16)
-            columns = [(g * split.width, step // parts, 0, split.width)]
-            listed.append((self.cuts[2], grads[4:6], (kept, split.extra, at), columns))
-        return listed
+        return [(self.cuts[0], grads[0:2], (0, split.half, 0), [(0, step // parts, into, chunk)])]
 
     def outer(self, grads, width):
         split = self.split
@@ -624,7 +623,7 @@
         split = cuts.split
         pairs = width // split.width
         copies = 2 * (chunk // split.half_outer) * pairs
-        copies += width // split.half * (1 + chunk // split.width)
+        copies += width // split.half
         copies_last = width // split.half * pairs
     return pl.pallas_call(
         functools.partial(feed_kernel, source, cuts, slots),
@@ -1064,18 +1063,16 @@
             return jnp.concatenate(halves, axis=0)
 
         one, rest, inner = pair_up((both(query, key, value), both(output, outer), inner))
-        self.one = [
-            jnp.concatenate([one[:half], small], axis=0)[None],
-            one[half : 2 * half][None],
-            one[2 * half :][None],
-        ]
+        third = third_of(half)
+        self.one = [one[:half], one[2 * half : 2 * half + third], small]
+        self.cut_at = sum(part.shape[0] for part in self.one)
+        self.one += [one[half : 2 * half], one[2 * half + third :]]
+        self.one = [jnp.concatenate(self.one, axis=0)[None]]
         split = self.split = FeedSplit(half, half_outer, 2 * query.shape[1], inner.shape[1])
-        folded = inner[half - split.extra :].reshape(split.extra, split.groups, split.width)
-        folded = folded.swapaxes(0, 1).reshape(split.groups * split.extra, split.width)
         self.two = [
-            inner[: half - split.extra][None],
+            inner[None],
             rest[half : half + split.most][None],
-            jnp.concatenate([rest[:half], rest[half + split.most :], folded], axis=0)[None],
+            jnp.concatenate([rest[:half], rest[half + split.most :]], axis=0)[None],
         ]
 
     def send(self, parts, stage):
@@ -1086,24 +1083,27 @@
 
     def first(self):
         self.prepare()
-        count = len(self.orders[0])
+        count, far = len(self.orders[0]), far_stages(self.mesh)
         self.stage = 0
-        for stage in range(count):
+        for stage in range(far):
+            self.one = self.join(self.one, self.send(self.one, stage))
+        joined = self.one[0]
+        self.one = [joined[:, : self.cut_at], joined[:, self.cut_at :]]
+        for stage in range(far, count):
             arriving = self.send(self.one, stage)
-            ahead = None
-            if stage >= count - 2:
-                self.two = after(self.two, self.one)
-                ahead = self.send(self.two, self.stage)
-                self.stage += 1
+            self.two = after(self.two, self.one)
+            ahead = self.send(self.two, self.stage)
+            self.stage += 1
             self.one = self.join(self.one, arriving)
-            if ahead is not None:
-                self.two = self.join(self.two, after(ahead, self.one))
+            self.two = self.join(self.two, after(ahead, self.one))
         self.two = after(self.two, self.one)
         others = [swap(part, "fsdp", 0) for part in self.one]
         half, width = self.shards[0].shape[0] // 2, self.one[0].shape[2]
-        spots = [(half, width, [(i, 0, 0, half, 0)]) for i in range(3)]
+        third = third_of(half)
+        thirds = [(0, half, 0, third, 0), (1, half, third, half - third, 0)]
+        spots = [(half, width, [(0, 0, 0, half, 0)]), (half, width, [(1, 0, 0, half, 0)]), (half, width, thirds)]
         operands = [array for pair in zip(self.one, others) for array in pair]
-        return Source(operands, self.orders, spots, self.mesh.shape["dp"], half), ()
+        return Source(operands, self.orders, spots, self.mesh.shape["dp"], half + third), ()
 
     def before(self, seq, inputs):
         if self.stage == len(self.orders[0]):
@@ -1141,6 +1141,13 @@
         self.keep = total_of(self.keep[:half], self.arriving[:half], jnp.bfloat16)
         self.arriving = arriving
         return send
+
+    def join(self, other):
+        both = Part.__new__(Part)
+        both.keep = jnp.concatenate([self.keep, other.keep], axis=1)
+        both.arriving = jnp.concatenate([self.arriving, other.arriving], axis=1)
+        both.stages = list(self.stages)
+        return both
 
     def finish(self):
         while self.stages:
@@ -1157,7 +1164,8 @@
         self.dp_size = mesh.shape["dp"]
         self.split = FeedSplit(half, half_outer, width, width_inner)
         self.feed_cuts = FeedCuts(self.orders, self.split)
-        self.third = half // 3 // 16 * 16
+        self.third = third_of(half)
+        self.far = far_stages(mesh)
         rows = (half + self.third + SMALL_ROWS, 2 * half - self.third)
         self.first_cuts = [Cut(order, r, width) for order, r in zip(self.orders, rows)]
 
@@ -1167,7 +1175,7 @@
         ]
 
     def step(self, at, state):
-        parts = {0: self.behind, 2: self.behind[2:], 3: self.behind}.get(at, [])
+        parts = {0: self.behind, 2: self.behind[2:], 3: self.behind[:2]}.get(at, [])
         if not parts:
             return state
         state = meet(state, parts)
@@ -1186,24 +1194,26 @@
     def totals(self, passing):
         half, half_outer = self.shards[0].shape[0] // 2, self.shards[5].shape[0] // 2
         columns = self.shards[6].shape[1]
-        parts = self.front + self.behind
+        parts, front = self.front + self.behind, self.front
         passing = meet(passing, parts)
-        while any(part.stages for part in parts):
+        while len(front[0].stages) > self.far:
             for part in parts:
                 if part.stages:
                     part.step()
-            meet((), parts)
-        one, two = [part.finish() for part in self.front]
-        third = self.third
+            meet((), front)
+        joint = front[0].join(front[1])
+        cut_at = front[0].keep.shape[1]
+        if joint.stages:
+            joint.step()
         inner, outer, rest = [part.finish() for part in self.behind]
+        split = self.split
+        outer = jnp.concatenate([outer, rest[half : split.folded]], axis=0)
+        settled = settle(jnp.concatenate([rest[:half], outer]), (half, half_outer)) + settle(inner, (half,))
+        output, outer, inner = meet(settled, [joint])
+        total = joint.finish()
+        one, two, third = total[:cut_at], total[cut_at:], self.third
         thirds = [one[half : half + third], two[half:]]
         query, key, value = settle(jnp.concatenate([one[:half], two[:half], *thirds]), (half,) * 3)
-        split = self.split
-        folded = rest[split.folded :].reshape(split.groups, split.extra, split.width)
-        folded = folded.swapaxes(0, 1).reshape(split.extra, split.width_inner)
-        (inner,) = settle(jnp.concatenate([inner, folded], axis=0), (half,))
-        outer = jnp.concatenate([outer, rest[half : split.folded]], axis=0)
-        output, outer = settle(jnp.concatenate([rest[:half], outer]), (half, half_outer))
         rows = one[half + third :, :columns]
         split = 4 + self.shards[7].shape[0] // columns
         return passing, (

time: 314 us -> 306 us (0.975)
  starting transfers between devices: 64.6 us -> 49.1 us
  waiting for transfers between devices: 58.5 us -> 69.9 us
    ppermute x61 -> x52, starting transfers between devices: 64.6 us -> 49.1 us  [swap(): return lax.ppermute(value, axis, [(i, i ^ 1 << bit) for i in range(size)])]
    ppermute x61 -> x52, waiting for transfers between devices: 58.5 us -> 69.9 us  [swap(): return lax.ppermute(value, axis, [(i, i ^ 1 << bit) for i in range(size)])]
    pallas_call x1, Pallas kernels: 66.4 us -> 60 us  [feed(): pl.pallas_call(functools.partial(feed_kernel, source, cuts, slots), in_sp...]
    unnamed x55 -> x51, local copies, waits for them, and re-layouts: 9.06 us -> 9.92 us
  transfers between devices with their start and end apart: 61 -> 52, of which waited for: 23 -> 17; matrix products, arithmetic and copies ran while one was open for 6% -> 6% of each run, Pallas kernels for 28% -> 30%
where the time goes in v5:
time: 306 us; the launch traced here: 300 us
  Pallas kernels  150 us (49%)
  waiting for transfers between devices  69.9 us (23%)
  starting transfers between devices  49.1 us (16%)
  local copies, waits for them, and re-layouts  16.8 us (5%)
  other arithmetic  12.9 us (4%)
    ppermute x52, waiting for transfers between devices, swap(): return lax.ppermute(value, axis, [(i, i ^ 1 << bit) for i in range(size)])  69.9 us
    pallas_call x1, Pallas kernels, feed(): pl.pallas_call(functools.partial(feed_kernel, source, cuts, slots), in_sp...  60 us
    ppermute x52, starting transfers between devices, swap(): return lax.ppermute(value, axis, [(i, i ^ 1 << bit) for i in range(size)])  49.1 us
    pallas_call x2, Pallas kernels, attend_forward(): pl.pallas_call(functools.partial(skip_refs, kernel, known, len(before)),...  33.2 us
    pallas_call x4, Pallas kernels, attend_backward(): pl.pallas_call(functools.partial(skip_refs, kernel, len(inputs), len(befo...  32.5 us
    pallas_call x1, Pallas kernels, input_grads(): pl.pallas_call(functools.partial(input_grad_kernel, source), in_specs=[SC...  13.4 us
    pallas_call x1, Pallas kernels, project_grads(): pl.pallas_call(functools.partial(project_grads_kernel, cuts, columns), in...  10.6 us
    unnamed x51, local copies, waits for them, and re-layouts  9.92 us
  transfers between devices with their start and end apart: 52, of which 17 were waited for; matrix products, arithmetic and copies ran while one was open for 6% of the time, Pallas kernels for 30%

profile of v5, /device:TPU:0, one launch (start us, length us, event | category | flops | bytes accessed | tf_op | source)
XLA Modules:
  0.0 300.1 jit_solution(16241830706442694924)
XLA Ops:
  6.0 4.1 %collective-permute-start.3 = (bf16[1,160,384]{2,1,0:T(8,128)(2,1)S(1)}, bf16[1,160,384]{2,1,0:T(8,128)(2,1)S(1)}, u32[]{:S(2)}, u32[]{:S(2)}) collective-permute-start(bf16[1,160,384]{2,1,0:T(8,128)(2,1)S(1)} %bitcast.43), channel_id=1, source_target_pairs={{0,16},{4,20},{8,24},{12,28},{16,0},{20,4},{24,8},{28,12},{1,17},{... | collective-permute-start | bytes 368648 | tf_op jit(solution)/shard_map/ppermute | solution.py:19
  10.4 5.8 %collective-permute-done.3 = bf16[1,160,384]{2,1,0:T(8,128)(2,1)S(1)} collective-permute-done((bf16[1,160,384]{2,1,0:T(8,128)(2,1)S(1)}, bf16[1,160,384]{2,1,0:T(8,128)(2,1)S(1)}, u32[]{:S(2)}, u32[]{:S(2)}) %collective-permute-start.3) | collective-permute-done | bytes 122912 | tf_op jit(solution)/shard_map/ppermute | solution.py:19
  17.2 6.4 %collective-permute-done.4 = bf16[2,160,384]{2,1,0:T(8,128)(2,1)S(1)} collective-permute-done((bf16[2,160,384]{2,1,0:T(8,128)(2,1)S(1)}, bf16[2,160,384]{2,1,0:T(8,128)(2,1)S(1)}, u32[]{:S(2)}, u32[]{:S(2)}) %collective-permute-start.4) | collective-permute-done | bytes 245792 | tf_op jit(solution)/shard_map/ppermute | solution.py:19
  23.8 1.3 collective-permute-start.9
  25.1 1.5 collective-permute-start.8
  27.2 3.2 %collective-permute-start.6 = (bf16[1,160,384]{2,1,0:T(8,128)(2,1)S(1)}, bf16[1,160,384]{2,1,0:T(8,128)(2,1)S(1)}, u32[]{:S(2)}, u32[]{:S(2)}) collective-permute-start(bf16[1,160,384]{2,1,0:T(8,128)(2,1)S(1)} %slice_bitcast_fusion.1), channel_id=1, source_target_pairs={{0,16},{4,20},{8,24},{12,28},{16,0},{20,4},{24,8},{28,12},{1,17},{... | collective-permute-start | bytes 368648 | tf_op jit(solution)/shard_map/ppermute | solution.py:19
  30.5 1.6 collective-permute-start.14
  32.1 1.2 collective-permute-start.13
  33.4 6.0 %collective-permute-done.6 = bf16[1,160,384]{2,1,0:T(8,128)(2,1)S(1)} collective-permute-done((bf16[1,160,384]{2,1,0:T(8,128)(2,1)S(1)}, bf16[1,160,384]{2,1,0:T(8,128)(2,1)S(1)}, u32[]{:S(2)}, u32[]{:S(2)}) %collective-permute-start.6) | collective-permute-done | bytes 122912 | tf_op jit(solution)/shard_map/ppermute | solution.py:19
  39.4 2.1 collective-permute-done.5
  43.4 1.3 collective-permute-start.11
  45.7 2.1 collective-permute-done.12
  47.8 7.1 %collective-permute-done.11 = bf16[2,160,384]{2,1,0:T(8,128)(2,1)S(1)} collective-permute-done((bf16[2,160,384]{2,1,0:T(8,128)(2,1)S(1)}, bf16[2,160,384]{2,1,0:T(8,128)(2,1)S(1)}, u32[]{:S(2)}, u32[]{:S(2)}) %collective-permute-start.11) | collective-permute-done | bytes 245792 | tf_op jit(solution)/shard_map/ppermute | solution.py:19
  55.1 3.3 %collective-permute-start.17 = (bf16[4,80,384]{2,1,0:T(8,128)(2,1)S(1)}, bf16[4,80,384]{2,1,0:T(8,128)(2,1)S(1)}, u32[]{:S(2)}, u32[]{:S(2)}) collective-permute-start(bf16[4,80,384]{2,1,0:T(8,128)(2,1)S(1)} %pad_maximum_fusion.14), channel_id=1, source_target_pairs={{0,16},{4,20},{8,24},{12,28},{16,0},{20,4},{24,8},{28,12},{1,17},{... | collective-permute-start | bytes 737288 | tf_op jit(solution)/shard_map/ppermute | solution.py:19
  58.9 1.5 collective-permute-start.15
  65.0 16.8 %attend_forward.2 = (bf16[2,512,768]{2,1,0:T(8,128)(2,1)}, bf16[2,512,768]{2,1,0:T(8,128)(2,1)}, bf16[2,512,768]{2,1,0:T(8,128)(2,1)}, bf16[2,512,768]{2,1,0:T(8...) custom-call(s32[2]{0:T(128)} %bitcast.52, s32[2]{0:T(128)} %pad_add_fusion.refs_1_.me_ref, ...), custom_call_target="tpu_custom_call" | custom-call | flops 14000000000 | bytes 14000000 | tf_op jit(solution)/shard_map/attend_forward/pallas_call | solution.py:372
  82.6 1.7 collective-permute-start.22
  86.1 1.5 collective-permute-start.20
  87.6 16.4 %attend_forward.3 = (bf16[2,512,768]{2,1,0:T(8,128)(2,1)}, bf16[2,512,768]{2,1,0:T(8,128)(2,1)}, bf16[2,512,768]{2,1,0:T(8,128)(2,1)}, bf16[2,512,768]{2,1,0:T(8...) custom-call(s32[2]{0:T(128)} %bitcast.53, ...), custom_call_target="tpu_custom_call", output_to_operand_aliasing={{0}: (7, {}), {1}: (8, {}), {2}: (9, {}), {3}: (10, {}), {4... | custom-call | flops 14000000000 | bytes 14000000 | tf_op jit(solution)/shard_map/attend_forward/pallas_call | solution.py:372
  104.0 2.2 collective-permute-done.21
  106.3 5.4 %collective-permute-done.20 = bf16[8,48,1536]{2,1,0:T(8,128)(2,1)S(1)} collective-permute-done((bf16[8,48,1536]{2,1,0:T(8,128)(2,1)S(1)}, bf16[8,48,1536]{2,1,0:T(8,128)(2,1)S(1)}, u32[]{:S(2)}, u32[]{:S(2)}) %collective-permute-start.20) | collective-permute-done | bytes 1179680 | tf_op jit(solution)/shard_map/ppermute | solution.py:19
  111.7 1.1 constant_dynamic-update-slice_fusion.11.refs_0_
  114.3 7.2 %collective-permute-done.25.refs_5_ = bf16[16,80,384]{2,1,0:T(8,128)(2,1)S(1)} collective-permute-done((bf16[16,80,384]{2,1,0:T(8,128)(2,1)S(1)}, bf16[16,80,384]{2,1,0:T(8,128)(2,1)S(1)}, u32[]{:S(2)}, u32[]{:S(2)}) %collective-permute-start.25) | collective-permute-done | bytes 983072 | tf_op jit(solution)/shard_map/ppermute | solution.py:19
  121.5 1.4 copy-done.15
  123.2 60.0 %feed.1 = (bf16[1024,768]{1,0:T(8,128)(2,1)}, f32[1024,768]{1,0:T(8,128)}, bf16[1024,768]{1,0:T(8,128)(2,1)}, f32[1,3072]{1,0:T(1,128)}, f32[8,768]{1,0:T(8,128)...) custom-call(s32[2]{0:T(128)} %bitcast.54, ...), custom_call_target="tpu_custom_call" | custom-call | flops 60000002048 | bytes 60000000 | tf_op jit(solution)/shard_map/feed/pallas_call | solution.py:628
  183.9 8.2 %attend_backward.4 = (bf16[2,512,768]{2,1,0:T(8,128)(2,1)}, bf16[2,512,768]{2,1,0:T(8,128)(2,1)}, bf16[2,512,768]{2,1,0:T(8,128)(2,1)}) custom-call(s32[2]{0:T(128)} %bitcast.55, bf16[2,512,768]{2,1,0:T(8,128)(2,1)} %bitcast.61, bf16[2,512,768]{2,1,0:T(8,128)(2,1)} %get-tuple-element.148.refs_2_, bf16[2,512,768]{2,1,0:T(8,128)(2,1)} %get-tuple-element.149.refs_3_, ...), custom_call_target="tpu_custom_call" | custom-call | flops 7000000000 | bytes 7000000 | tf_op jit(solution)/shard_map/attend_backward/pallas_call | solution.py:720
  193.9 1.5 add_convert_fusion.2
  195.3 1.5 collective-permute-start.31
  197.6 1.6 collective-permute-start.30
  199.2 8.0 %attend_backward.5 = (bf16[2,512,768]{2,1,0:T(8,128)(2,1)}, bf16[2,512,768]{2,1,0:T(8,128)(2,1)}, bf16[2,512,768]{2,1,0:T(8,128)(2,1)}) custom-call(s32[2]{0:T(128)} %bitcast.56, bf16[2,512,768]{2,1,0:T(8,128)(2,1)} %bitcast.62, bf16[2,512,768]{2,1,0:T(8,128)(2,1)} %get-tuple-element.148.refs_2_, ...), custom_call_target="tpu_custom_call", output_to_operand_aliasing={{0}: (7, {}), {1}: (8, {}), {2}: (9, {})} | custom-call | flops 7000000000 | bytes 7000000 | tf_op jit(solution)/shard_map/attend_backward/pallas_call | solution.py:720
  207.2 8.1 %attend_backward.6 = (bf16[2,512,768]{2,1,0:T(8,128)(2,1)}, bf16[2,512,768]{2,1,0:T(8,128)(2,1)}, bf16[2,512,768]{2,1,0:T(8,128)(2,1)}) custom-call(s32[2]{0:T(128)} %bitcast.57, bf16[2,512,768]{2,1,0:T(8,128)(2,1)} %bitcast.63, bf16[2,512,768]{2,1,0:T(8,128)(2,1)} %get-tuple-element.148.refs_2_, ...), custom_call_target="tpu_custom_call", output_to_operand_aliasing={{0}: (7, {}), {1}: (8, {}), {2}: (9, {})} | custom-call | flops 7000000000 | bytes 7000000 | tf_op jit(solution)/shard_map/attend_backward/pallas_call | solution.py:720
  215.3 1.2 add_convert_fusion.23
  216.9 8.2 %attend_backward.7 = (bf16[2,512,768]{2,1,0:T(8,128)(2,1)}, bf16[2,512,768]{2,1,0:T(8,128)(2,1)}, bf16[2,512,768]{2,1,0:T(8,128)(2,1)}) custom-call(s32[2]{0:T(128)} %bitcast.58, bf16[2,512,768]{2,1,0:T(8,128)(2,1)} %bitcast.64, bf16[2,512,768]{2,1,0:T(8,128)(2,1)} %get-tuple-element.148.refs_2_, ...), custom_call_target="tpu_custom_call", output_to_operand_aliasing={{0}: (7, {}), {1}: (8, {}), {2}: (9, {})} | custom-call | flops 7000000000 | bytes 7000000 | tf_op jit(solution)/shard_map/attend_backward/pallas_call | solution.py:720
  225.8 1.6 collective-permute-start.33
  228.6 10.6 %project_grads.1 = (bf16[16,80,384]{2,1,0:T(8,128)(2,1)}, bf16[16,80,384]{2,1,0:T(8,128)(2,1)}, bf16[16,80,384]{2,1,0:T(8,128)(2,1)}, bf16[16,80,384]{2,1,0:T(8,128)(2,1)}) custom-call(s32[2]{0:T(128)} %pad_add_fusion.refs_1_.me_ref, bf16[1024,768]{1,0:T(8,128)(2,1)} %bitcast.51, bf16[1024,768]{1,0:T(8,128)(2,1)} %bitcast.66, bf16[1024,768]{1,0:T(8,128)(2,1)} %bitcast.68, ...), custom_call_target="tpu_custom_call" | custom-call | flops 8000000000 | bytes 8000000 | tf_op jit(solution)/shard_map/project_grads/pallas_call | solution.py:817
  239.2 2.8 collective-permute-done.32
  244.3 1.3 collective-permute-start.39
  246.4 1.2 collective-permute-start.38
  248.9 13.4 %input_grads.1 = bf16[1024,768]{1,0:T(8,128)(2,1)} custom-call(s32[2]{0:T(128)} %pad_add_fusion.refs_1_.me_ref, f32[1024,768]{1,0:T(8,128)} %get-tuple-element.215.gf_ref, bf16[1024,768]{1,0:T(8,128)(2,1)} %bitcast.67, bf16[1024,768]{1,0:T(8,128)(2,1)} %bitcast.69, bf16[1024,768]{1,0:T(8,128)(2,1)} %bitcast.71, bf16[16,80,384]{2,1,0:T(8,128)(2,1)} %copy-done.2, ...), custom_call_target="tpu_custom_call" | custom-call | flops 8000000000 | bytes 8000000 | tf_op jit(solution)/shard_map/input_grads/pallas_call | solution.py:848
  263.4 2.0 collective-permute-start.45
  265.4 1.1 collective-permute-start.47
  266.6 1.2 collective-permute-start.43
  267.9 1.2 collective-permute-start.42
  269.1 5.9 %collective-permute-done.45 = bf16[1,160,384]{2,1,0:T(8,128)(2,1)S(1)} collective-permute-done((bf16[1,160,384]{2,1,0:T(8,128)(2,1)S(1)}, bf16[1,160,384]{2,1,0:T(8,128)(2,1)S(1)}, u32[]{:S(2)}, u32[]{:S(2)}) %collective-permute-start.45) | collective-permute-done | bytes 122912 | tf_op jit(solution)/shard_map/ppermute | solution.py:19
  275.3 2.1 collective-permute-done.47
  279.6 7.5 %collective-permute-done.49 = bf16[2,160,384]{2,1,0:T(8,128)(2,1)S(1)} collective-permute-done((bf16[2,160,384]{2,1,0:T(8,128)(2,1)S(1)}, bf16[2,160,384]{2,1,0:T(8,128)(2,1)S(1)}, u32[]{:S(2)}, u32[]{:S(2)}) %collective-permute-start.49) | collective-permute-done | bytes 245792 | tf_op jit(solution)/shard_map/ppermute | solution.py:19
  287.1 1.7 collective-permute-start.50
  289.7 5.9 %collective-permute-done.50 = bf16[1,160,384]{2,1,0:T(8,128)(2,1)S(1)} collective-permute-done((bf16[1,160,384]{2,1,0:T(8,128)(2,1)S(1)}, bf16[1,160,384]{2,1,0:T(8,128)(2,1)S(1)}, u32[]{:S(2)}, u32[]{:S(2)}) %collective-permute-start.50) | collective-permute-done | bytes 122912 | tf_op jit(solution)/shard_map/ppermute | solution.py:19
  (202 shorter events, 38.5 us)
Async XLA Ops:
  3.8 13.3 %collective-permute-start = (bf16[48,768]{1,0:T(8,128)(2,1)S(1)}, bf16[48,768]{1,0:T(8,128)(2,1)S(1)}, u32[]{:S(2)}, u32[]{:S(2)}) collective-permute-start(bf16[48,768]{1,0:T(8,128)(2,1)S(1)} %get-tuple-element.303), channel_id=1, source_target_pairs={{0,1},{1,0},{2,3},{3,2},{4,5},{5,4},{6,7},{7,6},{8,9},{9,8},{10,11... | collective-permute-start | bytes 221192 | tf_op jit(solution)/shard_map/ppermute | solution.py:19
  6.0 10.2 %collective-permute-start.3 = (bf16[1,160,384]{2,1,0:T(8,128)(2,1)S(1)}, bf16[1,160,384]{2,1,0:T(8,128)(2,1)S(1)}, u32[]{:S(2)}, u32[]{:S(2)}) collective-permute-start(bf16[1,160,384]{2,1,0:T(8,128)(2,1)S(1)} %bitcast.43), channel_id=1, source_target_pairs={{0,16},{4,20},{8,24},{12,28},{16,0},{20,4},{24,8},{28,12},{1,17},{... | collective-permute-start | bytes 368648 | tf_op jit(solution)/shard_map/ppermute | solution.py:19
  10.3 6.7 %collective-permute-start.1 = (bf16[240,192]{1,0:T(8,128)(2,1)S(1)}, bf16[240,192]{1,0:T(8,128)(2,1)S(1)}, u32[]{:S(2)}, u32[]{:S(2)}) collective-permute-start(bf16[240,192]{1,0:T(8,128)(2,1)S(1)} %get-tuple-element.291), channel_id=1, source_target_pairs={{0,1},{1,0},{2,3},{3,2},{4,5},{5,4},{6,7},{7,6},{8,9},{9,8},{10,11... | collective-permute-start | bytes 276488 | tf_op jit(solution)/shard_map/ppermute | solution.py:19
  16.2 7.4 %collective-permute-start.4 = (bf16[2,160,384]{2,1,0:T(8,128)(2,1)S(1)}, bf16[2,160,384]{2,1,0:T(8,128)(2,1)S(1)}, u32[]{:S(2)}, u32[]{:S(2)}) collective-permute-start(bf16[2,160,384]{2,1,0:T(8,128)(2,1)S(1)} %pad_maximum_fusion.12), channel_id=1, source_target_pairs={{0,8},{4,12},{8,0},{12,4},{16,24},{20,28},{24,16},{28,20},{1,9},{5... | collective-permute-start | bytes 737288 | tf_op jit(solution)/shard_map/ppermute | solution.py:19
  23.8 6.7 %collective-permute-start.9 = (bf16[4,80,384]{2,1,0:T(8,128)(2,1)S(1)}, bf16[4,80,384]{2,1,0:T(8,128)(2,1)S(1)}, u32[]{:S(2)}, u32[]{:S(2)}) collective-permute-start(bf16[4,80,384]{2,1,0:T(8,128)(2,1)S(1)} %get-tuple-element.278), channel_id=1, source_target_pairs={{0,4},{4,0},{8,12},{12,8},{16,20},{20,16},{24,28},{28,24},{1,5},{5... | collective-permute-start | bytes 737288 | tf_op jit(solution)/shard_map/ppermute | solution.py:19
  25.1 7.0 %collective-permute-start.8 = (bf16[4,80,384]{2,1,0:T(8,128)(2,1)S(1)}, bf16[4,80,384]{2,1,0:T(8,128)(2,1)S(1)}, u32[]{:S(2)}, u32[]{:S(2)}) collective-permute-start(bf16[4,80,384]{2,1,0:T(8,128)(2,1)S(1)} %get-tuple-element.279), channel_id=1, source_target_pairs={{0,2},{1,3},{2,0},{3,1},{4,6},{5,7},{6,4},{7,5},{8,10},{9,11},{10,... | collective-permute-start | bytes 737288 | tf_op jit(solution)/shard_map/ppermute | solution.py:19
  26.6 6.7 %collective-permute-start.7 = (bf16[1,80,384]{2,1,0:T(8,128)(2,1)S(1)}, bf16[1,80,384]{2,1,0:T(8,128)(2,1)S(1)}, u32[]{:S(2)}, u32[]{:S(2)}) collective-permute-start(bf16[1,80,384]{2,1,0:T(8,128)(2,1)S(1)} %maximum_bitcast_fusion), channel_id=1, source_target_pairs={{0,2},{1,3},{2,0},{3,1},{4,6},{5,7},{6,4},{7,5},{8,10},{9,11},{10,... | collective-permute-start | bytes 184328 | tf_op jit(solution)/shard_map/ppermute | solution.py:19
  27.2 12.1 %collective-permute-start.6 = (bf16[1,160,384]{2,1,0:T(8,128)(2,1)S(1)}, bf16[1,160,384]{2,1,0:T(8,128)(2,1)S(1)}, u32[]{:S(2)}, u32[]{:S(2)}) collective-permute-start(bf16[1,160,384]{2,1,0:T(8,128)(2,1)S(1)} %slice_bitcast_fusion.1), channel_id=1, source_target_pairs={{0,16},{4,20},{8,24},{12,28},{16,0},{20,4},{24,8},{28,12},{1,17},{... | collective-permute-start | bytes 368648 | tf_op jit(solution)/shard_map/ppermute | solution.py:19
  30.4 11.1 %collective-permute-start.5 = (bf16[1,48,1536]{2,1,0:T(8,128)(2,1)S(1)}, bf16[1,48,1536]{2,1,0:T(8,128)(2,1)S(1)}, u32[]{:S(2)}, u32[]{:S(2)}) collective-permute-start(bf16[1,48,1536]{2,1,0:T(8,128)(2,1)S(1)} %maximum_select_fusion.1), channel_id=1, source_target_pairs={{0,16},{4,20},{8,24},{12,28},{16,0},{20,4},{24,8},{28,12},{1,17},{... | collective-permute-start | bytes 442376 | tf_op jit(solution)/shard_map/ppermute | solution.py:19
  30.5 14.5 %collective-permute-start.14 = (bf16[8,80,384]{2,1,0:T(8,128)(2,1)S(1)}, bf16[8,80,384]{2,1,0:T(8,128)(2,1)S(1)}, u32[]{:S(2)}, u32[]{:S(2)}) collective-permute-start(bf16[8,80,384]{2,1,0:T(8,128)(2,1)S(1)} %pad_maximum_fusion.5), channel_id=1, source_target_pairs={{0,2},{1,3},{2,0},{3,1},{4,6},{5,7},{6,4},{7,5},{8,10},{9,11},{10,... | collective-permute-start | bytes 1474568 | tf_op jit(solution)/shard_map/ppermute | solution.py:19
  32.1 12.7 %collective-permute-start.13 = (bf16[8,80,384]{2,1,0:T(8,128)(2,1)S(1)}, bf16[8,80,384]{2,1,0:T(8,128)(2,1)S(1)}, u32[]{:S(2)}, u32[]{:S(2)}) collective-permute-start(bf16[8,80,384]{2,1,0:T(8,128)(2,1)S(1)} %pad_maximum_fusion.4), channel_id=1, source_target_pairs={{0,4},{4,0},{8,12},{12,8},{16,20},{20,16},{24,28},{28,24},{1,5},{5... | collective-permute-start | bytes 1474568 | tf_op jit(solution)/shard_map/ppermute | solution.py:19
  41.6 13.3 %collective-permute-start.10 = (bf16[2,48,1536]{2,1,0:T(8,128)(2,1)S(1)}, bf16[2,48,1536]{2,1,0:T(8,128)(2,1)S(1)}, u32[]{:S(2)}, u32[]{:S(2)}) collective-permute-start(bf16[2,48,1536]{2,1,0:T(8,128)(2,1)S(1)} %pad_maximum_fusion.9), channel_id=1, source_target_pairs={{0,8},{4,12},{8,0},{12,4},{16,24},{20,28},{24,16},{28,20},{1,9},{5... | collective-permute-start | bytes 884744 | tf_op jit(solution)/shard_map/ppermute | solution.py:19
  42.9 4.9 %collective-permute-start.12 = (bf16[2,80,384]{2,1,0:T(8,128)(2,1)S(1)}, bf16[2,80,384]{2,1,0:T(8,128)(2,1)S(1)}, u32[]{:S(2)}, u32[]{:S(2)}) collective-permute-start(bf16[2,80,384]{2,1,0:T(8,128)(2,1)S(1)} %pad_maximum_fusion.18), channel_id=1, source_target_pairs={{0,4},{4,0},{8,12},{12,8},{16,20},{20,16},{24,28},{28,24},{1,5},{5... | collective-permute-start | bytes 368648 | tf_op jit(solution)/shard_map/ppermute | solution.py:19
  43.4 11.5 %collective-permute-start.11 = (bf16[2,160,384]{2,1,0:T(8,128)(2,1)S(1)}, bf16[2,160,384]{2,1,0:T(8,128)(2,1)S(1)}, u32[]{:S(2)}, u32[]{:S(2)}) collective-permute-start(bf16[2,160,384]{2,1,0:T(8,128)(2,1)S(1)} %pad_maximum_fusion.13), channel_id=1, source_target_pairs={{0,8},{4,12},{8,0},{12,4},{16,24},{20,28},{24,16},{28,20},{1,9},{5... | collective-permute-start | bytes 737288 | tf_op jit(solution)/shard_map/ppermute | solution.py:19
  44.9 18.1 %collective-permute-start.18 = (bf16[16,80,384]{2,1,0:T(8,128)(2,1)S(1)}, bf16[16,80,384]{2,1,0:T(8,128)(2,1)S(1)}, u32[]{:S(2)}, u32[]{:S(2)}) collective-permute-start(bf16[16,80,384]{2,1,0:T(8,128)(2,1)S(1)} %pad_maximum_fusion.refs_3_.refs_0_), channel_id=1, source_target_pairs={{0,1},{1,0},{2,3},{3,2},{4,5},{5,4},{6,7},{7,6},{8,9},{9,8},{10,11... | collective-permute-start | bytes 2949128 | tf_op jit(solution)/shard_map/ppermute | solution.py:19
  45.1 17.9 %collective-permute-start.19 = (bf16[16,80,384]{2,1,0:T(8,128)(2,1)S(1)}, bf16[16,80,384]{2,1,0:T(8,128)(2,1)S(1)}, u32[]{:S(2)}, u32[]{:S(2)}) collective-permute-start(bf16[16,80,384]{2,1,0:T(8,128)(2,1)S(1)} %pad_maximum_fusion.1.refs_5_.refs_2_), channel_id=1, source_target_pairs={{0,1},{1,0},{2,3},{3,2},{4,5},{5,4},{6,7},{7,6},{8,9},{9,8},{10,11... | collective-permute-start | bytes 2949128 | tf_op jit(solution)/shard_map/ppermute | solution.py:19
  55.1 26.7 %collective-permute-start.17 = (bf16[4,80,384]{2,1,0:T(8,128)(2,1)S(1)}, bf16[4,80,384]{2,1,0:T(8,128)(2,1)S(1)}, u32[]{:S(2)}, u32[]{:S(2)}) collective-permute-start(bf16[4,80,384]{2,1,0:T(8,128)(2,1)S(1)} %pad_maximum_fusion.14), channel_id=1, source_target_pairs={{0,16},{4,20},{8,24},{12,28},{16,0},{20,4},{24,8},{28,12},{1,17},{... | collective-permute-start | bytes 737288 | tf_op jit(solution)/shard_map/ppermute | solution.py:19
  58.4 23.4 %collective-permute-start.16 = (bf16[4,160,384]{2,1,0:T(8,128)(2,1)S(1)}, bf16[4,160,384]{2,1,0:T(8,128)(2,1)S(1)}, u32[]{:S(2)}, u32[]{:S(2)}) collective-permute-start(bf16[4,160,384]{2,1,0:T(8,128)(2,1)S(1)} %pad_maximum_fusion.6), channel_id=1, source_target_pairs={{0,4},{4,0},{8,12},{12,8},{16,20},{20,16},{24,28},{28,24},{1,5},{5... | collective-permute-start | bytes 1474568 | tf_op jit(solution)/shard_map/ppermute | solution.py:19
  58.9 22.9 %collective-permute-start.15 = (bf16[4,48,1536]{2,1,0:T(8,128)(2,1)S(1)}, bf16[4,48,1536]{2,1,0:T(8,128)(2,1)S(1)}, u32[]{:S(2)}, u32[]{:S(2)}) collective-permute-start(bf16[4,48,1536]{2,1,0:T(8,128)(2,1)S(1)} %pad_maximum_fusion.2), channel_id=1, source_target_pairs={{0,2},{1,3},{2,0},{3,1},{4,6},{5,7},{6,4},{7,5},{8,10},{9,11},{10,... | collective-permute-start | bytes 1769480 | tf_op jit(solution)/shard_map/ppermute | solution.py:19
  82.6 21.4 %collective-permute-start.22 = (bf16[8,80,384]{2,1,0:T(8,128)(2,1)}, bf16[8,80,384]{2,1,0:T(8,128)(2,1)S(1)}, u32[]{:S(2)}, u32[]{:S(2)}) collective-permute-start(bf16[8,80,384]{2,1,0:T(8,128)(2,1)} %get-tuple-element.287), channel_id=1, source_target_pairs={{0,8},{4,12},{8,0},{12,4},{16,24},{20,28},{24,16},{28,20},{1,9},{5... | collective-permute-start | bytes 1474568 | tf_op jit(solution)/shard_map/ppermute | solution.py:19
  84.5 21.7 %collective-permute-start.21 = (bf16[8,160,384]{2,1,0:T(8,128)(2,1)S(1)}, bf16[8,160,384]{2,1,0:T(8,128)(2,1)S(1)}, u32[]{:S(2)}, u32[]{:S(2)}) collective-permute-start(bf16[8,160,384]{2,1,0:T(8,128)(2,1)S(1)} %get-tuple-element.275), channel_id=1, source_target_pairs={{0,2},{1,3},{2,0},{3,1},{4,6},{5,7},{6,4},{7,5},{8,10},{9,11},{10,... | collective-permute-start | bytes 2949128 | tf_op jit(solution)/shard_map/ppermute | solution.py:19
  86.1 25.6 %collective-permute-start.20 = (bf16[8,48,1536]{2,1,0:T(8,128)(2,1)S(1)}, bf16[8,48,1536]{2,1,0:T(8,128)(2,1)S(1)}, u32[]{:S(2)}, u32[]{:S(2)}) collective-permute-start(bf16[8,48,1536]{2,1,0:T(8,128)(2,1)S(1)} %get-tuple-element.267), channel_id=1, source_target_pairs={{0,4},{4,0},{8,12},{12,8},{16,20},{20,16},{24,28},{28,24},{1,5},{5... | collective-permute-start | bytes 3538952 | tf_op jit(solution)/shard_map/ppermute | solution.py:19
  112.8 10.1 %collective-permute-start.23 = (bf16[16,48,1536]{2,1,0:T(8,128)(2,1)}, bf16[16,48,1536]{2,1,0:T(8,128)(2,1)}, u32[]{:S(2)}, u32[]{:S(2)}) collective-permute-start(bf16[16,48,1536]{2,1,0:T(8,128)(2,1)} %constant_dynamic-update-slice_fusion.11.refs_0_), channel_id=1, source_target_pairs={{0,1},{1,0},{2,3},{3,2},{4,5},{5,4},{6,7},{7,6},{8,9},{9,8},{10,11... | collective-permute-start | bytes 7077896 | tf_op jit(solution)/shard_map/ppermute | solution.py:19
  113.0 8.5 %collective-permute-start.24 = (bf16[16,160,384]{2,1,0:T(8,128)(2,1)S(1)}, bf16[16,160,384]{2,1,0:T(8,128)(2,1)S(1)}, u32[]{:S(2)}, u32[]{:S(2)}) collective-permute-start(bf16[16,160,384]{2,1,0:T(8,128)(2,1)S(1)} %constant_dynamic-update-slice_fusion.14.refs_2_), channel_id=1, source_target_pairs={{0,1},{1,0},{2,3},{3,2},{4,5},{5,4},{6,7},{7,6},{8,9},{9,8},{10,11... | collective-permute-start | bytes 5898248 | tf_op jit(solution)/shard_map/ppermute | solution.py:19
  114.2 7.3 %collective-permute-start.25 = (bf16[16,80,384]{2,1,0:T(8,128)(2,1)S(1)}, bf16[16,80,384]{2,1,0:T(8,128)(2,1)S(1)}, u32[]{:S(2)}, u32[]{:S(2)}) collective-permute-start(bf16[16,80,384]{2,1,0:T(8,128)(2,1)S(1)} %constant_dynamic-update-slice_fusion.17.refs_4_), channel_id=1, source_target_pairs={{0,1},{1,0},{2,3},{3,2},{4,5},{5,4},{6,7},{7,6},{8,9},{9,8},{10,11... | collective-permute-start | bytes 2949128 | tf_op jit(solution)/shard_map/ppermute | solution.py:19
  183.2 9.0 %collective-permute-start.26 = (bf16[16,48,1536]{2,1,0:T(8,128)(2,1)}, bf16[16,48,1536]{2,1,0:T(8,128)(2,1)S(1)}, u32[]{:S(2)}, u32[]{:S(2)}) collective-permute-start(bf16[16,48,1536]{2,1,0:T(8,128)(2,1)} %get-tuple-element.162), channel_id=1, source_target_pairs={{0,1},{1,0},{2,3},{3,2},{4,5},{5,4},{6,7},{7,6},{8,9},{9,8},{10,11... | collective-permute-start | bytes 7077896 | tf_op jit(solution)/shard_map/ppermute | solution.py:19
  183.4 8.8 %collective-permute-start.27 = (bf16[16,160,384]{2,1,0:T(8,128)(2,1)}, bf16[16,160,384]{2,1,0:T(8,128)(2,1)S(1)}, u32[]{:S(2)}, u32[]{:S(2)}) collective-permute-start(bf16[16,160,384]{2,1,0:T(8,128)(2,1)} %get-tuple-element.163), channel_id=1, source_target_pairs={{0,1},{1,0},{2,3},{3,2},{4,5},{5,4},{6,7},{7,6},{8,9},{9,8},{10,11... | collective-permute-start | bytes 5898248 | tf_op jit(solution)/shard_map/ppermute | solution.py:19
  183.8 8.5 %collective-permute-start.28 = (bf16[16,80,384]{2,1,0:T(8,128)(2,1)}, bf16[16,80,384]{2,1,0:T(8,128)(2,1)S(1)}, u32[]{:S(2)}, u32[]{:S(2)}) collective-permute-start(bf16[16,80,384]{2,1,0:T(8,128)(2,1)} %get-tuple-element.164), channel_id=1, source_target_pairs={{0,1},{1,0},{2,3},{3,2},{4,5},{5,4},{6,7},{7,6},{8,9},{9,8},{10,11... | collective-permute-start | bytes 2949128 | tf_op jit(solution)/shard_map/ppermute | solution.py:19
  193.3 22.0 %collective-permute-start.29 = (bf16[8,80,384]{2,1,0:T(8,128)(2,1)}, bf16[8,80,384]{2,1,0:T(8,128)(2,1)}, u32[]{:S(2)}, u32[]{:S(2)}) collective-permute-start(bf16[8,80,384]{2,1,0:T(8,128)(2,1)} %get-tuple-element.253), channel_id=1, source_target_pairs={{0,8},{4,12},{8,0},{12,4},{16,24},{20,28},{24,16},{28,20},{1,9},{5... | collective-permute-start | bytes 1474568 | tf_op jit(solution)/shard_map/ppermute | solution.py:19
  195.3 29.7 %collective-permute-start.31 = (bf16[8,160,384]{2,1,0:T(8,128)(2,1)}, bf16[8,160,384]{2,1,0:T(8,128)(2,1)S(1)}, u32[]{:S(2)}, u32[]{:S(2)}) collective-permute-start(bf16[8,160,384]{2,1,0:T(8,128)(2,1)} %get-tuple-element.243), channel_id=1, source_target_pairs={{0,2},{1,3},{2,0},{3,1},{4,6},{5,7},{6,4},{7,5},{8,10},{9,11},{10,... | collective-permute-start | bytes 2949128 | tf_op jit(solution)/shard_map/ppermute | solution.py:19
  197.6 28.0 %collective-permute-start.30 = (bf16[8,48,1536]{2,1,0:T(8,128)(2,1)S(1)}, bf16[8,48,1536]{2,1,0:T(8,128)(2,1)S(1)}, u32[]{:S(2)}, u32[]{:S(2)}) collective-permute-start(bf16[8,48,1536]{2,1,0:T(8,128)(2,1)S(1)} %get-tuple-element.240), channel_id=1, source_target_pairs={{0,4},{4,0},{8,12},{12,8},{16,20},{20,16},{24,28},{28,24},{1,5},{5... | collective-permute-start | bytes 3538952 | tf_op jit(solution)/shard_map/ppermute | solution.py:19
  216.5 22.7 %collective-permute-start.34 = (bf16[4,80,384]{2,1,0:T(8,128)(2,1)S(1)}, bf16[4,80,384]{2,1,0:T(8,128)(2,1)S(1)}, u32[]{:S(2)}, u32[]{:S(2)}) collective-permute-start(bf16[4,80,384]{2,1,0:T(8,128)(2,1)S(1)} %get-tuple-element.265), channel_id=1, source_target_pairs={{0,16},{4,20},{8,24},{12,28},{16,0},{20,4},{24,8},{28,12},{1,17},{... | collective-permute-start | bytes 737288 | tf_op jit(solution)/shard_map/ppermute | solution.py:19
  225.8 13.4 %collective-permute-start.33 = (bf16[4,160,384]{2,1,0:T(8,128)(2,1)S(1)}, bf16[4,160,384]{2,1,0:T(8,128)(2,1)S(1)}, u32[]{:S(2)}, u32[]{:S(2)}) collective-permute-start(bf16[4,160,384]{2,1,0:T(8,128)(2,1)S(1)} %get-tuple-element.251), channel_id=1, source_target_pairs={{0,4},{4,0},{8,12},{12,8},{16,20},{20,16},{24,28},{28,24},{1,5},{5... | collective-permute-start | bytes 1474568 | tf_op jit(solution)/shard_map/ppermute | solution.py:19
  227.7 14.3 %collective-permute-start.32 = (bf16[4,48,1536]{2,1,0:T(8,128)(2,1)S(1)}, bf16[4,48,1536]{2,1,0:T(8,128)(2,1)S(1)}, u32[]{:S(2)}, u32[]{:S(2)}) collective-permute-start(bf16[4,48,1536]{2,1,0:T(8,128)(2,1)S(1)} %get-tuple-element.244), channel_id=1, source_target_pairs={{0,2},{1,3},{2,0},{3,1},{4,6},{5,7},{6,4},{7,5},{8,10},{9,11},{10,... | collective-permute-start | bytes 1769480 | tf_op jit(solution)/shard_map/ppermute | solution.py:19
  242.0 3.6 %collective-permute-start.35 = (bf16[16,80,384]{2,1,0:T(8,128)(2,1)}, bf16[16,80,384]{2,1,0:T(8,128)(2,1)S(1)}, u32[]{:S(2)}, u32[]{:S(2)}) collective-permute-start(bf16[16,80,384]{2,1,0:T(8,128)(2,1)} %get-tuple-element.210), channel_id=1, source_target_pairs={{0,1},{1,0},{2,3},{3,2},{4,5},{5,4},{6,7},{7,6},{8,9},{9,8},{10,11... | collective-permute-start | bytes 2949128 | tf_op jit(solution)/shard_map/ppermute | solution.py:19
  242.0 4.2 %collective-permute-start.36 = (bf16[16,80,384]{2,1,0:T(8,128)(2,1)}, bf16[16,80,384]{2,1,0:T(8,128)(2,1)S(1)}, u32[]{:S(2)}, u32[]{:S(2)}) collective-permute-start(bf16[16,80,384]{2,1,0:T(8,128)(2,1)} %get-tuple-element.211), channel_id=1, source_target_pairs={{0,1},{1,0},{2,3},{3,2},{4,5},{5,4},{6,7},{7,6},{8,9},{9,8},{10,11... | collective-permute-start | bytes 2949128 | tf_op jit(solution)/shard_map/ppermute | solution.py:19
  242.5 19.8 %collective-permute-start.41 = (bf16[2,80,384]{2,1,0:T(8,128)(2,1)S(1)}, bf16[2,80,384]{2,1,0:T(8,128)(2,1)S(1)}, u32[]{:S(2)}, u32[]{:S(2)}) collective-permute-start(bf16[2,80,384]{2,1,0:T(8,128)(2,1)S(1)} %get-tuple-element.273), channel_id=1, source_target_pairs={{0,4},{4,0},{8,12},{12,8},{16,20},{20,16},{24,28},{28,24},{1,5},{5... | collective-permute-start | bytes 368648 | tf_op jit(solution)/shard_map/ppermute | solution.py:19
  243.3 19.1 %collective-permute-start.40 = (bf16[2,160,384]{2,1,0:T(8,128)(2,1)S(1)}, bf16[2,160,384]{2,1,0:T(8,128)(2,1)S(1)}, u32[]{:S(2)}, u32[]{:S(2)}) collective-permute-start(bf16[2,160,384]{2,1,0:T(8,128)(2,1)S(1)} %get-tuple-element.259), channel_id=1, source_target_pairs={{0,8},{4,12},{8,0},{12,4},{16,24},{20,28},{24,16},{28,20},{1,9},{5... | collective-permute-start | bytes 737288 | tf_op jit(solution)/shard_map/ppermute | solution.py:19
  244.3 18.0 %collective-permute-start.39 = (bf16[2,48,1536]{2,1,0:T(8,128)(2,1)S(1)}, bf16[2,48,1536]{2,1,0:T(8,128)(2,1)S(1)}, u32[]{:S(2)}, u32[]{:S(2)}) collective-permute-start(bf16[2,48,1536]{2,1,0:T(8,128)(2,1)S(1)} %get-tuple-element.255), channel_id=1, source_target_pairs={{0,8},{4,12},{8,0},{12,4},{16,24},{20,28},{24,16},{28,20},{1,9},{5... | collective-permute-start | bytes 884744 | tf_op jit(solution)/shard_map/ppermute | solution.py:19
  246.4 15.9 %collective-permute-start.38 = (bf16[8,80,384]{2,1,0:T(8,128)(2,1)S(1)}, bf16[8,80,384]{2,1,0:T(8,128)(2,1)S(1)}, u32[]{:S(2)}, u32[]{:S(2)}) collective-permute-start(bf16[8,80,384]{2,1,0:T(8,128)(2,1)S(1)} %get-tuple-element.247), channel_id=1, source_target_pairs={{0,2},{1,3},{2,0},{3,1},{4,6},{5,7},{6,4},{7,5},{8,10},{9,11},{10,... | collective-permute-start | bytes 1474568 | tf_op jit(solution)/shard_map/ppermute | solution.py:19
  247.9 14.4 %collective-permute-start.37 = (bf16[8,80,384]{2,1,0:T(8,128)(2,1)S(1)}, bf16[8,80,384]{2,1,0:T(8,128)(2,1)S(1)}, u32[]{:S(2)}, u32[]{:S(2)}) collective-permute-start(bf16[8,80,384]{2,1,0:T(8,128)(2,1)S(1)} %get-tuple-element.249), channel_id=1, source_target_pairs={{0,4},{4,0},{8,12},{12,8},{16,20},{20,16},{24,28},{28,24},{1,5},{5... | collective-permute-start | bytes 1474568 | tf_op jit(solution)/shard_map/ppermute | solution.py:19
  262.4 6.7 %collective-permute-start.44 = (bf16[1,80,384]{2,1,0:T(8,128)(2,1)S(1)}, bf16[1,80,384]{2,1,0:T(8,128)(2,1)S(1)}, u32[]{:S(2)}, u32[]{:S(2)}) collective-permute-start(bf16[1,80,384]{2,1,0:T(8,128)(2,1)S(1)} %add_convert_fusion.34), channel_id=1, source_target_pairs={{0,2},{1,3},{2,0},{3,1},{4,6},{5,7},{6,4},{7,5},{8,10},{9,11},{10,... | collective-permute-start | bytes 184328 | tf_op jit(solution)/shard_map/ppermute | solution.py:19
  263.4 11.7 %collective-permute-start.45 = (bf16[1,160,384]{2,1,0:T(8,128)(2,1)S(1)}, bf16[1,160,384]{2,1,0:T(8,128)(2,1)S(1)}, u32[]{:S(2)}, u32[]{:S(2)}) collective-permute-start(bf16[1,160,384]{2,1,0:T(8,128)(2,1)S(1)} %add_convert_fusion.30), channel_id=1, source_target_pairs={{0,16},{4,20},{8,24},{12,28},{16,0},{20,4},{24,8},{28,12},{1,17},{... | collective-permute-start | bytes 368648 | tf_op jit(solution)/shard_map/ppermute | solution.py:19
  265.4 12.0 %collective-permute-start.47 = (bf16[1,48,1536]{2,1,0:T(8,128)(2,1)S(1)}, bf16[1,48,1536]{2,1,0:T(8,128)(2,1)S(1)}, u32[]{:S(2)}, u32[]{:S(2)}) collective-permute-start(bf16[1,48,1536]{2,1,0:T(8,128)(2,1)S(1)} %add_convert_fusion.26), channel_id=1, source_target_pairs={{0,16},{4,20},{8,24},{12,28},{16,0},{20,4},{24,8},{28,12},{1,17},{... | collective-permute-start | bytes 442376 | tf_op jit(solution)/shard_map/ppermute | solution.py:19
  266.6 11.9 %collective-permute-start.43 = (bf16[4,80,384]{2,1,0:T(8,128)(2,1)S(1)}, bf16[4,80,384]{2,1,0:T(8,128)(2,1)S(1)}, u32[]{:S(2)}, u32[]{:S(2)}) collective-permute-start(bf16[4,80,384]{2,1,0:T(8,128)(2,1)S(1)} %get-tuple-element.260), channel_id=1, source_target_pairs={{0,4},{4,0},{8,12},{12,8},{16,20},{20,16},{24,28},{28,24},{1,5},{5... | collective-permute-start | bytes 737288 | tf_op jit(solution)/shard_map/ppermute | solution.py:19
  267.9 10.6 %collective-permute-start.42 = (bf16[4,80,384]{2,1,0:T(8,128)(2,1)S(1)}, bf16[4,80,384]{2,1,0:T(8,128)(2,1)S(1)}, u32[]{:S(2)}, u32[]{:S(2)}) collective-permute-start(bf16[4,80,384]{2,1,0:T(8,128)(2,1)S(1)} %get-tuple-element.262), channel_id=1, source_target_pairs={{0,2},{1,3},{2,0},{3,1},{4,6},{5,7},{6,4},{7,5},{8,10},{9,11},{10,... | collective-permute-start | bytes 737288 | tf_op jit(solution)/shard_map/ppermute | solution.py:19
  278.7 8.4 %collective-permute-start.49 = (bf16[2,160,384]{2,1,0:T(8,128)(2,1)S(1)}, bf16[2,160,384]{2,1,0:T(8,128)(2,1)S(1)}, u32[]{:S(2)}, u32[]{:S(2)}) collective-permute-start(bf16[2,160,384]{2,1,0:T(8,128)(2,1)S(1)} %get-tuple-element.256), channel_id=1, source_target_pairs={{0,8},{4,12},{8,0},{12,4},{16,24},{20,28},{24,16},{28,20},{1,9},{5... | collective-permute-start | bytes 737288 | tf_op jit(solution)/shard_map/ppermute | solution.py:19
  287.1 8.5 %collective-permute-start.50 = (bf16[1,160,384]{2,1,0:T(8,128)(2,1)S(1)}, bf16[1,160,384]{2,1,0:T(8,128)(2,1)S(1)}, u32[]{:S(2)}, u32[]{:S(2)}) collective-permute-start(bf16[1,160,384]{2,1,0:T(8,128)(2,1)S(1)} %add_convert_fusion.28), channel_id=1, source_target_pairs={{0,16},{4,20},{8,24},{12,28},{16,0},{20,4},{24,8},{28,12},{1,17},{... | collective-permute-start | bytes 368648 | tf_op jit(solution)/shard_map/ppermute | solution.py:19
  (23 other events, 123.9 us)
